TPU v7x, 32 devices: a whole 2x2x4 slice. The times are simulated.
32 devices in a mesh: ctx: 8 (over z, x), rep: 4 (over y, core).
Axes of the slice: x: 2, y: 2, z: 4, core: 2. Of those that a mesh axis runs over, the one named last changes fastest.
Arguments:
- tokens: bfloat16 [4, 1024, 2880], P('rep', 'ctx'), may hold values from -6 to 6
- router_w: bfloat16 [2880, 32], replicated, may hold values from -0.109375 to 0.109375
- router_b: float32 [32], replicated, may hold values from -4 to 4
- hidden: bfloat16 [4, 1024, 4, 1536], P('rep', 'ctx'), may hold values from -6 to 6
- teacher_idx: int32 [4, 1024, 4], P('rep', 'ctx'), may hold values from 0 to 31, all different within a row
- merge_map: int32 [32], replicated, may hold values from 0 to 15, as said below
- merge_coef: float32 [32], replicated, may hold values from 0.3 to 1.5
- source_w: bfloat16 [32, 1536, 1536], P(None, 'ctx'), may hold values from -0.15625 to 0.15625
- out_grad: bfloat16 [4, 1024, 1536], P('rep', 'ctx'), may hold values from -6 to 6
Outputs:
- mixed: bfloat16 [4, 1024, 1536], P('rep', 'ctx')
- hidden_grad: bfloat16 [4, 1024, 4, 1536], P('rep', 'ctx')
- token_grad: bfloat16 [4, 1024, 2880], P('rep', 'ctx')
- router_w_grad: float32 [2880, 32], replicated
- router_b_grad: float32 [32], replicated
- coef_grad: float32 [32], replicated
- source_w_grad: float32 [32, 1536, 1536], P(None, 'ctx', 'rep')
Inputs may be any that keep to these rules, and one draw needn't show every extreme that they name: `teacher_idx`: each token names 4 different experts. `merge_map`: each of the 16 combinations takes exactly two of the 32 experts.
All inputs are finite; a program needn't handle non-finite values.
Results may differ from a plain program's by a relative error of at most 0.0064.
Values may be sent and summed in bfloat16 or wider, within the bound.
No kernel may reach another device: no remote copies, remote signals or barrier semaphores. Data moves between devices by JAX's collectives and lax.ppermute only.
A program may use at most 128 MiB of HBM per device.

v0:
```python
import math

import jax
import jax.numpy as jnp
from jax import lax
from jax.sharding import PartitionSpec as P

MERGED = 16


def expert_rows(rows_hidden, rows_grad, rows_member, lane_weights):
    row_count = rows_hidden.shape[0]
    out_rows = jnp.zeros((row_count, lane_weights.shape[1]), jnp.float32)
    back_rows = jnp.zeros((row_count, lane_weights.shape[2]), jnp.float32)
    grad_list = []
    for member_now in range(lane_weights.shape[0]):
        weight = lane_weights[member_now]
        selected = (rows_member == member_now)[:, None]
        forward = lax.dot_general(
            rows_hidden, weight, (((1,), (1,)), ((), ())), preferred_element_type=jnp.float32
        )
        out_rows = jnp.where(selected, forward, out_rows)
        backward = jnp.dot(rows_grad, weight, preferred_element_type=jnp.float32)
        back_rows = jnp.where(selected, backward, back_rows)
        masked = jnp.where(selected, rows_grad, jnp.zeros_like(rows_grad))
        grad_list.append(
            lax.dot_general(
                masked, rows_hidden, (((0,), (0,)), ((), ())), preferred_element_type=jnp.float32
            )
        )
    return (out_rows, back_rows, jnp.stack(grad_list))


def on_device(
    tokens, router_w, router_b, hidden, teacher_idx, merge_map, merge_coef, source_w, out_grad
):
    ctx_count = lax.axis_size("ctx")
    rep_count = lax.axis_size("rep")
    tok_count = tokens.shape[1]
    feature_count = tokens.shape[2]
    top_count = teacher_idx.shape[2]
    hidden_width = hidden.shape[3]
    out_width = out_grad.shape[2]
    source_count = router_w.shape[1]
    row_share = source_w.shape[1]
    per_lane = max(1, MERGED // ctx_count)
    copies = max(1, ctx_count // MERGED)
    capacity = 5 * tok_count * top_count // (4 * ctx_count)
    slot_count = tok_count * top_count
    grad_scale = 1.0 / math.sqrt(tok_count * ctx_count * rep_count)
    flat_x = tokens.reshape(tok_count, feature_count)
    logits = jnp.dot(flat_x, router_w, preferred_element_type=jnp.float32) + router_b
    choice_ids = teacher_idx.reshape(tok_count, top_count)
    pick_table = choice_ids[:, :, None] == jnp.arange(source_count, dtype=jnp.int32)[None, None, :]
    pick_float = pick_table.astype(jnp.float32)
    chosen = jnp.sum(pick_float * logits[:, None, :], axis=2)
    raised = jnp.exp(chosen)
    gate_probs = raised / jnp.sum(raised, axis=1, keepdims=True)
    merged_id = jnp.sum(jnp.where(pick_table, merge_map[None, None, :], 0), axis=2)
    position = lax.axis_index("ctx") * tok_count + jnp.arange(tok_count, dtype=jnp.int32)
    lane_id = merged_id // per_lane * copies + (position % copies)[:, None]
    member_id = (merged_id % per_lane).reshape(-1)
    lane_flat = lane_id.reshape(-1)
    onehot = (lane_flat[:, None] == jnp.arange(ctx_count, dtype=jnp.int32)[None, :]).astype(
        jnp.int32
    )
    before = jnp.cumsum(onehot, axis=0) - onehot
    slot_rank = jnp.sum(before * onehot, axis=1)
    is_kept = slot_rank < capacity
    slot_index = jnp.where(is_kept, lane_flat * capacity + slot_rank, ctx_count * capacity)
    slot_source = (
        jnp.full((ctx_count * capacity + 1,), slot_count, jnp.int32)
        .at[slot_index]
        .set(jnp.arange(slot_count, dtype=jnp.int32))[: ctx_count * capacity]
    )
    slot_grad = (gate_probs[:, :, None] * out_grad.reshape(tok_count, 1, out_width)).astype(
        jnp.bfloat16
    )
    pad_hidden = jnp.concatenate(
        [hidden.reshape(slot_count, hidden_width), jnp.zeros((1, hidden_width), jnp.bfloat16)],
        axis=0,
    )
    pad_grad = jnp.concatenate(
        [slot_grad.reshape(slot_count, out_width), jnp.zeros((1, out_width), jnp.bfloat16)], axis=0
    )
    pad_member = jnp.concatenate([member_id, jnp.zeros((1,), jnp.int32)], axis=0)
    send_hidden = pad_hidden[slot_source].reshape(ctx_count, capacity, hidden_width)
    send_grad = pad_grad[slot_source].reshape(ctx_count, capacity, out_width)
    send_member = pad_member[slot_source].reshape(ctx_count, capacity)
    lane_group = lax.axis_index("ctx") // copies
    same_group = merge_map[:, None] == merge_map[None, :]
    earlier = jnp.arange(source_count)[:, None] > jnp.arange(source_count)[None, :]
    member_rank = jnp.sum((same_group & earlier).astype(jnp.int32), axis=1)
    source_order = (
        jnp.zeros((source_count,), jnp.int32)
        .at[2 * merge_map + member_rank]
        .set(jnp.arange(source_count, dtype=jnp.int32))
    )
    picked = source_w[source_order].reshape(
        MERGED // per_lane, 2 * per_lane, row_share, hidden_width
    )
    outgoing = jnp.repeat(picked, copies, axis=0)
    arrived = lax.all_to_all(outgoing, "ctx", split_axis=0, concat_axis=2, tiled=True)
    pair_rows = arrived.reshape(per_lane, 2, row_share * ctx_count, hidden_width)
    coef_table = merge_coef[source_order].reshape(MERGED // per_lane, per_lane, 2)
    pair_coef = lax.dynamic_index_in_dim(coef_table, lane_group, 0, keepdims=False)
    lane_weights = (
        pair_coef[:, 0, None, None] * pair_rows[:, 0].astype(jnp.float32)
        + pair_coef[:, 1, None, None] * pair_rows[:, 1].astype(jnp.float32)
    ).astype(jnp.bfloat16)
    recv_hidden, recv_grad, recv_member = (
        lax.all_to_all(send_hidden, "ctx", split_axis=0, concat_axis=0, tiled=True),
        lax.all_to_all(send_grad, "ctx", split_axis=0, concat_axis=0, tiled=True),
        lax.all_to_all(send_member, "ctx", split_axis=0, concat_axis=0, tiled=True),
    )
    out_rows, back_rows, lane_grads = expert_rows(
        recv_hidden.reshape(-1, hidden_width),
        recv_grad.reshape(-1, out_width),
        recv_member.reshape(-1),
        lane_weights,
    )
    home_out, home_back = (
        lax.all_to_all(
            out_rows.astype(jnp.bfloat16).reshape(ctx_count, capacity, out_width),
            "ctx",
            split_axis=0,
            concat_axis=0,
            tiled=True,
        ),
        lax.all_to_all(
            back_rows.astype(jnp.bfloat16).reshape(ctx_count, capacity, hidden_width),
            "ctx",
            split_axis=0,
            concat_axis=0,
            tiled=True,
        ),
    )
    slot_out = jnp.concatenate(
        [home_out.reshape(-1, out_width), jnp.zeros((1, out_width), jnp.bfloat16)], axis=0
    )[slot_index].reshape(tok_count, top_count, out_width)
    hidden_grad = jnp.concatenate(
        [home_back.reshape(-1, hidden_width), jnp.zeros((1, hidden_width), jnp.bfloat16)], axis=0
    )[slot_index].reshape(1, tok_count, top_count, hidden_width)
    mixed = (
        jnp.sum(gate_probs[:, :, None] * slot_out.astype(jnp.float32), axis=1)
        .astype(jnp.bfloat16)
        .reshape(1, tok_count, out_width)
    )
    score_grad = jnp.einsum(
        "td,tkd->tk",
        out_grad.reshape(tok_count, out_width),
        slot_out,
        preferred_element_type=jnp.float32,
    )
    chosen_grad = gate_probs * (
        score_grad - jnp.sum(gate_probs * score_grad, axis=1, keepdims=True)
    )
    logit_grad = jnp.sum(pick_float * chosen_grad[:, :, None], axis=1)
    logit_half = logit_grad.astype(jnp.bfloat16)
    token_grad = (
        lax.dot_general(
            logit_half, router_w, (((1,), (1,)), ((), ())), preferred_element_type=jnp.float32
        )
        .astype(jnp.bfloat16)
        .reshape(1, tok_count, feature_count)
    )
    part_router_w = lax.dot_general(
        flat_x, logit_half, (((0,), (0,)), ((), ())), preferred_element_type=jnp.float32
    )
    part_router_b = jnp.sum(logit_grad, axis=0)
    arrived_grads = lax.all_to_all(
        lane_grads.reshape(per_lane, ctx_count, row_share, hidden_width),
        "ctx",
        split_axis=1,
        concat_axis=0,
        tiled=True,
    )
    merged_grad = (
        arrived_grads.reshape(MERGED // per_lane, copies, per_lane, row_share, hidden_width)
        .sum(axis=1)
        .reshape(MERGED, row_share, hidden_width)
    )
    source_grad = merged_grad[merge_map]
    coef_part = jnp.einsum(
        "edf,edf->e", source_grad, source_w.astype(jnp.float32), precision=lax.Precision.HIGHEST
    )
    summed = lax.psum_scatter(
        source_grad * merge_coef[:, None, None], "rep", scatter_dimension=2, tiled=True
    )
    source_w_grad = summed * grad_scale
    router_sum, bias_sum, coef_sum = lax.psum(
        (part_router_w, part_router_b, coef_part), ("ctx", "rep")
    )
    return (
        mixed,
        hidden_grad,
        token_grad,
        router_sum * grad_scale,
        bias_sum * grad_scale,
        coef_sum * grad_scale,
        source_w_grad,
    )


def solution(mesh):
    in_specs = (
        P("rep", "ctx", None),
        P(),
        P(),
        P("rep", "ctx", None, None),
        P("rep", "ctx", None),
        P(),
        P(),
        P(None, "ctx", None),
        P("rep", "ctx", None),
    )
    out_specs = (
        P("rep", "ctx", None),
        P("rep", "ctx", None, None),
        P("rep", "ctx", None),
        P(),
        P(),
        P(),
        P(None, "ctx", "rep"),
    )
    return jax.shard_map(
        on_device, mesh=mesh, in_specs=in_specs, out_specs=out_specs, check_vma=False
    )
```

profile of v0, /device:TPU:0, one launch (start us, length us, event | category | flops | bytes accessed | tf_op | source)
XLA Modules:
  0.0 1390.4 jit_solution(17182250357917047113)
XLA Ops:
  16.9 7.3 all-to-all-start
  25.0 14.5 %gather_fusion.3 = bf16[32,192,1536]{2,1,0:T(8,128)(2,1)} fusion(bf16[32,192,1536]{2,1,0:T(8,128)(2,1)} %param.16, s32[1024]{0:T(1024)S(1)} %pad_clamp_fusion.2), kind=kCustom, calls=%fused_computation.3 | custom fusion | bytes 37748864 | tf_op jit(solution)/shard_map/gather | solution.py:99
  39.5 6.1 all-to-all-start.2
  52.2 401.2 %all-to-all-done.2 = bf16[8,4,192,1536]{3,2,1,0:T(8,128)(2,1)} async-done(((bf16[8,4,192,1536]{3,2,1,0:T(8,128)(2,1)}), bf16[8,4,192,1536]{3,2,1,0:T(8,128)(2,1)}, u32[]{:S(2)}, u32[]{:S(2)}) %all-to-all-start.2) | async-done | bytes 18874400 | tf_op jit(solution)/shard_map/all_to_all | solution.py:103
  458.2 9.6 copy.48
  467.8 6.2 fusion.1
  474.0 28.6 %all-to-all-done.1 = bf16[8,80,1536]{2,1,0:T(8,128)(2,1)S(1)} async-done(((bf16[8,80,1536]{2,1,0:T(8,128)(2,1)}), bf16[8,80,1536]{2,1,0:T(8,128)(2,1)S(1)}, u32[]{:S(2)}, u32[]{:S(2)}) %all-to-all-start.1) | async-done | bytes 1966112 | tf_op jit(solution)/shard_map/all_to_all | solution.py:112
  502.6 6.4 fusion.3
  520.0 4.9 mul.128
  525.2 37.9 %all-to-all-done.3 = bf16[8,80,1536]{2,1,0:T(8,128)(2,1)S(1)} async-done(((bf16[8,80,1536]{2,1,0:T(8,128)(2,1)}), bf16[8,80,1536]{2,1,0:T(8,128)(2,1)S(1)}, u32[]{:S(2)}, u32[]{:S(2)}) %all-to-all-start.3) | async-done | bytes 1966112 | tf_op jit(solution)/shard_map/all_to_all | solution.py:123
  580.0 49.7 %all_to_all.59 = bf16[8,80,1536]{2,1,0:T(8,128)(2,1)S(1)} all-to-all(bf16[8,80,1536]{2,1,0:T(8,128)(2,1)} %bitcast.115), channel_id=1, replica_groups=mesh['ctx'=8,'rep'=4] {'ctx'}, dimensions={0} | all-to-all | bytes 3932160 | tf_op jit(solution)/shard_map/all_to_all | solution.py:113
  637.7 6.8 pad_maximum_fusion
  644.5 5.9 all-to-all-start.6
  652.1 407.3 %all-to-all-done.6 = f32[2,8,192,1536]{3,2,0,1:T(8,128)} async-done(((f32[2,8,192,1536]{3,2,0,1:T(8,128)}), f32[2,8,192,1536]{3,2,0,1:T(8,128)}, u32[]{:S(2)}, u32[]{:S(2)}) %all-to-all-start.6) | async-done | bytes 18874400 | tf_op jit(solution)/shard_map/all_to_all | solution.py:171
  1059.4 21.0 %gather_fusion.7 = f32[32,192,1536]{2,1,0:T(8,128)} fusion(f32[16,192,1536]{2,1,0:T(8,128)} %bitcast.41, s32[1024]{0:T(1024)S(1)} %pad_clamp_fusion), kind=kCustom, calls=%fused_computation.7 | custom fusion | bytes 75497600 | tf_op jit(solution)/shard_map/gather | solution.py:183
  1080.4 32.3 %broadcast_multiply_fusion = (f32[32,192,1536]{2,1,0:T(8,128)}, f32[32]{0:T(128)S(1)}) fusion(f32[32,192,1536]{2,1,0:T(8,128)} %gather_fusion.7, f32[32]{0:T(128)S(1)} %copy-done.1, bf16[32,192,1536]{2,1,0:T(8,128)(2,1)} %param.16), kind=kLoop, calls=%fused_computation.16 | loop fusion | flops 37748704 | bytes 94372096 | tf_op jit(solution)/shard_map/mul | solution.py:188
  1112.7 5.6 fusion.2
  1118.2 8.0 select_convert_fusion
  1131.2 4.9 multiply_reduce_fusion.1
  1136.1 8.3 all-reduce.7.cloned.1.call-done
  1146.3 29.1 %all-to-all-done.5 = bf16[8,80,1536]{2,1,0:T(8,128)(2,1)S(1)} async-done(((bf16[8,80,1536]{2,1,0:T(8,128)(2,1)}), bf16[8,80,1536]{2,1,0:T(8,128)(2,1)S(1)}, u32[]{:S(2)}, u32[]{:S(2)}) %all-to-all-start.5) | async-done | bytes 1966112 | tf_op jit(solution)/shard_map/all_to_all | solution.py:130
  1185.4 38.0 %all-reduce.4 = (f32[32]{0:T(128)S(1)}, f32[32]{0:T(128)S(1)}) all-reduce(f32[32]{0:T(128)S(1)} %get-tuple-element.7, f32[32]{0:T(128)S(1)} %get-tuple-element.16), channel_id=1, replica_groups=mesh['ctx'=8,'rep'=4] {'ctx','rep'}, use_global_device_ids=true, to_apply=%region_14.15 | all-reduce | flops 64 | bytes 512 | tf_op jit(solution)/shard_map/psum | solution.py:191
  1223.9 150.6 %reduce-scatter.2.cloned.1.call-done = f32[32,192,384]{2,1,0:T(8,128)} async-done(((f32[32,192,1536]{2,1,0:T(8,128)}), f32[32,192,384]{2,1,0:T(8,128)}) %reduce-scatter.2.cloned.1.call-update) | async-done | bytes 9437200 | tf_op jit(solution)/shard_map/reduce_scatter | solution.py:187
  1374.5 8.5 broadcast_multiply_fusion.1
  (103 shorter events, 76.0 us)
Async XLA Ops:
  8.0 516.9 %copy-start = (bf16[1,128,2880]{1,2,0:T(8,128)(2,1)S(1)}, bf16[1,128,2880]{1,2,0:T(8,128)(2,1)}, u32[]{:S(2)}) copy-start(bf16[1,128,2880]{1,2,0:T(8,128)(2,1)} %param.9) | copy-start | bytes 2211844
  8.0 16.1 %copy-start.12 = (s32[32]{0:T(128)S(1)}, s32[32]{0:T(128)}, u32[]{:S(2)}) copy-start(s32[32]{0:T(128)} %param.14) | copy-start | bytes 388
  16.9 22.6 %all-to-all-start = ((s32[8,1,80]{2,1,0:T(1,128)}), s32[8,1,80]{2,1,0:T(1,128)S(1)}, u32[]{:S(2)}, u32[]{:S(2)}) async-start(s32[8,1,80]{2,1,0:T(1,128)} %all_to_all.40), calls=%async_computation | async-start | bytes 8192 | tf_op jit(solution)/shard_map/all_to_all | solution.py:114
  39.5 6.1 copy-start.8
  39.5 413.8 %all-to-all-start.2 = ((bf16[8,4,192,1536]{3,2,1,0:T(8,128)(2,1)}), bf16[8,4,192,1536]{3,2,1,0:T(8,128)(2,1)}, u32[]{:S(2)}, u32[]{:S(2)}) async-start(bf16[8,4,192,1536]{3,2,1,0:T(8,128)(2,1)} %bitcast.108), calls=%async_computation.2 | async-start | bytes 37748736 | tf_op jit(solution)/shard_map/all_to_all | solution.py:103
  52.2 404.8 %copy-start.1 = (f32[32]{0:T(128)S(1)}, f32[32]{0:T(128)}, u32[]{:S(2)}) copy-start(f32[32]{0:T(128)} %param.15) | copy-start | bytes 388
  453.3 49.2 %all-to-all-start.1 = ((bf16[8,80,1536]{2,1,0:T(8,128)(2,1)}), bf16[8,80,1536]{2,1,0:T(8,128)(2,1)S(1)}, u32[]{:S(2)}, u32[]{:S(2)}) async-start(bf16[8,80,1536]{2,1,0:T(8,128)(2,1)} %bitcast.112), calls=%async_computation.1 | async-start | bytes 3932160 | tf_op jit(solution)/shard_map/all_to_all | solution.py:112
  502.6 6.4 copy-start.6
  502.6 6.4 copy-start.2
  513.7 3.9 copy-start.10
  513.7 49.4 %all-to-all-start.3 = ((bf16[8,80,1536]{2,1,0:T(8,128)(2,1)}), bf16[8,80,1536]{2,1,0:T(8,128)(2,1)S(1)}, u32[]{:S(2)}, u32[]{:S(2)}) async-start(bf16[8,80,1536]{2,1,0:T(8,128)(2,1)} %bitcast.121), calls=%async_computation.3 | async-start | bytes 3932160 | tf_op jit(solution)/shard_map/all_to_all | solution.py:123
  520.0 4.9 copy-start.9
  520.0 4.9 copy-start.13
  520.0 5.2 copy-start.11
  563.1 1.3 copy-start.4
  572.0 1.8 copy-start.5
  580.0 49.7 %copy-start.7 = (bf16[8,80,1536]{2,1,0:T(8,128)(2,1)S(1)}, bf16[8,80,1536]{2,1,0:T(8,128)(2,1)}, u32[]{:S(2)}) copy-start(bf16[8,80,1536]{2,1,0:T(8,128)(2,1)} %copy-done.6) | copy-start | bytes 5898244
  644.5 414.8 %all-to-all-start.6 = ((f32[2,8,192,1536]{3,2,0,1:T(8,128)}), f32[2,8,192,1536]{3,2,0,1:T(8,128)}, u32[]{:S(2)}, u32[]{:S(2)}) async-start(f32[2,8,192,1536]{3,2,0,1:T(8,128)} %pad_maximum_fusion), calls=%async_computation.6 | async-start | bytes 37748736 | tf_op jit(solution)/shard_map/all_to_all | solution.py:171
  650.4 494.0 %all-reduce.7.cloned.1.call-start = ((), (), s32[]{:S(2)}) async-start(), calls=%async_computation.8 | async-start | bytes 753664 | tf_op jit(solution)/shard_map/psum | solution.py:191
  651.8 722.7 %reduce-scatter.2.cloned.1.call-start = ((), (), s32[]{:S(2)}) async-start(), calls=%async_computation.9 | async-start | bytes 47185920 | tf_op jit(solution)/shard_map/reduce_scatter | solution.py:187
  1126.3 49.1 %all-to-all-start.5 = ((bf16[8,80,1536]{2,1,0:T(8,128)(2,1)}), bf16[8,80,1536]{2,1,0:T(8,128)(2,1)S(1)}, u32[]{:S(2)}, u32[]{:S(2)}) async-start(bf16[8,80,1536]{2,1,0:T(8,128)(2,1)} %bitcast.120), calls=%async_computation.5 | async-start | bytes 3932160 | tf_op jit(solution)/shard_map/all_to_all | solution.py:130
  1175.3 1.3 copy-start.3
Sparse Core Ops, SparseCore 0:
  657.2 487.1 all-reduce.6
Sparse Core Ops, SparseCore 1:
  1112.8 261.6 reduce-scatter.1
where the time goes:
time: 1390 us
  waiting for transfers between devices  1060 us (76%)
  local copies, waits for them, and re-layouts  90.1 us (6%)
  blocking collectives  87.7 us (6%)
  other arithmetic  65.8 us (5%)
  matrix products  37.2 us (3%)
  starting transfers between devices  30.8 us (2%)
  between operations  15.8 us (1%)
    all_to_all x1, waiting for transfers between devices, on_device(): lax.all_to_all(lane_grads.reshape(per_lane, ctx_count, row_share, hidden_...  407 us
    all_to_all x1, waiting for transfers between devices, on_device(): lax.all_to_all(outgoing, 'ctx', split_axis=0, concat_axis=2, tiled=True)  401 us
    reduce_scatter x1, waiting for transfers between devices, on_device(): lax.psum_scatter(source_grad * merge_coef[:, None, None], 'rep', scatter_...  151 us
    all_to_all x1, blocking collectives, on_device(): lax.all_to_all(send_grad, 'ctx', split_axis=0, concat_axis=0, tiled=True)  49.7 us
    psum x1, blocking collectives, on_device(): lax.psum((part_router_w, part_router_b, coef_part), ('ctx', 'rep'))  38 us
    all_to_all x1, waiting for transfers between devices, on_device(): lax.all_to_all(out_rows.astype(jnp.bfloat16).reshape(ctx_count, capacity,...  37.9 us
    mul x1, other arithmetic, on_device(): source_grad * merge_coef[:, None, None]  32.3 us
    all_to_all x1, waiting for transfers between devices, on_device(): lax.all_to_all(back_rows.astype(jnp.bfloat16).reshape(ctx_count, capacity...  29.1 us
  transfers between devices with their start and end apart: 8, of which 7 were waited for; matrix products, arithmetic and copies ran while one was open for 9% of the time, Pallas kernels for 0%

commit v1 on v0

--- a/solution.py
+++ b/solution.py
@@ -1,8 +1,11 @@
+import functools
 import math
 
 import jax
 import jax.numpy as jnp
 from jax import lax
+from jax.experimental import pallas as pl
+from jax.experimental.pallas import tpu as pltpu
 from jax.sharding import PartitionSpec as P
 
 MERGED = 16
@@ -202,27 +205,549 @@
     )
 
 
+BF = jnp.bfloat16
+F32 = jnp.float32
+I32 = jnp.int32
+TILE = 256
+
+
+def any_spec():
+    return pl.BlockSpec(memory_space=pl.ANY)
+
+
+def smem_spec():
+    return pl.BlockSpec(memory_space=pltpu.SMEM)
+
+
+def vmem_spec():
+    return pl.BlockSpec(memory_space=pltpu.VMEM)
+
+
+def params(mib):
+    return pltpu.CompilerParams(vmem_limit_bytes=mib * 1024 * 1024)
+
+
+def dot(a, b, dims):
+    return lax.dot_general(a, b, (dims, ((), ())), preferred_element_type=F32)
+
+
+def merge_kernel(order_ref, place_ref, coef_ref, one_ref, two_ref, out_ref):
+    first = 2 * combo_of(pl.program_id(0), pl.program_id(1), place_ref)
+    one = coef_ref[order_ref[first]]
+    two = coef_ref[order_ref[first + 1]]
+    out_ref[0, 0] = (one * one_ref[0].astype(F32) + two * two_ref[0].astype(F32)).astype(BF)
+
+
+def combo_of(step, member, place_ref):
+    return 4 * jnp.bitwise_xor(place_ref[0], step) + 2 * place_ref[1] + member
+
+
+def merge_experts(order, where_am_i, merge_coef, source_w, places):
+    _, rows, width = source_w.shape
+    half = width // 2
+
+    def pick(which):
+        def index(j, m, order_ref, place_ref):
+            return (order_ref[2 * combo_of(j, m, place_ref) + which], 0, place_ref[2])
+
+        return index
+
+    return pl.pallas_call(
+        merge_kernel,
+        grid_spec=pltpu.PrefetchScalarGridSpec(
+            num_scalar_prefetch=2,
+            grid=(places, 2),
+            in_specs=[
+                smem_spec(),
+                pl.BlockSpec((1, rows, half), pick(0)),
+                pl.BlockSpec((1, rows, half), pick(1)),
+            ],
+            out_specs=pl.BlockSpec((1, 1, rows, half), lambda j, m, *_: (j, m, 0, 0)),
+        ),
+        out_shape=jax.ShapeDtypeStruct((places, 2, rows, half), BF),
+        compiler_params=params(56),
+        name="merge_experts",
+    )(order, where_am_i, merge_coef, source_w, source_w)
+
+
+def column(row):
+    size = row.shape[1]
+    same = lax.broadcasted_iota(I32, (size, size), 0) == lax.broadcasted_iota(I32, (size, size), 1)
+    return jnp.sum(jnp.where(same, row, jnp.zeros_like(row)), axis=1, keepdims=True)
+
+
+def to_row(col):
+    size = col.shape[0]
+    same = lax.broadcasted_iota(I32, (size, size), 0) == lax.broadcasted_iota(I32, (size, size), 1)
+    return jnp.sum(jnp.where(same, col, jnp.zeros_like(col)), axis=0, keepdims=True)
+
+
+def picks_of(idx_ref, k, sources):
+    tok = idx_ref.shape[1]
+    return lax.broadcasted_iota(I32, (sources, tok), 0) == idx_ref[k : k + 1, :]
+
+
+def route_kernel(
+    capacity, lanes,
+    xt_ref, rwt_ref, rb_ref, idx_ref, map_ref, hid_ref, og_ref,
+    sh_ref, sg_ref, gate_ref, pos_ref, slot_ref,
+):
+    top, tok = idx_ref.shape
+    sources = rwt_ref.shape[0]
+    slots, width = hid_ref.shape
+    places = lanes * capacity
+    logits = jnp.dot(rwt_ref[...], xt_ref[...], preferred_element_type=F32) + rb_ref[...]
+    raised, merged = [], []
+    for k in range(top):
+        pick = picks_of(idx_ref, k, sources)
+        chosen = jnp.sum(jnp.where(pick, logits, 0.0), axis=0, keepdims=True)
+        raised.append(jnp.exp(chosen))
+        merged.append(jnp.sum(jnp.where(pick, map_ref[...], 0), axis=0, keepdims=True))
+    total = raised[0]
+    for k in range(1, top):
+        total = total + raised[k]
+    gates = [r / total for r in raised]
+    lane = [jnp.right_shift(g, 1) for g in merged]
+    member = [jnp.bitwise_and(g, 1) for g in merged]
+    onehot = [(lax.broadcasted_iota(I32, (lanes, tok), 0) == l).astype(F32) for l in lane]
+    all_hot = onehot[0]
+    for k in range(1, top):
+        all_hot = all_hot + onehot[k]
+    earlier = (
+        lax.broadcasted_iota(I32, (tok, tok), 0) < lax.broadcasted_iota(I32, (tok, tok), 1)
+    ).astype(BF)
+    before = jnp.dot(all_hot.astype(BF), earlier, preferred_element_type=F32)
+    position = []
+    for k in range(top):
+        rank = jnp.sum(before * onehot[k], axis=0, keepdims=True).astype(I32)
+        before = before + onehot[k]
+        position.append(jnp.where(rank < capacity, lane[k] * capacity + rank, -1))
+    gate_ref[...] = jnp.zeros_like(gate_ref)
+    pos_ref[...] = jnp.full_like(pos_ref, -1)
+    for k in range(top):
+        gate_ref[k : k + 1, :] = gates[k]
+        pos_ref[k : k + 1, :] = position[k]
+    spot = jnp.zeros((8, slots), F32)
+    for k in range(top):
+        spread = (
+            lax.broadcasted_iota(I32, (tok, slots), 1)
+            == lax.broadcasted_iota(I32, (tok, slots), 0) * top + k
+        ).astype(BF)
+        kept = position[k] >= 0
+        parts = [
+            jnp.where(kept, jnp.right_shift(position[k], 5), 0),
+            jnp.where(kept, jnp.bitwise_and(position[k], 31), 0),
+            jnp.where(kept, 1, 0),
+            member[k],
+        ]
+        stacked = jnp.concatenate(
+            [p.astype(F32) for p in parts] + [jnp.zeros((4, tok), F32)], axis=0
+        ).astype(BF)
+        spot = spot + jnp.dot(stacked, spread, preferred_element_type=F32)
+    spot = spot.astype(I32)
+    slot_pos = jnp.where(spot[2:3] > 0, spot[0:1] * 32 + spot[1:2], -1)
+    slot_ref[...] = jnp.broadcast_to(slot_pos, slot_ref.shape)
+    take = lax.broadcasted_iota(I32, (places, slots), 0) == slot_pos
+    placed = jnp.sum(jnp.where(take, spot[3:4].astype(F32), 0.0), axis=1, keepdims=True)
+    sh_ref[:, width:] = jnp.broadcast_to(placed, (places, sh_ref.shape[1] - width)).astype(BF)
+    take = take.astype(BF)
+    for n in range(0, width, TILE):
+        sh_ref[:, n : n + TILE] = jnp.dot(
+            take, hid_ref[:, n : n + TILE], preferred_element_type=F32
+        ).astype(BF)
+    takes = [
+        (lax.broadcasted_iota(I32, (places, tok), 0) == position[k]).astype(BF) for k in range(top)
+    ]
+    columns = [column(g) for g in gates]
+    for n in range(0, og_ref.shape[1], TILE):
+        og = og_ref[:, n : n + TILE].astype(F32)
+        rows = jnp.zeros((places, TILE), F32)
+        for k in range(top):
+            rows = rows + jnp.dot(takes[k], (columns[k] * og).astype(BF), preferred_element_type=F32)
+        sg_ref[:, n : n + TILE] = rows.astype(BF)
+
+
+def route(xt, rwt, router_b, idx_t, merge_map, hid, og, capacity, lanes):
+    places = lanes * capacity
+    slots, width = hid.shape
+    tok = idx_t.shape[1]
+    return pl.pallas_call(
+        functools.partial(route_kernel, capacity, lanes),
+        in_specs=[vmem_spec()] * 7,
+        out_specs=[vmem_spec()] * 5,
+        out_shape=[
+            jax.ShapeDtypeStruct((places, width + 128), BF),
+            jax.ShapeDtypeStruct((places, og.shape[1]), BF),
+            jax.ShapeDtypeStruct((8, tok), F32),
+            jax.ShapeDtypeStruct((8, tok), I32),
+            jax.ShapeDtypeStruct((8, slots), I32),
+        ],
+        compiler_params=params(56),
+        name="route",
+    )(xt, rwt, router_b[:, None], idx_t, merge_map[:, None], hid, og)
+
+
+def load_weights(spot_ref, mine, other, w_ref, sems):
+    rows = mine[0].shape[1]
+    core = spot_ref[8]
+    copies = []
+    for d in range(len(mine)):
+        at = pl.ds(pl.multiple_of(spot_ref[d], rows), rows)
+        for n, part in enumerate((mine[d], other[d])):
+            copies.append(
+                pltpu.make_async_copy(
+                    part, w_ref.at[core if n == 0 else 1 - core, :, at, :], sems.at[2 * d + n]
+                )
+            )
+    for copy in copies:
+        copy.start()
+    for copy in copies:
+        copy.wait()
+
+
+def forward_kernel(spot_ref, rows_ref, *refs):
+    parts, (out_ref, w_ref, sems) = refs[:-3], refs[-3:]
+    load_weights(spot_ref, parts[0::2], parts[1::2], w_ref, sems)
+    half = w_ref.shape[3]
+    member = rows_ref[:, 2 * half : 2 * half + 1].astype(F32)
+
+    @pl.loop(0, out_ref.shape[1] // TILE)
+    def _(n):
+        at = pl.ds(pl.multiple_of(n * TILE, TILE), TILE)
+        both = [
+            dot(rows_ref[:, :half], w_ref[0, m, at, :], ((1,), (1,)))
+            + dot(rows_ref[:, half : 2 * half], w_ref[1, m, at, :], ((1,), (1,)))
+            for m in range(2)
+        ]
+        out_ref[:, at] = jnp.where(member == 0.0, both[0], both[1]).astype(BF)
+
+
+def backward_kernel(spot_ref, rows_ref, flag_ref, *refs):
+    parts, (out_ref, w_ref, sems) = refs[:-3], refs[-3:]
+    load_weights(spot_ref, parts[0::2], parts[1::2], w_ref, sems)
+    half = w_ref.shape[3]
+    member = flag_ref[:, :1].astype(F32)
+    for h in range(2):
+
+        @pl.loop(0, half // TILE)
+        def _(n, h=h):
+            at = pl.ds(pl.multiple_of(n * TILE, TILE), TILE)
+            both = [dot(rows_ref[...], w_ref[h, m, :, at], ((1,), (0,))) for m in range(2)]
+            to = pl.ds(pl.multiple_of(h * half + n * TILE, TILE), TILE)
+            out_ref[:, to] = jnp.where(member == 0.0, both[0], both[1]).astype(BF)
+
+
+def run_lane(kernel, spots, row_args, row_specs, mine, other, out_width, name):
+    parts = [p for pair in zip(mine, other) for p in pair]
+    members, rows, half = mine[0].shape
+    depth = rows * len(mine)
+    count = row_args[0].shape[0]
+    return pl.pallas_call(
+        kernel,
+        grid=(1,),
+        in_specs=[smem_spec()] + row_specs + [any_spec()] * len(parts),
+        out_specs=pl.BlockSpec((count, out_width), lambda i: (0, 0)),
+        out_shape=jax.ShapeDtypeStruct((count, out_width), BF),
+        scratch_shapes=[
+            pltpu.VMEM((2, members, depth, half), BF),
+            pltpu.SemaphoreType.DMA((len(parts),)),
+        ],
+        compiler_params=params(56),
+        cost_estimate=pl.CostEstimate(
+            flops=4 * count * depth * 2 * half,
+            bytes_accessed=4 * members * depth * half + 8 * count * half,
+            transcendentals=0,
+        ),
+        name=name,
+    )(spots, *row_args, *parts)
+
+
+def lane_grad_kernel(has_other, _, hid_ref, flag_ref, grd_ref, *refs):
+    out_ref = refs[-1]
+    chosen = flag_ref[:, :1].astype(F32) == pl.program_id(1).astype(F32)
+    hid = jnp.where(chosen, hid_ref[...], jnp.zeros_like(hid_ref))
+    blocks, _, _, rows, cols = out_ref.shape
+    each = 2
+
+    @pl.loop(0, blocks // each)
+    def _(n):
+        at = pl.ds(pl.multiple_of(n * each * rows, each * rows), each * rows)
+        part = dot(grd_ref[:, at], hid, ((0,), (0,))).reshape(each, rows, cols)
+        to = pl.ds(n * each, each)
+        if has_other:
+            part = part + refs[0][to, 0, 0].astype(F32)
+        out_ref[to, 0, 0] = part.astype(BF)
+
+
+def lane_grads(select, hid, grd, other, blocks, reps):
+    count, depth = grd.shape
+    width = hid.shape[1] - 128
+    cols = width // reps
+    shape = (blocks, 2, 2, depth // blocks, cols)
+    block = pl.BlockSpec((blocks, 1, 1, depth // blocks, cols), lambda y, m, s: (0, y, m, 0, 0))
+    extra = [] if other is None else [other]
+    return pl.pallas_call(
+        functools.partial(lane_grad_kernel, other is not None),
+        grid_spec=pltpu.PrefetchScalarGridSpec(
+            num_scalar_prefetch=1,
+            grid=(2, 2),
+            in_specs=[
+                pl.BlockSpec((count, cols), lambda y, m, s: (0, 2 * y + s[0])),
+                pl.BlockSpec((count, 128), lambda y, m, s: (0, width // 128)),
+                pl.BlockSpec((count, depth), lambda y, m, s: (0, 0)),
+            ]
+            + [block] * len(extra),
+            out_specs=block,
+        ),
+        out_shape=jax.ShapeDtypeStruct(shape, BF),
+        compiler_params=params(56),
+        cost_estimate=pl.CostEstimate(
+            flops=4 * count * depth * cols * 2,
+            bytes_accessed=4 * depth * cols * 4 + 4 * count * depth,
+            transcendentals=0,
+        ),
+        name="lane_grads_add" if extra else "lane_grads_first",
+    )(select, hid, hid, grd, *extra)
+
+
+def combine_kernel(
+    out_ref, og_ref, gate_ref, pos_ref, idx_ref, rwt_ref, xt_ref, mixed_ref, tg_ref, part_ref
+):
+    places, width = out_ref.shape
+    top, tok = idx_ref.shape
+    sources, features = rwt_ref.shape
+    takes = [
+        (lax.broadcasted_iota(I32, (places, tok), 0) == pos_ref[k : k + 1, :]).astype(BF)
+        for k in range(top)
+    ]
+    gates = [gate_ref[k : k + 1, :] for k in range(top)]
+    columns = [column(g) for g in gates]
+    scores = [jnp.zeros((tok, 1), F32) for _ in range(top)]
+    for n in range(0, width, TILE):
+        og = og_ref[:, n : n + TILE].astype(F32)
+        rows = out_ref[:, n : n + TILE]
+        mixed = jnp.zeros((tok, TILE), F32)
+        for k in range(top):
+            slot_out = dot(takes[k], rows, ((0,), (0,)))
+            mixed = mixed + columns[k] * slot_out
+            scores[k] = scores[k] + jnp.sum(og * slot_out, axis=1, keepdims=True)
+        mixed_ref[:, n : n + TILE] = mixed.astype(BF)
+    scores = [to_row(s) for s in scores]
+    middle = gates[0] * scores[0]
+    for k in range(1, top):
+        middle = middle + gates[k] * scores[k]
+    logit_grad = jnp.zeros((sources, tok), F32)
+    for k in range(top):
+        chosen_grad = gates[k] * (scores[k] - middle)
+        logit_grad = logit_grad + jnp.where(picks_of(idx_ref, k, sources), chosen_grad, 0.0)
+    logit_half = logit_grad.astype(BF)
+    tg_ref[...] = dot(rwt_ref[...], logit_half, ((0,), (0,))).astype(BF)
+    part_ref[:sources, :] = dot(logit_half, xt_ref[...], ((1,), (1,)))
+    part_ref[sources:, :] = jnp.zeros_like(part_ref[sources:, :])
+    bias = to_row(jnp.sum(logit_grad, axis=1, keepdims=True))
+    part_ref[sources : sources + 1, :sources] = bias
+
+
+def combine(home_out, og, gates, pos, idx_t, rwt, xt):
+    sources, features = rwt.shape
+    tok = idx_t.shape[1]
+    return pl.pallas_call(
+        combine_kernel,
+        in_specs=[vmem_spec()] * 7,
+        out_specs=[vmem_spec()] * 3,
+        out_shape=[
+            jax.ShapeDtypeStruct(og.shape, BF),
+            jax.ShapeDtypeStruct((features, tok), BF),
+            jax.ShapeDtypeStruct((sources + 8, features), F32),
+        ],
+        compiler_params=params(56),
+        name="combine",
+    )(home_out, og, gates, pos, idx_t, rwt, xt)
+
+
+def unplace_kernel(back_ref, slot_ref, out_ref):
+    places, width = back_ref.shape
+    slots = slot_ref.shape[1]
+    take = (lax.broadcasted_iota(I32, (places, slots), 0) == slot_ref[0:1, :]).astype(BF)
+    for n in range(0, width, TILE):
+        out_ref[:, n : n + TILE] = dot(take, back_ref[:, n : n + TILE], ((0,), (0,))).astype(BF)
+
+
+def unplace(home_back, slot_pos):
+    return pl.pallas_call(
+        unplace_kernel,
+        in_specs=[vmem_spec()] * 2,
+        out_specs=vmem_spec(),
+        out_shape=jax.ShapeDtypeStruct((slot_pos.shape[1], home_back.shape[1]), BF),
+        compiler_params=params(56),
+        name="unplace",
+    )(home_back, slot_pos)
+
+
+def finish_kernel(scale, order_ref, rep_ref, coef_ref, got_ref, src_ref, out_ref, dot_ref):
+    merged = got_ref[0, 0].astype(F32) + got_ref[1, 0].astype(F32)
+    expert = order_ref[pl.program_id(0)]
+    out_ref[0] = merged * (coef_ref[expert] * scale)
+    product = merged * src_ref[0].astype(F32)
+    rows, cols = product.shape
+    folded = jnp.sum(product.reshape(rows // 8, 8, cols), axis=0)
+    total = folded[:, :128]
+    for n in range(128, cols, 128):
+        total = total + folded[:, n : n + 128]
+    dot_ref[0] = total
+
+
+def finish(order, rep_index, merge_coef, arrived, source_w, scale):
+    halves, _, rows, cols = arrived.shape
+    count = source_w.shape[0]
+    return pl.pallas_call(
+        functools.partial(finish_kernel, scale),
+        grid_spec=pltpu.PrefetchScalarGridSpec(
+            num_scalar_prefetch=2,
+            grid=(count,),
+            in_specs=[
+                smem_spec(),
+                pl.BlockSpec((halves, 1, rows, cols), lambda i, o, r: (0, i // 2, 0, 0)),
+                pl.BlockSpec((1, rows, cols), lambda i, o, r: (o[i], 0, r[0])),
+            ],
+            out_specs=[
+                pl.BlockSpec((1, rows, cols), lambda i, o, r: (o[i], 0, 0)),
+                pl.BlockSpec((1, 8, 128), lambda i, o, r: (o[i], 0, 0)),
+            ],
+        ),
+        out_shape=[
+            jax.ShapeDtypeStruct((count, rows, cols), F32),
+            jax.ShapeDtypeStruct((count, 8, 128), F32),
+        ],
+        compiler_params=params(56),
+        name="finish",
+    )(order, rep_index, merge_coef, arrived, source_w)
+
+
+def swap(x):
+    return lax.ppermute(x, "core", [(0, 1), (1, 0)])
+
+
+def on_pairs(
+    tokens, router_w, router_b, hidden, teacher_idx, merge_map, merge_coef, source_w, out_grad
+):
+    places = lax.axis_size("place")
+    blocks = 2 * places
+    reps = 4
+    tok = tokens.shape[1]
+    features = tokens.shape[2]
+    top = teacher_idx.shape[2]
+    width = hidden.shape[3]
+    depth = out_grad.shape[2]
+    sources = router_w.shape[1]
+    row_share = source_w.shape[1]
+    lanes = 2 * places
+    capacity = 5 * tok * top // (4 * blocks)
+    scale = 1.0 / math.sqrt(tok * blocks * reps)
+    half_i, place_i = lax.axis_index("half"), lax.axis_index("place")
+    row_i, core_i = lax.axis_index("row"), lax.axis_index("core")
+    ctx_i = half_i * places + place_i
+    numbers = jnp.arange(sources, dtype=I32)
+    same = merge_map[:, None] == merge_map[None, :]
+    rank = jnp.sum((same & (numbers[:, None] > numbers[None, :])).astype(I32), axis=1)
+    target = 2 * merge_map + rank
+    order = jnp.sum(jnp.where(target[None, :] == numbers[:, None], numbers[None, :], 0), axis=1)
+    order = order.astype(I32)
+    me = jnp.stack([place_i, row_i, core_i]).astype(I32)
+    rep_index = (2 * row_i + core_i).astype(I32)[None]
+
+    combos = merge_experts(order, me, merge_coef, source_w, places)
+    mine = [combos[0]]
+    for d in range(1, blocks):
+        mine.append(
+            lax.ppermute(
+                combos[d % places], ("half", "place"), [(i, i ^ d) for i in range(blocks)]
+            )
+        )
+    other = [swap(part) for part in mine]
+    spots = jnp.stack(
+        [jnp.bitwise_xor(ctx_i, d) * row_share for d in range(blocks)] + [core_i]
+    ).astype(I32)
+
+    xt = tokens.reshape(tok, features).T
+    rwt = router_w.T
+    idx_t = teacher_idx.reshape(tok, top).T
+    og = out_grad.reshape(tok, depth)
+    send_hidden, send_grad, gates, pos, slot_pos = route(
+        xt, rwt, router_b, idx_t, merge_map, hidden.reshape(tok * top, width), og, capacity, lanes
+    )
+
+    def trade(rows):
+        rows = rows.reshape(lanes, capacity, rows.shape[1])
+        rows = lax.all_to_all(rows, ("place", "row"), split_axis=0, concat_axis=0, tiled=True)
+        return rows.reshape(lanes * capacity, rows.shape[2])
+
+    hid = trade(send_hidden)
+    grd = trade(send_grad)
+    first = lane_grads((1 - core_i).astype(I32)[None], hid, grd, None, blocks, reps)
+    summed = lane_grads(core_i.astype(I32)[None], hid, grd, swap(first), blocks, reps)
+    whole = lambda rows: pl.BlockSpec(rows.shape, lambda i: (0, 0))
+    out_rows = run_lane(
+        forward_kernel, spots, [hid], [whole(hid)], mine, other, depth, "lane_forward"
+    )
+    back_rows = run_lane(
+        backward_kernel, spots, [grd, hid],
+        [whole(grd), pl.BlockSpec((hid.shape[0], 128), lambda i: (0, width // 128))],
+        mine, other, width, "lane_backward",
+    )
+    home_out = trade(out_rows)
+    mixed, token_grad, part = combine(home_out, og, gates, pos, idx_t, rwt, xt)
+    part = lax.psum(part, ("half", "place", "row", "core"))
+    home_back = trade(back_rows)
+    hidden_grad = unplace(home_back, slot_pos)
+    arrived = lax.all_to_all(
+        summed.reshape(2 * blocks, 2, row_share, width // reps),
+        ("half", "place", "row"), split_axis=0, concat_axis=0, tiled=True,
+    )
+    source_w_grad, coef_part = finish(
+        order, rep_index, merge_coef,
+        arrived.reshape(2, 2 * lanes, row_share, width // reps), source_w, scale,
+    )
+    coef_sum = lax.psum(jnp.sum(coef_part, axis=(1, 2)), ("half", "place", "row", "core"))
+    return (
+        mixed.reshape(1, tok, depth),
+        hidden_grad.reshape(1, tok, top, width),
+        token_grad.T.reshape(1, tok, features),
+        part[:sources].T * scale,
+        part[sources, :sources] * scale,
+        coef_sum * scale,
+        source_w_grad,
+    )
+
+
 def solution(mesh):
+    if mesh.shape["ctx"] == 8 and mesh.shape["rep"] == 4:
+        mesh = jax.sharding.Mesh(
+            mesh.devices.reshape(2, 4, 2, 2), ("half", "place", "row", "core")
+        )
+        ctx, rep, body = ("half", "place"), ("row", "core"), on_pairs
+    else:
+        ctx, rep, body = "ctx", "rep", on_device
     in_specs = (
-        P("rep", "ctx", None),
+        P(rep, ctx, None),
         P(),
         P(),
-        P("rep", "ctx", None, None),
-        P("rep", "ctx", None),
+        P(rep, ctx, None, None),
+        P(rep, ctx, None),
         P(),
         P(),
-        P(None, "ctx", None),
-        P("rep", "ctx", None),
+        P(None, ctx, None),
+        P(rep, ctx, None),
     )
     out_specs = (
-        P("rep", "ctx", None),
-        P("rep", "ctx", None, None),
-        P("rep", "ctx", None),
+        P(rep, ctx, None),
+        P(rep, ctx, None, None),
+        P(rep, ctx, None),
         P(),
         P(),
         P(),
-        P(None, "ctx", "rep"),
+        P(None, ctx, rep),
     )
     return jax.shard_map(
-        on_device, mesh=mesh, in_specs=in_specs, out_specs=out_specs, check_vma=False
-    )
+        body, mesh=mesh, in_specs=in_specs, out_specs=out_specs, check_vma=False
+    )

time: 1390 us -> 528 us (0.38)
  waiting for transfers between devices: 1060 us -> 290 us
  Pallas kernels: 0 us -> 95.9 us
  local copies, waits for them, and re-layouts: 90.1 us -> 15.4 us
  other arithmetic: 65.8 us -> 6.13 us
  matrix products: 37.2 us -> 0 us
  blocking collectives: 87.7 us -> 72 us
    all_to_all x6 -> x4, waiting for transfers between devices: 904 us -> 16.1 us  [the longest x3 16 us: trade(): lax.all_to_all(rows, ('place', 'row'), split_axis=0, concat_axis=0, tiled...]
    psum x1, waiting for transfers between devices: 8.31 us -> 178 us  [on_pairs(): part = lax.psum(part, ('half', 'place', 'row', 'core'))]
    reduce_scatter x1 -> x0, waiting for transfers between devices: 151 us -> none  [on_device(): lax.psum_scatter(source_grad * merge_coef[:, None, None], 'rep', scatter_...]
    pallas_call x0 -> x9, Pallas kernels: none -> 95.9 us  [the longest x2 27.8 us: run_lane(): pl.pallas_call(kernel, grid=(1,), in_specs=[smem_spec()] + row_specs + [a...]
    ppermute x0 -> x16, waiting for transfers between devices: none -> 95.6 us  [the longest x7 93.6 us: on_pairs(): lax.ppermute(combos[d % places], ('half', 'place'), [(i, i ^ d) for i in...]
    gather x8 -> x0, local copies, waits for them, and re-layouts: 52.2 us -> none  [the longest x1 21 us: on_device(): source_grad = merged_grad[merge_map]]
    mul x5 -> x3, other arithmetic: 43.1 us -> 3.46 us  [the longest x1 1.76 us: on_pairs(): part[:sources].T * scale]
    dot_general x10 -> x0, matrix products: 37.2 us -> none  [the longest x2 13.6 us: expert_rows(): backward = jnp.dot(rows_grad, weight, preferred_element_type=jnp.float32)]
  transfers between devices with their start and end apart: 8 -> 21, of which waited for: 7 -> 11; matrix products, arithmetic and copies ran while one was open for 9% -> 2% of each run, Pallas kernels for 0% -> 10%
where the time goes in v1:
time: 528 us; the launch traced here: 527 us
  waiting for transfers between devices  290 us (55%)
  Pallas kernels  95.9 us (18%)
  blocking collectives  72 us (14%)
  starting transfers between devices  32.9 us (6%)
  local copies, waits for them, and re-layouts  15.4 us (3%)
  between operations  14.2 us (3%)
  other arithmetic  6.13 us (1%)
    psum x1, waiting for transfers between devices, on_pairs(): part = lax.psum(part, ('half', 'place', 'row', 'core'))  178 us
    ppermute x7, waiting for transfers between devices, on_pairs(): lax.ppermute(combos[d % places], ('half', 'place'), [(i, i ^ d) for i in...  93.6 us
    psum x1, blocking collectives, on_pairs(): lax.psum(jnp.sum(coef_part, axis=(1, 2)), ('half', 'place', 'row', 'core'))  40.4 us
    all_to_all x1, blocking collectives, trade(): lax.all_to_all(rows, ('place', 'row'), split_axis=0, concat_axis=0, tiled...  31.6 us
    pallas_call x2, Pallas kernels, run_lane(): pl.pallas_call(kernel, grid=(1,), in_specs=[smem_spec()] + row_specs + [a...  27.8 us
    pallas_call x2, Pallas kernels, lane_grads(): pl.pallas_call(functools.partial(lane_grad_kernel, other is not None), gr...  23.3 us
    pallas_call x1, Pallas kernels, finish(): pl.pallas_call(functools.partial(finish_kernel, scale), grid_spec=pltpu.P...  21.3 us
    all_to_all x3, starting transfers between devices, trade(): lax.all_to_all(rows, ('place', 'row'), split_axis=0, concat_axis=0, tiled...  16.3 us
  transfers between devices with their start and end apart: 21, of which 11 were waited for; matrix products, arithmetic and copies ran while one was open for 2% of the time, Pallas kernels for 10%

profile of v1, /device:TPU:0, one launch (start us, length us, event | category | flops | bytes accessed | tf_op | source)
XLA Modules:
  0.0 526.5 jit_solution(2027361328600933523)
XLA Ops:
  13.5 6.9 %route.1 = (bf16[640,1664]{1,0:T(8,128)(2,1)}, bf16[640,1536]{1,0:T(8,128)(2,1)}, f32[8,128]{1,0:T(8,128)}, s32[8,128]{1,0:T(8,128)}, s32[8,512]{1,0:T(8,128)}) custom-call(bf16[2880,128]{1,0:T(8,128)(2,1)} %bitcast.60, bf16[32,2880]{1,0:T(8,128)(2,1)} %bitcast.68, f32[32,1]{1,0:T(8,128)} %copy.18.rb_ref, s32[4,128]{1,0:T(4,128)} %bitcast.70, ...), custom_call_target="tpu_custom_call" | custom-call | tf_op jit(solution)/shard_map/route/pallas_call | solution.py:374
  20.5 31.6 %all_to_all.25 = bf16[8,80,1536]{2,1,0:T(8,128)(2,1)} all-to-all(bf16[8,80,1536]{2,1,0:T(8,128)(2,1)} %bitcast.65), channel_id=1, replica_groups=mesh['half'=2,'place'=4,'row'=2,'core'=2] {'place','row'}, dimensions={0} | all-to-all | bytes 3932160 | tf_op jit(solution)/shard_map/all_to_all | solution.py:682
  52.1 3.7 all-to-all-start
  57.3 7.3 %merge_experts.1 = bf16[4,2,192,768]{3,2,1,0:T(8,128)(2,1)} custom-call(s32[32]{0:T(128)} %select_reduce_fusion.order_ref, s32[3]{0:T(128)} %pad_add_fusion.place_ref, f32[32]{0:T(128)} %coef_ref.3, bf16[32,192,1536]{2,1,0:T(8,128)(2,1)} %src_ref.1, bf16[32,192,1536]{2,1,0:T(8,128)(2,1)} %src_ref.1), custom_call_target="tpu_custom_call" | custom-call | tf_op jit(solution)/shard_map/merge_experts/pallas_call | solution.py:255
  66.3 4.9 collective-permute-start.13
  76.2 21.9 %collective-permute-done.13.refs_14_ = bf16[2,192,768]{2,1,0:T(8,128)(2,1)S(1)} collective-permute-done((bf16[2,192,768]{2,1,0:T(8,128)(2,1)S(1)}, bf16[2,192,768]{2,1,0:T(8,128)(2,1)S(1)}, u32[]{:S(2)}, u32[]{:S(2)}) %collective-permute-start.13) | collective-permute-done | bytes 589856 | tf_op jit(solution)/shard_map/ppermute | solution.py:663
  98.6 33.0 %collective-permute-done.5.refs_6_ = bf16[2,192,768]{2,1,0:T(8,128)(2,1)S(1)} collective-permute-done((bf16[2,192,768]{2,1,0:T(8,128)(2,1)S(1)}, bf16[2,192,768]{2,1,0:T(8,128)(2,1)S(1)}, u32[]{:S(2)}, u32[]{:S(2)}) %collective-permute-start.5) | collective-permute-done | bytes 589856 | tf_op jit(solution)/shard_map/ppermute | solution.py:663
  131.6 11.8 %collective-permute-done.3.refs_4_ = bf16[2,192,768]{2,1,0:T(8,128)(2,1)} collective-permute-done((bf16[2,192,768]{2,1,0:T(8,128)(2,1)S(1)}, bf16[2,192,768]{2,1,0:T(8,128)(2,1)}, u32[]{:S(2)}, u32[]{:S(2)}) %collective-permute-start.3) | collective-permute-done | bytes 589856 | tf_op jit(solution)/shard_map/ppermute | solution.py:663
  143.4 18.0 %collective-permute-done.9.refs_10_ = bf16[2,192,768]{2,1,0:T(8,128)(2,1)} collective-permute-done((bf16[2,192,768]{2,1,0:T(8,128)(2,1)S(1)}, bf16[2,192,768]{2,1,0:T(8,128)(2,1)}, u32[]{:S(2)}, u32[]{:S(2)}) %collective-permute-start.9) | collective-permute-done | bytes 589856 | tf_op jit(solution)/shard_map/ppermute | solution.py:663
  161.9 9.0 %collective-permute-done.7.refs_8_ = bf16[2,192,768]{2,1,0:T(8,128)(2,1)} collective-permute-done((bf16[2,192,768]{2,1,0:T(8,128)(2,1)S(1)}, bf16[2,192,768]{2,1,0:T(8,128)(2,1)}, u32[]{:S(2)}, u32[]{:S(2)}) %collective-permute-start.7) | collective-permute-done | bytes 589856 | tf_op jit(solution)/shard_map/ppermute | solution.py:663
  177.2 13.8 %lane_backward.1 = bf16[640,1536]{1,0:T(8,128)(2,1)} custom-call(s32[9]{0:T(128)} %stack.49.spot_ref, bf16[640,1536]{1,0:T(8,128)(2,1)} %bitcast.57, bf16[640,1664]{1,0:T(8,128)(2,1)} %bitcast.49, bf16[2,192,768]{2,1,0:T(8,128)(2,1)} %copy-done.2, bf16[2,192,768]{2,1,0:T(8,128)(2,1)} %copy-done.6, bf16[2,192,768]{2,1,0:T(8,128)(2,1)} %collective-permute-done.1.refs_2_, ...), custom_call_target="tpu_custom_call" | custom-call | flops 6039797760 | bytes 13369344 | tf_op jit(solution)/shard_map/lane_backward/pallas_call | solution.py:445
  191.1 7.8 %all-to-all-start.3 = ((bf16[8,80,1536]{2,1,0:T(8,128)(2,1)}), bf16[8,80,1536]{2,1,0:T(8,128)(2,1)S(1)}, u32[]{:S(2)}, u32[]{:S(2)}) async-start(bf16[8,80,1536]{2,1,0:T(8,128)(2,1)} %bitcast.64), calls=%async_computation.3 | async-start | bytes 3932160 | tf_op jit(solution)/shard_map/all_to_all | solution.py:682
  198.8 11.4 %lane_grads_first.1 = bf16[8,2,2,192,384]{4,3,2,1,0:T(8,128)(2,1)} custom-call(s32[1]{0:T(128)} %bitcast.37._, bf16[640,1664]{1,0:T(8,128)(2,1)} %bitcast.50, bf16[640,1664]{1,0:T(8,128)(2,1)} %bitcast.51, bf16[640,1536]{1,0:T(8,128)(2,1)} %bitcast.58), custom_call_target="tpu_custom_call" | custom-call | flops 3019898880 | bytes 13369344 | tf_op jit(solution)/shard_map/lane_grads_first/pallas_call | solution.py:489
  210.3 14.0 %lane_forward.1 = bf16[640,1536]{1,0:T(8,128)(2,1)} custom-call(s32[9]{0:T(128)} %stack.49.spot_ref, bf16[640,1664]{1,0:T(8,128)(2,1)} %bitcast.52, bf16[2,192,768]{2,1,0:T(8,128)(2,1)} %copy-done.2, bf16[2,192,768]{2,1,0:T(8,128)(2,1)} %copy-done.6, bf16[2,192,768]{2,1,0:T(8,128)(2,1)} %collective-permute-done.1.refs_2_, ...), custom_call_target="tpu_custom_call" | custom-call | flops 6039797760 | bytes 13369344 | tf_op jit(solution)/shard_map/lane_forward/pallas_call | solution.py:445
  224.6 4.8 all-to-all-start.1
  229.4 11.9 %lane_grads_add.1 = bf16[8,2,2,192,384]{4,3,2,1,0:T(8,128)(2,1)} custom-call(s32[1]{0:T(128)} %bitcast.8._, bf16[640,1664]{1,0:T(8,128)(2,1)} %bitcast.53, bf16[640,1664]{1,0:T(8,128)(2,1)} %bitcast.54, bf16[640,1536]{1,0:T(8,128)(2,1)} %bitcast.59, bf16[8,2,2,192,384]{4,3,2,1,0:T(8,128)(2,1)} %collective-permute-done.15.refs_0_), custom_call_target="tpu_custom_call" | custom-call | flops 3019898880 | bytes 13369344 | tf_op jit(solution)/shard_map/lane_grads_add/pallas_call | solution.py:489
  241.3 15.7 %all-to-all-done.1 = bf16[8,80,1536]{2,1,0:T(8,128)(2,1)} async-done(((bf16[8,80,1536]{2,1,0:T(8,128)(2,1)}), bf16[8,80,1536]{2,1,0:T(8,128)(2,1)}, u32[]{:S(2)}, u32[]{:S(2)}) %all-to-all-start.1) | async-done | bytes 1966112 | tf_op jit(solution)/shard_map/all_to_all | solution.py:682
  257.0 4.6 all-to-all-start.4
  261.8 5.0 combine.1
  266.9 4.2 unplace.1
  271.0 3.8 reshape.83
  274.9 178.4 %all-reduce.2.cloned.1.call-done = f32[40,2880]{1,0:T(8,128)} async-done(((f32[40,2880]{1,0:T(8,128)}), f32[40,2880]{1,0:T(8,128)}) %all-reduce.2.cloned.1.call-update) | async-done | bytes 460816 | tf_op jit(solution)/shard_map/psum | solution.py:700
  455.0 21.3 %finish.1 = (f32[32,192,384]{2,1,0:T(8,128)}, f32[32,8,128]{2,1,0:T(8,128)}) custom-call(s32[32]{0:T(128)} %select_reduce_fusion.order_ref, s32[1]{0:T(128)} %bitcast.36.rep_ref, f32[32]{0:T(128)} %coef_ref.3, bf16[2,16,192,384]{3,2,1,0:T(8,128)(2,1)} %bitcast.39.got_ref, bf16[32,192,1536]{2,1,0:T(8,128)(2,1)} %src_ref.1), custom_call_target="tpu_custom_call" | custom-call | tf_op jit(solution)/shard_map/finish/pallas_call | solution.py:603
  478.8 40.4 %psum.15 = f32[32]{0:T(128)S(1)} all-reduce(f32[32]{0:T(128)S(1)} %reduce_sum.29), channel_id=1, replica_groups=mesh['half'=2,'place'=4,'row'=2,'core'=2] {'half','place','row','core'}, use_global_device_ids=true, to_apply=%region_4.5 | all-reduce | flops 32 | bytes 256 | tf_op jit(solution)/shard_map/psum | solution.py:711
  (62 shorter events, 27.1 us)
Async XLA Ops:
  52.1 123.8 %all-to-all-start = ((bf16[8,80,1664]{2,1,0:T(8,128)(2,1)}), bf16[8,80,1664]{2,1,0:T(8,128)(2,1)S(1)}, u32[]{:S(2)}, u32[]{:S(2)}) async-start(bf16[8,80,1664]{2,1,0:T(8,128)(2,1)} %bitcast.62), calls=%async_computation | async-start | bytes 4259840 | tf_op jit(solution)/shard_map/all_to_all | solution.py:682
  66.3 109.6 %copy-start.2 = (bf16[2,192,768]{2,1,0:T(8,128)(2,1)}, bf16[2,192,768]{2,1,0:T(8,128)(2,1)S(1)}, u32[]{:S(2)}) copy-start(bf16[2,192,768]{2,1,0:T(8,128)(2,1)S(1)} %get-tuple-element.30.refs_0_) | copy-start | bytes 1769476
  66.3 31.7 %collective-permute-start.13 = (bf16[2,192,768]{2,1,0:T(8,128)(2,1)S(1)}, bf16[2,192,768]{2,1,0:T(8,128)(2,1)S(1)}, u32[]{:S(2)}, u32[]{:S(2)}) collective-permute-start(bf16[2,192,768]{2,1,0:T(8,128)(2,1)S(1)} %get-tuple-element.27), channel_id=1, source_target_pairs={{0,28},{4,24},{8,20},{12,16},{16,12},{20,8},{24,4},{28,0},{1,29},{... | collective-permute-start | bytes 1769480 | tf_op jit(solution)/shard_map/ppermute | solution.py:663
  71.2 60.3 %collective-permute-start.5 = (bf16[2,192,768]{2,1,0:T(8,128)(2,1)S(1)}, bf16[2,192,768]{2,1,0:T(8,128)(2,1)S(1)}, u32[]{:S(2)}, u32[]{:S(2)}) collective-permute-start(bf16[2,192,768]{2,1,0:T(8,128)(2,1)S(1)} %get-tuple-element.27), channel_id=1, source_target_pairs={{0,12},{4,8},{8,4},{12,0},{16,28},{20,24},{24,20},{28,16},{1,13},{... | collective-permute-start | bytes 1769480 | tf_op jit(solution)/shard_map/ppermute | solution.py:663
  71.2 60.3 %collective-permute-start.11 = (bf16[2,192,768]{2,1,0:T(8,128)(2,1)S(1)}, bf16[2,192,768]{2,1,0:T(8,128)(2,1)}, u32[]{:S(2)}, u32[]{:S(2)}) collective-permute-start(bf16[2,192,768]{2,1,0:T(8,128)(2,1)S(1)} %get-tuple-element.28), channel_id=1, source_target_pairs={{0,24},{4,28},{8,16},{12,20},{16,8},{20,12},{24,0},{28,4},{1,25},{... | collective-permute-start | bytes 1769480 | tf_op jit(solution)/shard_map/ppermute | solution.py:663
  72.1 71.3 %collective-permute-start.3 = (bf16[2,192,768]{2,1,0:T(8,128)(2,1)S(1)}, bf16[2,192,768]{2,1,0:T(8,128)(2,1)}, u32[]{:S(2)}, u32[]{:S(2)}) collective-permute-start(bf16[2,192,768]{2,1,0:T(8,128)(2,1)S(1)} %get-tuple-element.28), channel_id=1, source_target_pairs={{0,8},{4,12},{8,0},{12,4},{16,24},{20,28},{24,16},{28,20},{1,9},{5... | collective-permute-start | bytes 1769480 | tf_op jit(solution)/shard_map/ppermute | solution.py:663
  73.3 88.2 %collective-permute-start.9 = (bf16[2,192,768]{2,1,0:T(8,128)(2,1)S(1)}, bf16[2,192,768]{2,1,0:T(8,128)(2,1)}, u32[]{:S(2)}, u32[]{:S(2)}) collective-permute-start(bf16[2,192,768]{2,1,0:T(8,128)(2,1)S(1)} %get-tuple-element.29), channel_id=1, source_target_pairs={{0,20},{4,16},{8,28},{12,24},{16,4},{20,0},{24,12},{28,8},{1,21},{... | collective-permute-start | bytes 1769480 | tf_op jit(solution)/shard_map/ppermute | solution.py:663
  98.0 77.8 %copy-start.4 = (bf16[2,192,768]{2,1,0:T(8,128)(2,1)}, bf16[2,192,768]{2,1,0:T(8,128)(2,1)S(1)}, u32[]{:S(2)}) copy-start(bf16[2,192,768]{2,1,0:T(8,128)(2,1)S(1)} %collective-permute-done.13.refs_14_) | copy-start | bytes 1769476
  98.1 63.4 %collective-permute-start.1 = (bf16[2,192,768]{2,1,0:T(8,128)(2,1)S(1)}, bf16[2,192,768]{2,1,0:T(8,128)(2,1)}, u32[]{:S(2)}, u32[]{:S(2)}) collective-permute-start(bf16[2,192,768]{2,1,0:T(8,128)(2,1)S(1)} %get-tuple-element.29), channel_id=1, source_target_pairs={{0,4},{4,0},{8,12},{12,8},{16,20},{20,16},{24,28},{28,24},{1,5},{5... | collective-permute-start | bytes 1769480 | tf_op jit(solution)/shard_map/ppermute | solution.py:663
  131.6 39.9 %copy-start.5 = (bf16[2,192,768]{2,1,0:T(8,128)(2,1)}, bf16[2,192,768]{2,1,0:T(8,128)(2,1)S(1)}, u32[]{:S(2)}) copy-start(bf16[2,192,768]{2,1,0:T(8,128)(2,1)S(1)} %collective-permute-done.5.refs_6_) | copy-start | bytes 1769476
  131.6 39.4 %collective-permute-start.7 = (bf16[2,192,768]{2,1,0:T(8,128)(2,1)S(1)}, bf16[2,192,768]{2,1,0:T(8,128)(2,1)}, u32[]{:S(2)}, u32[]{:S(2)}) collective-permute-start(bf16[2,192,768]{2,1,0:T(8,128)(2,1)S(1)} %get-tuple-element.30.refs_0_), channel_id=1, source_target_pairs={{0,16},{4,20},{8,24},{12,28},{16,0},{20,4},{24,8},{28,12},{1,17},{... | collective-permute-start | bytes 1769480 | tf_op jit(solution)/shard_map/ppermute | solution.py:663
  131.6 39.4 %collective-permute-start = (bf16[2,192,768]{2,1,0:T(8,128)(2,1)S(1)}, bf16[2,192,768]{2,1,0:T(8,128)(2,1)S(1)}, u32[]{:S(2)}, u32[]{:S(2)}) collective-permute-start(bf16[2,192,768]{2,1,0:T(8,128)(2,1)S(1)} %get-tuple-element.30.refs_0_), channel_id=1, source_target_pairs={{0,1},{1,0},{2,3},{3,2},{4,5},{5,4},{6,7},{7,6},{8,9},{9,8},{10,11... | collective-permute-start | bytes 1769480 | tf_op jit(solution)/shard_map/ppermute | solution.py:628
  143.4 28.1 %collective-permute-start.14 = (bf16[2,192,768]{2,1,0:T(8,128)(2,1)S(1)}, bf16[2,192,768]{2,1,0:T(8,128)(2,1)S(1)}, u32[]{:S(2)}, u32[]{:S(2)}) collective-permute-start(bf16[2,192,768]{2,1,0:T(8,128)(2,1)S(1)} %collective-permute-done.13.refs_14_), channel_id=1, source_target_pairs={{0,1},{1,0},{2,3},{3,2},{4,5},{5,4},{6,7},{7,6},{8,9},{9,8},{10,11... | collective-permute-start | bytes 1769480 | tf_op jit(solution)/shard_map/ppermute | solution.py:628
  161.4 10.2 %collective-permute-start.6 = (bf16[2,192,768]{2,1,0:T(8,128)(2,1)S(1)}, bf16[2,192,768]{2,1,0:T(8,128)(2,1)S(1)}, u32[]{:S(2)}, u32[]{:S(2)}) collective-permute-start(bf16[2,192,768]{2,1,0:T(8,128)(2,1)S(1)} %collective-permute-done.5.refs_6_), channel_id=1, source_target_pairs={{0,1},{1,0},{2,3},{3,2},{4,5},{5,4},{6,7},{7,6},{8,9},{9,8},{10,11... | collective-permute-start | bytes 1769480 | tf_op jit(solution)/shard_map/ppermute | solution.py:628
  161.4 12.5 %collective-permute-start.12 = (bf16[2,192,768]{2,1,0:T(8,128)(2,1)}, bf16[2,192,768]{2,1,0:T(8,128)(2,1)}, u32[]{:S(2)}, u32[]{:S(2)}) collective-permute-start(bf16[2,192,768]{2,1,0:T(8,128)(2,1)} %collective-permute-done.11.refs_12_), channel_id=1, source_target_pairs={{0,1},{1,0},{2,3},{3,2},{4,5},{5,4},{6,7},{7,6},{8,9},{9,8},{10,11... | collective-permute-start | bytes 1769480 | tf_op jit(solution)/shard_map/ppermute | solution.py:628
  171.0 3.0 collective-permute-start.4
  171.0 3.2 collective-permute-start.10
  171.5 3.5 collective-permute-start.2
  173.1 2.7 collective-permute-start.8
  191.1 33.6 %all-to-all-start.3 = ((bf16[8,80,1536]{2,1,0:T(8,128)(2,1)}), bf16[8,80,1536]{2,1,0:T(8,128)(2,1)S(1)}, u32[]{:S(2)}, u32[]{:S(2)}) async-start(bf16[8,80,1536]{2,1,0:T(8,128)(2,1)} %bitcast.64), calls=%async_computation.3 | async-start | bytes 3932160 | tf_op jit(solution)/shard_map/all_to_all | solution.py:682
  210.3 19.1 %collective-permute-start.15 = (bf16[8,2,2,192,384]{4,3,2,1,0:T(8,128)(2,1)}, bf16[8,2,2,192,384]{4,3,2,1,0:T(8,128)(2,1)}, u32[]{:S(2)}, u32[]{:S(2)}) collective-permute-start(bf16[8,2,2,192,384]{4,3,2,1,0:T(8,128)(2,1)} %lane_grads_first.1), channel_id=1, source_target_pairs={{0,1},{1,0},{2,3},{3,2},{4,5},{5,4},{6,7},{7,6},{8,9},{9,8},{10,11... | collective-permute-start | bytes 14155784 | tf_op jit(solution)/shard_map/ppermute | solution.py:628
  224.6 32.4 %all-to-all-start.1 = ((bf16[8,80,1536]{2,1,0:T(8,128)(2,1)}), bf16[8,80,1536]{2,1,0:T(8,128)(2,1)}, u32[]{:S(2)}, u32[]{:S(2)}) async-start(bf16[8,80,1536]{2,1,0:T(8,128)(2,1)} %bitcast.63), calls=%async_computation.1 | async-start | bytes 3932160 | tf_op jit(solution)/shard_map/all_to_all | solution.py:682
  257.0 198.1 %all-to-all-start.4 = ((bf16[16,2,192,384]{3,2,1,0:T(8,128)(2,1)}), bf16[16,2,192,384]{3,2,1,0:T(8,128)(2,1)}, u32[]{:S(2)}, u32[]{:S(2)}) async-start(bf16[16,2,192,384]{3,2,1,0:T(8,128)(2,1)} %bitcast.55), calls=%async_computation.4 | async-start | bytes 9437184 | tf_op jit(solution)/shard_map/all_to_all | solution.py:703
  261.6 191.7 %all-reduce.2.cloned.1.call-start = ((), (), s32[]{:S(2)}) async-start(), calls=%async_computation.5 | async-start | bytes 942080 | tf_op jit(solution)/shard_map/psum | solution.py:700
  (6 other events, 24.8 us)
Sparse Core Ops, SparseCore 0:
  267.7 185.5 all-reduce.1

commit v2 on v1

--- a/solution.py
+++ b/solution.py
@@ -231,43 +231,80 @@
     return lax.dot_general(a, b, (dims, ((), ())), preferred_element_type=F32)
 
 
-def merge_kernel(order_ref, place_ref, coef_ref, one_ref, two_ref, out_ref):
-    first = 2 * combo_of(pl.program_id(0), pl.program_id(1), place_ref)
-    one = coef_ref[order_ref[first]]
-    two = coef_ref[order_ref[first + 1]]
-    out_ref[0, 0] = (one * one_ref[0].astype(F32) + two * two_ref[0].astype(F32)).astype(BF)
-
-
-def combo_of(step, member, place_ref):
-    return 4 * jnp.bitwise_xor(place_ref[0], step) + 2 * place_ref[1] + member
-
-
-def merge_experts(order, where_am_i, merge_coef, source_w, places):
-    _, rows, width = source_w.shape
+def merge_kernel(map_ref, coef_ref, place_ref, src_ref, out_ref, order_ref, count_ref, held, sems):
+    halves, places = out_ref.shape[:2]
+    half = held.shape[2]
+    expert_order(map_ref, order_ref, count_ref)
+    at = pl.ds(pl.multiple_of(place_ref[1] * half, half), half)
+    copies, experts = [], []
+    for j in range(places):
+        for m in range(2):
+            combo = 4 * j + 2 * place_ref[0] + m
+            for n in range(2):
+                expert = order_ref[2 * combo + n]
+                experts.append(expert)
+                i = len(copies)
+                copies.append(
+                    pltpu.make_async_copy(src_ref.at[expert, :, at], held.at[i], sems.at[i])
+                )
+                copies[-1].start()
+    for j in range(places):
+        for m in range(2):
+            i = 4 * j + 2 * m
+            copies[i].wait()
+            copies[i + 1].wait()
+            one, two = coef_ref[experts[i]], coef_ref[experts[i + 1]]
+            merged = (one * held[i].astype(F32) + two * held[i + 1].astype(F32)).astype(BF)
+            for h in range(halves):
+                out_ref[h, j, m] = merged
+
+
+def expert_order(map_ref, order_ref, count_ref):
+    @pl.loop(0, count_ref.shape[0])
+    def _(g):
+        count_ref[g] = 0
+
+    @pl.loop(0, order_ref.shape[0])
+    def _(e):
+        g = map_ref[e]
+        n = count_ref[g]
+        order_ref[2 * g + n] = e
+        count_ref[g] = n + 1
+
+
+def merge_experts(where_am_i, merge_map, merge_coef, source_w, places):
+    count, rows, width = source_w.shape
     half = width // 2
-
-    def pick(which):
-        def index(j, m, order_ref, place_ref):
-            return (order_ref[2 * combo_of(j, m, place_ref) + which], 0, place_ref[2])
-
-        return index
-
     return pl.pallas_call(
         merge_kernel,
-        grid_spec=pltpu.PrefetchScalarGridSpec(
-            num_scalar_prefetch=2,
-            grid=(places, 2),
-            in_specs=[
-                smem_spec(),
-                pl.BlockSpec((1, rows, half), pick(0)),
-                pl.BlockSpec((1, rows, half), pick(1)),
-            ],
-            out_specs=pl.BlockSpec((1, 1, rows, half), lambda j, m, *_: (j, m, 0, 0)),
-        ),
-        out_shape=jax.ShapeDtypeStruct((places, 2, rows, half), BF),
+        in_specs=[smem_spec(), smem_spec(), smem_spec(), any_spec()],
+        out_specs=vmem_spec(),
+        out_shape=jax.ShapeDtypeStruct((2, places, 2, rows, half), BF),
+        scratch_shapes=[
+            pltpu.SMEM((count,), I32),
+            pltpu.SMEM((count // 2,), I32),
+            pltpu.VMEM((4 * places, rows, half), BF),
+            pltpu.SemaphoreType.DMA((4 * places,)),
+        ],
         compiler_params=params(56),
         name="merge_experts",
-    )(order, where_am_i, merge_coef, source_w, source_w)
+    )(merge_map, merge_coef, where_am_i, source_w)
+
+
+def hbm_spec():
+    return pl.BlockSpec(memory_space=pltpu.HBM)
+
+
+def hold(arrays, *after):
+    count = len(arrays)
+    return pl.pallas_call(
+        lambda *refs: None,
+        in_specs=[hbm_spec()] * count + [any_spec()] * len(after),
+        out_specs=[hbm_spec()] * count,
+        out_shape=[jax.ShapeDtypeStruct(a.shape, a.dtype) for a in arrays],
+        input_output_aliases={i: i for i in range(count)},
+        name="hold",
+    )(*arrays, *after)
 
 
 def column(row):
@@ -287,28 +324,37 @@
     return lax.broadcasted_iota(I32, (sources, tok), 0) == idx_ref[k : k + 1, :]
 
 
+def place_rows(refs, at, rows):
+    each = refs[0].shape[0]
+    rows = rows.astype(BF)
+    for d, ref in enumerate(refs):
+        ref[:, at : at + rows.shape[1]] = rows[d * each : (d + 1) * each]
+
+
 def route_kernel(
     capacity, lanes,
-    xt_ref, rwt_ref, rb_ref, idx_ref, map_ref, hid_ref, og_ref,
-    sh_ref, sg_ref, gate_ref, pos_ref, slot_ref,
+    me_ref, xt_ref, rwt_ref, rb_ref, idx_ref, map_ref, hid_ref, og_ref, _, *refs
 ):
+    sends, (gate_ref, pos_ref, slot_ref) = refs[:-3], refs[-3:]
     top, tok = idx_ref.shape
     sources = rwt_ref.shape[0]
     slots, width = hid_ref.shape
     places = lanes * capacity
-    logits = jnp.dot(rwt_ref[...], xt_ref[...], preferred_element_type=F32) + rb_ref[...]
+    logits = jnp.dot(rwt_ref[...], xt_ref[...], preferred_element_type=F32) + column(rb_ref[...])
     raised, merged = [], []
+    combos = column(map_ref[...])
     for k in range(top):
         pick = picks_of(idx_ref, k, sources)
         chosen = jnp.sum(jnp.where(pick, logits, 0.0), axis=0, keepdims=True)
         raised.append(jnp.exp(chosen))
-        merged.append(jnp.sum(jnp.where(pick, map_ref[...], 0), axis=0, keepdims=True))
+        merged.append(jnp.sum(jnp.where(pick, combos, 0), axis=0, keepdims=True))
     total = raised[0]
     for k in range(1, top):
         total = total + raised[k]
     gates = [r / total for r in raised]
     lane = [jnp.right_shift(g, 1) for g in merged]
     member = [jnp.bitwise_and(g, 1) for g in merged]
+    partner = [jnp.bitwise_xor(l, me_ref[0]) for l in lane]
     onehot = [(lax.broadcasted_iota(I32, (lanes, tok), 0) == l).astype(F32) for l in lane]
     all_hot = onehot[0]
     for k in range(1, top):
@@ -321,7 +367,7 @@
     for k in range(top):
         rank = jnp.sum(before * onehot[k], axis=0, keepdims=True).astype(I32)
         before = before + onehot[k]
-        position.append(jnp.where(rank < capacity, lane[k] * capacity + rank, -1))
+        position.append(jnp.where(rank < capacity, partner[k] * capacity + rank, -1))
     gate_ref[...] = jnp.zeros_like(gate_ref)
     pos_ref[...] = jnp.full_like(pos_ref, -1)
     for k in range(top):
@@ -349,55 +395,53 @@
     slot_ref[...] = jnp.broadcast_to(slot_pos, slot_ref.shape)
     take = lax.broadcasted_iota(I32, (places, slots), 0) == slot_pos
     placed = jnp.sum(jnp.where(take, spot[3:4].astype(F32), 0.0), axis=1, keepdims=True)
-    sh_ref[:, width:] = jnp.broadcast_to(placed, (places, sh_ref.shape[1] - width)).astype(BF)
+    depth = og_ref.shape[1]
+    place_rows(sends, depth + width, jnp.broadcast_to(placed, (places, 128)))
     take = take.astype(BF)
     for n in range(0, width, TILE):
-        sh_ref[:, n : n + TILE] = jnp.dot(
-            take, hid_ref[:, n : n + TILE], preferred_element_type=F32
-        ).astype(BF)
+        rows = jnp.dot(take, hid_ref[:, n : n + TILE], preferred_element_type=F32)
+        place_rows(sends, depth + n, rows)
     takes = [
         (lax.broadcasted_iota(I32, (places, tok), 0) == position[k]).astype(BF) for k in range(top)
     ]
     columns = [column(g) for g in gates]
-    for n in range(0, og_ref.shape[1], TILE):
+    for n in range(0, depth, TILE):
         og = og_ref[:, n : n + TILE].astype(F32)
         rows = jnp.zeros((places, TILE), F32)
         for k in range(top):
             rows = rows + jnp.dot(takes[k], (columns[k] * og).astype(BF), preferred_element_type=F32)
-        sg_ref[:, n : n + TILE] = rows.astype(BF)
-
-
-def route(xt, rwt, router_b, idx_t, merge_map, hid, og, capacity, lanes):
-    places = lanes * capacity
+        place_rows(sends, n, rows)
+
+
+def route(me, xt, rwt, router_b, idx_t, merge_map, hid, og, after, capacity, lanes):
     slots, width = hid.shape
     tok = idx_t.shape[1]
     return pl.pallas_call(
         functools.partial(route_kernel, capacity, lanes),
-        in_specs=[vmem_spec()] * 7,
-        out_specs=[vmem_spec()] * 5,
-        out_shape=[
-            jax.ShapeDtypeStruct((places, width + 128), BF),
-            jax.ShapeDtypeStruct((places, og.shape[1]), BF),
+        in_specs=[smem_spec()] + [vmem_spec()] * 7 + [any_spec()],
+        out_specs=[vmem_spec()] * (lanes + 3),
+        out_shape=[jax.ShapeDtypeStruct((capacity, og.shape[1] + width + 128), BF)] * lanes
+        + [
             jax.ShapeDtypeStruct((8, tok), F32),
             jax.ShapeDtypeStruct((8, tok), I32),
             jax.ShapeDtypeStruct((8, slots), I32),
         ],
         compiler_params=params(56),
         name="route",
-    )(xt, rwt, router_b[:, None], idx_t, merge_map[:, None], hid, og)
-
-
-def load_weights(spot_ref, mine, other, w_ref, sems):
-    rows = mine[0].shape[1]
-    core = spot_ref[8]
+    )(me, xt, rwt, router_b[None, :], idx_t, merge_map[None, :], hid, og, after)
+
+
+def load_weights(core_ref, mine, other, w_ref, sems):
+    core = core_ref[0]
+    blocks, _, rows, _ = mine.shape
     copies = []
-    for d in range(len(mine)):
-        at = pl.ds(pl.multiple_of(spot_ref[d], rows), rows)
-        for n, part in enumerate((mine[d], other[d])):
+    for c in range(blocks):
+        at = pl.ds(c * rows, rows)
+        for n, part in enumerate((mine, other)):
+            to = core if n == 0 else 1 - core
+            i = 2 * c + n
             copies.append(
-                pltpu.make_async_copy(
-                    part, w_ref.at[core if n == 0 else 1 - core, :, at, :], sems.at[2 * d + n]
-                )
+                pltpu.make_async_copy(part.at[c], w_ref.at[to, :, at, :], sems.at[i])
             )
     for copy in copies:
         copy.start()
@@ -405,52 +449,54 @@
         copy.wait()
 
 
-def forward_kernel(spot_ref, rows_ref, *refs):
-    parts, (out_ref, w_ref, sems) = refs[:-3], refs[-3:]
-    load_weights(spot_ref, parts[0::2], parts[1::2], w_ref, sems)
+def forward_kernel(core_ref, rows_ref, flag_ref, mine, other, *refs):
+    outs, (w_ref, sems) = refs[:-2], refs[-2:]
+    load_weights(core_ref, mine, other, w_ref, sems)
     half = w_ref.shape[3]
-    member = rows_ref[:, 2 * half : 2 * half + 1].astype(F32)
-
-    @pl.loop(0, out_ref.shape[1] // TILE)
-    def _(n):
-        at = pl.ds(pl.multiple_of(n * TILE, TILE), TILE)
+    member = flag_ref[:, :1].astype(F32)
+
+    for n in range(0, w_ref.shape[2], TILE):
+        at = slice(n, n + TILE)
         both = [
             dot(rows_ref[:, :half], w_ref[0, m, at, :], ((1,), (1,)))
             + dot(rows_ref[:, half : 2 * half], w_ref[1, m, at, :], ((1,), (1,)))
             for m in range(2)
         ]
-        out_ref[:, at] = jnp.where(member == 0.0, both[0], both[1]).astype(BF)
-
-
-def backward_kernel(spot_ref, rows_ref, flag_ref, *refs):
-    parts, (out_ref, w_ref, sems) = refs[:-3], refs[-3:]
-    load_weights(spot_ref, parts[0::2], parts[1::2], w_ref, sems)
+        place_rows(outs, n, jnp.where(member == 0.0, both[0], both[1]))
+
+
+def backward_kernel(core_ref, rows_ref, flag_ref, mine, other, *refs):
+    outs, (w_ref, sems) = refs[:-2], refs[-2:]
+    load_weights(core_ref, mine, other, w_ref, sems)
     half = w_ref.shape[3]
     member = flag_ref[:, :1].astype(F32)
     for h in range(2):
-
-        @pl.loop(0, half // TILE)
-        def _(n, h=h):
-            at = pl.ds(pl.multiple_of(n * TILE, TILE), TILE)
+        for n in range(0, half, TILE):
+            at = slice(n, n + TILE)
             both = [dot(rows_ref[...], w_ref[h, m, :, at], ((1,), (0,))) for m in range(2)]
-            to = pl.ds(pl.multiple_of(h * half + n * TILE, TILE), TILE)
-            out_ref[:, to] = jnp.where(member == 0.0, both[0], both[1]).astype(BF)
-
-
-def run_lane(kernel, spots, row_args, row_specs, mine, other, out_width, name):
-    parts = [p for pair in zip(mine, other) for p in pair]
-    members, rows, half = mine[0].shape
-    depth = rows * len(mine)
-    count = row_args[0].shape[0]
+            place_rows(outs, h * half + n, jnp.where(member == 0.0, both[0], both[1]))
+
+
+def run_lane(kernel, core, rows, which, mine, other, lanes, name):
+    blocks, members, share, half = mine.shape
+    depth = share * blocks
+    count = rows.shape[0]
+    wide = (rows.shape[1] - 128) // 2
     return pl.pallas_call(
         kernel,
         grid=(1,),
-        in_specs=[smem_spec()] + row_specs + [any_spec()] * len(parts),
-        out_specs=pl.BlockSpec((count, out_width), lambda i: (0, 0)),
-        out_shape=jax.ShapeDtypeStruct((count, out_width), BF),
+        in_specs=[
+            smem_spec(),
+            pl.BlockSpec((count, wide), lambda i: (0, which)),
+            pl.BlockSpec((count, 128), lambda i: (0, 2 * wide // 128)),
+            hbm_spec(),
+            hbm_spec(),
+        ],
+        out_specs=[pl.BlockSpec((count // lanes, wide), lambda i: (0, 0))] * lanes,
+        out_shape=[jax.ShapeDtypeStruct((count // lanes, wide), BF)] * lanes,
         scratch_shapes=[
             pltpu.VMEM((2, members, depth, half), BF),
-            pltpu.SemaphoreType.DMA((len(parts),)),
+            pltpu.SemaphoreType.DMA((2 * blocks,)),
         ],
         compiler_params=params(56),
         cost_estimate=pl.CostEstimate(
@@ -459,32 +505,29 @@
             transcendentals=0,
         ),
         name=name,
-    )(spots, *row_args, *parts)
-
-
-def lane_grad_kernel(has_other, _, hid_ref, flag_ref, grd_ref, *refs):
+    )(core, rows, rows, mine, other)
+
+
+def lane_grad_kernel(has_other, _, grd_ref, hid_ref, flag_ref, *refs):
     out_ref = refs[-1]
     chosen = flag_ref[:, :1].astype(F32) == pl.program_id(1).astype(F32)
     hid = jnp.where(chosen, hid_ref[...], jnp.zeros_like(hid_ref))
     blocks, _, _, rows, cols = out_ref.shape
-    each = 2
-
-    @pl.loop(0, blocks // each)
-    def _(n):
-        at = pl.ds(pl.multiple_of(n * each * rows, each * rows), each * rows)
-        part = dot(grd_ref[:, at], hid, ((0,), (0,))).reshape(each, rows, cols)
-        to = pl.ds(n * each, each)
+    each = 2 if blocks % 2 == 0 and 2 * rows % 128 == 0 else blocks
+    for n in range(0, blocks, each):
+        part = dot(grd_ref[:, n * rows : (n + each) * rows], hid, ((0,), (0,)))
+        part = part.reshape(each, rows, cols)
         if has_other:
-            part = part + refs[0][to, 0, 0].astype(F32)
-        out_ref[to, 0, 0] = part.astype(BF)
-
-
-def lane_grads(select, hid, grd, other, blocks, reps):
-    count, depth = grd.shape
-    width = hid.shape[1] - 128
+            part = part + refs[0][n : n + each, 0, 0].astype(F32)
+        out_ref[n : n + each, 0, 0] = part.astype(BF)
+
+
+def lane_grads(core, rows, other, blocks, reps):
+    count = rows.shape[0]
+    width = (rows.shape[1] - 128) // 2
     cols = width // reps
-    shape = (blocks, 2, 2, depth // blocks, cols)
-    block = pl.BlockSpec((blocks, 1, 1, depth // blocks, cols), lambda y, m, s: (0, y, m, 0, 0))
+    shape = (blocks, 2, 2, width // blocks, cols)
+    block = pl.BlockSpec((blocks, 1, 1, width // blocks, cols), lambda y, m, s: (0, y, m, 0, 0))
     extra = [] if other is None else [other]
     return pl.pallas_call(
         functools.partial(lane_grad_kernel, other is not None),
@@ -492,9 +535,9 @@
             num_scalar_prefetch=1,
             grid=(2, 2),
             in_specs=[
-                pl.BlockSpec((count, cols), lambda y, m, s: (0, 2 * y + s[0])),
-                pl.BlockSpec((count, 128), lambda y, m, s: (0, width // 128)),
-                pl.BlockSpec((count, depth), lambda y, m, s: (0, 0)),
+                pl.BlockSpec((count, width), lambda y, m, s: (0, 0)),
+                pl.BlockSpec((count, cols), lambda y, m, s: (0, reps + 2 * y + s[0])),
+                pl.BlockSpec((count, 128), lambda y, m, s: (0, 2 * width // 128)),
             ]
             + [block] * len(extra),
             out_specs=block,
@@ -502,17 +545,23 @@
         out_shape=jax.ShapeDtypeStruct(shape, BF),
         compiler_params=params(56),
         cost_estimate=pl.CostEstimate(
-            flops=4 * count * depth * cols * 2,
-            bytes_accessed=4 * depth * cols * 4 + 4 * count * depth,
+            flops=8 * count * width * cols,
+            bytes_accessed=8 * width * cols + 4 * count * width,
             transcendentals=0,
         ),
         name="lane_grads_add" if extra else "lane_grads_first",
-    )(select, hid, hid, grd, *extra)
-
-
-def combine_kernel(
-    out_ref, og_ref, gate_ref, pos_ref, idx_ref, rwt_ref, xt_ref, mixed_ref, tg_ref, part_ref
-):
+    )(core, rows, rows, rows, *extra)
+
+
+def gather_rows(refs, keep):
+    each = refs[0].shape[0]
+    for d, ref in enumerate(refs):
+        keep[d * each : (d + 1) * each, :] = ref[...]
+
+
+def combine_kernel(og_ref, gate_ref, pos_ref, idx_ref, rwt_ref, xt_ref, *refs):
+    homes, (mixed_ref, tg_ref, part_ref, out_ref) = refs[:-4], refs[-4:]
+    gather_rows(homes, out_ref)
     places, width = out_ref.shape
     top, tok = idx_ref.shape
     sources, features = rwt_ref.shape
@@ -542,30 +591,34 @@
         logit_grad = logit_grad + jnp.where(picks_of(idx_ref, k, sources), chosen_grad, 0.0)
     logit_half = logit_grad.astype(BF)
     tg_ref[...] = dot(rwt_ref[...], logit_half, ((0,), (0,))).astype(BF)
-    part_ref[:sources, :] = dot(logit_half, xt_ref[...], ((1,), (1,)))
-    part_ref[sources:, :] = jnp.zeros_like(part_ref[sources:, :])
-    bias = to_row(jnp.sum(logit_grad, axis=1, keepdims=True))
-    part_ref[sources : sources + 1, :sources] = bias
-
-
-def combine(home_out, og, gates, pos, idx_t, rwt, xt):
+    part_ref[...] = jnp.zeros_like(part_ref)
+    part_ref[:, :features] = dot(logit_half, xt_ref[...], ((1,), (1,)))
+    bias = jnp.sum(logit_grad, axis=1, keepdims=True)
+    last = part_ref.shape[1] - 128
+    part_ref[:, last:] = jnp.broadcast_to(bias, (sources, 128))
+
+
+def combine(homes, og, gates, pos, idx_t, rwt, xt):
     sources, features = rwt.shape
     tok = idx_t.shape[1]
     return pl.pallas_call(
         combine_kernel,
-        in_specs=[vmem_spec()] * 7,
+        in_specs=[vmem_spec()] * (6 + len(homes)),
         out_specs=[vmem_spec()] * 3,
         out_shape=[
             jax.ShapeDtypeStruct(og.shape, BF),
             jax.ShapeDtypeStruct((features, tok), BF),
-            jax.ShapeDtypeStruct((sources + 8, features), F32),
+            jax.ShapeDtypeStruct((sources, (features + 127) // 128 * 128 + 128), F32),
         ],
+        scratch_shapes=[pltpu.VMEM((len(homes) * homes[0].shape[0], homes[0].shape[1]), BF)],
         compiler_params=params(56),
         name="combine",
-    )(home_out, og, gates, pos, idx_t, rwt, xt)
-
-
-def unplace_kernel(back_ref, slot_ref, out_ref):
+    )(og, gates, pos, idx_t, rwt, xt, *homes)
+
+
+def unplace_kernel(slot_ref, *refs):
+    homes, (out_ref, back_ref) = refs[:-2], refs[-2:]
+    gather_rows(homes, back_ref)
     places, width = back_ref.shape
     slots = slot_ref.shape[1]
     take = (lax.broadcasted_iota(I32, (places, slots), 0) == slot_ref[0:1, :]).astype(BF)
@@ -573,55 +626,132 @@
         out_ref[:, n : n + TILE] = dot(take, back_ref[:, n : n + TILE], ((0,), (0,))).astype(BF)
 
 
-def unplace(home_back, slot_pos):
+def unplace(homes, slot_pos):
+    rows, width = homes[0].shape
     return pl.pallas_call(
         unplace_kernel,
-        in_specs=[vmem_spec()] * 2,
+        in_specs=[vmem_spec()] * (1 + len(homes)),
         out_specs=vmem_spec(),
-        out_shape=jax.ShapeDtypeStruct((slot_pos.shape[1], home_back.shape[1]), BF),
+        out_shape=jax.ShapeDtypeStruct((slot_pos.shape[1], width), BF),
+        scratch_shapes=[pltpu.VMEM((len(homes) * rows, width), BF)],
         compiler_params=params(56),
         name="unplace",
-    )(home_back, slot_pos)
-
-
-def finish_kernel(scale, order_ref, rep_ref, coef_ref, got_ref, src_ref, out_ref, dot_ref):
-    merged = got_ref[0, 0].astype(F32) + got_ref[1, 0].astype(F32)
-    expert = order_ref[pl.program_id(0)]
-    out_ref[0] = merged * (coef_ref[expert] * scale)
-    product = merged * src_ref[0].astype(F32)
-    rows, cols = product.shape
-    folded = jnp.sum(product.reshape(rows // 8, 8, cols), axis=0)
-    total = folded[:, :128]
-    for n in range(128, cols, 128):
-        total = total + folded[:, n : n + 128]
-    dot_ref[0] = total
-
-
-def finish(order, rep_index, merge_coef, arrived, source_w, scale):
-    halves, _, rows, cols = arrived.shape
+    )(slot_pos, *homes)
+
+
+def coef_kernel(rep_ref, map_ref, src_ref, got_ref, out_ref, order_ref, count_ref, held, weights, sems):
+    count, rows, cols = weights.shape
+    at = pl.ds(pl.multiple_of(rep_ref[0] * cols, cols), cols)
+    copies = [
+        pltpu.make_async_copy(src_ref.at[:, :, at], weights, sems.at[0]),
+        pltpu.make_async_copy(got_ref, held, sems.at[1]),
+    ]
+    for copy in copies:
+        copy.start()
+    expert_order(map_ref, order_ref, count_ref)
+    for copy in copies:
+        copy.wait()
+    lane = lax.broadcasted_iota(I32, (8, 128), 1)
+
+    def one(g, total):
+        merged = held[0, g].astype(F32) + held[1, g].astype(F32)
+        for n in range(2):
+            expert = order_ref[2 * g + n]
+            product = merged * weights[expert].astype(F32)
+            folded = jnp.sum(product.reshape(rows // 8, 8, cols), axis=0)
+            small = folded[:, :128]
+            for c in range(128, cols, 128):
+                small = small + folded[:, c : c + 128]
+            small = jnp.sum(jnp.sum(small, axis=0, keepdims=True), axis=1, keepdims=True)
+            total = total + jnp.where(lane == expert, small, 0.0)
+        return total
+
+    out_ref[...] = lax.fori_loop(0, count // 2, one, jnp.zeros((8, 128), F32))
+
+
+def finish_kernel(scale, map_ref, coef_ref, got_ref, out_ref, order_ref, count_ref, held, ready, sems, more):
+    count = ready.shape[0]
+
+    def load(g):
+        return pltpu.make_async_copy(got_ref.at[:, g], held.at[:, g], sems.at[g])
+
+    def send(i):
+        return pltpu.make_async_copy(ready.at[i], out_ref.at[order_ref[i]], more.at[i])
+
+    @pl.loop(0, count // 2)
+    def _(g):
+        load(g).start()
+
+    expert_order(map_ref, order_ref, count_ref)
+
+    @pl.loop(0, count // 2)
+    def _(g):
+        load(g).wait()
+        merged = held[0, g].astype(F32) + held[1, g].astype(F32)
+        for n in range(2):
+            i = 2 * g + n
+            ready[i] = merged * (coef_ref[order_ref[i]] * scale)
+            send(i).start()
+
+    @pl.loop(0, count)
+    def _(i):
+        send(i).wait()
+
+
+def coef_dots(rep_index, merge_map, source_w, arrived):
     count = source_w.shape[0]
+    _, _, rows, cols = arrived.shape
     return pl.pallas_call(
-        functools.partial(finish_kernel, scale),
-        grid_spec=pltpu.PrefetchScalarGridSpec(
-            num_scalar_prefetch=2,
-            grid=(count,),
-            in_specs=[
-                smem_spec(),
-                pl.BlockSpec((halves, 1, rows, cols), lambda i, o, r: (0, i // 2, 0, 0)),
-                pl.BlockSpec((1, rows, cols), lambda i, o, r: (o[i], 0, r[0])),
-            ],
-            out_specs=[
-                pl.BlockSpec((1, rows, cols), lambda i, o, r: (o[i], 0, 0)),
-                pl.BlockSpec((1, 8, 128), lambda i, o, r: (o[i], 0, 0)),
-            ],
-        ),
-        out_shape=[
-            jax.ShapeDtypeStruct((count, rows, cols), F32),
-            jax.ShapeDtypeStruct((count, 8, 128), F32),
+        coef_kernel,
+        in_specs=[smem_spec(), smem_spec(), hbm_spec(), hbm_spec()],
+        out_specs=vmem_spec(),
+        out_shape=jax.ShapeDtypeStruct((8, 128), F32),
+        scratch_shapes=[
+            pltpu.SMEM((count,), I32),
+            pltpu.SMEM((count // 2,), I32),
+            pltpu.VMEM(arrived.shape, BF),
+            pltpu.VMEM((count, rows, cols), BF),
+            pltpu.SemaphoreType.DMA((2,)),
         ],
         compiler_params=params(56),
+        name="coef_dots",
+    )(rep_index, merge_map, source_w, arrived)
+
+
+def finish(merge_map, merge_coef, arrived, after, scale):
+    count = merge_map.shape[0]
+    _, _, rows, cols = arrived.shape
+    return pl.pallas_call(
+        lambda a, b, c, _, *refs: finish_kernel(scale, a, b, c, *refs),
+        in_specs=[smem_spec(), smem_spec(), hbm_spec(), any_spec()],
+        out_specs=hbm_spec(),
+        out_shape=jax.ShapeDtypeStruct((count, rows, cols), F32),
+        scratch_shapes=[
+            pltpu.SMEM((count,), I32),
+            pltpu.SMEM((count // 2,), I32),
+            pltpu.VMEM(arrived.shape, BF),
+            pltpu.VMEM((count, rows, cols), F32),
+            pltpu.SemaphoreType.DMA((count // 2,)),
+            pltpu.SemaphoreType.DMA((count,)),
+        ],
+        compiler_params=params(56),
+        cost_estimate=pl.CostEstimate(
+            flops=4 * count * rows * cols,
+            bytes_accessed=8 * count * rows * cols,
+            transcendentals=0,
+        ),
         name="finish",
-    )(order, rep_index, merge_coef, arrived, source_w)
+    )(merge_map, merge_coef, arrived, after)
+
+
+def add_up(x, bits):
+    for axis, distance, bit in bits:
+        x = x.reshape((2, x.shape[0] // 2) + x.shape[1:])
+        keep = lax.dynamic_index_in_dim(x, bit, 0, keepdims=False)
+        give = lax.dynamic_index_in_dim(x, 1 - bit, 0, keepdims=False)
+        size = lax.axis_size(axis)
+        x = keep + lax.ppermute(give, axis, [(i, i ^ distance) for i in range(size)])
+    return x
 
 
 def swap(x):
@@ -647,75 +777,77 @@
     half_i, place_i = lax.axis_index("half"), lax.axis_index("place")
     row_i, core_i = lax.axis_index("row"), lax.axis_index("core")
     ctx_i = half_i * places + place_i
-    numbers = jnp.arange(sources, dtype=I32)
-    same = merge_map[:, None] == merge_map[None, :]
-    rank = jnp.sum((same & (numbers[:, None] > numbers[None, :])).astype(I32), axis=1)
-    target = 2 * merge_map + rank
-    order = jnp.sum(jnp.where(target[None, :] == numbers[:, None], numbers[None, :], 0), axis=1)
-    order = order.astype(I32)
-    me = jnp.stack([place_i, row_i, core_i]).astype(I32)
-    rep_index = (2 * row_i + core_i).astype(I32)[None]
-
-    combos = merge_experts(order, me, merge_coef, source_w, places)
-    mine = [combos[0]]
-    for d in range(1, blocks):
-        mine.append(
-            lax.ppermute(
-                combos[d % places], ("half", "place"), [(i, i ^ d) for i in range(blocks)]
-            )
-        )
-    other = [swap(part) for part in mine]
-    spots = jnp.stack(
-        [jnp.bitwise_xor(ctx_i, d) * row_share for d in range(blocks)] + [core_i]
-    ).astype(I32)
+    everyone = ("half", "place", "row", "core")
+    devices = blocks * reps
+
+    def stack(numbers):
+        return jnp.stack([jnp.asarray(n, I32) for n in numbers])
+
+    combos = merge_experts(stack([row_i, core_i]), merge_map, merge_coef, source_w, places)
+    mine = lax.all_to_all(
+        combos.reshape((blocks,) + combos.shape[2:]), ("half", "place"),
+        split_axis=0, concat_axis=0, tiled=True,
+    )
 
     xt = tokens.reshape(tok, features).T
     rwt = router_w.T
     idx_t = teacher_idx.reshape(tok, top).T
     og = out_grad.reshape(tok, depth)
-    send_hidden, send_grad, gates, pos, slot_pos = route(
-        xt, rwt, router_b, idx_t, merge_map, hidden.reshape(tok * top, width), og, capacity, lanes
-    )
-
-    def trade(rows):
-        rows = rows.reshape(lanes, capacity, rows.shape[1])
-        rows = lax.all_to_all(rows, ("place", "row"), split_axis=0, concat_axis=0, tiled=True)
-        return rows.reshape(lanes * capacity, rows.shape[2])
-
-    hid = trade(send_hidden)
-    grd = trade(send_grad)
-    first = lane_grads((1 - core_i).astype(I32)[None], hid, grd, None, blocks, reps)
-    summed = lane_grads(core_i.astype(I32)[None], hid, grd, swap(first), blocks, reps)
-    whole = lambda rows: pl.BlockSpec(rows.shape, lambda i: (0, 0))
-    out_rows = run_lane(
-        forward_kernel, spots, [hid], [whole(hid)], mine, other, depth, "lane_forward"
-    )
-    back_rows = run_lane(
-        backward_kernel, spots, [grd, hid],
-        [whole(grd), pl.BlockSpec((hid.shape[0], 128), lambda i: (0, width // 128))],
-        mine, other, width, "lane_backward",
-    )
-    home_out = trade(out_rows)
-    mixed, token_grad, part = combine(home_out, og, gates, pos, idx_t, rwt, xt)
-    part = lax.psum(part, ("half", "place", "row", "core"))
-    home_back = trade(back_rows)
-    hidden_grad = unplace(home_back, slot_pos)
+    *parts, gates, pos, slot_pos = route(
+        stack([2 * place_i + row_i]), xt, rwt, router_b, idx_t, merge_map,
+        hidden.reshape(tok * top, width), og, combos, capacity, lanes,
+    )
+
+    def trade(parts):
+        return [parts[0]] + [
+            lax.ppermute(parts[d], ("place", "row"), [(i, i ^ d) for i in range(lanes)])
+            for d in range(1, lanes)
+        ]
+
+    rows = jnp.concatenate(trade(parts), axis=0)
+    here = stack([core_i])
+    first = lane_grads(stack([1 - core_i]), rows, None, blocks, reps)
+    summed = lane_grads(here, rows, swap(first), blocks, reps)
     arrived = lax.all_to_all(
         summed.reshape(2 * blocks, 2, row_share, width // reps),
         ("half", "place", "row"), split_axis=0, concat_axis=0, tiled=True,
     )
-    source_w_grad, coef_part = finish(
-        order, rep_index, merge_coef,
-        arrived.reshape(2, 2 * lanes, row_share, width // reps), source_w, scale,
-    )
-    coef_sum = lax.psum(jnp.sum(coef_part, axis=(1, 2)), ("half", "place", "row", "core"))
+
+    (mine,) = hold([mine], summed)
+    other = swap(mine)
+    out_parts = run_lane(forward_kernel, here, rows, 1, mine, other, lanes, "lane_forward")
+    home_out = trade(out_parts)
+    back_parts = run_lane(backward_kernel, here, rows, 0, mine, other, lanes, "lane_backward")
+    mixed, token_grad, part = combine(home_out, og, gates, pos, idx_t, rwt, xt)
+    hidden_grad = unplace(trade(back_parts), slot_pos)
+
+    part = add_up(
+        part,
+        [
+            ("half", 1, half_i),
+            ("place", 2, place_i // 2),
+            ("place", 1, place_i % 2),
+            ("row", 1, row_i),
+            ("core", 1, core_i),
+        ],
+    )
+    (arrived,) = hold([arrived], hidden_grad, part)
+    arrived = arrived.reshape(2, 2 * lanes, row_share, width // reps)
+    dots = coef_dots(stack([2 * row_i + core_i]), merge_map, source_w, arrived)
+    news = jnp.concatenate([part, dots[:1]], axis=1)
+    news = lax.all_to_all(
+        jnp.broadcast_to(news[None], (devices,) + news.shape), everyone,
+        split_axis=0, concat_axis=0, tiled=True,
+    )
+    source_w_grad = finish(merge_map, merge_coef, arrived, dots, scale)
+    end = part.shape[1]
     return (
         mixed.reshape(1, tok, depth),
         hidden_grad.reshape(1, tok, top, width),
         token_grad.T.reshape(1, tok, features),
-        part[:sources].T * scale,
-        part[sources, :sources] * scale,
-        coef_sum * scale,
+        news[:, 0, :features].T * scale,
+        news[:, 0, end - 1] * scale,
+        jnp.sum(news[:, 0, end : end + sources], axis=0) * scale,
         source_w_grad,
     )
 

time: 528 us -> 407 us (0.77)
  blocking collectives: 72 us -> 0 us
  waiting for transfers between devices: 290 us -> 245 us
  starting transfers between devices: 32.9 us -> 57.2 us
  Pallas kernels: 95.9 us -> 79.8 us
  between operations: 14.2 us -> 1.01 us
    psum x1 -> x0, waiting for transfers between devices: 178 us -> none  [on_pairs(): part = lax.psum(part, ('half', 'place', 'row', 'core'))]
    ppermute x7 -> x26, waiting for transfers between devices: 93.6 us -> 229 us  [the longest x21 213 us: trade(): lax.ppermute(parts[d], ('place', 'row'), [(i, i ^ d) for i in range(lanes)])]
    psum x1 -> x0, blocking collectives: 40.4 us -> none  [on_pairs(): lax.psum(jnp.sum(coef_part, axis=(1, 2)), ('half', 'place', 'row', 'core'))]
    all_to_all x1 -> x0, blocking collectives: 31.6 us -> none  [trade(): lax.all_to_all(rows, ('place', 'row'), split_axis=0, concat_axis=0, tiled...]
    ppermute x7 -> x26, starting transfers between devices: 10.4 us -> 41.5 us  [the longest x21 37.2 us: trade(): lax.ppermute(parts[d], ('place', 'row'), [(i, i ^ d) for i in range(lanes)])]
    pallas_call x6 -> x9, Pallas kernels: 65.6 us -> 54.9 us  [the longest x2 25.6 us: run_lane(): pl.pallas_call(kernel, grid=(1,), in_specs=[smem_spec(), pl.BlockSpec((co...]
    all_to_all x3 -> x2, waiting for transfers between devices: 16 us -> 6.43 us  [the longest x1 6.43 us: on_pairs(): lax.all_to_all(jnp.broadcast_to(news[None], (devices,) + news.shape), eve...]
    all_to_all x3 -> x2, starting transfers between devices: 16.3 us -> 8.53 us  [the longest x1 5.94 us: on_pairs(): lax.all_to_all(combos.reshape((blocks,) + combos.shape[2:]), ('half', 'pl...]
  transfers between devices with their start and end apart: 21 -> 31, of which waited for: 11 -> 20; matrix products, arithmetic and copies ran while one was open for 2% -> 3% of each run, Pallas kernels for 10% -> 14%
where the time goes in v2:
time: 407 us; the launch traced here: 406 us
  waiting for transfers between devices  245 us (60%)
  Pallas kernels  79.8 us (20%)
  starting transfers between devices  57.2 us (14%)
  local copies, waits for them, and re-layouts  18.8 us (5%)
  other arithmetic  4.13 us (1%)
    ppermute x21, waiting for transfers between devices, trade(): lax.ppermute(parts[d], ('place', 'row'), [(i, i ^ d) for i in range(lanes)])  213 us
    ppermute x21, starting transfers between devices, trade(): lax.ppermute(parts[d], ('place', 'row'), [(i, i ^ d) for i in range(lanes)])  37.2 us
    pallas_call x2, Pallas kernels, run_lane(): pl.pallas_call(kernel, grid=(1,), in_specs=[smem_spec(), pl.BlockSpec((co...  25.6 us
    pallas_call x2, Pallas kernels, lane_grads(): pl.pallas_call(functools.partial(lane_grad_kernel, other is not None), gr...  17.5 us
    ppermute x5, waiting for transfers between devices, add_up(): lax.ppermute(give, axis, [(i, i ^ distance) for i in range(size)])  16.5 us
    unnamed x44, local copies, waits for them, and re-layouts  10.2 us
    ppermute x2, waiting for transfers between devices, swap(): return lax.ppermute(x, 'core', [(0, 1), (1, 0)])  9.32 us
    pallas_call x1, Pallas kernels, coef_dots(): pl.pallas_call(coef_kernel, in_specs=[smem_spec(), smem_spec(), hbm_spec(...  8.28 us
  transfers between devices with their start and end apart: 31, of which 20 were waited for; matrix products, arithmetic and copies ran while one was open for 3% of the time, Pallas kernels for 14%

profile of v2, /device:TPU:0, one launch (start us, length us, event | category | flops | bytes accessed | tf_op | source)
XLA Modules:
  0.0 405.8 jit_solution(8589419181805953002)
XLA Ops:
  4.9 5.9 %merge_experts.1._ = bf16[2,4,2,192,768]{4,3,2,1,0:T(8,128)(2,1)} custom-call(s32[32]{0:T(128)} %a.1, f32[32]{0:T(128)} %b.1, s32[2]{0:T(128)} %pad_add_fusion.place_ref, bf16[32,192,1536]{2,1,0:T(8,128)(2,1)} %src_ref.3), custom_call_target="tpu_custom_call" | custom-call | tf_op jit(solution)/shard_map/merge_experts/pallas_call | solution.py:278
  10.9 7.4 %route.1 = (bf16[80,3200]{1,0:T(8,128)(2,1)}, bf16[80,3200]{1,0:T(8,128)(2,1)}, bf16[80,3200]{1,0:T(8,128)(2,1)}, bf16[80,3200]{1,0:T(8,128)(2,1)}, bf16[80,3200...) custom-call(s32[1]{0:T(128)} %bitcast.1.me_ref, ...), custom_call_target="tpu_custom_call" | custom-call | tf_op jit(solution)/shard_map/route/pallas_call | solution.py:419
  26.3 5.9 %all-to-all-start = ((bf16[8,2,192,768]{3,2,1,0:T(8,128)(2,1)}), bf16[8,2,192,768]{3,2,1,0:T(8,128)(2,1)}, u32[]{:S(2)}, u32[]{:S(2)}) async-start(bf16[8,2,192,768]{3,2,1,0:T(8,128)(2,1)} %bitcast.49), calls=%async_computation | async-start | bytes 9437184 | tf_op jit(solution)/shard_map/all_to_all | solution.py:787
  36.9 10.2 %collective-permute-done.1 = bf16[80,3200]{1,0:T(8,128)(2,1)S(1)} collective-permute-done((bf16[80,3200]{1,0:T(8,128)(2,1)}, bf16[80,3200]{1,0:T(8,128)(2,1)S(1)}, u32[]{:S(2)}, u32[]{:S(2)}) %collective-permute-start.1) | collective-permute-done | bytes 512032 | tf_op jit(solution)/shard_map/ppermute | solution.py:803
  52.1 7.3 %collective-permute-done.2 = bf16[80,3200]{1,0:T(8,128)(2,1)S(1)} collective-permute-done((bf16[80,3200]{1,0:T(8,128)(2,1)}, bf16[80,3200]{1,0:T(8,128)(2,1)S(1)}, u32[]{:S(2)}, u32[]{:S(2)}) %collective-permute-start.2) | collective-permute-done | bytes 512032 | tf_op jit(solution)/shard_map/ppermute | solution.py:803
  61.9 79.9 %collective-permute-done.5 = bf16[80,3200]{1,0:T(8,128)(2,1)S(1)} collective-permute-done((bf16[80,3200]{1,0:T(8,128)(2,1)}, bf16[80,3200]{1,0:T(8,128)(2,1)S(1)}, u32[]{:S(2)}, u32[]{:S(2)}) %collective-permute-start.5) | collective-permute-done | bytes 512032 | tf_op jit(solution)/shard_map/ppermute | solution.py:803
  142.6 8.1 %collective-permute-done.6 = bf16[80,3200]{1,0:T(8,128)(2,1)S(1)} collective-permute-done((bf16[80,3200]{1,0:T(8,128)(2,1)}, bf16[80,3200]{1,0:T(8,128)(2,1)S(1)}, u32[]{:S(2)}, u32[]{:S(2)}) %collective-permute-start.6) | collective-permute-done | bytes 512032 | tf_op jit(solution)/shard_map/ppermute | solution.py:803
  151.5 8.4 %lane_grads_first.1 = bf16[8,2,2,192,384]{4,3,2,1,0:T(8,128)(2,1)} custom-call(s32[1]{0:T(128)} %bitcast.12._, bf16[640,3200]{1,0:T(8,128)(2,1)} %constant_dynamic-update-slice_fusion.grd_ref.hid_ref.flag_ref.rows_ref, bf16[640,3200]{1,0:T(8,128)(2,1)} %constant_dynamic-update-slice_fusion.grd_ref.hid_ref.flag_ref.rows_ref, ...), custom_call_target="tpu_custom_call" | custom-call | flops 3019898880 | bytes 8650752 | tf_op jit(solution)/shard_map/lane_grads_first/pallas_call | solution.py:532
  159.9 8.1 %collective-permute-done.7.refs_0_ = bf16[8,2,2,192,384]{4,3,2,1,0:T(8,128)(2,1)S(1)} collective-permute-done((bf16[8,2,2,192,384]{4,3,2,1,0:T(8,128)(2,1)}, bf16[8,2,2,192,384]{4,3,2,1,0:T(8,128)(2,1)S(1)}, u32[]{:S(2)}, u32[]{:S(2)}) %collective-permute-start.7) | collective-permute-done | bytes 4718624 | tf_op jit(solution)/shard_map/ppermute | solution.py:758
  170.2 9.2 %lane_grads_add.1.refs_1_ = bf16[8,2,2,192,384]{4,3,2,1,0:T(8,128)(2,1)} custom-call(s32[1]{0:T(128)} %bitcast.10._.core_ref, bf16[640,3200]{1,0:T(8,128)(2,1)} %constant_dynamic-update-slice_fusion.grd_ref.hid_ref.flag_ref.rows_ref, bf16[640,3200]{1,0:T(8,128)(2,1)} %constant_dynamic-update-slice_fusion.grd_ref.hid_ref.flag_ref.rows_ref, ...), custom_call_target="tpu_custom_call" | custom-call | flops 3019898880 | bytes 8650752 | tf_op jit(solution)/shard_map/lane_grads_add/pallas_call | solution.py:532
  179.6 6.9 %all-to-all-start.1 = ((bf16[16,2,192,384]{3,2,1,0:T(8,128)(2,1)}), bf16[16,2,192,384]{3,2,1,0:T(8,128)(2,1)}, u32[]{:S(2)}, u32[]{:S(2)}) async-start(bf16[16,2,192,384]{3,2,1,0:T(8,128)(2,1)} %bitcast.48), calls=%async_computation.1 | async-start | bytes 9437184 | tf_op jit(solution)/shard_map/all_to_all | solution.py:811
  187.7 12.8 %lane_forward.1 = (bf16[80,1536]{1,0:T(8,128)(2,1)}, bf16[80,1536]{1,0:T(8,128)(2,1)}, bf16[80,1536]{1,0:T(8,128)(2,1)}, bf16[80,1536]{1,0:T(8,128)(2,1)}, bf16[...) custom-call(s32[1]{0:T(128)} %bitcast.10._.core_ref, ...), custom_call_target="tpu_custom_call" | custom-call | flops 6039797760 | bytes 13369344 | tf_op jit(solution)/shard_map/lane_forward/pallas_call | solution.py:485
  209.8 11.6 %collective-permute-done.10.refs_2_ = bf16[80,1536]{1,0:T(8,128)(2,1)S(1)} collective-permute-done((bf16[80,1536]{1,0:T(8,128)(2,1)}, bf16[80,1536]{1,0:T(8,128)(2,1)S(1)}, u32[]{:S(2)}, u32[]{:S(2)}) %collective-permute-start.10) | collective-permute-done | bytes 245792 | tf_op jit(solution)/shard_map/ppermute | solution.py:803
  222.8 23.5 %collective-permute-done.11.refs_3_ = bf16[80,1536]{1,0:T(8,128)(2,1)S(1)} collective-permute-done((bf16[80,1536]{1,0:T(8,128)(2,1)}, bf16[80,1536]{1,0:T(8,128)(2,1)S(1)}, u32[]{:S(2)}, u32[]{:S(2)}) %collective-permute-start.11) | collective-permute-done | bytes 245792 | tf_op jit(solution)/shard_map/ppermute | solution.py:803
  246.8 27.0 %collective-permute-done.12.refs_4_ = bf16[80,1536]{1,0:T(8,128)(2,1)S(1)} collective-permute-done((bf16[80,1536]{1,0:T(8,128)(2,1)}, bf16[80,1536]{1,0:T(8,128)(2,1)S(1)}, u32[]{:S(2)}, u32[]{:S(2)}) %collective-permute-start.12) | collective-permute-done | bytes 245792 | tf_op jit(solution)/shard_map/ppermute | solution.py:803
  273.8 11.8 %collective-permute-done.13.refs_5_ = bf16[80,1536]{1,0:T(8,128)(2,1)S(1)} collective-permute-done((bf16[80,1536]{1,0:T(8,128)(2,1)}, bf16[80,1536]{1,0:T(8,128)(2,1)S(1)}, u32[]{:S(2)}, u32[]{:S(2)}) %collective-permute-start.13) | collective-permute-done | bytes 245792 | tf_op jit(solution)/shard_map/ppermute | solution.py:803
  285.5 8.7 %collective-permute-done.14.refs_6_ = bf16[80,1536]{1,0:T(8,128)(2,1)S(1)} collective-permute-done((bf16[80,1536]{1,0:T(8,128)(2,1)}, bf16[80,1536]{1,0:T(8,128)(2,1)S(1)}, u32[]{:S(2)}, u32[]{:S(2)}) %collective-permute-start.14) | collective-permute-done | bytes 245792 | tf_op jit(solution)/shard_map/ppermute | solution.py:803
  294.2 5.3 %collective-permute-done.15.refs_7_ = bf16[80,1536]{1,0:T(8,128)(2,1)S(1)} collective-permute-done((bf16[80,1536]{1,0:T(8,128)(2,1)}, bf16[80,1536]{1,0:T(8,128)(2,1)S(1)}, u32[]{:S(2)}, u32[]{:S(2)}) %collective-permute-start.15) | collective-permute-done | bytes 245792 | tf_op jit(solution)/shard_map/ppermute | solution.py:803
  309.6 7.8 %collective-permute-done.23 = f32[16,3072]{1,0:T(8,128)S(1)} collective-permute-done((f32[16,3072]{1,0:T(8,128)S(1)}, f32[16,3072]{1,0:T(8,128)S(1)}, u32[]{:S(2)}, u32[]{:S(2)}) %collective-permute-start.23) | collective-permute-done | bytes 196640 | tf_op jit(solution)/shard_map/ppermute | solution.py:753
  328.1 12.8 %lane_backward.1 = (bf16[80,1536]{1,0:T(8,128)(2,1)}, bf16[80,1536]{1,0:T(8,128)(2,1)}, bf16[80,1536]{1,0:T(8,128)(2,1)}, bf16[80,1536]{1,0:T(8,128)(2,1)}, bf16...) custom-call(s32[1]{0:T(128)} %bitcast.10._.core_ref, ...), custom_call_target="tpu_custom_call" | custom-call | flops 6039797760 | bytes 13369344 | tf_op jit(solution)/shard_map/lane_backward/pallas_call | solution.py:485
  347.3 12.3 %collective-permute-done.16.refs_1_ = bf16[80,1536]{1,0:T(8,128)(2,1)S(1)} collective-permute-done((bf16[80,1536]{1,0:T(8,128)(2,1)}, bf16[80,1536]{1,0:T(8,128)(2,1)S(1)}, u32[]{:S(2)}, u32[]{:S(2)}) %collective-permute-start.16) | collective-permute-done | bytes 245792 | tf_op jit(solution)/shard_map/ppermute | solution.py:803
  377.0 8.3 %coef_dots.1._ = f32[8,128]{1,0:T(8,128)} custom-call(s32[1]{0:T(128)} %bitcast.26.rep_ref, s32[32]{0:T(128)} %a.1, bf16[32,192,1536]{2,1,0:T(8,128)(2,1)} %src_ref.3, bf16[2,16,192,384]{3,2,1,0:T(8,128)(2,1)} %bitcast.28.got_ref.c), custom_call_target="tpu_custom_call" | custom-call | tf_op jit(solution)/shard_map/coef_dots/pallas_call | solution.py:704
  391.0 5.7 %finish.1 = f32[32,192,384]{2,1,0:T(8,128)} custom-call(s32[32]{0:T(128)} %a.1, f32[32]{0:T(128)} %b.1, bf16[2,16,192,384]{3,2,1,0:T(8,128)(2,1)} %bitcast.28.got_ref.c, f32[8,128]{1,0:T(8,128)} %coef_dots.1._), custom_call_target="tpu_custom_call" | custom-call | flops 9437184 | bytes 18874368 | tf_op jit(solution)/shard_map/finish/pallas_call | solution.py:724
  396.7 6.4 %all-to-all-done.2 = f32[32,1,3200]{2,1,0:T(1,128)S(1)} async-done(((f32[32,1,3200]{2,1,0:T(1,128)}), f32[32,1,3200]{2,1,0:T(1,128)S(1)}, u32[]{:S(2)}, u32[]{:S(2)}) %all-to-all-start.2) | async-done | bytes 409632 | tf_op jit(solution)/shard_map/all_to_all | solution.py:838
  (117 shorter events, 93.5 us)
Async XLA Ops:
  18.3 14.9 %collective-permute-start = (bf16[80,3200]{1,0:T(8,128)(2,1)}, bf16[80,3200]{1,0:T(8,128)(2,1)S(1)}, u32[]{:S(2)}, u32[]{:S(2)}) collective-permute-start(bf16[80,3200]{1,0:T(8,128)(2,1)} %get-tuple-element.40), channel_id=1, source_target_pairs={{0,2},{2,0},{4,6},{6,4},{8,10},{10,8},{12,14},{14,12},{1,3},{3,1},... | collective-permute-start | bytes 1536008 | tf_op jit(solution)/shard_map/ppermute | solution.py:803
  21.4 25.7 %collective-permute-start.1 = (bf16[80,3200]{1,0:T(8,128)(2,1)}, bf16[80,3200]{1,0:T(8,128)(2,1)S(1)}, u32[]{:S(2)}, u32[]{:S(2)}) collective-permute-start(bf16[80,3200]{1,0:T(8,128)(2,1)} %get-tuple-element.41), channel_id=1, source_target_pairs={{0,4},{2,6},{4,0},{6,2},{8,12},{10,14},{12,8},{14,10},{1,5},{3,7},... | collective-permute-start | bytes 1536008 | tf_op jit(solution)/shard_map/ppermute | solution.py:803
  22.8 36.5 %collective-permute-start.2 = (bf16[80,3200]{1,0:T(8,128)(2,1)}, bf16[80,3200]{1,0:T(8,128)(2,1)S(1)}, u32[]{:S(2)}, u32[]{:S(2)}) collective-permute-start(bf16[80,3200]{1,0:T(8,128)(2,1)} %get-tuple-element.42), channel_id=1, source_target_pairs={{0,6},{2,4},{4,2},{6,0},{8,14},{10,12},{12,10},{14,8},{1,7},{3,5},... | collective-permute-start | bytes 1536008 | tf_op jit(solution)/shard_map/ppermute | solution.py:803
  22.9 37.3 %collective-permute-start.3 = (bf16[80,3200]{1,0:T(8,128)(2,1)}, bf16[80,3200]{1,0:T(8,128)(2,1)S(1)}, u32[]{:S(2)}, u32[]{:S(2)}) collective-permute-start(bf16[80,3200]{1,0:T(8,128)(2,1)} %get-tuple-element.43), channel_id=1, source_target_pairs={{0,8},{2,10},{4,12},{6,14},{8,0},{10,2},{12,4},{14,6},{1,9},{3,11}... | collective-permute-start | bytes 1536008 | tf_op jit(solution)/shard_map/ppermute | solution.py:803
  24.9 36.1 %collective-permute-start.4 = (bf16[80,3200]{1,0:T(8,128)(2,1)}, bf16[80,3200]{1,0:T(8,128)(2,1)S(1)}, u32[]{:S(2)}, u32[]{:S(2)}) collective-permute-start(bf16[80,3200]{1,0:T(8,128)(2,1)} %get-tuple-element.44), channel_id=1, source_target_pairs={{0,10},{2,8},{4,14},{6,12},{8,2},{10,0},{12,6},{14,4},{1,11},{3,9}... | collective-permute-start | bytes 1536008 | tf_op jit(solution)/shard_map/ppermute | solution.py:803
  26.3 153.0 %all-to-all-start = ((bf16[8,2,192,768]{3,2,1,0:T(8,128)(2,1)}), bf16[8,2,192,768]{3,2,1,0:T(8,128)(2,1)}, u32[]{:S(2)}, u32[]{:S(2)}) async-start(bf16[8,2,192,768]{3,2,1,0:T(8,128)(2,1)} %bitcast.49), calls=%async_computation | async-start | bytes 9437184 | tf_op jit(solution)/shard_map/all_to_all | solution.py:787
  33.2 108.5 %collective-permute-start.5 = (bf16[80,3200]{1,0:T(8,128)(2,1)}, bf16[80,3200]{1,0:T(8,128)(2,1)S(1)}, u32[]{:S(2)}, u32[]{:S(2)}) collective-permute-start(bf16[80,3200]{1,0:T(8,128)(2,1)} %get-tuple-element.45), channel_id=1, source_target_pairs={{0,12},{2,14},{4,8},{6,10},{8,4},{10,6},{12,0},{14,2},{1,13},{3,15... | collective-permute-start | bytes 1536008 | tf_op jit(solution)/shard_map/ppermute | solution.py:803
  47.1 103.6 %collective-permute-start.6 = (bf16[80,3200]{1,0:T(8,128)(2,1)}, bf16[80,3200]{1,0:T(8,128)(2,1)S(1)}, u32[]{:S(2)}, u32[]{:S(2)}) collective-permute-start(bf16[80,3200]{1,0:T(8,128)(2,1)} %get-tuple-element.46), channel_id=1, source_target_pairs={{0,14},{2,12},{4,10},{6,8},{8,6},{10,4},{12,2},{14,0},{1,15},{3,13... | collective-permute-start | bytes 1536008 | tf_op jit(solution)/shard_map/ppermute | solution.py:803
  179.6 197.5 %all-to-all-start.1 = ((bf16[16,2,192,384]{3,2,1,0:T(8,128)(2,1)}), bf16[16,2,192,384]{3,2,1,0:T(8,128)(2,1)}, u32[]{:S(2)}, u32[]{:S(2)}) async-start(bf16[16,2,192,384]{3,2,1,0:T(8,128)(2,1)} %bitcast.48), calls=%async_computation.1 | async-start | bytes 9437184 | tf_op jit(solution)/shard_map/all_to_all | solution.py:811
  200.5 20.9 %collective-permute-start.10 = (bf16[80,1536]{1,0:T(8,128)(2,1)}, bf16[80,1536]{1,0:T(8,128)(2,1)S(1)}, u32[]{:S(2)}, u32[]{:S(2)}) collective-permute-start(bf16[80,1536]{1,0:T(8,128)(2,1)} %get-tuple-element.49), channel_id=1, source_target_pairs={{0,4},{2,6},{4,0},{6,2},{8,12},{10,14},{12,8},{14,10},{1,5},{3,7},... | collective-permute-start | bytes 737288 | tf_op jit(solution)/shard_map/ppermute | solution.py:803
  201.1 45.3 %collective-permute-start.11 = (bf16[80,1536]{1,0:T(8,128)(2,1)}, bf16[80,1536]{1,0:T(8,128)(2,1)S(1)}, u32[]{:S(2)}, u32[]{:S(2)}) collective-permute-start(bf16[80,1536]{1,0:T(8,128)(2,1)} %get-tuple-element.50), channel_id=1, source_target_pairs={{0,6},{2,4},{4,2},{6,0},{8,14},{10,12},{12,10},{14,8},{1,7},{3,5},... | collective-permute-start | bytes 737288 | tf_op jit(solution)/shard_map/ppermute | solution.py:803
  203.6 70.1 %collective-permute-start.12 = (bf16[80,1536]{1,0:T(8,128)(2,1)}, bf16[80,1536]{1,0:T(8,128)(2,1)S(1)}, u32[]{:S(2)}, u32[]{:S(2)}) collective-permute-start(bf16[80,1536]{1,0:T(8,128)(2,1)} %get-tuple-element.51), channel_id=1, source_target_pairs={{0,8},{2,10},{4,12},{6,14},{8,0},{10,2},{12,4},{14,6},{1,9},{3,11}... | collective-permute-start | bytes 737288 | tf_op jit(solution)/shard_map/ppermute | solution.py:803
  205.4 80.1 %collective-permute-start.13 = (bf16[80,1536]{1,0:T(8,128)(2,1)}, bf16[80,1536]{1,0:T(8,128)(2,1)S(1)}, u32[]{:S(2)}, u32[]{:S(2)}) collective-permute-start(bf16[80,1536]{1,0:T(8,128)(2,1)} %get-tuple-element.52), channel_id=1, source_target_pairs={{0,10},{2,8},{4,14},{6,12},{8,2},{10,0},{12,6},{14,4},{1,11},{3,9}... | collective-permute-start | bytes 737288 | tf_op jit(solution)/shard_map/ppermute | solution.py:803
  206.4 87.8 %collective-permute-start.14 = (bf16[80,1536]{1,0:T(8,128)(2,1)}, bf16[80,1536]{1,0:T(8,128)(2,1)S(1)}, u32[]{:S(2)}, u32[]{:S(2)}) collective-permute-start(bf16[80,1536]{1,0:T(8,128)(2,1)} %get-tuple-element.53), channel_id=1, source_target_pairs={{0,12},{2,14},{4,8},{6,10},{8,4},{10,6},{12,0},{14,2},{1,13},{3,15... | collective-permute-start | bytes 737288 | tf_op jit(solution)/shard_map/ppermute | solution.py:803
  221.4 78.1 %collective-permute-start.15 = (bf16[80,1536]{1,0:T(8,128)(2,1)}, bf16[80,1536]{1,0:T(8,128)(2,1)S(1)}, u32[]{:S(2)}, u32[]{:S(2)}) collective-permute-start(bf16[80,1536]{1,0:T(8,128)(2,1)} %get-tuple-element.54), channel_id=1, source_target_pairs={{0,14},{2,12},{4,10},{6,8},{8,6},{10,4},{12,2},{14,0},{1,15},{3,13... | collective-permute-start | bytes 737288 | tf_op jit(solution)/shard_map/ppermute | solution.py:803
  246.4 53.1 %collective-permute-start.9 = (bf16[80,1536]{1,0:T(8,128)(2,1)}, bf16[80,1536]{1,0:T(8,128)(2,1)S(1)}, u32[]{:S(2)}, u32[]{:S(2)}) collective-permute-start(bf16[80,1536]{1,0:T(8,128)(2,1)} %get-tuple-element.48), channel_id=1, source_target_pairs={{0,2},{2,0},{4,6},{6,4},{8,10},{10,8},{12,14},{14,12},{1,3},{3,1},... | collective-permute-start | bytes 737288 | tf_op jit(solution)/shard_map/ppermute | solution.py:803
  327.4 17.3 %collective-permute-start.26 = (f32[2,3072]{1,0:T(2,128)S(1)}, f32[2,3072]{1,0:T(2,128)S(1)}, u32[]{:S(2)}, u32[]{:S(2)}) collective-permute-start(f32[2,3072]{1,0:T(2,128)S(1)} %dynamic-slice_bitcast_fusion.3), channel_id=1, source_target_pairs={{0,2},{2,0},{1,3},{3,1},{4,6},{6,4},{5,7},{7,5},{8,10},{10,8},{9,1... | collective-permute-start | bytes 73736 | tf_op jit(solution)/shard_map/ppermute | solution.py:753
  340.9 18.7 %collective-permute-start.16 = (bf16[80,1536]{1,0:T(8,128)(2,1)}, bf16[80,1536]{1,0:T(8,128)(2,1)S(1)}, u32[]{:S(2)}, u32[]{:S(2)}) collective-permute-start(bf16[80,1536]{1,0:T(8,128)(2,1)} %get-tuple-element.58), channel_id=1, source_target_pairs={{0,2},{2,0},{4,6},{6,4},{8,10},{10,8},{12,14},{14,12},{1,3},{3,1},... | collective-permute-start | bytes 737288 | tf_op jit(solution)/shard_map/ppermute | solution.py:803
  342.3 17.2 %collective-permute-start.17 = (bf16[80,1536]{1,0:T(8,128)(2,1)}, bf16[80,1536]{1,0:T(8,128)(2,1)S(1)}, u32[]{:S(2)}, u32[]{:S(2)}) collective-permute-start(bf16[80,1536]{1,0:T(8,128)(2,1)} %get-tuple-element.59), channel_id=1, source_target_pairs={{0,4},{2,6},{4,0},{6,2},{8,12},{10,14},{12,8},{14,10},{1,5},{3,7},... | collective-permute-start | bytes 737288 | tf_op jit(solution)/shard_map/ppermute | solution.py:803
  342.3 22.0 %collective-permute-start.18 = (bf16[80,1536]{1,0:T(8,128)(2,1)}, bf16[80,1536]{1,0:T(8,128)(2,1)S(1)}, u32[]{:S(2)}, u32[]{:S(2)}) collective-permute-start(bf16[80,1536]{1,0:T(8,128)(2,1)} %get-tuple-element.60), channel_id=1, source_target_pairs={{0,6},{2,4},{4,2},{6,0},{8,14},{10,12},{12,10},{14,8},{1,7},{3,5},... | collective-permute-start | bytes 737288 | tf_op jit(solution)/shard_map/ppermute | solution.py:803
  344.4 20.0 %collective-permute-start.19 = (bf16[80,1536]{1,0:T(8,128)(2,1)}, bf16[80,1536]{1,0:T(8,128)(2,1)S(1)}, u32[]{:S(2)}, u32[]{:S(2)}) collective-permute-start(bf16[80,1536]{1,0:T(8,128)(2,1)} %get-tuple-element.61), channel_id=1, source_target_pairs={{0,8},{2,10},{4,12},{6,14},{8,0},{10,2},{12,4},{14,6},{1,9},{3,11}... | collective-permute-start | bytes 737288 | tf_op jit(solution)/shard_map/ppermute | solution.py:803
  344.7 19.7 %collective-permute-start.20 = (bf16[80,1536]{1,0:T(8,128)(2,1)}, bf16[80,1536]{1,0:T(8,128)(2,1)S(1)}, u32[]{:S(2)}, u32[]{:S(2)}) collective-permute-start(bf16[80,1536]{1,0:T(8,128)(2,1)} %get-tuple-element.62), channel_id=1, source_target_pairs={{0,10},{2,8},{4,14},{6,12},{8,2},{10,0},{12,6},{14,4},{1,11},{3,9}... | collective-permute-start | bytes 737288 | tf_op jit(solution)/shard_map/ppermute | solution.py:803
  364.3 12.1 %collective-permute-start.27 = (f32[1,3072]{1,0:T(1,128)S(1)}, f32[1,3072]{1,0:T(1,128)S(1)}, u32[]{:S(2)}, u32[]{:S(2)}) collective-permute-start(f32[1,3072]{1,0:T(1,128)S(1)} %constant_dynamic-slice_fusion), channel_id=1, source_target_pairs={{0,1},{1,0},{2,3},{3,2},{4,5},{5,4},{6,7},{7,6},{8,9},{9,8},{10,11... | collective-permute-start | bytes 36872 | tf_op jit(solution)/shard_map/ppermute | solution.py:753
  387.0 16.1 %all-to-all-start.2 = ((f32[32,1,3200]{2,1,0:T(1,128)}), f32[32,1,3200]{2,1,0:T(1,128)S(1)}, u32[]{:S(2)}, u32[]{:S(2)}) async-start(f32[32,1,3200]{2,1,0:T(1,128)} %broadcast_in_dim.17), calls=%async_computation.2 | async-start | bytes 819200 | tf_op jit(solution)/shard_map/all_to_all | solution.py:838
  (25 other events, 312.4 us)

commit v3 on v2

--- a/solution.py
+++ b/solution.py
@@ -209,6 +209,7 @@
 F32 = jnp.float32
 I32 = jnp.int32
 TILE = 256
+BRIEF = pl.CostEstimate(flops=1, bytes_accessed=1, transcendentals=0)
 
 
 def any_spec():
@@ -231,14 +232,14 @@
     return lax.dot_general(a, b, (dims, ((), ())), preferred_element_type=F32)
 
 
-def merge_kernel(map_ref, coef_ref, place_ref, src_ref, out_ref, order_ref, count_ref, held, sems):
-    halves, places = out_ref.shape[:2]
+def merge_kernel(map_ref, coef_ref, place_ref, src_ref, *refs):
+    outs, (order_ref, count_ref, held, sems) = refs[:-4], refs[-4:]
     half = held.shape[2]
     expert_order(map_ref, order_ref, count_ref)
     at = pl.ds(pl.multiple_of(place_ref[1] * half, half), half)
     copies, experts = [], []
-    for j in range(places):
-        for m in range(2):
+    for m in range(2):
+        for j in range(outs[0].shape[0]):
             combo = 4 * j + 2 * place_ref[0] + m
             for n in range(2):
                 expert = order_ref[2 * combo + n]
@@ -248,15 +249,13 @@
                     pltpu.make_async_copy(src_ref.at[expert, :, at], held.at[i], sems.at[i])
                 )
                 copies[-1].start()
-    for j in range(places):
-        for m in range(2):
-            i = 4 * j + 2 * m
+    for m, out_ref in enumerate(outs):
+        for j in range(out_ref.shape[0]):
+            i = 2 * (m * out_ref.shape[0] + j)
             copies[i].wait()
             copies[i + 1].wait()
             one, two = coef_ref[experts[i]], coef_ref[experts[i + 1]]
-            merged = (one * held[i].astype(F32) + two * held[i + 1].astype(F32)).astype(BF)
-            for h in range(halves):
-                out_ref[h, j, m] = merged
+            out_ref[j] = (one * held[i].astype(F32) + two * held[i + 1].astype(F32)).astype(BF)
 
 
 def expert_order(map_ref, order_ref, count_ref):
@@ -278,8 +277,8 @@
     return pl.pallas_call(
         merge_kernel,
         in_specs=[smem_spec(), smem_spec(), smem_spec(), any_spec()],
-        out_specs=vmem_spec(),
-        out_shape=jax.ShapeDtypeStruct((2, places, 2, rows, half), BF),
+        out_specs=[vmem_spec()] * 2,
+        out_shape=[jax.ShapeDtypeStruct((places, rows, half), BF)] * 2,
         scratch_shapes=[
             pltpu.SMEM((count,), I32),
             pltpu.SMEM((count // 2,), I32),
@@ -287,6 +286,7 @@
             pltpu.SemaphoreType.DMA((4 * places,)),
         ],
         compiler_params=params(56),
+        cost_estimate=BRIEF,
         name="merge_experts",
     )(merge_map, merge_coef, where_am_i, source_w)
 
@@ -303,6 +303,7 @@
         out_specs=[hbm_spec()] * count,
         out_shape=[jax.ShapeDtypeStruct(a.shape, a.dtype) for a in arrays],
         input_output_aliases={i: i for i in range(count)},
+        cost_estimate=BRIEF,
         name="hold",
     )(*arrays, *after)
 
@@ -324,18 +325,11 @@
     return lax.broadcasted_iota(I32, (sources, tok), 0) == idx_ref[k : k + 1, :]
 
 
-def place_rows(refs, at, rows):
-    each = refs[0].shape[0]
-    rows = rows.astype(BF)
-    for d, ref in enumerate(refs):
-        ref[:, at : at + rows.shape[1]] = rows[d * each : (d + 1) * each]
-
-
 def route_kernel(
     capacity, lanes,
-    me_ref, xt_ref, rwt_ref, rb_ref, idx_ref, map_ref, hid_ref, og_ref, _, *refs
+    xt_ref, rwt_ref, rb_ref, idx_ref, map_ref, hid_ref, og_ref, _,
+    send_ref, gate_ref, pos_ref, slot_ref,
 ):
-    sends, (gate_ref, pos_ref, slot_ref) = refs[:-3], refs[-3:]
     top, tok = idx_ref.shape
     sources = rwt_ref.shape[0]
     slots, width = hid_ref.shape
@@ -354,7 +348,6 @@
     gates = [r / total for r in raised]
     lane = [jnp.right_shift(g, 1) for g in merged]
     member = [jnp.bitwise_and(g, 1) for g in merged]
-    partner = [jnp.bitwise_xor(l, me_ref[0]) for l in lane]
     onehot = [(lax.broadcasted_iota(I32, (lanes, tok), 0) == l).astype(F32) for l in lane]
     all_hot = onehot[0]
     for k in range(1, top):
@@ -367,7 +360,7 @@
     for k in range(top):
         rank = jnp.sum(before * onehot[k], axis=0, keepdims=True).astype(I32)
         before = before + onehot[k]
-        position.append(jnp.where(rank < capacity, partner[k] * capacity + rank, -1))
+        position.append(jnp.where(rank < capacity, lane[k] * capacity + rank, -1))
     gate_ref[...] = jnp.zeros_like(gate_ref)
     pos_ref[...] = jnp.full_like(pos_ref, -1)
     for k in range(top):
@@ -396,11 +389,11 @@
     take = lax.broadcasted_iota(I32, (places, slots), 0) == slot_pos
     placed = jnp.sum(jnp.where(take, spot[3:4].astype(F32), 0.0), axis=1, keepdims=True)
     depth = og_ref.shape[1]
-    place_rows(sends, depth + width, jnp.broadcast_to(placed, (places, 128)))
+    send_ref[:, depth + width :] = jnp.broadcast_to(placed, (places, 128)).astype(BF)
     take = take.astype(BF)
     for n in range(0, width, TILE):
         rows = jnp.dot(take, hid_ref[:, n : n + TILE], preferred_element_type=F32)
-        place_rows(sends, depth + n, rows)
+        send_ref[:, depth + n : depth + n + TILE] = rows.astype(BF)
     takes = [
         (lax.broadcasted_iota(I32, (places, tok), 0) == position[k]).astype(BF) for k in range(top)
     ]
@@ -410,48 +403,46 @@
         rows = jnp.zeros((places, TILE), F32)
         for k in range(top):
             rows = rows + jnp.dot(takes[k], (columns[k] * og).astype(BF), preferred_element_type=F32)
-        place_rows(sends, n, rows)
-
-
-def route(me, xt, rwt, router_b, idx_t, merge_map, hid, og, after, capacity, lanes):
+        send_ref[:, n : n + TILE] = rows.astype(BF)
+
+
+def route(xt, rwt, router_b, idx_t, merge_map, hid, og, after, capacity, lanes):
     slots, width = hid.shape
     tok = idx_t.shape[1]
     return pl.pallas_call(
         functools.partial(route_kernel, capacity, lanes),
-        in_specs=[smem_spec()] + [vmem_spec()] * 7 + [any_spec()],
-        out_specs=[vmem_spec()] * (lanes + 3),
-        out_shape=[jax.ShapeDtypeStruct((capacity, og.shape[1] + width + 128), BF)] * lanes
-        + [
+        in_specs=[vmem_spec()] * 7 + [any_spec()],
+        out_specs=[vmem_spec()] * 4,
+        out_shape=[
+            jax.ShapeDtypeStruct((lanes * capacity, og.shape[1] + width + 128), BF),
             jax.ShapeDtypeStruct((8, tok), F32),
             jax.ShapeDtypeStruct((8, tok), I32),
             jax.ShapeDtypeStruct((8, slots), I32),
         ],
         compiler_params=params(56),
+        cost_estimate=BRIEF,
         name="route",
-    )(me, xt, rwt, router_b[None, :], idx_t, merge_map[None, :], hid, og, after)
+    )(xt, rwt, router_b[None, :], idx_t, merge_map[None, :], hid, og, after)
 
 
 def load_weights(core_ref, mine, other, w_ref, sems):
     core = core_ref[0]
-    blocks, _, rows, _ = mine.shape
     copies = []
-    for c in range(blocks):
-        at = pl.ds(c * rows, rows)
-        for n, part in enumerate((mine, other)):
-            to = core if n == 0 else 1 - core
-            i = 2 * c + n
-            copies.append(
-                pltpu.make_async_copy(part.at[c], w_ref.at[to, :, at, :], sems.at[i])
-            )
+    for m in range(len(mine)):
+        blocks, rows, half = mine[m].shape
+        for n, part in enumerate((mine[m], other[m])):
+            for c in range(blocks):
+                to = w_ref.at[core if n == 0 else 1 - core, m, pl.ds(c * rows, rows), :]
+                copies.append(pltpu.make_async_copy(part.at[c], to, sems.at[len(copies)]))
     for copy in copies:
         copy.start()
     for copy in copies:
         copy.wait()
 
 
-def forward_kernel(core_ref, rows_ref, flag_ref, mine, other, *refs):
-    outs, (w_ref, sems) = refs[:-2], refs[-2:]
-    load_weights(core_ref, mine, other, w_ref, sems)
+def forward_kernel(core_ref, rows_ref, flag_ref, *refs):
+    out_ref, w_ref, sems = refs[-3:]
+    load_weights(core_ref, refs[:2], refs[2:4], w_ref, sems)
     half = w_ref.shape[3]
     member = flag_ref[:, :1].astype(F32)
 
@@ -462,23 +453,25 @@
             + dot(rows_ref[:, half : 2 * half], w_ref[1, m, at, :], ((1,), (1,)))
             for m in range(2)
         ]
-        place_rows(outs, n, jnp.where(member == 0.0, both[0], both[1]))
-
-
-def backward_kernel(core_ref, rows_ref, flag_ref, mine, other, *refs):
-    outs, (w_ref, sems) = refs[:-2], refs[-2:]
-    load_weights(core_ref, mine, other, w_ref, sems)
+        out_ref[:, at] = jnp.where(member == 0.0, both[0], both[1]).astype(BF)
+
+
+def backward_kernel(core_ref, rows_ref, flag_ref, *refs):
+    out_ref, w_ref, sems = refs[-3:]
+    load_weights(core_ref, refs[:2], refs[2:4], w_ref, sems)
     half = w_ref.shape[3]
     member = flag_ref[:, :1].astype(F32)
     for h in range(2):
         for n in range(0, half, TILE):
             at = slice(n, n + TILE)
             both = [dot(rows_ref[...], w_ref[h, m, :, at], ((1,), (0,))) for m in range(2)]
-            place_rows(outs, h * half + n, jnp.where(member == 0.0, both[0], both[1]))
-
-
-def run_lane(kernel, core, rows, which, mine, other, lanes, name):
-    blocks, members, share, half = mine.shape
+            both = jnp.where(member == 0.0, both[0], both[1])
+            out_ref[:, h * half + n : h * half + n + TILE] = both.astype(BF)
+
+
+def run_lane(kernel, core, rows, which, mine, other, name):
+    blocks, share, half = mine[0].shape
+    members = len(mine)
     depth = share * blocks
     count = rows.shape[0]
     wide = (rows.shape[1] - 128) // 2
@@ -489,79 +482,64 @@
             smem_spec(),
             pl.BlockSpec((count, wide), lambda i: (0, which)),
             pl.BlockSpec((count, 128), lambda i: (0, 2 * wide // 128)),
-            hbm_spec(),
-            hbm_spec(),
-        ],
-        out_specs=[pl.BlockSpec((count // lanes, wide), lambda i: (0, 0))] * lanes,
-        out_shape=[jax.ShapeDtypeStruct((count // lanes, wide), BF)] * lanes,
+        ]
+        + [any_spec()] * (2 * members),
+        out_specs=pl.BlockSpec((count, wide), lambda i: (0, 0)),
+        out_shape=jax.ShapeDtypeStruct((count, wide), BF),
         scratch_shapes=[
             pltpu.VMEM((2, members, depth, half), BF),
-            pltpu.SemaphoreType.DMA((2 * blocks,)),
+            pltpu.SemaphoreType.DMA((2 * members * blocks,)),
         ],
         compiler_params=params(56),
-        cost_estimate=pl.CostEstimate(
-            flops=4 * count * depth * 2 * half,
-            bytes_accessed=4 * members * depth * half + 8 * count * half,
-            transcendentals=0,
-        ),
+        cost_estimate=BRIEF,
         name=name,
-    )(core, rows, rows, mine, other)
-
-
-def lane_grad_kernel(has_other, _, grd_ref, hid_ref, flag_ref, *refs):
+    )(core, rows, rows, *mine, *other)
+
+
+def lane_grad_kernel(member, has_other, _, grd_ref, hid_ref, flag_ref, *refs):
     out_ref = refs[-1]
-    chosen = flag_ref[:, :1].astype(F32) == pl.program_id(1).astype(F32)
+    chosen = flag_ref[:, :1].astype(F32) == float(member)
     hid = jnp.where(chosen, hid_ref[...], jnp.zeros_like(hid_ref))
-    blocks, _, _, rows, cols = out_ref.shape
+    blocks, _, rows, cols = out_ref.shape
     each = 2 if blocks % 2 == 0 and 2 * rows % 128 == 0 else blocks
     for n in range(0, blocks, each):
         part = dot(grd_ref[:, n * rows : (n + each) * rows], hid, ((0,), (0,)))
         part = part.reshape(each, rows, cols)
         if has_other:
-            part = part + refs[0][n : n + each, 0, 0].astype(F32)
-        out_ref[n : n + each, 0, 0] = part.astype(BF)
-
-
-def lane_grads(core, rows, other, blocks, reps):
+            part = part + refs[0][n : n + each, 0].astype(F32)
+        out_ref[n : n + each, 0] = part.astype(BF)
+
+
+def lane_grads(core, rows, member, other, blocks, reps):
     count = rows.shape[0]
     width = (rows.shape[1] - 128) // 2
     cols = width // reps
-    shape = (blocks, 2, 2, width // blocks, cols)
-    block = pl.BlockSpec((blocks, 1, 1, width // blocks, cols), lambda y, m, s: (0, y, m, 0, 0))
+    shape = (blocks, 2, width // blocks, cols)
+    block = pl.BlockSpec((blocks, 1, width // blocks, cols), lambda y, s: (0, y, 0, 0))
     extra = [] if other is None else [other]
     return pl.pallas_call(
-        functools.partial(lane_grad_kernel, other is not None),
+        functools.partial(lane_grad_kernel, member, other is not None),
         grid_spec=pltpu.PrefetchScalarGridSpec(
             num_scalar_prefetch=1,
-            grid=(2, 2),
+            grid=(2,),
             in_specs=[
-                pl.BlockSpec((count, width), lambda y, m, s: (0, 0)),
-                pl.BlockSpec((count, cols), lambda y, m, s: (0, reps + 2 * y + s[0])),
-                pl.BlockSpec((count, 128), lambda y, m, s: (0, 2 * width // 128)),
+                pl.BlockSpec((count, width), lambda y, s: (0, 0)),
+                pl.BlockSpec((count, cols), lambda y, s: (0, reps + 2 * y + s[0])),
+                pl.BlockSpec((count, 128), lambda y, s: (0, 2 * width // 128)),
             ]
             + [block] * len(extra),
             out_specs=block,
         ),
         out_shape=jax.ShapeDtypeStruct(shape, BF),
         compiler_params=params(56),
-        cost_estimate=pl.CostEstimate(
-            flops=8 * count * width * cols,
-            bytes_accessed=8 * width * cols + 4 * count * width,
-            transcendentals=0,
-        ),
+        cost_estimate=BRIEF,
         name="lane_grads_add" if extra else "lane_grads_first",
     )(core, rows, rows, rows, *extra)
 
 
-def gather_rows(refs, keep):
-    each = refs[0].shape[0]
-    for d, ref in enumerate(refs):
-        keep[d * each : (d + 1) * each, :] = ref[...]
-
-
-def combine_kernel(og_ref, gate_ref, pos_ref, idx_ref, rwt_ref, xt_ref, *refs):
-    homes, (mixed_ref, tg_ref, part_ref, out_ref) = refs[:-4], refs[-4:]
-    gather_rows(homes, out_ref)
+def combine_kernel(
+    og_ref, gate_ref, pos_ref, idx_ref, rwt_ref, xt_ref, out_ref, mixed_ref, tg_ref, part_ref
+):
     places, width = out_ref.shape
     top, tok = idx_ref.shape
     sources, features = rwt_ref.shape
@@ -598,27 +576,25 @@
     part_ref[:, last:] = jnp.broadcast_to(bias, (sources, 128))
 
 
-def combine(homes, og, gates, pos, idx_t, rwt, xt):
+def combine(home_out, og, gates, pos, idx_t, rwt, xt):
     sources, features = rwt.shape
     tok = idx_t.shape[1]
     return pl.pallas_call(
         combine_kernel,
-        in_specs=[vmem_spec()] * (6 + len(homes)),
+        in_specs=[vmem_spec()] * 7,
         out_specs=[vmem_spec()] * 3,
         out_shape=[
             jax.ShapeDtypeStruct(og.shape, BF),
             jax.ShapeDtypeStruct((features, tok), BF),
             jax.ShapeDtypeStruct((sources, (features + 127) // 128 * 128 + 128), F32),
         ],
-        scratch_shapes=[pltpu.VMEM((len(homes) * homes[0].shape[0], homes[0].shape[1]), BF)],
         compiler_params=params(56),
+        cost_estimate=BRIEF,
         name="combine",
-    )(og, gates, pos, idx_t, rwt, xt, *homes)
-
-
-def unplace_kernel(slot_ref, *refs):
-    homes, (out_ref, back_ref) = refs[:-2], refs[-2:]
-    gather_rows(homes, back_ref)
+    )(og, gates, pos, idx_t, rwt, xt, home_out)
+
+
+def unplace_kernel(slot_ref, back_ref, out_ref):
     places, width = back_ref.shape
     slots = slot_ref.shape[1]
     take = (lax.broadcasted_iota(I32, (places, slots), 0) == slot_ref[0:1, :]).astype(BF)
@@ -626,26 +602,25 @@
         out_ref[:, n : n + TILE] = dot(take, back_ref[:, n : n + TILE], ((0,), (0,))).astype(BF)
 
 
-def unplace(homes, slot_pos):
-    rows, width = homes[0].shape
+def unplace(home_back, slot_pos):
     return pl.pallas_call(
         unplace_kernel,
-        in_specs=[vmem_spec()] * (1 + len(homes)),
+        in_specs=[vmem_spec()] * 2,
         out_specs=vmem_spec(),
-        out_shape=jax.ShapeDtypeStruct((slot_pos.shape[1], width), BF),
-        scratch_shapes=[pltpu.VMEM((len(homes) * rows, width), BF)],
+        out_shape=jax.ShapeDtypeStruct((slot_pos.shape[1], home_back.shape[1]), BF),
         compiler_params=params(56),
+        cost_estimate=BRIEF,
         name="unplace",
-    )(slot_pos, *homes)
-
-
-def coef_kernel(rep_ref, map_ref, src_ref, got_ref, out_ref, order_ref, count_ref, held, weights, sems):
+    )(slot_pos, home_back)
+
+
+def coef_kernel(rep_ref, map_ref, src_ref, *refs):
+    parts, (out_ref, order_ref, count_ref, held, weights, sems) = refs[:-6], refs[-6:]
     count, rows, cols = weights.shape
     at = pl.ds(pl.multiple_of(rep_ref[0] * cols, cols), cols)
-    copies = [
-        pltpu.make_async_copy(src_ref.at[:, :, at], weights, sems.at[0]),
-        pltpu.make_async_copy(got_ref, held, sems.at[1]),
-    ]
+    copies = [pltpu.make_async_copy(src_ref.at[:, :, at], weights, sems.at[len(parts)])]
+    for m, part in enumerate(parts):
+        copies.append(pltpu.make_async_copy(part, held.at[m], sems.at[m]))
     for copy in copies:
         copy.start()
     expert_order(map_ref, order_ref, count_ref)
@@ -654,7 +629,7 @@
     lane = lax.broadcasted_iota(I32, (8, 128), 1)
 
     def one(g, total):
-        merged = held[0, g].astype(F32) + held[1, g].astype(F32)
+        merged = held[jnp.bitwise_and(g, 1), jnp.right_shift(g, 1)].astype(F32)
         for n in range(2):
             expert = order_ref[2 * g + n]
             product = merged * weights[expert].astype(F32)
@@ -669,29 +644,29 @@
     out_ref[...] = lax.fori_loop(0, count // 2, one, jnp.zeros((8, 128), F32))
 
 
-def finish_kernel(scale, map_ref, coef_ref, got_ref, out_ref, order_ref, count_ref, held, ready, sems, more):
+def finish_kernel(scale, map_ref, coef_ref, _, *refs):
+    parts, (out_ref, order_ref, count_ref, held, ready, sems, more) = refs[:-7], refs[-7:]
     count = ready.shape[0]
-
-    def load(g):
-        return pltpu.make_async_copy(got_ref.at[:, g], held.at[:, g], sems.at[g])
+    copies = [
+        pltpu.make_async_copy(part, held.at[m], sems.at[m]) for m, part in enumerate(parts)
+    ]
+    for copy in copies:
+        copy.start()
+    expert_order(map_ref, order_ref, count_ref)
 
     def send(i):
         return pltpu.make_async_copy(ready.at[i], out_ref.at[order_ref[i]], more.at[i])
 
-    @pl.loop(0, count // 2)
-    def _(g):
-        load(g).start()
-
-    expert_order(map_ref, order_ref, count_ref)
-
-    @pl.loop(0, count // 2)
-    def _(g):
-        load(g).wait()
-        merged = held[0, g].astype(F32) + held[1, g].astype(F32)
-        for n in range(2):
-            i = 2 * g + n
-            ready[i] = merged * (coef_ref[order_ref[i]] * scale)
-            send(i).start()
+    for m, copy in enumerate(copies):
+        copy.wait()
+
+        @pl.loop(0, count // 4)
+        def _(lane, m=m):
+            merged = held[m, lane].astype(F32)
+            for n in range(2):
+                i = 4 * lane + 2 * m + n
+                ready[i] = merged * (coef_ref[order_ref[i]] * scale)
+                send(i).start()
 
     @pl.loop(0, count)
     def _(i):
@@ -700,48 +675,45 @@
 
 def coef_dots(rep_index, merge_map, source_w, arrived):
     count = source_w.shape[0]
-    _, _, rows, cols = arrived.shape
+    _, rows, cols = arrived[0].shape
     return pl.pallas_call(
         coef_kernel,
-        in_specs=[smem_spec(), smem_spec(), hbm_spec(), hbm_spec()],
+        in_specs=[smem_spec(), smem_spec(), hbm_spec()] + [any_spec()] * len(arrived),
         out_specs=vmem_spec(),
         out_shape=jax.ShapeDtypeStruct((8, 128), F32),
         scratch_shapes=[
             pltpu.SMEM((count,), I32),
             pltpu.SMEM((count // 2,), I32),
-            pltpu.VMEM(arrived.shape, BF),
+            pltpu.VMEM((len(arrived),) + arrived[0].shape, BF),
             pltpu.VMEM((count, rows, cols), BF),
-            pltpu.SemaphoreType.DMA((2,)),
+            pltpu.SemaphoreType.DMA((len(arrived) + 1,)),
         ],
         compiler_params=params(56),
+        cost_estimate=BRIEF,
         name="coef_dots",
-    )(rep_index, merge_map, source_w, arrived)
+    )(rep_index, merge_map, source_w, *arrived)
 
 
 def finish(merge_map, merge_coef, arrived, after, scale):
     count = merge_map.shape[0]
-    _, _, rows, cols = arrived.shape
+    _, rows, cols = arrived[0].shape
     return pl.pallas_call(
-        lambda a, b, c, _, *refs: finish_kernel(scale, a, b, c, *refs),
-        in_specs=[smem_spec(), smem_spec(), hbm_spec(), any_spec()],
+        functools.partial(finish_kernel, scale),
+        in_specs=[smem_spec(), smem_spec(), any_spec()] + [any_spec()] * len(arrived),
         out_specs=hbm_spec(),
         out_shape=jax.ShapeDtypeStruct((count, rows, cols), F32),
         scratch_shapes=[
             pltpu.SMEM((count,), I32),
             pltpu.SMEM((count // 2,), I32),
-            pltpu.VMEM(arrived.shape, BF),
+            pltpu.VMEM((len(arrived),) + arrived[0].shape, BF),
             pltpu.VMEM((count, rows, cols), F32),
-            pltpu.SemaphoreType.DMA((count // 2,)),
+            pltpu.SemaphoreType.DMA((len(arrived),)),
             pltpu.SemaphoreType.DMA((count,)),
         ],
         compiler_params=params(56),
-        cost_estimate=pl.CostEstimate(
-            flops=4 * count * rows * cols,
-            bytes_accessed=8 * count * rows * cols,
-            transcendentals=0,
-        ),
+        cost_estimate=BRIEF,
         name="finish",
-    )(merge_map, merge_coef, arrived, after)
+    )(merge_map, merge_coef, after, *arrived)
 
 
 def add_up(x, bits):
@@ -784,42 +756,45 @@
         return jnp.stack([jnp.asarray(n, I32) for n in numbers])
 
     combos = merge_experts(stack([row_i, core_i]), merge_map, merge_coef, source_w, places)
-    mine = lax.all_to_all(
-        combos.reshape((blocks,) + combos.shape[2:]), ("half", "place"),
-        split_axis=0, concat_axis=0, tiled=True,
-    )
+
+    def trade(x, axes):
+        return lax.all_to_all(x, axes, split_axis=0, concat_axis=0, tiled=True)
+
+    shares = [trade(c, "place") for c in combos]
+    mine = [lax.all_gather(x, "half", axis=0, tiled=True) for x in shares]
 
     xt = tokens.reshape(tok, features).T
     rwt = router_w.T
     idx_t = teacher_idx.reshape(tok, top).T
     og = out_grad.reshape(tok, depth)
-    *parts, gates, pos, slot_pos = route(
-        stack([2 * place_i + row_i]), xt, rwt, router_b, idx_t, merge_map,
-        hidden.reshape(tok * top, width), og, combos, capacity, lanes,
-    )
-
-    def trade(parts):
-        return [parts[0]] + [
-            lax.ppermute(parts[d], ("place", "row"), [(i, i ^ d) for i in range(lanes)])
-            for d in range(1, lanes)
-        ]
-
-    rows = jnp.concatenate(trade(parts), axis=0)
-    here = stack([core_i])
-    first = lane_grads(stack([1 - core_i]), rows, None, blocks, reps)
-    summed = lane_grads(here, rows, swap(first), blocks, reps)
-    arrived = lax.all_to_all(
-        summed.reshape(2 * blocks, 2, row_share, width // reps),
-        ("half", "place", "row"), split_axis=0, concat_axis=0, tiled=True,
-    )
-
-    (mine,) = hold([mine], summed)
-    other = swap(mine)
-    out_parts = run_lane(forward_kernel, here, rows, 1, mine, other, lanes, "lane_forward")
-    home_out = trade(out_parts)
-    back_parts = run_lane(backward_kernel, here, rows, 0, mine, other, lanes, "lane_backward")
+    send_rows, gates, pos, slot_pos = route(
+        xt, rwt, router_b, idx_t, merge_map, hidden.reshape(tok * top, width), og,
+        combos[0], capacity, lanes,
+    )
+
+    def trade_rows(rows):
+        parts = rows.reshape(lanes, capacity, rows.shape[1])
+        return trade(parts, ("place", "row")).reshape(rows.shape)
+
+    (send_rows,) = hold([send_rows], shares[1])
+    rows = trade_rows(send_rows)
+    here, there = stack([core_i]), stack([1 - core_i])
+    firsts = [swap(lane_grads(there, rows, m, None, blocks, reps)) for m in range(2)]
+    summed = [lane_grads(here, rows, m, firsts[m], blocks, reps) for m in range(2)]
+    arrived = [
+        lax.psum_scatter(
+            part.reshape((2, lanes) + part.shape[2:]), "half", scatter_dimension=0, tiled=False
+        )
+        for part in summed
+    ]
+
+    mine = hold(mine, *summed)
+    other = [swap(part) for part in mine]
+    out_rows = run_lane(forward_kernel, here, rows, 1, mine, other, "lane_forward")
+    home_out = trade_rows(out_rows)
+    back_rows = run_lane(backward_kernel, here, rows, 0, mine, other, "lane_backward")
     mixed, token_grad, part = combine(home_out, og, gates, pos, idx_t, rwt, xt)
-    hidden_grad = unplace(trade(back_parts), slot_pos)
+    hidden_grad = unplace(trade_rows(back_rows), slot_pos)
 
     part = add_up(
         part,
@@ -831,8 +806,7 @@
             ("core", 1, core_i),
         ],
     )
-    (arrived,) = hold([arrived], hidden_grad, part)
-    arrived = arrived.reshape(2, 2 * lanes, row_share, width // reps)
+    arrived = [trade(x, ("place", "row")) for x in hold(arrived, hidden_grad, part)]
     dots = coef_dots(stack([2 * row_i + core_i]), merge_map, source_w, arrived)
     news = jnp.concatenate([part, dots[:1]], axis=1)
     news = lax.all_to_all(

time: 407 us -> 434 us (1.066)
  blocking collectives: 0 us -> 21.8 us
  starting transfers between devices: 57.2 us -> 36.2 us
  waiting for transfers between devices: 245 us -> 259 us
  between operations: 1.01 us -> 14 us
    ppermute x21 -> x0, waiting for transfers between devices: 213 us -> none  [trade(): lax.ppermute(parts[d], ('place', 'row'), [(i, i ^ d) for i in range(lanes)])]
    all_to_all x2 -> x6, waiting for transfers between devices: 0.01 us -> 143 us  [trade(): return lax.all_to_all(x, axes, split_axis=0, concat_axis=0, tiled=True)]
    all_gather x0 -> x2, waiting for transfers between devices: none -> 49.2 us  [on_pairs(): mine = [lax.all_gather(x, 'half', axis=0, tiled=True) for x in shares]]
    ppermute x21 -> x0, starting transfers between devices: 37.2 us -> none  [trade(): lax.ppermute(parts[d], ('place', 'row'), [(i, i ^ d) for i in range(lanes)])]
    ppermute x5, waiting for transfers between devices: 16.5 us -> 52.4 us  [add_up(): lax.ppermute(give, axis, [(i, i ^ distance) for i in range(size)])]
    all_to_all x0 -> x1, blocking collectives: none -> 21.8 us  [trade(): return lax.all_to_all(x, axes, split_axis=0, concat_axis=0, tiled=True)]
    all_to_all x2 -> x6, starting transfers between devices: 12.8 us -> 26.5 us  [trade(): return lax.all_to_all(x, axes, split_axis=0, concat_axis=0, tiled=True)]
    pallas_call x5 -> x7, Pallas kernels: 32.6 us -> 38.2 us  [the longest x4 23.2 us: lane_grads(): pl.pallas_call(functools.partial(lane_grad_kernel, member, other is not N...]
  transfers between devices with their start and end apart: 31 -> 20, of which waited for: 20 -> 13; matrix products, arithmetic and copies ran while one was open for 3% -> 1% of each run, Pallas kernels for 14% -> 17%
where the time goes in v3:
time: 434 us; the launch traced here: 433 us
  waiting for transfers between devices  259 us (60%)
  Pallas kernels  83.7 us (19%)
  starting transfers between devices  36.2 us (8%)
  blocking collectives  21.8 us (5%)
  local copies, waits for them, and re-layouts  14.6 us (3%)
  between operations  14 us (3%)
    all_to_all x6, waiting for transfers between devices, trade(): return lax.all_to_all(x, axes, split_axis=0, concat_axis=0, tiled=True)  143 us
    ppermute x5, waiting for transfers between devices, add_up(): lax.ppermute(give, axis, [(i, i ^ distance) for i in range(size)])  52.4 us
    all_gather x2, waiting for transfers between devices, on_pairs(): mine = [lax.all_gather(x, 'half', axis=0, tiled=True) for x in shares]  49.2 us
    all_to_all x6, starting transfers between devices, trade(): return lax.all_to_all(x, axes, split_axis=0, concat_axis=0, tiled=True)  26.5 us
    pallas_call x2, Pallas kernels, run_lane(): pl.pallas_call(kernel, grid=(1,), in_specs=[smem_spec(), pl.BlockSpec((co...  26.1 us
    pallas_call x4, Pallas kernels, lane_grads(): pl.pallas_call(functools.partial(lane_grad_kernel, member, other is not N...  23.2 us
    all_to_all x1, blocking collectives, trade(): return lax.all_to_all(x, axes, split_axis=0, concat_axis=0, tiled=True)  21.8 us
    unnamed x23, local copies, waits for them, and re-layouts  9.18 us
  transfers between devices with their start and end apart: 20, of which 13 were waited for; matrix products, arithmetic and copies ran while one was open for 1% of the time, Pallas kernels for 17%

profile of v3, /device:TPU:0, one launch (start us, length us, event | category | flops | bytes accessed | tf_op | source)
XLA Modules:
  0.0 432.8 jit_solution(343070499291978260)
XLA Ops:
  7.8 5.1 %merge_experts.1 = (bf16[4,192,768]{2,1,0:T(8,128)(2,1)}, bf16[4,192,768]{2,1,0:T(8,128)(2,1)}) custom-call(s32[32]{0:T(128)} %map_ref.5, f32[32]{0:T(128)} %coef_ref.3, s32[2]{0:T(128)} %pad_add_fusion.place_ref, bf16[32,192,1536]{2,1,0:T(8,128)(2,1)} %src_ref.3), custom_call_target="tpu_custom_call" | custom-call | flops 1 | bytes 1 | tf_op jit(solution)/shard_map/merge_experts/pallas_call | solution.py:277
  12.9 5.4 %all-to-all-start = ((bf16[4,192,768]{2,1,0:T(8,128)(2,1)}), bf16[4,192,768]{2,1,0:T(8,128)(2,1)S(1)}, u32[]{:S(2)}, u32[]{:S(2)}) async-start(bf16[4,192,768]{2,1,0:T(8,128)(2,1)} %get-tuple-element.24), calls=%async_computation | async-start | bytes 2359296 | tf_op jit(solution)/shard_map/all_to_all | solution.py:761
  19.5 7.6 %route.1 = (bf16[640,3200]{1,0:T(8,128)(2,1)}, f32[8,128]{1,0:T(8,128)}, s32[8,128]{1,0:T(8,128)}, s32[8,512]{1,0:T(8,128)}) custom-call(bf16[2880,128]{1,0:T(8,128)(2,1)} %bitcast.62, bf16[32,2880]{1,0:T(8,128)(2,1)} %bitcast.66, f32[1,32]{1,0:T(1,128)} %bitcast.74, s32[4,128]{1,0:T(4,128)} %bitcast.72, s32[1,32]{1,0:T(1,128)} %bitcast.71, ...), custom_call_target="tpu_custom_call" | custom-call | flops 1 | bytes 1 | tf_op jit(solution)/shard_map/route/pallas_call | solution.py:412
  27.2 6.1 %all-to-all-done.refs_1_ = bf16[4,192,768]{2,1,0:T(8,128)(2,1)S(1)} async-done(((bf16[4,192,768]{2,1,0:T(8,128)(2,1)}), bf16[4,192,768]{2,1,0:T(8,128)(2,1)S(1)}, u32[]{:S(2)}, u32[]{:S(2)}) %all-to-all-start) | async-done | bytes 1179680 | tf_op jit(solution)/shard_map/all_to_all | solution.py:761
  34.3 4.5 %all-to-all-start.1 = ((bf16[8,80,3200]{2,1,0:T(8,128)(2,1)}), bf16[8,80,3200]{2,1,0:T(8,128)(2,1)}, u32[]{:S(2)}, u32[]{:S(2)}) async-start(bf16[8,80,3200]{2,1,0:T(8,128)(2,1)} %bitcast.56), calls=%async_computation.1 | async-start | bytes 8192000 | tf_op jit(solution)/shard_map/all_to_all | solution.py:761
  39.6 71.0 %all-to-all-done.1 = bf16[8,80,3200]{2,1,0:T(8,128)(2,1)} async-done(((bf16[8,80,3200]{2,1,0:T(8,128)(2,1)}), bf16[8,80,3200]{2,1,0:T(8,128)(2,1)}, u32[]{:S(2)}, u32[]{:S(2)}) %all-to-all-start.1) | async-done | bytes 4096032 | tf_op jit(solution)/shard_map/all_to_all | solution.py:761
  114.2 5.5 %lane_grads_first.2 = bf16[8,2,192,384]{3,2,1,0:T(8,128)(2,1)} custom-call(s32[1]{0:T(128)} %bitcast.12._, bf16[640,3200]{1,0:T(8,128)(2,1)} %bitcast.11.grd_ref.hid_ref.flag_ref.rows_ref, bf16[640,3200]{1,0:T(8,128)(2,1)} %bitcast.11.grd_ref.hid_ref.flag_ref.rows_ref, bf16[640,3200]{1,0:T(8,128)(2,1)} %bitcast.11.grd_ref.hid_ref.flag_ref.rows_ref), custom_call_target="tpu_custom_call" | custom-call | flops 1 | bytes 1 | tf_op jit(solution)/shard_map/lane_grads_first/pallas_call | solution.py:520
  119.7 5.6 %lane_grads_first.3 = bf16[8,2,192,384]{3,2,1,0:T(8,128)(2,1)} custom-call(s32[1]{0:T(128)} %bitcast.12._, bf16[640,3200]{1,0:T(8,128)(2,1)} %bitcast.11.grd_ref.hid_ref.flag_ref.rows_ref, bf16[640,3200]{1,0:T(8,128)(2,1)} %bitcast.11.grd_ref.hid_ref.flag_ref.rows_ref, bf16[640,3200]{1,0:T(8,128)(2,1)} %bitcast.11.grd_ref.hid_ref.flag_ref.rows_ref), custom_call_target="tpu_custom_call" | custom-call | flops 1 | bytes 1 | tf_op jit(solution)/shard_map/lane_grads_first/pallas_call | solution.py:520
  129.7 5.9 %lane_grads_add.2.refs_2_ = bf16[8,2,192,384]{3,2,1,0:T(8,128)(2,1)} custom-call(s32[1]{0:T(128)} %bitcast.9._.core_ref, bf16[640,3200]{1,0:T(8,128)(2,1)} %bitcast.11.grd_ref.hid_ref.flag_ref.rows_ref, bf16[640,3200]{1,0:T(8,128)(2,1)} %bitcast.11.grd_ref.hid_ref.flag_ref.rows_ref, bf16[640,3200]{1,0:T(8,128)(2,1)} %bitcast.11.grd_ref.hid_ref.flag_ref.rows_ref, ...), custom_call_target="tpu_custom_call" | custom-call | flops 1 | bytes 1 | tf_op jit(solution)/shard_map/lane_grads_add/pallas_call | solution.py:520
  137.1 6.2 %lane_grads_add.3.refs_3_ = bf16[8,2,192,384]{3,2,1,0:T(8,128)(2,1)} custom-call(s32[1]{0:T(128)} %bitcast.9._.core_ref, bf16[640,3200]{1,0:T(8,128)(2,1)} %bitcast.11.grd_ref.hid_ref.flag_ref.rows_ref, bf16[640,3200]{1,0:T(8,128)(2,1)} %bitcast.11.grd_ref.hid_ref.flag_ref.rows_ref, bf16[640,3200]{1,0:T(8,128)(2,1)} %bitcast.11.grd_ref.hid_ref.flag_ref.rows_ref, ...), custom_call_target="tpu_custom_call" | custom-call | flops 1 | bytes 1 | tf_op jit(solution)/shard_map/lane_grads_add/pallas_call | solution.py:520
  143.2 49.2 %all-gather.3.cloned.1.call-done.refs_0_ = bf16[8,192,768]{2,1,0:T(8,128)(2,1)} async-done(((bf16[4,192,768]{2,1,0:T(8,128)(2,1)}), bf16[8,192,768]{2,1,0:T(8,128)(2,1)}) %all-gather.3.cloned.1.call-update) | async-done | bytes 2359312 | tf_op jit(solution)/shard_map/all_gather | solution.py:764
  193.0 7.6 %collective-permute-done.2.refs_2_ = bf16[8,192,768]{2,1,0:T(8,128)(2,1)S(1)} collective-permute-done((bf16[8,192,768]{2,1,0:T(8,128)(2,1)}, bf16[8,192,768]{2,1,0:T(8,128)(2,1)S(1)}, u32[]{:S(2)}, u32[]{:S(2)}) %collective-permute-start.2) | collective-permute-done | bytes 2359328 | tf_op jit(solution)/shard_map/ppermute | solution.py:730
  202.1 13.0 %lane_forward.1 = bf16[640,1536]{1,0:T(8,128)(2,1)} custom-call(s32[1]{0:T(128)} %bitcast.9._.core_ref, bf16[640,3200]{1,0:T(8,128)(2,1)} %bitcast.11.grd_ref.hid_ref.flag_ref.rows_ref, bf16[640,3200]{1,0:T(8,128)(2,1)} %bitcast.11.grd_ref.hid_ref.flag_ref.rows_ref, bf16[8,192,768]{2,1,0:T(8,128)(2,1)} %get-tuple-element.25.refs_0_, ...), custom_call_target="tpu_custom_call" | custom-call | flops 1 | bytes 1 | tf_op jit(solution)/shard_map/lane_forward/pallas_call | solution.py:478
  219.0 47.9 %all-to-all-done.3 = bf16[8,80,1536]{2,1,0:T(8,128)(2,1)S(1)} async-done(((bf16[8,80,1536]{2,1,0:T(8,128)(2,1)}), bf16[8,80,1536]{2,1,0:T(8,128)(2,1)S(1)}, u32[]{:S(2)}, u32[]{:S(2)}) %all-to-all-start.3) | async-done | bytes 1966112 | tf_op jit(solution)/shard_map/all_to_all | solution.py:761
  268.2 5.0 %combine.1 = (bf16[128,1536]{1,0:T(8,128)(2,1)}, bf16[2880,128]{1,0:T(8,128)(2,1)}, f32[32,3072]{1,0:T(8,128)}) custom-call(bf16[128,1536]{1,0:T(8,128)(2,1)} %bitcast.65, f32[8,128]{1,0:T(8,128)} %get-tuple-element.21.gate_ref, s32[8,128]{1,0:T(8,128)} %get-tuple-element.22.pos_ref, s32[4,128]{1,0:T(4,128)} %bitcast.73, bf16[32,2880]{1,0:T(8,128)(2,1)} %bitcast.67, ...), custom_call_target="tpu_custom_call" | custom-call | flops 1 | bytes 1 | tf_op jit(solution)/shard_map/combine/pallas_call | solution.py:582
  274.4 13.0 %lane_backward.1 = bf16[640,1536]{1,0:T(8,128)(2,1)} custom-call(s32[1]{0:T(128)} %bitcast.9._.core_ref, bf16[640,3200]{1,0:T(8,128)(2,1)} %bitcast.11.grd_ref.hid_ref.flag_ref.rows_ref, bf16[640,3200]{1,0:T(8,128)(2,1)} %bitcast.11.grd_ref.hid_ref.flag_ref.rows_ref, bf16[8,192,768]{2,1,0:T(8,128)(2,1)} %get-tuple-element.25.refs_0_, ...), custom_call_target="tpu_custom_call" | custom-call | flops 1 | bytes 1 | tf_op jit(solution)/shard_map/lane_backward/pallas_call | solution.py:478
  287.4 5.9 %all-to-all-start.4 = ((bf16[8,80,1536]{2,1,0:T(8,128)(2,1)}), bf16[8,80,1536]{2,1,0:T(8,128)(2,1)S(1)}, u32[]{:S(2)}, u32[]{:S(2)}) async-start(bf16[8,80,1536]{2,1,0:T(8,128)(2,1)} %bitcast.59), calls=%async_computation.4 | async-start | bytes 3932160 | tf_op jit(solution)/shard_map/all_to_all | solution.py:761
  293.3 4.1 collective-permute-done.4
  299.7 43.1 %collective-permute-done.5 = f32[8,3072]{1,0:T(8,128)S(1)} collective-permute-done((f32[8,3072]{1,0:T(8,128)S(1)}, f32[8,3072]{1,0:T(8,128)S(1)}, u32[]{:S(2)}, u32[]{:S(2)}) %collective-permute-start.5) | collective-permute-done | bytes 98336 | tf_op jit(solution)/shard_map/ppermute | solution.py:725
  357.2 21.8 %all_to_all.40.refs_0_ = bf16[8,192,384]{2,1,0:T(8,128)(2,1)} all-to-all(bf16[8,192,384]{2,1,0:T(8,128)(2,1)} %get-tuple-element.31), channel_id=1, replica_groups=mesh['half'=2,'place'=4,'row'=2,'core'=2] {'place','row'}, dimensions={0} | all-to-all | bytes 2359296 | tf_op jit(solution)/shard_map/all_to_all | solution.py:761
  382.6 15.5 %all-to-all-done.6.refs_1_ = bf16[8,192,384]{2,1,0:T(8,128)(2,1)S(1)} async-done(((bf16[8,192,384]{2,1,0:T(8,128)(2,1)}), bf16[8,192,384]{2,1,0:T(8,128)(2,1)S(1)}, u32[]{:S(2)}, u32[]{:S(2)}) %all-to-all-start.6) | async-done | bytes 1179680 | tf_op jit(solution)/shard_map/all_to_all | solution.py:761
  399.1 6.6 %coef_dots.1._ = f32[8,128]{1,0:T(8,128)} custom-call(s32[1]{0:T(128)} %bitcast.30.rep_ref, s32[32]{0:T(128)} %map_ref.5, bf16[32,192,1536]{2,1,0:T(8,128)(2,1)} %src_ref.3, bf16[8,192,384]{2,1,0:T(8,128)(2,1)} %all_to_all.40.refs_0_, bf16[8,192,384]{2,1,0:T(8,128)(2,1)} %copy-done.2), custom_call_target="tpu_custom_call" | custom-call | flops 1 | bytes 1 | tf_op jit(solution)/shard_map/coef_dots/pallas_call | solution.py:679
  411.5 5.9 %finish.1 = f32[32,192,384]{2,1,0:T(8,128)} custom-call(s32[32]{0:T(128)} %map_ref.5, f32[32]{0:T(128)} %coef_ref.3, f32[8,128]{1,0:T(8,128)} %coef_dots.1._, bf16[8,192,384]{2,1,0:T(8,128)(2,1)} %all_to_all.40.refs_0_, bf16[8,192,384]{2,1,0:T(8,128)(2,1)} %copy-done.2), custom_call_target="tpu_custom_call" | custom-call | flops 1 | bytes 1 | tf_op jit(solution)/shard_map/finish/pallas_call | solution.py:700
  417.4 6.3 %all-to-all-done.7 = f32[32,1,3200]{2,1,0:T(1,128)S(1)} async-done(((f32[32,1,3200]{2,1,0:T(1,128)}), f32[32,1,3200]{2,1,0:T(1,128)S(1)}, u32[]{:S(2)}, u32[]{:S(2)}) %all-to-all-start.7) | async-done | bytes 409632 | tf_op jit(solution)/shard_map/all_to_all | solution.py:812
  (81 shorter events, 51.0 us)
Async XLA Ops:
  12.9 5.4 %copy-start.8 = (bf16[1,128,4,1536]{3,2,1,0:T(4,128)(2,1)S(1)}, bf16[1,128,4,1536]{3,2,1,0:T(4,128)(2,1)}, u32[]{:S(2)}) copy-start(bf16[1,128,4,1536]{3,2,1,0:T(4,128)(2,1)} %param.12) | copy-start | bytes 4718596
  12.9 20.4 %all-to-all-start = ((bf16[4,192,768]{2,1,0:T(8,128)(2,1)}), bf16[4,192,768]{2,1,0:T(8,128)(2,1)S(1)}, u32[]{:S(2)}, u32[]{:S(2)}) async-start(bf16[4,192,768]{2,1,0:T(8,128)(2,1)} %get-tuple-element.24), calls=%async_computation | async-start | bytes 2359296 | tf_op jit(solution)/shard_map/all_to_all | solution.py:761
  34.3 76.3 %all-to-all-start.1 = ((bf16[8,80,3200]{2,1,0:T(8,128)(2,1)}), bf16[8,80,3200]{2,1,0:T(8,128)(2,1)}, u32[]{:S(2)}, u32[]{:S(2)}) async-start(bf16[8,80,3200]{2,1,0:T(8,128)(2,1)} %bitcast.56), calls=%async_computation.1 | async-start | bytes 8192000 | tf_op jit(solution)/shard_map/all_to_all | solution.py:761
  38.9 104.4 %all-gather.5.cloned.1.call-start = ((), (), s32[]{:S(2)}) async-start(), calls=%async_computation.11 | async-start | bytes 3538944 | tf_op jit(solution)/shard_map/all_gather | solution.py:764
  110.6 17.8 %all-to-all-start.2 = ((bf16[4,192,768]{2,1,0:T(8,128)(2,1)}), bf16[4,192,768]{2,1,0:T(8,128)(2,1)S(1)}, u32[]{:S(2)}, u32[]{:S(2)}) async-start(bf16[4,192,768]{2,1,0:T(8,128)(2,1)} %get-tuple-element.20._), calls=%async_computation.2 | async-start | bytes 2359296 | tf_op jit(solution)/shard_map/all_to_all | solution.py:761
  114.1 78.3 %all-gather.3.cloned.1.call-start = ((), (), s32[]{:S(2)}) async-start(), calls=%async_computation.10 | async-start | bytes 3538944 | tf_op jit(solution)/shard_map/all_gather | solution.py:764
  119.7 10.0 %collective-permute-start = (bf16[8,2,192,384]{3,2,1,0:T(8,128)(2,1)}, bf16[8,2,192,384]{3,2,1,0:T(8,128)(2,1)}, u32[]{:S(2)}, u32[]{:S(2)}) collective-permute-start(bf16[8,2,192,384]{3,2,1,0:T(8,128)(2,1)} %lane_grads_first.2), channel_id=1, source_target_pairs={{0,1},{1,0},{2,3},{3,2},{4,5},{5,4},{6,7},{7,6},{8,9},{9,8},{10,11... | collective-permute-start | bytes 7077896 | tf_op jit(solution)/shard_map/ppermute | solution.py:730
  125.3 10.4 %collective-permute-start.1 = (bf16[8,2,192,384]{3,2,1,0:T(8,128)(2,1)}, bf16[8,2,192,384]{3,2,1,0:T(8,128)(2,1)S(1)}, u32[]{:S(2)}, u32[]{:S(2)}) collective-permute-start(bf16[8,2,192,384]{3,2,1,0:T(8,128)(2,1)} %lane_grads_first.3), channel_id=1, source_target_pairs={{0,1},{1,0},{2,3},{3,2},{4,5},{5,4},{6,7},{7,6},{8,9},{9,8},{10,11... | collective-permute-start | bytes 7077896 | tf_op jit(solution)/shard_map/ppermute | solution.py:730
  129.5 227.7 %reduce-scatter.3.cloned.1.call-start = ((), (), s32[]{:S(2)}) async-start(), calls=%async_computation.12 | async-start | bytes 3538944 | tf_op jit(solution)/shard_map/reduce_scatter | solution.py:785
  192.5 8.1 %collective-permute-start.2 = (bf16[8,192,768]{2,1,0:T(8,128)(2,1)}, bf16[8,192,768]{2,1,0:T(8,128)(2,1)S(1)}, u32[]{:S(2)}, u32[]{:S(2)}) collective-permute-start(bf16[8,192,768]{2,1,0:T(8,128)(2,1)} %get-tuple-element.25.refs_0_), channel_id=1, source_target_pairs={{0,1},{1,0},{2,3},{3,2},{4,5},{5,4},{6,7},{7,6},{8,9},{9,8},{10,11... | collective-permute-start | bytes 7077896 | tf_op jit(solution)/shard_map/ppermute | solution.py:730
  192.5 8.2 %collective-permute-start.3 = (bf16[8,192,768]{2,1,0:T(8,128)(2,1)}, bf16[8,192,768]{2,1,0:T(8,128)(2,1)}, u32[]{:S(2)}, u32[]{:S(2)}) collective-permute-start(bf16[8,192,768]{2,1,0:T(8,128)(2,1)} %get-tuple-element.26.refs_1_), channel_id=1, source_target_pairs={{0,1},{1,0},{2,3},{3,2},{4,5},{5,4},{6,7},{7,6},{8,9},{9,8},{10,11... | collective-permute-start | bytes 7077896 | tf_op jit(solution)/shard_map/ppermute | solution.py:730
  215.1 51.8 %all-to-all-start.3 = ((bf16[8,80,1536]{2,1,0:T(8,128)(2,1)}), bf16[8,80,1536]{2,1,0:T(8,128)(2,1)S(1)}, u32[]{:S(2)}, u32[]{:S(2)}) async-start(bf16[8,80,1536]{2,1,0:T(8,128)(2,1)} %bitcast.60), calls=%async_computation.3 | async-start | bytes 3932160 | tf_op jit(solution)/shard_map/all_to_all | solution.py:761
  218.8 138.4 %reduce-scatter.5.cloned.1.call-start = ((), (), s32[]{:S(2)}) async-start(), calls=%async_computation.13 | async-start | bytes 3538944 | tf_op jit(solution)/shard_map/reduce_scatter | solution.py:785
  274.2 23.2 %collective-permute-start.4 = (f32[16,3072]{1,0:T(8,128)S(1)}, f32[16,3072]{1,0:T(8,128)S(1)}, u32[]{:S(2)}, u32[]{:S(2)}) collective-permute-start(f32[16,3072]{1,0:T(8,128)S(1)} %dynamic-slice_bitcast_fusion), channel_id=1, source_target_pairs={{0,16},{16,0},{1,17},{17,1},{2,18},{18,2},{3,19},{19,3},{4,20},{20... | collective-permute-start | bytes 589832 | tf_op jit(solution)/shard_map/ppermute | solution.py:725
  287.4 10.0 %copy-start.9 = (f32[32,3072]{1,0:T(8,128)S(1)}, f32[32,3072]{1,0:T(8,128)}, u32[]{:S(2)}) copy-start(f32[32,3072]{1,0:T(8,128)} %get-tuple-element.30) | copy-start | bytes 1179652
  287.4 63.8 %all-to-all-start.4 = ((bf16[8,80,1536]{2,1,0:T(8,128)(2,1)}), bf16[8,80,1536]{2,1,0:T(8,128)(2,1)S(1)}, u32[]{:S(2)}, u32[]{:S(2)}) async-start(bf16[8,80,1536]{2,1,0:T(8,128)(2,1)} %bitcast.59), calls=%async_computation.4 | async-start | bytes 3932160 | tf_op jit(solution)/shard_map/all_to_all | solution.py:761
  297.5 45.4 %collective-permute-start.5 = (f32[8,3072]{1,0:T(8,128)S(1)}, f32[8,3072]{1,0:T(8,128)S(1)}, u32[]{:S(2)}, u32[]{:S(2)}) collective-permute-start(f32[8,3072]{1,0:T(8,128)S(1)} %dynamic-slice_bitcast_fusion.1), channel_id=1, source_target_pairs={{0,8},{4,12},{8,0},{12,4},{1,9},{5,13},{9,1},{13,5},{2,10},{6,14},... | collective-permute-start | bytes 294920 | tf_op jit(solution)/shard_map/ppermute | solution.py:725
  342.9 4.2 collective-permute-start.6
  347.1 3.9 collective-permute-start.7
  351.1 5.5 %collective-permute-start.8 = (f32[1,3072]{1,0:T(1,128)S(1)}, f32[1,3072]{1,0:T(1,128)S(1)}, u32[]{:S(2)}, u32[]{:S(2)}) collective-permute-start(f32[1,3072]{1,0:T(1,128)S(1)} %constant_dynamic-slice_fusion), channel_id=1, source_target_pairs={{0,1},{1,0},{2,3},{3,2},{4,5},{5,4},{6,7},{7,6},{8,9},{9,8},{10,11... | collective-permute-start | bytes 36872 | tf_op jit(solution)/shard_map/ppermute | solution.py:725
  379.0 19.1 %all-to-all-start.6 = ((bf16[8,192,384]{2,1,0:T(8,128)(2,1)}), bf16[8,192,384]{2,1,0:T(8,128)(2,1)S(1)}, u32[]{:S(2)}, u32[]{:S(2)}) async-start(bf16[8,192,384]{2,1,0:T(8,128)(2,1)} %get-tuple-element.32), calls=%async_computation.8 | async-start | bytes 2359296 | tf_op jit(solution)/shard_map/all_to_all | solution.py:761
  399.1 7.3 %copy-start.10 = (f32[1,3072]{1,0:T(1,128)S(1)}, f32[1,3072]{1,0:T(1,128)}, u32[]{:S(2)}) copy-start(f32[1,3072]{1,0:T(1,128)} %dynamic-slice_add_fusion.refs_3_) | copy-start | bytes 36868
  399.1 11.1 %copy-start = (bf16[512,1536]{1,0:T(8,128)(2,1)S(1)}, bf16[512,1536]{1,0:T(8,128)(2,1)}, u32[]{:S(2)}) copy-start(bf16[512,1536]{1,0:T(8,128)(2,1)} %unplace.1.refs_2_) | copy-start | bytes 4718596
  407.4 16.2 %all-to-all-start.7 = ((f32[32,1,3200]{2,1,0:T(1,128)}), f32[32,1,3200]{2,1,0:T(1,128)S(1)}, u32[]{:S(2)}, u32[]{:S(2)}) async-start(f32[32,1,3200]{2,1,0:T(1,128)} %broadcast_in_dim.17), calls=%async_computation.9 | async-start | bytes 819200 | tf_op jit(solution)/shard_map/all_to_all | solution.py:812
  (7 other events, 8.6 us)
Sparse Core Ops, SparseCore 0:
  41.8 62.8 all-gather.4
  129.6 62.8 all-gather.2
  195.3 59.9 reduce-scatter.2
  274.5 62.2 reduce-scatter.4

commit v4 on v3

--- a/solution.py
+++ b/solution.py
@@ -209,7 +209,10 @@
 F32 = jnp.float32
 I32 = jnp.int32
 TILE = 256
-BRIEF = pl.CostEstimate(flops=1, bytes_accessed=1, transcendentals=0)
+
+
+def cost(us):
+    return pl.CostEstimate(flops=us * 10**9, bytes_accessed=us * 10**6, transcendentals=0)
 
 
 def any_spec():
@@ -232,30 +235,22 @@
     return lax.dot_general(a, b, (dims, ((), ())), preferred_element_type=F32)
 
 
-def merge_kernel(map_ref, coef_ref, place_ref, src_ref, *refs):
-    outs, (order_ref, count_ref, held, sems) = refs[:-4], refs[-4:]
-    half = held.shape[2]
+def merge_kernel(rep_ref, map_ref, coef_ref, src_ref, out_ref, order_ref, count_ref, held, sems):
+    combos, _, cols = out_ref.shape
     expert_order(map_ref, order_ref, count_ref)
-    at = pl.ds(pl.multiple_of(place_ref[1] * half, half), half)
-    copies, experts = [], []
-    for m in range(2):
-        for j in range(outs[0].shape[0]):
-            combo = 4 * j + 2 * place_ref[0] + m
-            for n in range(2):
-                expert = order_ref[2 * combo + n]
-                experts.append(expert)
-                i = len(copies)
-                copies.append(
-                    pltpu.make_async_copy(src_ref.at[expert, :, at], held.at[i], sems.at[i])
-                )
-                copies[-1].start()
-    for m, out_ref in enumerate(outs):
-        for j in range(out_ref.shape[0]):
-            i = 2 * (m * out_ref.shape[0] + j)
-            copies[i].wait()
-            copies[i + 1].wait()
-            one, two = coef_ref[experts[i]], coef_ref[experts[i + 1]]
-            out_ref[j] = (one * held[i].astype(F32) + two * held[i + 1].astype(F32)).astype(BF)
+    at = pl.ds(pl.multiple_of(rep_ref[0] * cols, cols), cols)
+    copies = [
+        pltpu.make_async_copy(src_ref.at[order_ref[i], :, at], held.at[i], sems.at[i])
+        for i in range(2 * combos)
+    ]
+    for copy in copies:
+        copy.start()
+    for g in range(combos):
+        copies[2 * g].wait()
+        copies[2 * g + 1].wait()
+        one, two = coef_ref[order_ref[2 * g]], coef_ref[order_ref[2 * g + 1]]
+        merged = one * held[2 * g].astype(F32) + two * held[2 * g + 1].astype(F32)
+        out_ref[g] = merged.astype(BF)
 
 
 def expert_order(map_ref, order_ref, count_ref):
@@ -271,24 +266,24 @@
         count_ref[g] = n + 1
 
 
-def merge_experts(where_am_i, merge_map, merge_coef, source_w, places):
+def merge_experts(rep_index, merge_map, merge_coef, source_w, reps):
     count, rows, width = source_w.shape
-    half = width // 2
+    cols = width // reps
     return pl.pallas_call(
         merge_kernel,
         in_specs=[smem_spec(), smem_spec(), smem_spec(), any_spec()],
-        out_specs=[vmem_spec()] * 2,
-        out_shape=[jax.ShapeDtypeStruct((places, rows, half), BF)] * 2,
+        out_specs=vmem_spec(),
+        out_shape=jax.ShapeDtypeStruct((count // 2, rows, cols), BF),
         scratch_shapes=[
             pltpu.SMEM((count,), I32),
             pltpu.SMEM((count // 2,), I32),
-            pltpu.VMEM((4 * places, rows, half), BF),
-            pltpu.SemaphoreType.DMA((4 * places,)),
+            pltpu.VMEM((count, rows, cols), BF),
+            pltpu.SemaphoreType.DMA((count,)),
         ],
         compiler_params=params(56),
-        cost_estimate=BRIEF,
+        cost_estimate=cost(5),
         name="merge_experts",
-    )(merge_map, merge_coef, where_am_i, source_w)
+    )(rep_index, merge_map, merge_coef, source_w)
 
 
 def hbm_spec():
@@ -303,7 +298,7 @@
         out_specs=[hbm_spec()] * count,
         out_shape=[jax.ShapeDtypeStruct(a.shape, a.dtype) for a in arrays],
         input_output_aliases={i: i for i in range(count)},
-        cost_estimate=BRIEF,
+        cost_estimate=cost(0),
         name="hold",
     )(*arrays, *after)
 
@@ -328,7 +323,7 @@
 def route_kernel(
     capacity, lanes,
     xt_ref, rwt_ref, rb_ref, idx_ref, map_ref, hid_ref, og_ref, _,
-    send_ref, gate_ref, pos_ref, slot_ref,
+    sh_ref, sg_ref, gate_ref, pos_ref, slot_ref,
 ):
     top, tok = idx_ref.shape
     sources = rwt_ref.shape[0]
@@ -388,22 +383,21 @@
     slot_ref[...] = jnp.broadcast_to(slot_pos, slot_ref.shape)
     take = lax.broadcasted_iota(I32, (places, slots), 0) == slot_pos
     placed = jnp.sum(jnp.where(take, spot[3:4].astype(F32), 0.0), axis=1, keepdims=True)
-    depth = og_ref.shape[1]
-    send_ref[:, depth + width :] = jnp.broadcast_to(placed, (places, 128)).astype(BF)
+    sh_ref[:, width:] = jnp.broadcast_to(placed, (places, 128)).astype(BF)
     take = take.astype(BF)
     for n in range(0, width, TILE):
         rows = jnp.dot(take, hid_ref[:, n : n + TILE], preferred_element_type=F32)
-        send_ref[:, depth + n : depth + n + TILE] = rows.astype(BF)
+        sh_ref[:, n : n + TILE] = rows.astype(BF)
     takes = [
         (lax.broadcasted_iota(I32, (places, tok), 0) == position[k]).astype(BF) for k in range(top)
     ]
     columns = [column(g) for g in gates]
-    for n in range(0, depth, TILE):
+    for n in range(0, og_ref.shape[1], TILE):
         og = og_ref[:, n : n + TILE].astype(F32)
         rows = jnp.zeros((places, TILE), F32)
         for k in range(top):
             rows = rows + jnp.dot(takes[k], (columns[k] * og).astype(BF), preferred_element_type=F32)
-        send_ref[:, n : n + TILE] = rows.astype(BF)
+        sg_ref[:, n : n + TILE] = rows.astype(BF)
 
 
 def route(xt, rwt, router_b, idx_t, merge_map, hid, og, after, capacity, lanes):
@@ -412,93 +406,83 @@
     return pl.pallas_call(
         functools.partial(route_kernel, capacity, lanes),
         in_specs=[vmem_spec()] * 7 + [any_spec()],
-        out_specs=[vmem_spec()] * 4,
+        out_specs=[vmem_spec()] * 5,
         out_shape=[
-            jax.ShapeDtypeStruct((lanes * capacity, og.shape[1] + width + 128), BF),
+            jax.ShapeDtypeStruct((lanes * capacity, width + 128), BF),
+            jax.ShapeDtypeStruct((lanes * capacity, og.shape[1]), BF),
             jax.ShapeDtypeStruct((8, tok), F32),
             jax.ShapeDtypeStruct((8, tok), I32),
             jax.ShapeDtypeStruct((8, slots), I32),
         ],
         compiler_params=params(56),
-        cost_estimate=BRIEF,
+        cost_estimate=cost(5),
         name="route",
     )(xt, rwt, router_b[None, :], idx_t, merge_map[None, :], hid, og, after)
 
 
-def load_weights(core_ref, mine, other, w_ref, sems):
-    core = core_ref[0]
+def load_weights(rep_ref, pieces, w_ref, sems):
     copies = []
-    for m in range(len(mine)):
-        blocks, rows, half = mine[m].shape
-        for n, part in enumerate((mine[m], other[m])):
-            for c in range(blocks):
-                to = w_ref.at[core if n == 0 else 1 - core, m, pl.ds(c * rows, rows), :]
-                copies.append(pltpu.make_async_copy(part.at[c], to, sems.at[len(copies)]))
+    for i, piece in enumerate(pieces):
+        blocks, _, rows, cols = piece.shape
+        owner = jnp.bitwise_xor(rep_ref[0], i)
+        at = pl.ds(pl.multiple_of(owner * cols, cols), cols)
+        for c in range(blocks):
+            to = w_ref.at[:, pl.ds(c * rows, rows), at]
+            copies.append(pltpu.make_async_copy(piece.at[c], to, sems.at[len(copies)]))
     for copy in copies:
         copy.start()
     for copy in copies:
         copy.wait()
 
 
-def forward_kernel(core_ref, rows_ref, flag_ref, *refs):
+def forward_kernel(rep_ref, rows_ref, flag_ref, *refs):
     out_ref, w_ref, sems = refs[-3:]
-    load_weights(core_ref, refs[:2], refs[2:4], w_ref, sems)
-    half = w_ref.shape[3]
+    load_weights(rep_ref, refs[:-3], w_ref, sems)
     member = flag_ref[:, :1].astype(F32)
-
+    for n in range(0, w_ref.shape[1], TILE):
+        at = slice(n, n + TILE)
+        both = [dot(rows_ref[...], w_ref[m, at, :], ((1,), (1,))) for m in range(2)]
+        out_ref[:, at] = jnp.where(member == 0.0, both[0], both[1]).astype(BF)
+
+
+def backward_kernel(rep_ref, rows_ref, flag_ref, *refs):
+    out_ref, w_ref, sems = refs[-3:]
+    load_weights(rep_ref, refs[:-3], w_ref, sems)
+    member = flag_ref[:, :1].astype(F32)
     for n in range(0, w_ref.shape[2], TILE):
         at = slice(n, n + TILE)
-        both = [
-            dot(rows_ref[:, :half], w_ref[0, m, at, :], ((1,), (1,)))
-            + dot(rows_ref[:, half : 2 * half], w_ref[1, m, at, :], ((1,), (1,)))
-            for m in range(2)
-        ]
+        both = [dot(rows_ref[...], w_ref[m, :, at], ((1,), (0,))) for m in range(2)]
         out_ref[:, at] = jnp.where(member == 0.0, both[0], both[1]).astype(BF)
 
 
-def backward_kernel(core_ref, rows_ref, flag_ref, *refs):
-    out_ref, w_ref, sems = refs[-3:]
-    load_weights(core_ref, refs[:2], refs[2:4], w_ref, sems)
-    half = w_ref.shape[3]
-    member = flag_ref[:, :1].astype(F32)
-    for h in range(2):
-        for n in range(0, half, TILE):
-            at = slice(n, n + TILE)
-            both = [dot(rows_ref[...], w_ref[h, m, :, at], ((1,), (0,))) for m in range(2)]
-            both = jnp.where(member == 0.0, both[0], both[1])
-            out_ref[:, h * half + n : h * half + n + TILE] = both.astype(BF)
-
-
-def run_lane(kernel, core, rows, which, mine, other, name):
-    blocks, share, half = mine[0].shape
-    members = len(mine)
-    depth = share * blocks
+def run_lane(kernel, rep_index, rows, hid, pieces, name):
+    blocks, members, share, cols = pieces[0].shape
+    depth, width = share * blocks, cols * len(pieces)
     count = rows.shape[0]
-    wide = (rows.shape[1] - 128) // 2
     return pl.pallas_call(
         kernel,
         grid=(1,),
         in_specs=[
             smem_spec(),
-            pl.BlockSpec((count, wide), lambda i: (0, which)),
-            pl.BlockSpec((count, 128), lambda i: (0, 2 * wide // 128)),
+            pl.BlockSpec((count, width), lambda i: (0, 0)),
+            pl.BlockSpec((count, 128), lambda i: (0, width // 128)),
         ]
-        + [any_spec()] * (2 * members),
-        out_specs=pl.BlockSpec((count, wide), lambda i: (0, 0)),
-        out_shape=jax.ShapeDtypeStruct((count, wide), BF),
+        + [any_spec()] * len(pieces),
+        out_specs=pl.BlockSpec((count, width), lambda i: (0, 0)),
+        out_shape=jax.ShapeDtypeStruct((count, width), BF),
         scratch_shapes=[
-            pltpu.VMEM((2, members, depth, half), BF),
-            pltpu.SemaphoreType.DMA((2 * members * blocks,)),
+            pltpu.VMEM((members, depth, width), BF),
+            pltpu.SemaphoreType.DMA((blocks * len(pieces),)),
         ],
         compiler_params=params(56),
-        cost_estimate=BRIEF,
+        cost_estimate=cost(12),
         name=name,
-    )(core, rows, rows, *mine, *other)
-
-
-def lane_grad_kernel(member, has_other, _, grd_ref, hid_ref, flag_ref, *refs):
+    )(rep_index, rows, hid, *pieces)
+
+
+def lane_grad_kernel(has_other, _, grd_ref, hid_ref, flag_ref, *refs):
     out_ref = refs[-1]
-    chosen = flag_ref[:, :1].astype(F32) == float(member)
+    chosen = flag_ref[:, :1].astype(F32) == pl.program_id(0).astype(F32)
     hid = jnp.where(chosen, hid_ref[...], jnp.zeros_like(hid_ref))
     blocks, _, rows, cols = out_ref.shape
     each = 2 if blocks % 2 == 0 and 2 * rows % 128 == 0 else blocks
@@ -510,31 +494,31 @@
         out_ref[n : n + each, 0] = part.astype(BF)
 
 
-def lane_grads(core, rows, member, other, blocks, reps):
-    count = rows.shape[0]
-    width = (rows.shape[1] - 128) // 2
+def lane_grads(owner, grd, hid, other, blocks, reps):
+    count, depth = grd.shape
+    width = hid.shape[1] - 128
     cols = width // reps
-    shape = (blocks, 2, width // blocks, cols)
-    block = pl.BlockSpec((blocks, 1, width // blocks, cols), lambda y, s: (0, y, 0, 0))
+    shape = (blocks, 2, depth // blocks, cols)
+    block = pl.BlockSpec((blocks, 1, depth // blocks, cols), lambda m, s: (0, m, 0, 0))
     extra = [] if other is None else [other]
     return pl.pallas_call(
-        functools.partial(lane_grad_kernel, member, other is not None),
+        functools.partial(lane_grad_kernel, other is not None),
         grid_spec=pltpu.PrefetchScalarGridSpec(
             num_scalar_prefetch=1,
             grid=(2,),
             in_specs=[
-                pl.BlockSpec((count, width), lambda y, s: (0, 0)),
-                pl.BlockSpec((count, cols), lambda y, s: (0, reps + 2 * y + s[0])),
-                pl.BlockSpec((count, 128), lambda y, s: (0, 2 * width // 128)),
+                pl.BlockSpec((count, depth), lambda m, s: (0, 0)),
+                pl.BlockSpec((count, cols), lambda m, s: (0, s[0])),
+                pl.BlockSpec((count, 128), lambda m, s: (0, width // 128)),
             ]
             + [block] * len(extra),
             out_specs=block,
         ),
         out_shape=jax.ShapeDtypeStruct(shape, BF),
         compiler_params=params(56),
-        cost_estimate=BRIEF,
+        cost_estimate=cost(6),
         name="lane_grads_add" if extra else "lane_grads_first",
-    )(core, rows, rows, rows, *extra)
+    )(owner, grd, hid, hid, *extra)
 
 
 def combine_kernel(
@@ -589,7 +573,7 @@
             jax.ShapeDtypeStruct((sources, (features + 127) // 128 * 128 + 128), F32),
         ],
         compiler_params=params(56),
-        cost_estimate=BRIEF,
+        cost_estimate=cost(5),
         name="combine",
     )(og, gates, pos, idx_t, rwt, xt, home_out)
 
@@ -609,18 +593,18 @@
         out_specs=vmem_spec(),
         out_shape=jax.ShapeDtypeStruct((slot_pos.shape[1], home_back.shape[1]), BF),
         compiler_params=params(56),
-        cost_estimate=BRIEF,
+        cost_estimate=cost(5),
         name="unplace",
     )(slot_pos, home_back)
 
 
-def coef_kernel(rep_ref, map_ref, src_ref, *refs):
-    parts, (out_ref, order_ref, count_ref, held, weights, sems) = refs[:-6], refs[-6:]
+def coef_kernel(rep_ref, map_ref, src_ref, got_ref, out_ref, order_ref, count_ref, held, weights, sems):
     count, rows, cols = weights.shape
     at = pl.ds(pl.multiple_of(rep_ref[0] * cols, cols), cols)
-    copies = [pltpu.make_async_copy(src_ref.at[:, :, at], weights, sems.at[len(parts)])]
-    for m, part in enumerate(parts):
-        copies.append(pltpu.make_async_copy(part, held.at[m], sems.at[m]))
+    copies = [
+        pltpu.make_async_copy(src_ref.at[:, :, at], weights, sems.at[0]),
+        pltpu.make_async_copy(got_ref, held, sems.at[1]),
+    ]
     for copy in copies:
         copy.start()
     expert_order(map_ref, order_ref, count_ref)
@@ -629,7 +613,7 @@
     lane = lax.broadcasted_iota(I32, (8, 128), 1)
 
     def one(g, total):
-        merged = held[jnp.bitwise_and(g, 1), jnp.right_shift(g, 1)].astype(F32)
+        merged = held[g].astype(F32)
         for n in range(2):
             expert = order_ref[2 * g + n]
             product = merged * weights[expert].astype(F32)
@@ -644,29 +628,31 @@
     out_ref[...] = lax.fori_loop(0, count // 2, one, jnp.zeros((8, 128), F32))
 
 
-def finish_kernel(scale, map_ref, coef_ref, _, *refs):
-    parts, (out_ref, order_ref, count_ref, held, ready, sems, more) = refs[:-7], refs[-7:]
+def finish_kernel(
+    scale, map_ref, coef_ref, _, got_ref, out_ref, order_ref, count_ref, held, ready, sems, more
+):
     count = ready.shape[0]
-    copies = [
-        pltpu.make_async_copy(part, held.at[m], sems.at[m]) for m, part in enumerate(parts)
-    ]
-    for copy in copies:
-        copy.start()
-    expert_order(map_ref, order_ref, count_ref)
+
+    def load(g):
+        return pltpu.make_async_copy(got_ref.at[g], held.at[g], sems.at[g])
 
     def send(i):
         return pltpu.make_async_copy(ready.at[i], out_ref.at[order_ref[i]], more.at[i])
 
-    for m, copy in enumerate(copies):
-        copy.wait()
-
-        @pl.loop(0, count // 4)
-        def _(lane, m=m):
-            merged = held[m, lane].astype(F32)
-            for n in range(2):
-                i = 4 * lane + 2 * m + n
-                ready[i] = merged * (coef_ref[order_ref[i]] * scale)
-                send(i).start()
+    @pl.loop(0, count // 2)
+    def _(g):
+        load(g).start()
+
+    expert_order(map_ref, order_ref, count_ref)
+
+    @pl.loop(0, count // 2)
+    def _(g):
+        load(g).wait()
+        merged = held[g].astype(F32)
+        for n in range(2):
+            i = 2 * g + n
+            ready[i] = merged * (coef_ref[order_ref[i]] * scale)
+            send(i).start()
 
     @pl.loop(0, count)
     def _(i):
@@ -675,45 +661,45 @@
 
 def coef_dots(rep_index, merge_map, source_w, arrived):
     count = source_w.shape[0]
-    _, rows, cols = arrived[0].shape
+    _, rows, cols = arrived.shape
     return pl.pallas_call(
         coef_kernel,
-        in_specs=[smem_spec(), smem_spec(), hbm_spec()] + [any_spec()] * len(arrived),
+        in_specs=[smem_spec(), smem_spec(), hbm_spec(), any_spec()],
         out_specs=vmem_spec(),
         out_shape=jax.ShapeDtypeStruct((8, 128), F32),
         scratch_shapes=[
             pltpu.SMEM((count,), I32),
             pltpu.SMEM((count // 2,), I32),
-            pltpu.VMEM((len(arrived),) + arrived[0].shape, BF),
+            pltpu.VMEM(arrived.shape, BF),
             pltpu.VMEM((count, rows, cols), BF),
-            pltpu.SemaphoreType.DMA((len(arrived) + 1,)),
+            pltpu.SemaphoreType.DMA((2,)),
         ],
         compiler_params=params(56),
-        cost_estimate=BRIEF,
+        cost_estimate=cost(5),
         name="coef_dots",
-    )(rep_index, merge_map, source_w, *arrived)
+    )(rep_index, merge_map, source_w, arrived)
 
 
 def finish(merge_map, merge_coef, arrived, after, scale):
     count = merge_map.shape[0]
-    _, rows, cols = arrived[0].shape
+    _, rows, cols = arrived.shape
     return pl.pallas_call(
         functools.partial(finish_kernel, scale),
-        in_specs=[smem_spec(), smem_spec(), any_spec()] + [any_spec()] * len(arrived),
+        in_specs=[smem_spec(), smem_spec(), any_spec(), any_spec()],
         out_specs=hbm_spec(),
         out_shape=jax.ShapeDtypeStruct((count, rows, cols), F32),
         scratch_shapes=[
             pltpu.SMEM((count,), I32),
             pltpu.SMEM((count // 2,), I32),
-            pltpu.VMEM((len(arrived),) + arrived[0].shape, BF),
+            pltpu.VMEM(arrived.shape, BF),
             pltpu.VMEM((count, rows, cols), F32),
-            pltpu.SemaphoreType.DMA((len(arrived),)),
+            pltpu.SemaphoreType.DMA((count // 2,)),
             pltpu.SemaphoreType.DMA((count,)),
         ],
         compiler_params=params(56),
-        cost_estimate=BRIEF,
+        cost_estimate=cost(5),
         name="finish",
-    )(merge_map, merge_coef, after, *arrived)
+    )(merge_map, merge_coef, after, arrived)
 
 
 def add_up(x, bits):
@@ -726,16 +712,12 @@
     return x
 
 
-def swap(x):
-    return lax.ppermute(x, "core", [(0, 1), (1, 0)])
-
-
 def on_pairs(
     tokens, router_w, router_b, hidden, teacher_idx, merge_map, merge_coef, source_w, out_grad
 ):
-    places = lax.axis_size("place")
-    blocks = 2 * places
-    reps = 4
+    blocks = lax.axis_size("ctx")
+    reps = lax.axis_size("row") * lax.axis_size("core")
+    devices = blocks * reps
     tok = tokens.shape[1]
     features = tokens.shape[2]
     top = teacher_idx.shape[2]
@@ -743,74 +725,77 @@
     depth = out_grad.shape[2]
     sources = router_w.shape[1]
     row_share = source_w.shape[1]
-    lanes = 2 * places
+    lanes = blocks
     capacity = 5 * tok * top // (4 * blocks)
-    scale = 1.0 / math.sqrt(tok * blocks * reps)
-    half_i, place_i = lax.axis_index("half"), lax.axis_index("place")
-    row_i, core_i = lax.axis_index("row"), lax.axis_index("core")
-    ctx_i = half_i * places + place_i
-    everyone = ("half", "place", "row", "core")
-    devices = blocks * reps
-
-    def stack(numbers):
-        return jnp.stack([jnp.asarray(n, I32) for n in numbers])
-
-    combos = merge_experts(stack([row_i, core_i]), merge_map, merge_coef, source_w, places)
-
-    def trade(x, axes):
-        return lax.all_to_all(x, axes, split_axis=0, concat_axis=0, tiled=True)
-
-    shares = [trade(c, "place") for c in combos]
-    mine = [lax.all_gather(x, "half", axis=0, tiled=True) for x in shares]
+    scale = 1.0 / math.sqrt(tok * devices)
+    ctx_i, row_i, core_i = lax.axis_index("ctx"), lax.axis_index("row"), lax.axis_index("core")
+    rep_i = 2 * row_i + core_i
+
+    def one(number):
+        return jnp.asarray(number, I32)[None]
+
+    def swap(x, axis):
+        return lax.ppermute(x, axis, [(0, 1), (1, 0)])
+
+    def trade(x):
+        return lax.all_to_all(x, "ctx", split_axis=0, concat_axis=0, tiled=True)
+
+    def trade_rows(rows):
+        return trade(rows.reshape(lanes, capacity, rows.shape[1])).reshape(rows.shape)
+
+    combos = merge_experts(one(rep_i), merge_map, merge_coef, source_w, reps)
+    mine = trade(combos.reshape((lanes, 2) + combos.shape[1:]))
 
     xt = tokens.reshape(tok, features).T
     rwt = router_w.T
     idx_t = teacher_idx.reshape(tok, top).T
     og = out_grad.reshape(tok, depth)
-    send_rows, gates, pos, slot_pos = route(
+    send_hid, send_grd, gates, pos, slot_pos = route(
         xt, rwt, router_b, idx_t, merge_map, hidden.reshape(tok * top, width), og,
-        combos[0], capacity, lanes,
-    )
-
-    def trade_rows(rows):
-        parts = rows.reshape(lanes, capacity, rows.shape[1])
-        return trade(parts, ("place", "row")).reshape(rows.shape)
-
-    (send_rows,) = hold([send_rows], shares[1])
-    rows = trade_rows(send_rows)
-    here, there = stack([core_i]), stack([1 - core_i])
-    firsts = [swap(lane_grads(there, rows, m, None, blocks, reps)) for m in range(2)]
-    summed = [lane_grads(here, rows, m, firsts[m], blocks, reps) for m in range(2)]
-    arrived = [
-        lax.psum_scatter(
-            part.reshape((2, lanes) + part.shape[2:]), "half", scatter_dimension=0, tiled=False
-        )
-        for part in summed
-    ]
-
-    mine = hold(mine, *summed)
-    other = [swap(part) for part in mine]
-    out_rows = run_lane(forward_kernel, here, rows, 1, mine, other, "lane_forward")
+        combos, capacity, lanes,
+    )
+    (send_hid,) = hold([send_hid], mine)
+    hid = trade_rows(send_hid)
+    far = swap(mine, "row")
+    pieces = [mine, swap(mine, "core"), far, swap(far, "core")]
+    (send_grd,) = hold([send_grd], hid)
+    grd = trade_rows(send_grd)
+    out_rows = run_lane(forward_kernel, one(rep_i), hid, hid, pieces, "lane_forward")
+    grd, out_rows = hold([grd, out_rows])
     home_out = trade_rows(out_rows)
-    back_rows = run_lane(backward_kernel, here, rows, 0, mine, other, "lane_backward")
+
+    def summed(row):
+        first = lane_grads(one(2 * row + 1 - core_i), grd, hid, None, blocks, reps)
+        return lane_grads(one(2 * row + core_i), grd, hid, swap(first, "core"), blocks, reps)
+
+    distant, near = summed(1 - row_i), summed(row_i)
+    away = swap(distant, "row")
+    (last_grd,) = hold([grd], distant, near)
+    back_rows = run_lane(backward_kernel, one(rep_i), last_grd, hid, pieces, "lane_backward")
+    total = (near.astype(F32) + away.astype(F32)).astype(BF)
+
     mixed, token_grad, part = combine(home_out, og, gates, pos, idx_t, rwt, xt)
-    hidden_grad = unplace(trade_rows(back_rows), slot_pos)
-
+    home_back = trade_rows(back_rows)
+    hidden_grad = unplace(home_back, slot_pos)
+
+    (part,) = hold([part], back_rows)
     part = add_up(
         part,
         [
-            ("half", 1, half_i),
-            ("place", 2, place_i // 2),
-            ("place", 1, place_i % 2),
+            ("ctx", 4, ctx_i // 4),
+            ("ctx", 2, ctx_i // 2 % 2),
+            ("ctx", 1, ctx_i % 2),
             ("row", 1, row_i),
             ("core", 1, core_i),
         ],
     )
-    arrived = [trade(x, ("place", "row")) for x in hold(arrived, hidden_grad, part)]
-    dots = coef_dots(stack([2 * row_i + core_i]), merge_map, source_w, arrived)
+    (total,) = hold([total], home_back)
+    arrived = trade(total).reshape(2 * lanes, row_share, width // reps)
+    (arrived,) = hold([arrived], hidden_grad, part)
+    dots = coef_dots(one(rep_i), merge_map, source_w, arrived)
     news = jnp.concatenate([part, dots[:1]], axis=1)
     news = lax.all_to_all(
-        jnp.broadcast_to(news[None], (devices,) + news.shape), everyone,
+        jnp.broadcast_to(news[None], (devices,) + news.shape), ("ctx", "row", "core"),
         split_axis=0, concat_axis=0, tiled=True,
     )
     source_w_grad = finish(merge_map, merge_coef, arrived, dots, scale)
@@ -828,10 +813,8 @@
 
 def solution(mesh):
     if mesh.shape["ctx"] == 8 and mesh.shape["rep"] == 4:
-        mesh = jax.sharding.Mesh(
-            mesh.devices.reshape(2, 4, 2, 2), ("half", "place", "row", "core")
-        )
-        ctx, rep, body = ("half", "place"), ("row", "core"), on_pairs
+        mesh = jax.sharding.Mesh(mesh.devices.reshape(8, 2, 2), ("ctx", "row", "core"))
+        ctx, rep, body = "ctx", ("row", "core"), on_pairs
     else:
         ctx, rep, body = "ctx", "rep", on_device
     in_specs = (

time: 434 us -> 391 us (0.901)
  blocking collectives: 21.8 us -> 0 us
  between operations: 14 us -> 0.89 us
  waiting for transfers between devices: 259 us -> 246 us
  starting transfers between devices: 36.2 us -> 43 us
    all_gather x2 -> x0, waiting for transfers between devices: 49.2 us -> none  [on_pairs(): mine = [lax.all_gather(x, 'half', axis=0, tiled=True) for x in shares]]
    ppermute x4 -> x6, waiting for transfers between devices: 7.72 us -> 51.6 us  [swap(): return lax.ppermute(x, axis, [(0, 1), (1, 0)])]
    all_to_all x1 -> x0, blocking collectives: 21.8 us -> none  [trade(): return lax.all_to_all(x, axes, split_axis=0, concat_axis=0, tiled=True)]
    all_to_all x7, waiting for transfers between devices: 149 us -> 129 us  [the longest x6 123 us: trade(): return lax.all_to_all(x, 'ctx', split_axis=0, concat_axis=0, tiled=True)]
    ppermute x5, waiting for transfers between devices: 52.4 us -> 64.5 us  [add_up(): lax.ppermute(give, axis, [(i, i ^ distance) for i in range(size)])]
    unnamed x23 -> x17, local copies, waits for them, and re-layouts: 9.18 us -> 4.85 us
  transfers between devices with their start and end apart: 20 -> 18, of which waited for: 13 -> 10; matrix products, arithmetic and copies ran while one was open for 1% -> 2% of each run, Pallas kernels for 17% -> 17%
where the time goes in v4:
time: 391 us; the launch traced here: 390 us
  waiting for transfers between devices  246 us (63%)
  Pallas kernels  82.6 us (21%)
  starting transfers between devices  43 us (11%)
  local copies, waits for them, and re-layouts  10.4 us (3%)
  other arithmetic  7.29 us (2%)
    all_to_all x6, waiting for transfers between devices, trade(): return lax.all_to_all(x, 'ctx', split_axis=0, concat_axis=0, tiled=True)  123 us
    ppermute x5, waiting for transfers between devices, add_up(): lax.ppermute(give, axis, [(i, i ^ distance) for i in range(size)])  64.5 us
    ppermute x6, waiting for transfers between devices, swap(): return lax.ppermute(x, axis, [(0, 1), (1, 0)])  51.6 us
    all_to_all x6, starting transfers between devices, trade(): return lax.all_to_all(x, 'ctx', split_axis=0, concat_axis=0, tiled=True)  29 us
    pallas_call x2, Pallas kernels, run_lane(): pl.pallas_call(kernel, grid=(1,), in_specs=[smem_spec(), pl.BlockSpec((co...  26.1 us
    pallas_call x4, Pallas kernels, lane_grads(): pl.pallas_call(functools.partial(lane_grad_kernel, other is not None), gr...  22.5 us
  transfers between devices with their start and end apart: 18, of which 10 were waited for; matrix products, arithmetic and copies ran while one was open for 2% of the time, Pallas kernels for 17%

profile of v4, /device:TPU:0, one launch (start us, length us, event | category | flops | bytes accessed | tf_op | source)
XLA Modules:
  0.0 389.9 jit_solution(12196393829580316443)
XLA Ops:
  0.6 5.4 %merge_experts.1._ = bf16[16,192,384]{2,1,0:T(8,128)(2,1)} custom-call(s32[1]{0:T(128)} %bitcast.8.rep_ref._, s32[32]{0:T(128)} %map_ref.5, f32[32]{0:T(128)} %coef_ref.3, bf16[32,192,1536]{2,1,0:T(8,128)(2,1)} %src_ref.3), custom_call_target="tpu_custom_call" | custom-call | flops 5000000000 | bytes 5000000 | tf_op jit(solution)/shard_map/merge_experts/pallas_call | solution.py:272
  6.1 7.4 %all-to-all-start = ((bf16[8,2,192,384]{3,2,1,0:T(8,128)(2,1)}), bf16[8,2,192,384]{3,2,1,0:T(8,128)(2,1)}, u32[]{:S(2)}, u32[]{:S(2)}) async-start(bf16[8,2,192,384]{3,2,1,0:T(8,128)(2,1)} %bitcast.56), calls=%async_computation | async-start | bytes 4718592 | tf_op jit(solution)/shard_map/all_to_all | solution.py:741
  14.8 7.0 %route.1 = (bf16[640,1664]{1,0:T(8,128)(2,1)}, bf16[640,1536]{1,0:T(8,128)(2,1)}, f32[8,128]{1,0:T(8,128)}, s32[8,128]{1,0:T(8,128)}, s32[8,512]{1,0:T(8,128)}) custom-call(bf16[2880,128]{1,0:T(8,128)(2,1)} %bitcast.77, bf16[32,2880]{1,0:T(8,128)(2,1)} %bitcast.81, f32[1,32]{1,0:T(1,128)} %bitcast.85, s32[4,128]{1,0:T(4,128)} %bitcast.83, s32[1,32]{1,0:T(1,128)} %bitcast.76, ...), custom_call_target="tpu_custom_call" | custom-call | flops 5000000000 | bytes 5000000 | tf_op jit(solution)/shard_map/route/pallas_call | solution.py:406
  21.8 45.6 %all-to-all-done.refs_1_.refs_0_ = bf16[8,2,192,384]{3,2,1,0:T(8,128)(2,1)} async-done(((bf16[8,2,192,384]{3,2,1,0:T(8,128)(2,1)}), bf16[8,2,192,384]{3,2,1,0:T(8,128)(2,1)}, u32[]{:S(2)}, u32[]{:S(2)}) %all-to-all-start) | async-done | bytes 2359328 | tf_op jit(solution)/shard_map/all_to_all | solution.py:741
  72.6 51.6 %collective-permute-done.1.refs_2_ = bf16[8,2,192,384]{3,2,1,0:T(8,128)(2,1)} collective-permute-done((bf16[8,2,192,384]{3,2,1,0:T(8,128)(2,1)}, bf16[8,2,192,384]{3,2,1,0:T(8,128)(2,1)}, u32[]{:S(2)}, u32[]{:S(2)}) %collective-permute-start.1) | collective-permute-done | bytes 2359328 | tf_op jit(solution)/shard_map/ppermute | solution.py:738
  125.6 5.7 %all-to-all-start.2 = ((bf16[8,80,1536]{2,1,0:T(8,128)(2,1)}), bf16[8,80,1536]{2,1,0:T(8,128)(2,1)S(1)}, u32[]{:S(2)}, u32[]{:S(2)}) async-start(bf16[8,80,1536]{2,1,0:T(8,128)(2,1)} %bitcast.71), calls=%async_computation.2 | async-start | bytes 3932160 | tf_op jit(solution)/shard_map/all_to_all | solution.py:741
  131.3 13.0 %lane_forward.1.refs_1_ = bf16[640,1536]{1,0:T(8,128)(2,1)} custom-call(s32[1]{0:T(128)} %bitcast.8.rep_ref._, bf16[640,1664]{1,0:T(8,128)(2,1)} %bitcast.58, bf16[640,1664]{1,0:T(8,128)(2,1)} %bitcast.59, bf16[8,2,192,384]{3,2,1,0:T(8,128)(2,1)} %all-to-all-done.refs_1_.refs_0_, bf16[8,2,192,384]{3,2,1,0:T(8,128)(2,1)} %collective-permute-done.refs_1_, ...), custom_call_target="tpu_custom_call" | custom-call | flops 12000000000 | bytes 12000000 | tf_op jit(solution)/shard_map/lane_forward/pallas_call | solution.py:462
  144.4 33.0 %all-to-all-done.2 = bf16[8,80,1536]{2,1,0:T(8,128)(2,1)S(1)} async-done(((bf16[8,80,1536]{2,1,0:T(8,128)(2,1)}), bf16[8,80,1536]{2,1,0:T(8,128)(2,1)S(1)}, u32[]{:S(2)}, u32[]{:S(2)}) %all-to-all-start.2) | async-done | bytes 1966112 | tf_op jit(solution)/shard_map/all_to_all | solution.py:741
  178.7 5.4 %lane_grads_first.3 = bf16[8,2,192,384]{3,2,1,0:T(8,128)(2,1)} custom-call(s32[1]{0:T(128)} %bitcast.19._, bf16[640,1536]{1,0:T(8,128)(2,1)} %get-tuple-element.24.grd_ref.refs_0_, bf16[640,1664]{1,0:T(8,128)(2,1)} %bitcast.60, bf16[640,1664]{1,0:T(8,128)(2,1)} %bitcast.61), custom_call_target="tpu_custom_call" | custom-call | flops 6000000000 | bytes 6000000 | tf_op jit(solution)/shard_map/lane_grads_first/pallas_call | solution.py:504
  184.2 5.4 %lane_grads_first.2 = bf16[8,2,192,384]{3,2,1,0:T(8,128)(2,1)} custom-call(s32[1]{0:T(128)} %bitcast.18._, bf16[640,1536]{1,0:T(8,128)(2,1)} %get-tuple-element.24.grd_ref.refs_0_, bf16[640,1664]{1,0:T(8,128)(2,1)} %bitcast.62, bf16[640,1664]{1,0:T(8,128)(2,1)} %bitcast.63), custom_call_target="tpu_custom_call" | custom-call | flops 6000000000 | bytes 6000000 | tf_op jit(solution)/shard_map/lane_grads_first/pallas_call | solution.py:504
  193.9 5.8 %lane_grads_add.3.refs_2_ = bf16[8,2,192,384]{3,2,1,0:T(8,128)(2,1)} custom-call(s32[1]{0:T(128)} %bitcast.8.rep_ref._, bf16[640,1536]{1,0:T(8,128)(2,1)} %get-tuple-element.24.grd_ref.refs_0_, bf16[640,1664]{1,0:T(8,128)(2,1)} %bitcast.64, bf16[640,1664]{1,0:T(8,128)(2,1)} %bitcast.65, bf16[8,2,192,384]{3,2,1,0:T(8,128)(2,1)} %collective-permute-done.4.refs_0_), custom_call_target="tpu_custom_call" | custom-call | flops 6000000000 | bytes 6000000 | tf_op jit(solution)/shard_map/lane_grads_add/pallas_call | solution.py:504
  199.8 5.8 %lane_grads_add.2.refs_1_ = bf16[8,2,192,384]{3,2,1,0:T(8,128)(2,1)} custom-call(s32[1]{0:T(128)} %bitcast.17._, bf16[640,1536]{1,0:T(8,128)(2,1)} %get-tuple-element.24.grd_ref.refs_0_, bf16[640,1664]{1,0:T(8,128)(2,1)} %bitcast.66, bf16[640,1664]{1,0:T(8,128)(2,1)} %bitcast.67, bf16[8,2,192,384]{3,2,1,0:T(8,128)(2,1)} %collective-permute-done.3.refs_0_), custom_call_target="tpu_custom_call" | custom-call | flops 6000000000 | bytes 6000000 | tf_op jit(solution)/shard_map/lane_grads_add/pallas_call | solution.py:504
  205.6 13.1 %lane_backward.1.refs_1_ = bf16[640,1536]{1,0:T(8,128)(2,1)} custom-call(s32[1]{0:T(128)} %bitcast.8.rep_ref._, bf16[640,1536]{1,0:T(8,128)(2,1)} %hold.10.rows_ref, bf16[640,1664]{1,0:T(8,128)(2,1)} %bitcast.68, bf16[8,2,192,384]{3,2,1,0:T(8,128)(2,1)} %all-to-all-done.refs_1_.refs_0_, bf16[8,2,192,384]{3,2,1,0:T(8,128)(2,1)} %collective-permute-done.refs_1_, ...), custom_call_target="tpu_custom_call" | custom-call | flops 12000000000 | bytes 12000000 | tf_op jit(solution)/shard_map/lane_backward/pallas_call | solution.py:462
  218.7 21.0 %all-to-all-done.3 = bf16[8,80,1536]{2,1,0:T(8,128)(2,1)S(1)} async-done(((bf16[8,80,1536]{2,1,0:T(8,128)(2,1)}), bf16[8,80,1536]{2,1,0:T(8,128)(2,1)S(1)}, u32[]{:S(2)}, u32[]{:S(2)}) %all-to-all-start.3) | async-done | bytes 1966112 | tf_op jit(solution)/shard_map/all_to_all | solution.py:741
  239.7 4.3 %all-to-all-start.4 = ((bf16[8,80,1536]{2,1,0:T(8,128)(2,1)}), bf16[8,80,1536]{2,1,0:T(8,128)(2,1)}, u32[]{:S(2)}, u32[]{:S(2)}) async-start(bf16[8,80,1536]{2,1,0:T(8,128)(2,1)} %bitcast.70), calls=%async_computation.4 | async-start | bytes 3932160 | tf_op jit(solution)/shard_map/all_to_all | solution.py:741
  245.6 5.1 %combine.1 = (bf16[128,1536]{1,0:T(8,128)(2,1)}, bf16[2880,128]{1,0:T(8,128)(2,1)}, f32[32,3072]{1,0:T(8,128)}) custom-call(bf16[128,1536]{1,0:T(8,128)(2,1)} %bitcast.80, f32[8,128]{1,0:T(8,128)} %get-tuple-element.17.gate_ref, s32[8,128]{1,0:T(8,128)} %get-tuple-element.18.pos_ref, s32[4,128]{1,0:T(4,128)} %bitcast.84, bf16[32,2880]{1,0:T(8,128)(2,1)} %bitcast.82, ...), custom_call_target="tpu_custom_call" | custom-call | flops 5000000000 | bytes 5000000 | tf_op jit(solution)/shard_map/combine/pallas_call | solution.py:566
  254.6 42.8 %collective-permute-done.5 = f32[16,3072]{1,0:T(8,128)S(1)} collective-permute-done((f32[16,3072]{1,0:T(8,128)S(1)}, f32[16,3072]{1,0:T(8,128)S(1)}, u32[]{:S(2)}, u32[]{:S(2)}) %collective-permute-start.5) | collective-permute-done | bytes 196640 | tf_op jit(solution)/shard_map/ppermute | solution.py:711
  302.2 4.2 %all-to-all-start.5 = ((bf16[8,2,192,384]{3,2,1,0:T(8,128)(2,1)}), bf16[8,2,192,384]{3,2,1,0:T(8,128)(2,1)S(1)}, u32[]{:S(2)}, u32[]{:S(2)}) async-start(bf16[8,2,192,384]{3,2,1,0:T(8,128)(2,1)} %hold.12), calls=%async_computation.5 | async-start | bytes 4718592 | tf_op jit(solution)/shard_map/all_to_all | solution.py:741
  308.6 18.2 %collective-permute-done.7 = f32[4,3072]{1,0:T(4,128)S(1)} collective-permute-done((f32[4,3072]{1,0:T(4,128)S(1)}, f32[4,3072]{1,0:T(4,128)S(1)}, u32[]{:S(2)}, u32[]{:S(2)}) %collective-permute-start.7) | collective-permute-done | bytes 49184 | tf_op jit(solution)/shard_map/ppermute | solution.py:711
  332.7 4.1 %unplace.1.refs_1_ = bf16[512,1536]{1,0:T(8,128)(2,1)} custom-call(s32[8,512]{1,0:T(8,128)} %get-tuple-element.23.slot_ref, bf16[640,1536]{1,0:T(8,128)(2,1)} %bitcast.21.back_ref.refs_1_), custom_call_target="tpu_custom_call" | custom-call | flops 5000000000 | bytes 5000000 | tf_op jit(solution)/shard_map/unplace/pallas_call | solution.py:590
  336.8 23.3 %all-to-all-done.5 = bf16[8,2,192,384]{3,2,1,0:T(8,128)(2,1)S(1)} async-done(((bf16[8,2,192,384]{3,2,1,0:T(8,128)(2,1)}), bf16[8,2,192,384]{3,2,1,0:T(8,128)(2,1)S(1)}, u32[]{:S(2)}, u32[]{:S(2)}) %all-to-all-start.5) | async-done | bytes 2359328 | tf_op jit(solution)/shard_map/all_to_all | solution.py:741
  361.6 6.7 %coef_dots.1._ = f32[8,128]{1,0:T(8,128)} custom-call(s32[1]{0:T(128)} %bitcast.8.rep_ref._, s32[32]{0:T(128)} %map_ref.5, bf16[32,192,1536]{2,1,0:T(8,128)(2,1)} %src_ref.3, bf16[16,192,384]{2,1,0:T(8,128)(2,1)} %hold.13.got_ref), custom_call_target="tpu_custom_call" | custom-call | flops 5000000000 | bytes 5000000 | tf_op jit(solution)/shard_map/coef_dots/pallas_call | solution.py:665
  375.1 5.6 %finish.1 = f32[32,192,384]{2,1,0:T(8,128)} custom-call(s32[32]{0:T(128)} %map_ref.5, f32[32]{0:T(128)} %coef_ref.3, f32[8,128]{1,0:T(8,128)} %coef_dots.1._, bf16[16,192,384]{2,1,0:T(8,128)(2,1)} %hold.13.got_ref), custom_call_target="tpu_custom_call" | custom-call | flops 5000000000 | bytes 5000000 | tf_op jit(solution)/shard_map/finish/pallas_call | solution.py:686
  380.7 6.5 %all-to-all-done.6 = f32[32,1,3200]{2,1,0:T(1,128)S(1)} async-done(((f32[32,1,3200]{2,1,0:T(1,128)}), f32[32,1,3200]{2,1,0:T(1,128)S(1)}, u32[]{:S(2)}, u32[]{:S(2)}) %all-to-all-start.6) | async-done | bytes 409632 | tf_op jit(solution)/shard_map/all_to_all | solution.py:797
  (70 shorter events, 42.6 us)
Async XLA Ops:
  6.0 7.4 %copy-start.6 = (bf16[1,128,4,1536]{3,2,1,0:T(4,128)(2,1)S(1)}, bf16[1,128,4,1536]{3,2,1,0:T(4,128)(2,1)}, u32[]{:S(2)}) copy-start(bf16[1,128,4,1536]{3,2,1,0:T(4,128)(2,1)} %param.12) | copy-start | bytes 4718596
  6.1 61.4 %all-to-all-start = ((bf16[8,2,192,384]{3,2,1,0:T(8,128)(2,1)}), bf16[8,2,192,384]{3,2,1,0:T(8,128)(2,1)}, u32[]{:S(2)}, u32[]{:S(2)}) async-start(bf16[8,2,192,384]{3,2,1,0:T(8,128)(2,1)} %bitcast.56), calls=%async_computation | async-start | bytes 4718592 | tf_op jit(solution)/shard_map/all_to_all | solution.py:741
  67.4 56.8 %all-to-all-start.1 = ((bf16[8,80,1664]{2,1,0:T(8,128)(2,1)}), bf16[8,80,1664]{2,1,0:T(8,128)(2,1)S(1)}, u32[]{:S(2)}, u32[]{:S(2)}) async-start(bf16[8,80,1664]{2,1,0:T(8,128)(2,1)} %bitcast.69), calls=%async_computation.1 | async-start | bytes 4259840 | tf_op jit(solution)/shard_map/all_to_all | solution.py:741
  71.1 53.2 %collective-permute-start.1 = (bf16[8,2,192,384]{3,2,1,0:T(8,128)(2,1)}, bf16[8,2,192,384]{3,2,1,0:T(8,128)(2,1)}, u32[]{:S(2)}, u32[]{:S(2)}) collective-permute-start(bf16[8,2,192,384]{3,2,1,0:T(8,128)(2,1)} %all-to-all-done.refs_1_.refs_0_), channel_id=1, source_target_pairs={{0,2},{2,0},{1,3},{3,1},{4,6},{6,4},{5,7},{7,5},{8,10},{10,8},{9,1... | collective-permute-start | bytes 7077896 | tf_op jit(solution)/shard_map/ppermute | solution.py:738
  72.6 58.7 %collective-permute-start = (bf16[8,2,192,384]{3,2,1,0:T(8,128)(2,1)}, bf16[8,2,192,384]{3,2,1,0:T(8,128)(2,1)}, u32[]{:S(2)}, u32[]{:S(2)}) collective-permute-start(bf16[8,2,192,384]{3,2,1,0:T(8,128)(2,1)} %all-to-all-done.refs_1_.refs_0_), channel_id=1, source_target_pairs={{0,1},{1,0},{2,3},{3,2},{4,5},{5,4},{6,7},{7,6},{8,9},{9,8},{10,11... | collective-permute-start | bytes 7077896 | tf_op jit(solution)/shard_map/ppermute | solution.py:738
  124.3 7.1 %collective-permute-start.2 = (bf16[8,2,192,384]{3,2,1,0:T(8,128)(2,1)}, bf16[8,2,192,384]{3,2,1,0:T(8,128)(2,1)}, u32[]{:S(2)}, u32[]{:S(2)}) collective-permute-start(bf16[8,2,192,384]{3,2,1,0:T(8,128)(2,1)} %collective-permute-done.1.refs_2_), channel_id=1, source_target_pairs={{0,1},{1,0},{2,3},{3,2},{4,5},{5,4},{6,7},{7,6},{8,9},{9,8},{10,11... | collective-permute-start | bytes 7077896 | tf_op jit(solution)/shard_map/ppermute | solution.py:738
  125.6 51.8 %all-to-all-start.2 = ((bf16[8,80,1536]{2,1,0:T(8,128)(2,1)}), bf16[8,80,1536]{2,1,0:T(8,128)(2,1)S(1)}, u32[]{:S(2)}, u32[]{:S(2)}) async-start(bf16[8,80,1536]{2,1,0:T(8,128)(2,1)} %bitcast.71), calls=%async_computation.2 | async-start | bytes 3932160 | tf_op jit(solution)/shard_map/all_to_all | solution.py:741
  184.2 9.7 %collective-permute-start.4 = (bf16[8,2,192,384]{3,2,1,0:T(8,128)(2,1)}, bf16[8,2,192,384]{3,2,1,0:T(8,128)(2,1)}, u32[]{:S(2)}, u32[]{:S(2)}) collective-permute-start(bf16[8,2,192,384]{3,2,1,0:T(8,128)(2,1)} %lane_grads_first.3), channel_id=1, source_target_pairs={{0,1},{1,0},{2,3},{3,2},{4,5},{5,4},{6,7},{7,6},{8,9},{9,8},{10,11... | collective-permute-start | bytes 7077896 | tf_op jit(solution)/shard_map/ppermute | solution.py:738
  189.6 10.2 %collective-permute-start.3 = (bf16[8,2,192,384]{3,2,1,0:T(8,128)(2,1)}, bf16[8,2,192,384]{3,2,1,0:T(8,128)(2,1)}, u32[]{:S(2)}, u32[]{:S(2)}) collective-permute-start(bf16[8,2,192,384]{3,2,1,0:T(8,128)(2,1)} %lane_grads_first.2), channel_id=1, source_target_pairs={{0,1},{1,0},{2,3},{3,2},{4,5},{5,4},{6,7},{7,6},{8,9},{9,8},{10,11... | collective-permute-start | bytes 7077896 | tf_op jit(solution)/shard_map/ppermute | solution.py:738
  190.1 49.6 %all-to-all-start.3 = ((bf16[8,80,1536]{2,1,0:T(8,128)(2,1)}), bf16[8,80,1536]{2,1,0:T(8,128)(2,1)S(1)}, u32[]{:S(2)}, u32[]{:S(2)}) async-start(bf16[8,80,1536]{2,1,0:T(8,128)(2,1)} %bitcast.14), calls=%async_computation.3 | async-start | bytes 3932160 | tf_op jit(solution)/shard_map/all_to_all | solution.py:741
  239.7 5.9 %copy-start.5 = (bf16[8,80,1536]{2,1,0:T(8,128)(2,1)}, bf16[8,80,1536]{2,1,0:T(8,128)(2,1)S(1)}, u32[]{:S(2)}) copy-start(bf16[8,80,1536]{2,1,0:T(8,128)(2,1)S(1)} %all-to-all-done.3) | copy-start | bytes 5898244
  239.7 62.5 %all-to-all-start.4 = ((bf16[8,80,1536]{2,1,0:T(8,128)(2,1)}), bf16[8,80,1536]{2,1,0:T(8,128)(2,1)}, u32[]{:S(2)}, u32[]{:S(2)}) async-start(bf16[8,80,1536]{2,1,0:T(8,128)(2,1)} %bitcast.70), calls=%async_computation.4 | async-start | bytes 3932160 | tf_op jit(solution)/shard_map/all_to_all | solution.py:741
  244.0 54.4 %collective-permute-start.10 = (bf16[8,2,192,384]{3,2,1,0:T(8,128)(2,1)}, bf16[8,2,192,384]{3,2,1,0:T(8,128)(2,1)}, u32[]{:S(2)}, u32[]{:S(2)}) collective-permute-start(bf16[8,2,192,384]{3,2,1,0:T(8,128)(2,1)} %lane_grads_add.2.refs_1_), channel_id=1, source_target_pairs={{0,2},{2,0},{1,3},{3,1},{4,6},{6,4},{5,7},{7,5},{8,10},{10,8},{9,1... | collective-permute-start | bytes 7077896 | tf_op jit(solution)/shard_map/ppermute | solution.py:738
  250.7 47.8 %copy-start.2 = (bf16[8,2,192,384]{3,2,1,0:T(8,128)(2,1)S(1)}, bf16[8,2,192,384]{3,2,1,0:T(8,128)(2,1)}, u32[]{:S(2)}) copy-start(bf16[8,2,192,384]{3,2,1,0:T(8,128)(2,1)} %lane_grads_add.3.refs_2_) | copy-start | bytes 7077892
  251.8 45.6 %collective-permute-start.5 = (f32[16,3072]{1,0:T(8,128)S(1)}, f32[16,3072]{1,0:T(8,128)S(1)}, u32[]{:S(2)}, u32[]{:S(2)}) collective-permute-start(f32[16,3072]{1,0:T(8,128)S(1)} %dynamic-slice_bitcast_fusion), channel_id=1, source_target_pairs={{0,16},{4,20},{8,24},{12,28},{16,0},{20,4},{24,8},{28,12},{1,17},{... | collective-permute-start | bytes 589832 | tf_op jit(solution)/shard_map/ppermute | solution.py:711
  298.4 8.0 %collective-permute-start.6 = (f32[8,3072]{1,0:T(8,128)S(1)}, f32[8,3072]{1,0:T(8,128)S(1)}, u32[]{:S(2)}, u32[]{:S(2)}) collective-permute-start(f32[8,3072]{1,0:T(8,128)S(1)} %dynamic-slice_bitcast_fusion.1), channel_id=1, source_target_pairs={{0,8},{4,12},{8,0},{12,4},{16,24},{20,28},{24,16},{28,20},{1,9},{5... | collective-permute-start | bytes 294920 | tf_op jit(solution)/shard_map/ppermute | solution.py:711
  302.2 57.9 %all-to-all-start.5 = ((bf16[8,2,192,384]{3,2,1,0:T(8,128)(2,1)}), bf16[8,2,192,384]{3,2,1,0:T(8,128)(2,1)S(1)}, u32[]{:S(2)}, u32[]{:S(2)}) async-start(bf16[8,2,192,384]{3,2,1,0:T(8,128)(2,1)} %hold.12), calls=%async_computation.5 | async-start | bytes 4718592 | tf_op jit(solution)/shard_map/all_to_all | solution.py:741
  306.5 20.3 %collective-permute-start.7 = (f32[4,3072]{1,0:T(4,128)S(1)}, f32[4,3072]{1,0:T(4,128)S(1)}, u32[]{:S(2)}, u32[]{:S(2)}) collective-permute-start(f32[4,3072]{1,0:T(4,128)S(1)} %dynamic-slice_bitcast_fusion.2), channel_id=1, source_target_pairs={{0,4},{4,0},{8,12},{12,8},{16,20},{20,16},{24,28},{28,24},{1,5},{5... | collective-permute-start | bytes 147464 | tf_op jit(solution)/shard_map/ppermute | solution.py:711
  326.9 3.9 collective-permute-start.8
  330.8 1.2 collective-permute-start.9
  360.1 1.4 copy-start
  361.6 7.4 %copy-start.7 = (f32[1,3072]{1,0:T(1,128)S(1)}, f32[1,3072]{1,0:T(1,128)}, u32[]{:S(2)}) copy-start(f32[1,3072]{1,0:T(1,128)} %dynamic-slice_add_fusion.refs_2_) | copy-start | bytes 36868
  361.6 12.2 %copy-start.4 = (bf16[512,1536]{1,0:T(8,128)(2,1)S(1)}, bf16[512,1536]{1,0:T(8,128)(2,1)}, u32[]{:S(2)}) copy-start(bf16[512,1536]{1,0:T(8,128)(2,1)} %unplace.1.refs_1_) | copy-start | bytes 4718596
  370.0 17.2 %all-to-all-start.6 = ((f32[32,1,3200]{2,1,0:T(1,128)}), f32[32,1,3200]{2,1,0:T(1,128)S(1)}, u32[]{:S(2)}, u32[]{:S(2)}) async-start(f32[32,1,3200]{2,1,0:T(1,128)} %broadcast_in_dim.37), calls=%async_computation.6 | async-start | bytes 819200 | tf_op jit(solution)/shard_map/all_to_all | solution.py:797
  (2 other events, 2.6 us)

commit v5 on v4

--- a/solution.py
+++ b/solution.py
@@ -320,11 +320,44 @@
     return lax.broadcasted_iota(I32, (sources, tok), 0) == idx_ref[k : k + 1, :]
 
 
+def place_rows(refs, at, rows):
+    each = refs[0].shape[0]
+    rows = rows.astype(BF)
+    for d, ref in enumerate(refs):
+        ref[:, at : at + rows.shape[1]] = rows[d * each : (d + 1) * each]
+
+
+def assemble_kernel(me_ref, *refs):
+    parts, (out_ref, sems) = refs[:-2], refs[-2:]
+    each = parts[0].shape[0]
+    copies = []
+    for d, part in enumerate(parts):
+        at = pl.ds(pl.multiple_of(jnp.bitwise_xor(me_ref[0], d) * each, each), each)
+        copies.append(pltpu.make_async_copy(part, out_ref.at[at, :], sems.at[d]))
+        copies[-1].start()
+    for copy in copies:
+        copy.wait()
+
+
+def assemble(me, parts):
+    each, width = parts[0].shape
+    return pl.pallas_call(
+        assemble_kernel,
+        in_specs=[smem_spec()] + [any_spec()] * len(parts),
+        out_specs=vmem_spec(),
+        out_shape=jax.ShapeDtypeStruct((each * len(parts), width), BF),
+        scratch_shapes=[pltpu.SemaphoreType.DMA((len(parts),))],
+        compiler_params=params(56),
+        cost_estimate=cost(2),
+        name="assemble",
+    )(me, *parts)
+
+
 def route_kernel(
     capacity, lanes,
-    xt_ref, rwt_ref, rb_ref, idx_ref, map_ref, hid_ref, og_ref, _,
-    sh_ref, sg_ref, gate_ref, pos_ref, slot_ref,
+    me_ref, xt_ref, rwt_ref, rb_ref, idx_ref, map_ref, hid_ref, og_ref, _, *refs
 ):
+    sends, (sg_ref, gate_ref, pos_ref, slot_ref) = refs[:-4], refs[-4:]
     top, tok = idx_ref.shape
     sources = rwt_ref.shape[0]
     slots, width = hid_ref.shape
@@ -351,9 +384,10 @@
         lax.broadcasted_iota(I32, (tok, tok), 0) < lax.broadcasted_iota(I32, (tok, tok), 1)
     ).astype(BF)
     before = jnp.dot(all_hot.astype(BF), earlier, preferred_element_type=F32)
-    position = []
+    position, ranks = [], []
     for k in range(top):
         rank = jnp.sum(before * onehot[k], axis=0, keepdims=True).astype(I32)
+        ranks.append(rank)
         before = before + onehot[k]
         position.append(jnp.where(rank < capacity, lane[k] * capacity + rank, -1))
     gate_ref[...] = jnp.zeros_like(gate_ref)
@@ -369,8 +403,8 @@
         ).astype(BF)
         kept = position[k] >= 0
         parts = [
-            jnp.where(kept, jnp.right_shift(position[k], 5), 0),
-            jnp.where(kept, jnp.bitwise_and(position[k], 31), 0),
+            jnp.where(kept, lane[k], 0),
+            jnp.where(kept, ranks[k], 0),
             jnp.where(kept, 1, 0),
             member[k],
         ]
@@ -379,15 +413,17 @@
         ).astype(BF)
         spot = spot + jnp.dot(stacked, spread, preferred_element_type=F32)
     spot = spot.astype(I32)
-    slot_pos = jnp.where(spot[2:3] > 0, spot[0:1] * 32 + spot[1:2], -1)
+    slot_pos = jnp.where(spot[2:3] > 0, spot[0:1] * capacity + spot[1:2], -1)
     slot_ref[...] = jnp.broadcast_to(slot_pos, slot_ref.shape)
-    take = lax.broadcasted_iota(I32, (places, slots), 0) == slot_pos
+    partner = jnp.bitwise_xor(spot[0:1], me_ref[0])
+    part_pos = jnp.where(spot[2:3] > 0, partner * capacity + spot[1:2], -1)
+    take = lax.broadcasted_iota(I32, (places, slots), 0) == part_pos
     placed = jnp.sum(jnp.where(take, spot[3:4].astype(F32), 0.0), axis=1, keepdims=True)
-    sh_ref[:, width:] = jnp.broadcast_to(placed, (places, 128)).astype(BF)
+    place_rows(sends, width, jnp.broadcast_to(placed, (places, 128)))
     take = take.astype(BF)
     for n in range(0, width, TILE):
         rows = jnp.dot(take, hid_ref[:, n : n + TILE], preferred_element_type=F32)
-        sh_ref[:, n : n + TILE] = rows.astype(BF)
+        place_rows(sends, n, rows)
     takes = [
         (lax.broadcasted_iota(I32, (places, tok), 0) == position[k]).astype(BF) for k in range(top)
     ]
@@ -400,15 +436,15 @@
         sg_ref[:, n : n + TILE] = rows.astype(BF)
 
 
-def route(xt, rwt, router_b, idx_t, merge_map, hid, og, after, capacity, lanes):
+def route(me, xt, rwt, router_b, idx_t, merge_map, hid, og, after, capacity, lanes):
     slots, width = hid.shape
     tok = idx_t.shape[1]
     return pl.pallas_call(
         functools.partial(route_kernel, capacity, lanes),
-        in_specs=[vmem_spec()] * 7 + [any_spec()],
-        out_specs=[vmem_spec()] * 5,
-        out_shape=[
-            jax.ShapeDtypeStruct((lanes * capacity, width + 128), BF),
+        in_specs=[smem_spec()] + [vmem_spec()] * 7 + [any_spec()],
+        out_specs=[vmem_spec()] * (lanes + 4),
+        out_shape=[jax.ShapeDtypeStruct((capacity, width + 128), BF)] * lanes
+        + [
             jax.ShapeDtypeStruct((lanes * capacity, og.shape[1]), BF),
             jax.ShapeDtypeStruct((8, tok), F32),
             jax.ShapeDtypeStruct((8, tok), I32),
@@ -417,7 +453,7 @@
         compiler_params=params(56),
         cost_estimate=cost(5),
         name="route",
-    )(xt, rwt, router_b[None, :], idx_t, merge_map[None, :], hid, og, after)
+    )(me, xt, rwt, router_b[None, :], idx_t, merge_map[None, :], hid, og, after)
 
 
 def load_weights(rep_ref, pieces, w_ref, sems):
@@ -435,19 +471,23 @@
         copy.wait()
 
 
-def forward_kernel(rep_ref, rows_ref, flag_ref, *refs):
-    out_ref, w_ref, sems = refs[-3:]
-    load_weights(rep_ref, refs[:-3], w_ref, sems)
+def forward_kernel(rep_ref, me_ref, rows_ref, flag_ref, *refs):
+    pieces, outs, (keep, w_ref, sems) = refs[:4], refs[4:-3], refs[-3:]
+    load_weights(rep_ref, pieces, w_ref, sems)
     member = flag_ref[:, :1].astype(F32)
     for n in range(0, w_ref.shape[1], TILE):
         at = slice(n, n + TILE)
         both = [dot(rows_ref[...], w_ref[m, at, :], ((1,), (1,))) for m in range(2)]
-        out_ref[:, at] = jnp.where(member == 0.0, both[0], both[1]).astype(BF)
-
-
-def backward_kernel(rep_ref, rows_ref, flag_ref, *refs):
-    out_ref, w_ref, sems = refs[-3:]
-    load_weights(rep_ref, refs[:-3], w_ref, sems)
+        keep[:, at] = jnp.where(member == 0.0, both[0], both[1]).astype(BF)
+    each = outs[0].shape[0]
+    for d, out_ref in enumerate(outs):
+        at = pl.ds(pl.multiple_of(jnp.bitwise_xor(me_ref[0], d) * each, each), each)
+        out_ref[...] = keep[at, :]
+
+
+def backward_kernel(rep_ref, _, rows_ref, flag_ref, *refs):
+    pieces, (out_ref, w_ref, sems) = refs[:4], refs[4:]
+    load_weights(rep_ref, pieces, w_ref, sems)
     member = flag_ref[:, :1].astype(F32)
     for n in range(0, w_ref.shape[2], TILE):
         at = slice(n, n + TILE)
@@ -455,29 +495,35 @@
         out_ref[:, at] = jnp.where(member == 0.0, both[0], both[1]).astype(BF)
 
 
-def run_lane(kernel, rep_index, rows, hid, pieces, name):
+def run_lane(kernel, rep_index, me, rows, hid, pieces, lanes, name):
     blocks, members, share, cols = pieces[0].shape
     depth, width = share * blocks, cols * len(pieces)
     count = rows.shape[0]
+    whole = pl.BlockSpec((count, width), lambda i: (0, 0))
+    if lanes is None:
+        out_specs, out_shape, keep = whole, jax.ShapeDtypeStruct((count, width), BF), []
+    else:
+        part = (count // lanes, width)
+        out_specs = [pl.BlockSpec(part, lambda i: (0, 0))] * lanes
+        out_shape = [jax.ShapeDtypeStruct(part, BF)] * lanes
+        keep = [pltpu.VMEM((count, width), BF)]
     return pl.pallas_call(
         kernel,
         grid=(1,),
-        in_specs=[
-            smem_spec(),
-            pl.BlockSpec((count, width), lambda i: (0, 0)),
-            pl.BlockSpec((count, 128), lambda i: (0, width // 128)),
-        ]
+        in_specs=[smem_spec(), smem_spec(), whole]
+        + [pl.BlockSpec((count, 128), lambda i: (0, width // 128))]
         + [any_spec()] * len(pieces),
-        out_specs=pl.BlockSpec((count, width), lambda i: (0, 0)),
-        out_shape=jax.ShapeDtypeStruct((count, width), BF),
-        scratch_shapes=[
+        out_specs=out_specs,
+        out_shape=out_shape,
+        scratch_shapes=keep
+        + [
             pltpu.VMEM((members, depth, width), BF),
             pltpu.SemaphoreType.DMA((blocks * len(pieces),)),
         ],
         compiler_params=params(56),
         cost_estimate=cost(12),
         name=name,
-    )(rep_index, rows, hid, *pieces)
+    )(rep_index, me, rows, hid, *pieces)
 
 
 def lane_grad_kernel(has_other, _, grd_ref, hid_ref, flag_ref, *refs):
@@ -598,7 +644,9 @@
     )(slot_pos, home_back)
 
 
-def coef_kernel(rep_ref, map_ref, src_ref, got_ref, out_ref, order_ref, count_ref, held, weights, sems):
+def coef_kernel(
+    rep_ref, map_ref, row_ref, src_ref, got_ref, out_ref, order_ref, count_ref, held, weights, sems
+):
     count, rows, cols = weights.shape
     at = pl.ds(pl.multiple_of(rep_ref[0] * cols, cols), cols)
     copies = [
@@ -625,7 +673,11 @@
             total = total + jnp.where(lane == expert, small, 0.0)
         return total
 
-    out_ref[...] = lax.fori_loop(0, count // 2, one, jnp.zeros((8, 128), F32))
+    total = lax.fori_loop(0, count // 2, one, jnp.zeros((8, 128), F32))[:1]
+    end = row_ref.shape[1]
+    for n in range(out_ref.shape[0]):
+        out_ref[n, :, :end] = row_ref[...]
+        out_ref[n, :, end:] = total
 
 
 def finish_kernel(
@@ -659,14 +711,14 @@
         send(i).wait()
 
 
-def coef_dots(rep_index, merge_map, source_w, arrived):
+def coef_dots(rep_index, merge_map, row, source_w, arrived, devices):
     count = source_w.shape[0]
     _, rows, cols = arrived.shape
     return pl.pallas_call(
         coef_kernel,
-        in_specs=[smem_spec(), smem_spec(), hbm_spec(), any_spec()],
+        in_specs=[smem_spec(), smem_spec(), vmem_spec(), hbm_spec(), any_spec()],
         out_specs=vmem_spec(),
-        out_shape=jax.ShapeDtypeStruct((8, 128), F32),
+        out_shape=jax.ShapeDtypeStruct((devices, 1, row.shape[1] + 128), F32),
         scratch_shapes=[
             pltpu.SMEM((count,), I32),
             pltpu.SMEM((count // 2,), I32),
@@ -677,7 +729,7 @@
         compiler_params=params(56),
         cost_estimate=cost(5),
         name="coef_dots",
-    )(rep_index, merge_map, source_w, arrived)
+    )(rep_index, merge_map, row, source_w, arrived)
 
 
 def finish(merge_map, merge_coef, arrived, after, scale):
@@ -750,19 +802,27 @@
     rwt = router_w.T
     idx_t = teacher_idx.reshape(tok, top).T
     og = out_grad.reshape(tok, depth)
-    send_hid, send_grd, gates, pos, slot_pos = route(
-        xt, rwt, router_b, idx_t, merge_map, hidden.reshape(tok * top, width), og,
+    *hid_parts, send_grd, gates, pos, slot_pos = route(
+        one(ctx_i), xt, rwt, router_b, idx_t, merge_map, hidden.reshape(tok * top, width), og,
         combos, capacity, lanes,
     )
-    (send_hid,) = hold([send_hid], mine)
-    hid = trade_rows(send_hid)
+
+    def trade_parts(parts):
+        return [parts[0]] + [
+            lax.ppermute(parts[d], "ctx", [(i, i ^ d) for i in range(lanes)])
+            for d in range(1, lanes)
+        ]
+
+    hid = assemble(one(ctx_i), trade_parts(hid_parts))
     far = swap(mine, "row")
     pieces = [mine, swap(mine, "core"), far, swap(far, "core")]
-    (send_grd,) = hold([send_grd], hid)
+    (send_grd,) = hold([send_grd], mine)
     grd = trade_rows(send_grd)
-    out_rows = run_lane(forward_kernel, one(rep_i), hid, hid, pieces, "lane_forward")
-    grd, out_rows = hold([grd, out_rows])
-    home_out = trade_rows(out_rows)
+    out_parts = run_lane(
+        forward_kernel, one(rep_i), one(ctx_i), hid, hid, pieces, lanes, "lane_forward"
+    )
+    home_parts = trade_parts(out_parts)
+    (grd,) = hold([grd], out_parts[0])
 
     def summed(row):
         first = lane_grads(one(2 * row + 1 - core_i), grd, hid, None, blocks, reps)
@@ -771,14 +831,17 @@
     distant, near = summed(1 - row_i), summed(row_i)
     away = swap(distant, "row")
     (last_grd,) = hold([grd], distant, near)
-    back_rows = run_lane(backward_kernel, one(rep_i), last_grd, hid, pieces, "lane_backward")
+    back_rows = run_lane(
+        backward_kernel, one(rep_i), one(ctx_i), last_grd, hid, pieces, None, "lane_backward"
+    )
+    home_out = assemble(one(ctx_i), hold(home_parts, back_rows))
     total = (near.astype(F32) + away.astype(F32)).astype(BF)
 
     mixed, token_grad, part = combine(home_out, og, gates, pos, idx_t, rwt, xt)
     home_back = trade_rows(back_rows)
     hidden_grad = unplace(home_back, slot_pos)
 
-    (part,) = hold([part], back_rows)
+    (part,) = hold([part], away)
     part = add_up(
         part,
         [
@@ -792,11 +855,9 @@
     (total,) = hold([total], home_back)
     arrived = trade(total).reshape(2 * lanes, row_share, width // reps)
     (arrived,) = hold([arrived], hidden_grad, part)
-    dots = coef_dots(one(rep_i), merge_map, source_w, arrived)
-    news = jnp.concatenate([part, dots[:1]], axis=1)
+    dots = coef_dots(one(rep_i), merge_map, part, source_w, arrived, devices)
     news = lax.all_to_all(
-        jnp.broadcast_to(news[None], (devices,) + news.shape), ("ctx", "row", "core"),
-        split_axis=0, concat_axis=0, tiled=True,
+        dots, ("ctx", "row", "core"), split_axis=0, concat_axis=0, tiled=True
     )
     source_w_grad = finish(merge_map, merge_coef, arrived, dots, scale)
     end = part.shape[1]

time: 391 us -> 483 us (1.24)
  blocking collectives: 0 us -> 61.4 us
  starting transfers between devices: 43 us -> 74.5 us
  waiting for transfers between devices: 246 us -> 238 us
  Pallas kernels: 82.6 us -> 88.6 us
    ppermute x0 -> x14, waiting for transfers between devices: none -> 127 us  [trade_parts(): lax.ppermute(parts[d], 'ctx', [(i, i ^ d) for i in range(lanes)])]
    all_to_all x6 -> x3, waiting for transfers between devices: 123 us -> 23.4 us  [trade(): return lax.all_to_all(x, 'ctx', split_axis=0, concat_axis=0, tiled=True)]
    all_to_all x0 -> x1, blocking collectives: none -> 61.4 us  [trade(): return lax.all_to_all(x, 'ctx', split_axis=0, concat_axis=0, tiled=True)]
    ppermute x0 -> x14, starting transfers between devices: none -> 33.5 us  [trade_parts(): lax.ppermute(parts[d], 'ctx', [(i, i ^ d) for i in range(lanes)])]
    ppermute x5, waiting for transfers between devices: 64.5 us -> 32 us  [add_up(): lax.ppermute(give, axis, [(i, i ^ distance) for i in range(size)])]
    all_to_all x6 -> x3, starting transfers between devices: 29 us -> 21.8 us  [trade(): return lax.all_to_all(x, 'ctx', split_axis=0, concat_axis=0, tiled=True)]
    ppermute x5, starting transfers between devices: 6.61 us -> 12.9 us  [add_up(): lax.ppermute(give, axis, [(i, i ^ distance) for i in range(size)])]
    pallas_call x3 -> x5, Pallas kernels: 32.9 us -> 39 us  [the longest x2 26.1 us: run_lane(): pl.pallas_call(kernel, grid=(1,), in_specs=[smem_spec(), smem_spec(), who...]
  transfers between devices with their start and end apart: 18 -> 29, of which waited for: 10 -> 17; matrix products, arithmetic and copies ran while one was open for 2% -> 2% of each run, Pallas kernels for 17% -> 15%
where the time goes in v5:
time: 483 us; the launch traced here: 482 us
  waiting for transfers between devices  238 us (49%)
  Pallas kernels  88.6 us (18%)
  starting transfers between devices  74.5 us (15%)
  blocking collectives  61.4 us (13%)
  local copies, waits for them, and re-layouts  10.8 us (2%)
  other arithmetic  7.97 us (2%)
    ppermute x14, waiting for transfers between devices, trade_parts(): lax.ppermute(parts[d], 'ctx', [(i, i ^ d) for i in range(lanes)])  127 us
    all_to_all x1, blocking collectives, trade(): return lax.all_to_all(x, 'ctx', split_axis=0, concat_axis=0, tiled=True)  61.4 us
    ppermute x6, waiting for transfers between devices, swap(): return lax.ppermute(x, axis, [(0, 1), (1, 0)])  49.3 us
    ppermute x14, starting transfers between devices, trade_parts(): lax.ppermute(parts[d], 'ctx', [(i, i ^ d) for i in range(lanes)])  33.5 us
    ppermute x5, waiting for transfers between devices, add_up(): lax.ppermute(give, axis, [(i, i ^ distance) for i in range(size)])  32 us
    pallas_call x2, Pallas kernels, run_lane(): pl.pallas_call(kernel, grid=(1,), in_specs=[smem_spec(), smem_spec(), who...  26.1 us
    all_to_all x3, waiting for transfers between devices, trade(): return lax.all_to_all(x, 'ctx', split_axis=0, concat_axis=0, tiled=True)  23.4 us
    pallas_call x4, Pallas kernels, lane_grads(): pl.pallas_call(functools.partial(lane_grad_kernel, other is not None), gr...  22.5 us
  transfers between devices with their start and end apart: 29, of which 17 were waited for; matrix products, arithmetic and copies ran while one was open for 2% of the time, Pallas kernels for 15%

profile of v5, /device:TPU:0, one launch (start us, length us, event | category | flops | bytes accessed | tf_op | source)
XLA Modules:
  0.0 482.2 jit_solution(8195192652609584363)
XLA Ops:
  6.1 61.4 %all_to_all.25.refs_0_.refs_1_ = bf16[8,2,192,384]{3,2,1,0:T(8,128)(2,1)} all-to-all(bf16[8,2,192,384]{3,2,1,0:T(8,128)(2,1)} %bitcast.53), channel_id=1, replica_groups=mesh['ctx'=8,'row'=2,'core'=2] {'ctx'}, dimensions={0} | all-to-all | bytes 4718592 | tf_op jit(solution)/shard_map/all_to_all | solution.py:793
  70.3 49.3 %collective-permute-done.8.refs_2_ = bf16[8,2,192,384]{3,2,1,0:T(8,128)(2,1)} collective-permute-done((bf16[8,2,192,384]{3,2,1,0:T(8,128)(2,1)}, bf16[8,2,192,384]{3,2,1,0:T(8,128)(2,1)}, u32[]{:S(2)}, u32[]{:S(2)}) %collective-permute-start.8) | collective-permute-done | bytes 2359328 | tf_op jit(solution)/shard_map/ppermute | solution.py:790
  119.6 6.9 %route.1 = (bf16[80,1664]{1,0:T(8,128)(2,1)}, bf16[80,1664]{1,0:T(8,128)(2,1)}, bf16[80,1664]{1,0:T(8,128)(2,1)}, bf16[80,1664]{1,0:T(8,128)(2,1)}, bf16[80,1664...) custom-call(s32[1]{0:T(128)} %bitcast.1.me_ref._, ...), custom_call_target="tpu_custom_call" | custom-call | flops 5000000000 | bytes 5000000 | tf_op jit(solution)/shard_map/route/pallas_call | solution.py:442
  134.5 20.0 %collective-permute-done.refs_1_ = bf16[80,1664]{1,0:T(8,128)(2,1)S(1)} collective-permute-done((bf16[80,1664]{1,0:T(8,128)(2,1)}, bf16[80,1664]{1,0:T(8,128)(2,1)S(1)}, u32[]{:S(2)}, u32[]{:S(2)}) %collective-permute-start) | collective-permute-done | bytes 266272 | tf_op jit(solution)/shard_map/ppermute | solution.py:812
  156.1 14.8 %collective-permute-done.1.refs_2_ = bf16[80,1664]{1,0:T(8,128)(2,1)S(1)} collective-permute-done((bf16[80,1664]{1,0:T(8,128)(2,1)}, bf16[80,1664]{1,0:T(8,128)(2,1)S(1)}, u32[]{:S(2)}, u32[]{:S(2)}) %collective-permute-start.1) | collective-permute-done | bytes 266272 | tf_op jit(solution)/shard_map/ppermute | solution.py:812
  182.1 18.6 %collective-permute-done.3.refs_4_ = bf16[80,1664]{1,0:T(8,128)(2,1)S(1)} collective-permute-done((bf16[80,1664]{1,0:T(8,128)(2,1)}, bf16[80,1664]{1,0:T(8,128)(2,1)S(1)}, u32[]{:S(2)}, u32[]{:S(2)}) %collective-permute-start.3) | collective-permute-done | bytes 266272 | tf_op jit(solution)/shard_map/ppermute | solution.py:812
  203.2 9.9 %collective-permute-done.4.refs_5_ = bf16[80,1664]{1,0:T(8,128)(2,1)} collective-permute-done((bf16[80,1664]{1,0:T(8,128)(2,1)S(1)}, bf16[80,1664]{1,0:T(8,128)(2,1)}, u32[]{:S(2)}, u32[]{:S(2)}) %collective-permute-start.4) | collective-permute-done | bytes 266272 | tf_op jit(solution)/shard_map/ppermute | solution.py:812
  216.0 13.1 %lane_forward.1 = (bf16[80,1536]{1,0:T(8,128)(2,1)}, bf16[80,1536]{1,0:T(8,128)(2,1)}, bf16[80,1536]{1,0:T(8,128)(2,1)}, bf16[80,1536]{1,0:T(8,128)(2,1)}, bf16[...) custom-call(s32[1]{0:T(128)} %bitcast.9.rep_ref._, ...), custom_call_target="tpu_custom_call" | custom-call | flops 12000000000 | bytes 12000000 | tf_op jit(solution)/shard_map/lane_forward/pallas_call | solution.py:510
  235.8 5.4 %lane_grads_first.3 = bf16[8,2,192,384]{3,2,1,0:T(8,128)(2,1)} custom-call(s32[1]{0:T(128)} %bitcast.15._, bf16[640,1536]{1,0:T(8,128)(2,1)} %hold.8.grd_ref.refs_0_, bf16[640,1664]{1,0:T(8,128)(2,1)} %assemble.2.rows_ref.flag_ref.hid_ref, bf16[640,1664]{1,0:T(8,128)(2,1)} %assemble.2.rows_ref.flag_ref.hid_ref), custom_call_target="tpu_custom_call" | custom-call | flops 6000000000 | bytes 6000000 | tf_op jit(solution)/shard_map/lane_grads_first/pallas_call | solution.py:550
  243.2 5.8 %lane_grads_add.2.refs_1_ = bf16[8,2,192,384]{3,2,1,0:T(8,128)(2,1)} custom-call(s32[1]{0:T(128)} %bitcast.13._, bf16[640,1536]{1,0:T(8,128)(2,1)} %hold.8.grd_ref.refs_0_, bf16[640,1664]{1,0:T(8,128)(2,1)} %assemble.2.rows_ref.flag_ref.hid_ref, bf16[640,1664]{1,0:T(8,128)(2,1)} %assemble.2.rows_ref.flag_ref.hid_ref, bf16[8,2,192,384]{3,2,1,0:T(8,128)(2,1)} %copy-done.9), custom_call_target="tpu_custom_call" | custom-call | flops 6000000000 | bytes 6000000 | tf_op jit(solution)/shard_map/lane_grads_add/pallas_call | solution.py:550
  250.5 5.8 %lane_grads_add.3.refs_2_ = bf16[8,2,192,384]{3,2,1,0:T(8,128)(2,1)} custom-call(s32[1]{0:T(128)} %bitcast.9.rep_ref._, bf16[640,1536]{1,0:T(8,128)(2,1)} %hold.8.grd_ref.refs_0_, bf16[640,1664]{1,0:T(8,128)(2,1)} %assemble.2.rows_ref.flag_ref.hid_ref, bf16[640,1664]{1,0:T(8,128)(2,1)} %assemble.2.rows_ref.flag_ref.hid_ref, ...), custom_call_target="tpu_custom_call" | custom-call | flops 6000000000 | bytes 6000000 | tf_op jit(solution)/shard_map/lane_grads_add/pallas_call | solution.py:550
  256.4 13.1 %lane_backward.1.refs_8_ = bf16[640,1536]{1,0:T(8,128)(2,1)} custom-call(s32[1]{0:T(128)} %bitcast.9.rep_ref._, s32[1]{0:T(128)} %bitcast.1.me_ref._, bf16[640,1536]{1,0:T(8,128)(2,1)} %hold.9.rows_ref, bf16[640,1664]{1,0:T(8,128)(2,1)} %assemble.2.rows_ref.flag_ref.hid_ref, bf16[8,2,192,384]{3,2,1,0:T(8,128)(2,1)} %all_to_all.25.refs_0_.refs_1_, ...), custom_call_target="tpu_custom_call" | custom-call | flops 12000000000 | bytes 12000000 | tf_op jit(solution)/shard_map/lane_backward/pallas_call | solution.py:510
  269.4 13.3 %all-to-all-start.2 = ((bf16[8,80,1536]{2,1,0:T(8,128)(2,1)}), bf16[8,80,1536]{2,1,0:T(8,128)(2,1)}, u32[]{:S(2)}, u32[]{:S(2)}) async-start(bf16[8,80,1536]{2,1,0:T(8,128)(2,1)} %bitcast.54), calls=%async_computation.2 | async-start | bytes 3932160 | tf_op jit(solution)/shard_map/all_to_all | solution.py:793
  289.2 16.2 %collective-permute-done.10.refs_1_ = bf16[80,1536]{1,0:T(8,128)(2,1)S(1)} collective-permute-done((bf16[80,1536]{1,0:T(8,128)(2,1)}, bf16[80,1536]{1,0:T(8,128)(2,1)S(1)}, u32[]{:S(2)}, u32[]{:S(2)}) %collective-permute-start.10) | collective-permute-done | bytes 245792 | tf_op jit(solution)/shard_map/ppermute | solution.py:812
  308.9 13.2 %collective-permute-done.11.refs_2_ = bf16[80,1536]{1,0:T(8,128)(2,1)S(1)} collective-permute-done((bf16[80,1536]{1,0:T(8,128)(2,1)}, bf16[80,1536]{1,0:T(8,128)(2,1)S(1)}, u32[]{:S(2)}, u32[]{:S(2)}) %collective-permute-start.11) | collective-permute-done | bytes 245792 | tf_op jit(solution)/shard_map/ppermute | solution.py:812
  331.2 24.8 %collective-permute-done.13.refs_4_ = bf16[80,1536]{1,0:T(8,128)(2,1)S(1)} collective-permute-done((bf16[80,1536]{1,0:T(8,128)(2,1)}, bf16[80,1536]{1,0:T(8,128)(2,1)S(1)}, u32[]{:S(2)}, u32[]{:S(2)}) %collective-permute-start.13) | collective-permute-done | bytes 245792 | tf_op jit(solution)/shard_map/ppermute | solution.py:812
  356.0 5.8 %collective-permute-done.14.refs_5_ = bf16[80,1536]{1,0:T(8,128)(2,1)} collective-permute-done((bf16[80,1536]{1,0:T(8,128)(2,1)}, bf16[80,1536]{1,0:T(8,128)(2,1)}, u32[]{:S(2)}, u32[]{:S(2)}) %collective-permute-start.14) | collective-permute-done | bytes 245792 | tf_op jit(solution)/shard_map/ppermute | solution.py:812
  372.3 10.1 %collective-permute-start.20 = (f32[16,3072]{1,0:T(8,128)S(1)}, f32[16,3072]{1,0:T(8,128)S(1)}, u32[]{:S(2)}, u32[]{:S(2)}) collective-permute-start(f32[16,3072]{1,0:T(8,128)S(1)} %dynamic-slice_bitcast_fusion), channel_id=1, source_target_pairs={{0,16},{4,20},{8,24},{12,28},{16,0},{20,4},{24,8},{28,12},{1,17},{... | collective-permute-start | bytes 589832 | tf_op jit(solution)/shard_map/ppermute | solution.py:763
  382.4 9.3 %collective-permute-done.20 = f32[16,3072]{1,0:T(8,128)S(1)} collective-permute-done((f32[16,3072]{1,0:T(8,128)S(1)}, f32[16,3072]{1,0:T(8,128)S(1)}, u32[]{:S(2)}, u32[]{:S(2)}) %collective-permute-start.20) | collective-permute-done | bytes 196640 | tf_op jit(solution)/shard_map/ppermute | solution.py:763
  403.3 18.2 %collective-permute-done.22 = f32[4,3072]{1,0:T(4,128)S(1)} collective-permute-done((f32[4,3072]{1,0:T(4,128)S(1)}, f32[4,3072]{1,0:T(4,128)S(1)}, u32[]{:S(2)}, u32[]{:S(2)}) %collective-permute-start.22) | collective-permute-done | bytes 49184 | tf_op jit(solution)/shard_map/ppermute | solution.py:763
  431.5 23.4 %all-to-all-done.3 = bf16[8,2,192,384]{3,2,1,0:T(8,128)(2,1)S(1)} async-done(((bf16[8,2,192,384]{3,2,1,0:T(8,128)(2,1)}), bf16[8,2,192,384]{3,2,1,0:T(8,128)(2,1)S(1)}, u32[]{:S(2)}, u32[]{:S(2)}) %all-to-all-start.3) | async-done | bytes 2359328 | tf_op jit(solution)/shard_map/all_to_all | solution.py:793
  456.4 6.9 %coef_dots.1._ = f32[32,1,3200]{2,1,0:T(1,128)} custom-call(s32[1]{0:T(128)} %bitcast.9.rep_ref._, s32[32]{0:T(128)} %map_ref.5, f32[1,3072]{1,0:T(1,128)} %dynamic-slice_add_fusion.refs_2_.row_ref, bf16[32,192,1536]{2,1,0:T(8,128)(2,1)} %src_ref.3, bf16[16,192,384]{2,1,0:T(8,128)(2,1)} %hold.13.got_ref), custom_call_target="tpu_custom_call" | custom-call | flops 5000000000 | bytes 5000000 | tf_op jit(solution)/shard_map/coef_dots/pallas_call | solution.py:717
  467.4 5.6 %finish.1 = f32[32,192,384]{2,1,0:T(8,128)} custom-call(s32[32]{0:T(128)} %map_ref.5, f32[32]{0:T(128)} %coef_ref.3, f32[32,1,3200]{2,1,0:T(1,128)} %coef_dots.1._, bf16[16,192,384]{2,1,0:T(8,128)(2,1)} %hold.13.got_ref), custom_call_target="tpu_custom_call" | custom-call | flops 5000000000 | bytes 5000000 | tf_op jit(solution)/shard_map/finish/pallas_call | solution.py:738
  473.0 6.5 %all-to-all-done.4 = f32[32,1,3200]{2,1,0:T(1,128)S(1)} async-done(((f32[32,1,3200]{2,1,0:T(1,128)}), f32[32,1,3200]{2,1,0:T(1,128)S(1)}, u32[]{:S(2)}, u32[]{:S(2)}) %all-to-all-start.4) | async-done | bytes 409632 | tf_op jit(solution)/shard_map/all_to_all | solution.py:859
  (110 shorter events, 103.8 us)
Async XLA Ops:
  67.4 52.2 %collective-permute-start.8 = (bf16[8,2,192,384]{3,2,1,0:T(8,128)(2,1)}, bf16[8,2,192,384]{3,2,1,0:T(8,128)(2,1)}, u32[]{:S(2)}, u32[]{:S(2)}) collective-permute-start(bf16[8,2,192,384]{3,2,1,0:T(8,128)(2,1)} %all_to_all.25.refs_0_.refs_1_), channel_id=1, source_target_pairs={{0,2},{2,0},{1,3},{3,1},{4,6},{6,4},{5,7},{7,5},{8,10},{10,8},{9,1... | collective-permute-start | bytes 7077896 | tf_op jit(solution)/shard_map/ppermute | solution.py:790
  70.3 145.8 %collective-permute-start.7 = (bf16[8,2,192,384]{3,2,1,0:T(8,128)(2,1)}, bf16[8,2,192,384]{3,2,1,0:T(8,128)(2,1)}, u32[]{:S(2)}, u32[]{:S(2)}) collective-permute-start(bf16[8,2,192,384]{3,2,1,0:T(8,128)(2,1)} %all_to_all.25.refs_0_.refs_1_), channel_id=1, source_target_pairs={{0,1},{1,0},{2,3},{3,2},{4,5},{5,4},{6,7},{7,6},{8,9},{9,8},{10,11... | collective-permute-start | bytes 7077896 | tf_op jit(solution)/shard_map/ppermute | solution.py:790
  119.6 96.4 %collective-permute-start.9 = (bf16[8,2,192,384]{3,2,1,0:T(8,128)(2,1)}, bf16[8,2,192,384]{3,2,1,0:T(8,128)(2,1)}, u32[]{:S(2)}, u32[]{:S(2)}) collective-permute-start(bf16[8,2,192,384]{3,2,1,0:T(8,128)(2,1)} %collective-permute-done.8.refs_2_), channel_id=1, source_target_pairs={{0,1},{1,0},{2,3},{3,2},{4,5},{5,4},{6,7},{7,6},{8,9},{9,8},{10,11... | collective-permute-start | bytes 7077896 | tf_op jit(solution)/shard_map/ppermute | solution.py:790
  126.5 102.6 %all-to-all-start.1 = ((bf16[8,80,1536]{2,1,0:T(8,128)(2,1)}), bf16[8,80,1536]{2,1,0:T(8,128)(2,1)S(1)}, u32[]{:S(2)}, u32[]{:S(2)}) async-start(bf16[8,80,1536]{2,1,0:T(8,128)(2,1)} %bitcast.55), calls=%async_computation.1 | async-start | bytes 3932160 | tf_op jit(solution)/shard_map/all_to_all | solution.py:793
  131.0 23.5 %collective-permute-start = (bf16[80,1664]{1,0:T(8,128)(2,1)}, bf16[80,1664]{1,0:T(8,128)(2,1)S(1)}, u32[]{:S(2)}, u32[]{:S(2)}) collective-permute-start(bf16[80,1664]{1,0:T(8,128)(2,1)} %get-tuple-element.41), channel_id=1, source_target_pairs={{0,4},{4,0},{8,12},{12,8},{16,20},{20,16},{24,28},{28,24},{1,5},{5... | collective-permute-start | bytes 798728 | tf_op jit(solution)/shard_map/ppermute | solution.py:812
  133.0 37.9 %collective-permute-start.1 = (bf16[80,1664]{1,0:T(8,128)(2,1)}, bf16[80,1664]{1,0:T(8,128)(2,1)S(1)}, u32[]{:S(2)}, u32[]{:S(2)}) collective-permute-start(bf16[80,1664]{1,0:T(8,128)(2,1)} %get-tuple-element.42), channel_id=1, source_target_pairs={{0,8},{4,12},{8,0},{12,4},{16,24},{20,28},{24,16},{28,20},{1,9},{5... | collective-permute-start | bytes 798728 | tf_op jit(solution)/shard_map/ppermute | solution.py:812
  134.5 42.2 %collective-permute-start.2 = (bf16[80,1664]{1,0:T(8,128)(2,1)}, bf16[80,1664]{1,0:T(8,128)(2,1)S(1)}, u32[]{:S(2)}, u32[]{:S(2)}) collective-permute-start(bf16[80,1664]{1,0:T(8,128)(2,1)} %get-tuple-element.43), channel_id=1, source_target_pairs={{0,12},{4,8},{8,4},{12,0},{16,28},{20,24},{24,20},{28,16},{1,13},{... | collective-permute-start | bytes 798728 | tf_op jit(solution)/shard_map/ppermute | solution.py:812
  154.5 46.1 %collective-permute-start.3 = (bf16[80,1664]{1,0:T(8,128)(2,1)}, bf16[80,1664]{1,0:T(8,128)(2,1)S(1)}, u32[]{:S(2)}, u32[]{:S(2)}) collective-permute-start(bf16[80,1664]{1,0:T(8,128)(2,1)} %get-tuple-element.44), channel_id=1, source_target_pairs={{0,16},{4,20},{8,24},{12,28},{16,0},{20,4},{24,8},{28,12},{1,17},{... | collective-permute-start | bytes 798728 | tf_op jit(solution)/shard_map/ppermute | solution.py:812
  170.9 42.1 %collective-permute-start.4 = (bf16[80,1664]{1,0:T(8,128)(2,1)S(1)}, bf16[80,1664]{1,0:T(8,128)(2,1)}, u32[]{:S(2)}, u32[]{:S(2)}) collective-permute-start(bf16[80,1664]{1,0:T(8,128)(2,1)S(1)} %copy-done.12), channel_id=1, source_target_pairs={{0,20},{4,16},{8,28},{12,24},{16,4},{20,0},{24,12},{28,8},{1,21},{... | collective-permute-start | bytes 798728 | tf_op jit(solution)/shard_map/ppermute | solution.py:812
  176.6 36.4 %collective-permute-start.5 = (bf16[80,1664]{1,0:T(8,128)(2,1)S(1)}, bf16[80,1664]{1,0:T(8,128)(2,1)}, u32[]{:S(2)}, u32[]{:S(2)}) collective-permute-start(bf16[80,1664]{1,0:T(8,128)(2,1)S(1)} %copy-done.11), channel_id=1, source_target_pairs={{0,24},{4,28},{8,16},{12,20},{16,8},{20,12},{24,0},{28,4},{1,25},{... | collective-permute-start | bytes 798728 | tf_op jit(solution)/shard_map/ppermute | solution.py:812
  201.3 11.7 %collective-permute-start.6 = (bf16[80,1664]{1,0:T(8,128)(2,1)S(1)}, bf16[80,1664]{1,0:T(8,128)(2,1)}, u32[]{:S(2)}, u32[]{:S(2)}) collective-permute-start(bf16[80,1664]{1,0:T(8,128)(2,1)S(1)} %copy-done.10), channel_id=1, source_target_pairs={{0,28},{4,24},{8,20},{12,16},{16,12},{20,8},{24,4},{28,0},{1,29},{... | collective-permute-start | bytes 798728 | tf_op jit(solution)/shard_map/ppermute | solution.py:812
  249.0 120.9 %collective-permute-start.19 = (bf16[8,2,192,384]{3,2,1,0:T(8,128)(2,1)}, bf16[8,2,192,384]{3,2,1,0:T(8,128)(2,1)S(1)}, u32[]{:S(2)}, u32[]{:S(2)}) collective-permute-start(bf16[8,2,192,384]{3,2,1,0:T(8,128)(2,1)} %lane_grads_add.2.refs_1_), channel_id=1, source_target_pairs={{0,2},{2,0},{1,3},{3,1},{4,6},{6,4},{5,7},{7,5},{8,10},{10,8},{9,1... | collective-permute-start | bytes 7077896 | tf_op jit(solution)/shard_map/ppermute | solution.py:790
  269.4 127.8 %all-to-all-start.2 = ((bf16[8,80,1536]{2,1,0:T(8,128)(2,1)}), bf16[8,80,1536]{2,1,0:T(8,128)(2,1)}, u32[]{:S(2)}, u32[]{:S(2)}) async-start(bf16[8,80,1536]{2,1,0:T(8,128)(2,1)} %bitcast.54), calls=%async_computation.2 | async-start | bytes 3932160 | tf_op jit(solution)/shard_map/all_to_all | solution.py:793
  282.8 22.6 %collective-permute-start.10 = (bf16[80,1536]{1,0:T(8,128)(2,1)}, bf16[80,1536]{1,0:T(8,128)(2,1)S(1)}, u32[]{:S(2)}, u32[]{:S(2)}) collective-permute-start(bf16[80,1536]{1,0:T(8,128)(2,1)} %get-tuple-element.49), channel_id=1, source_target_pairs={{0,4},{4,0},{8,12},{12,8},{16,20},{20,16},{24,28},{28,24},{1,5},{5... | collective-permute-start | bytes 737288 | tf_op jit(solution)/shard_map/ppermute | solution.py:812
  284.8 37.3 %collective-permute-start.11 = (bf16[80,1536]{1,0:T(8,128)(2,1)}, bf16[80,1536]{1,0:T(8,128)(2,1)S(1)}, u32[]{:S(2)}, u32[]{:S(2)}) collective-permute-start(bf16[80,1536]{1,0:T(8,128)(2,1)} %get-tuple-element.50), channel_id=1, source_target_pairs={{0,8},{4,12},{8,0},{12,4},{16,24},{20,28},{24,16},{28,20},{1,9},{5... | collective-permute-start | bytes 737288 | tf_op jit(solution)/shard_map/ppermute | solution.py:812
  286.2 41.1 %collective-permute-start.12 = (bf16[80,1536]{1,0:T(8,128)(2,1)}, bf16[80,1536]{1,0:T(8,128)(2,1)S(1)}, u32[]{:S(2)}, u32[]{:S(2)}) collective-permute-start(bf16[80,1536]{1,0:T(8,128)(2,1)} %get-tuple-element.51), channel_id=1, source_target_pairs={{0,12},{4,8},{8,4},{12,0},{16,28},{20,24},{24,20},{28,16},{1,13},{... | collective-permute-start | bytes 737288 | tf_op jit(solution)/shard_map/ppermute | solution.py:812
  286.5 69.5 %collective-permute-start.13 = (bf16[80,1536]{1,0:T(8,128)(2,1)}, bf16[80,1536]{1,0:T(8,128)(2,1)S(1)}, u32[]{:S(2)}, u32[]{:S(2)}) collective-permute-start(bf16[80,1536]{1,0:T(8,128)(2,1)} %get-tuple-element.52), channel_id=1, source_target_pairs={{0,16},{4,20},{8,24},{12,28},{16,0},{20,4},{24,8},{28,12},{1,17},{... | collective-permute-start | bytes 737288 | tf_op jit(solution)/shard_map/ppermute | solution.py:812
  305.3 56.4 %collective-permute-start.14 = (bf16[80,1536]{1,0:T(8,128)(2,1)}, bf16[80,1536]{1,0:T(8,128)(2,1)}, u32[]{:S(2)}, u32[]{:S(2)}) collective-permute-start(bf16[80,1536]{1,0:T(8,128)(2,1)} %get-tuple-element.53), channel_id=1, source_target_pairs={{0,20},{4,16},{8,28},{12,24},{16,4},{20,0},{24,12},{28,8},{1,21},{... | collective-permute-start | bytes 737288 | tf_op jit(solution)/shard_map/ppermute | solution.py:812
  322.1 39.7 %collective-permute-start.15 = (bf16[80,1536]{1,0:T(8,128)(2,1)}, bf16[80,1536]{1,0:T(8,128)(2,1)}, u32[]{:S(2)}, u32[]{:S(2)}) collective-permute-start(bf16[80,1536]{1,0:T(8,128)(2,1)} %get-tuple-element.54), channel_id=1, source_target_pairs={{0,24},{4,28},{8,16},{12,20},{16,8},{20,12},{24,0},{28,4},{1,25},{... | collective-permute-start | bytes 737288 | tf_op jit(solution)/shard_map/ppermute | solution.py:812
  327.4 34.4 %collective-permute-start.16 = (bf16[80,1536]{1,0:T(8,128)(2,1)}, bf16[80,1536]{1,0:T(8,128)(2,1)}, u32[]{:S(2)}, u32[]{:S(2)}) collective-permute-start(bf16[80,1536]{1,0:T(8,128)(2,1)} %get-tuple-element.55), channel_id=1, source_target_pairs={{0,28},{4,24},{8,20},{12,16},{16,12},{20,8},{24,4},{28,0},{1,29},{... | collective-permute-start | bytes 737288 | tf_op jit(solution)/shard_map/ppermute | solution.py:812
  372.3 19.4 %collective-permute-start.20 = (f32[16,3072]{1,0:T(8,128)S(1)}, f32[16,3072]{1,0:T(8,128)S(1)}, u32[]{:S(2)}, u32[]{:S(2)}) collective-permute-start(f32[16,3072]{1,0:T(8,128)S(1)} %dynamic-slice_bitcast_fusion), channel_id=1, source_target_pairs={{0,16},{4,20},{8,24},{12,28},{16,0},{20,4},{24,8},{28,12},{1,17},{... | collective-permute-start | bytes 589832 | tf_op jit(solution)/shard_map/ppermute | solution.py:763
  397.2 57.7 %all-to-all-start.3 = ((bf16[8,2,192,384]{3,2,1,0:T(8,128)(2,1)}), bf16[8,2,192,384]{3,2,1,0:T(8,128)(2,1)S(1)}, u32[]{:S(2)}, u32[]{:S(2)}) async-start(bf16[8,2,192,384]{3,2,1,0:T(8,128)(2,1)} %hold.12), calls=%async_computation.3 | async-start | bytes 4718592 | tf_op jit(solution)/shard_map/all_to_all | solution.py:793
  401.2 20.3 %collective-permute-start.22 = (f32[4,3072]{1,0:T(4,128)S(1)}, f32[4,3072]{1,0:T(4,128)S(1)}, u32[]{:S(2)}, u32[]{:S(2)}) collective-permute-start(f32[4,3072]{1,0:T(4,128)S(1)} %dynamic-slice_bitcast_fusion.2), channel_id=1, source_target_pairs={{0,4},{4,0},{8,12},{12,8},{16,20},{20,16},{24,28},{28,24},{1,5},{5... | collective-permute-start | bytes 147464 | tf_op jit(solution)/shard_map/ppermute | solution.py:763
  463.3 16.2 %all-to-all-start.4 = ((f32[32,1,3200]{2,1,0:T(1,128)}), f32[32,1,3200]{2,1,0:T(1,128)S(1)}, u32[]{:S(2)}, u32[]{:S(2)}) async-start(f32[32,1,3200]{2,1,0:T(1,128)} %coef_dots.1._), calls=%async_computation.4 | async-start | bytes 819200 | tf_op jit(solution)/shard_map/all_to_all | solution.py:859
  (22 other events, 538.2 us)

commit v6 on v4

--- a/solution.py
+++ b/solution.py
@@ -235,7 +235,9 @@
     return lax.dot_general(a, b, (dims, ((), ())), preferred_element_type=F32)
 
 
-def merge_kernel(rep_ref, map_ref, coef_ref, src_ref, out_ref, order_ref, count_ref, held, sems):
+def merge_kernel(
+    rep_ref, map_ref, coef_ref, src_ref, _, out_ref, order_ref, count_ref, held, sems
+):
     combos, _, cols = out_ref.shape
     expert_order(map_ref, order_ref, count_ref)
     at = pl.ds(pl.multiple_of(rep_ref[0] * cols, cols), cols)
@@ -266,12 +268,12 @@
         count_ref[g] = n + 1
 
 
-def merge_experts(rep_index, merge_map, merge_coef, source_w, reps):
+def merge_experts(rep_index, merge_map, merge_coef, source_w, after, reps):
     count, rows, width = source_w.shape
     cols = width // reps
     return pl.pallas_call(
         merge_kernel,
-        in_specs=[smem_spec(), smem_spec(), smem_spec(), any_spec()],
+        in_specs=[smem_spec()] * 3 + [any_spec()] * 2,
         out_specs=vmem_spec(),
         out_shape=jax.ShapeDtypeStruct((count // 2, rows, cols), BF),
         scratch_shapes=[
@@ -283,7 +285,7 @@
         compiler_params=params(56),
         cost_estimate=cost(5),
         name="merge_experts",
-    )(rep_index, merge_map, merge_coef, source_w)
+    )(rep_index, merge_map, merge_coef, source_w, after)
 
 
 def hbm_spec():
@@ -322,8 +324,8 @@
 
 def route_kernel(
     capacity, lanes,
-    xt_ref, rwt_ref, rb_ref, idx_ref, map_ref, hid_ref, og_ref, _,
-    sh_ref, sg_ref, gate_ref, pos_ref, slot_ref,
+    xt_ref, rwt_ref, rb_ref, idx_ref, map_ref, hid_ref, og_ref,
+    send_ref, gate_ref, pos_ref, slot_ref,
 ):
     top, tok = idx_ref.shape
     sources = rwt_ref.shape[0]
@@ -383,33 +385,33 @@
     slot_ref[...] = jnp.broadcast_to(slot_pos, slot_ref.shape)
     take = lax.broadcasted_iota(I32, (places, slots), 0) == slot_pos
     placed = jnp.sum(jnp.where(take, spot[3:4].astype(F32), 0.0), axis=1, keepdims=True)
-    sh_ref[:, width:] = jnp.broadcast_to(placed, (places, 128)).astype(BF)
+    depth = og_ref.shape[1]
+    send_ref[:, depth + width :] = jnp.broadcast_to(placed, (places, 128)).astype(BF)
     take = take.astype(BF)
     for n in range(0, width, TILE):
         rows = jnp.dot(take, hid_ref[:, n : n + TILE], preferred_element_type=F32)
-        sh_ref[:, n : n + TILE] = rows.astype(BF)
+        send_ref[:, depth + n : depth + n + TILE] = rows.astype(BF)
     takes = [
         (lax.broadcasted_iota(I32, (places, tok), 0) == position[k]).astype(BF) for k in range(top)
     ]
     columns = [column(g) for g in gates]
-    for n in range(0, og_ref.shape[1], TILE):
+    for n in range(0, depth, TILE):
         og = og_ref[:, n : n + TILE].astype(F32)
         rows = jnp.zeros((places, TILE), F32)
         for k in range(top):
             rows = rows + jnp.dot(takes[k], (columns[k] * og).astype(BF), preferred_element_type=F32)
-        sg_ref[:, n : n + TILE] = rows.astype(BF)
-
-
-def route(xt, rwt, router_b, idx_t, merge_map, hid, og, after, capacity, lanes):
+        send_ref[:, n : n + TILE] = rows.astype(BF)
+
+
+def route(xt, rwt, router_b, idx_t, merge_map, hid, og, capacity, lanes):
     slots, width = hid.shape
     tok = idx_t.shape[1]
     return pl.pallas_call(
         functools.partial(route_kernel, capacity, lanes),
-        in_specs=[vmem_spec()] * 7 + [any_spec()],
-        out_specs=[vmem_spec()] * 5,
+        in_specs=[vmem_spec()] * 7,
+        out_specs=[vmem_spec()] * 4,
         out_shape=[
-            jax.ShapeDtypeStruct((lanes * capacity, width + 128), BF),
-            jax.ShapeDtypeStruct((lanes * capacity, og.shape[1]), BF),
+            jax.ShapeDtypeStruct((lanes * capacity, og.shape[1] + width + 128), BF),
             jax.ShapeDtypeStruct((8, tok), F32),
             jax.ShapeDtypeStruct((8, tok), I32),
             jax.ShapeDtypeStruct((8, slots), I32),
@@ -417,7 +419,7 @@
         compiler_params=params(56),
         cost_estimate=cost(5),
         name="route",
-    )(xt, rwt, router_b[None, :], idx_t, merge_map[None, :], hid, og, after)
+    )(xt, rwt, router_b[None, :], idx_t, merge_map[None, :], hid, og)
 
 
 def load_weights(rep_ref, pieces, w_ref, sems):
@@ -455,7 +457,7 @@
         out_ref[:, at] = jnp.where(member == 0.0, both[0], both[1]).astype(BF)
 
 
-def run_lane(kernel, rep_index, rows, hid, pieces, name):
+def run_lane(kernel, rep_index, rows, which, pieces, name):
     blocks, members, share, cols = pieces[0].shape
     depth, width = share * blocks, cols * len(pieces)
     count = rows.shape[0]
@@ -464,8 +466,8 @@
         grid=(1,),
         in_specs=[
             smem_spec(),
-            pl.BlockSpec((count, width), lambda i: (0, 0)),
-            pl.BlockSpec((count, 128), lambda i: (0, width // 128)),
+            pl.BlockSpec((count, width), lambda i: (0, which)),
+            pl.BlockSpec((count, 128), lambda i: (0, 2 * width // 128)),
         ]
         + [any_spec()] * len(pieces),
         out_specs=pl.BlockSpec((count, width), lambda i: (0, 0)),
@@ -477,7 +479,7 @@
         compiler_params=params(56),
         cost_estimate=cost(12),
         name=name,
-    )(rep_index, rows, hid, *pieces)
+    )(rep_index, rows, rows, *pieces)
 
 
 def lane_grad_kernel(has_other, _, grd_ref, hid_ref, flag_ref, *refs):
@@ -494,9 +496,9 @@
         out_ref[n : n + each, 0] = part.astype(BF)
 
 
-def lane_grads(owner, grd, hid, other, blocks, reps):
-    count, depth = grd.shape
-    width = hid.shape[1] - 128
+def lane_grads(owner, rows, other, blocks, reps):
+    count = rows.shape[0]
+    depth = width = (rows.shape[1] - 128) // 2
     cols = width // reps
     shape = (blocks, 2, depth // blocks, cols)
     block = pl.BlockSpec((blocks, 1, depth // blocks, cols), lambda m, s: (0, m, 0, 0))
@@ -508,8 +510,8 @@
             grid=(2,),
             in_specs=[
                 pl.BlockSpec((count, depth), lambda m, s: (0, 0)),
-                pl.BlockSpec((count, cols), lambda m, s: (0, s[0])),
-                pl.BlockSpec((count, 128), lambda m, s: (0, width // 128)),
+                pl.BlockSpec((count, cols), lambda m, s: (0, reps + s[0])),
+                pl.BlockSpec((count, 128), lambda m, s: (0, 2 * width // 128)),
             ]
             + [block] * len(extra),
             out_specs=block,
@@ -518,7 +520,7 @@
         compiler_params=params(56),
         cost_estimate=cost(6),
         name="lane_grads_add" if extra else "lane_grads_first",
-    )(owner, grd, hid, hid, *extra)
+    )(owner, rows, rows, rows, *extra)
 
 
 def combine_kernel(
@@ -743,62 +745,69 @@
     def trade_rows(rows):
         return trade(rows.reshape(lanes, capacity, rows.shape[1])).reshape(rows.shape)
 
-    combos = merge_experts(one(rep_i), merge_map, merge_coef, source_w, reps)
-    mine = trade(combos.reshape((lanes, 2) + combos.shape[1:]))
+    def later(x):
+        return swap(hold([jnp.zeros((8, 128), F32)], x)[0], "core")
 
     xt = tokens.reshape(tok, features).T
     rwt = router_w.T
     idx_t = teacher_idx.reshape(tok, top).T
     og = out_grad.reshape(tok, depth)
-    send_hid, send_grd, gates, pos, slot_pos = route(
+    send_rows, gates, pos, slot_pos = route(
         xt, rwt, router_b, idx_t, merge_map, hidden.reshape(tok * top, width), og,
-        combos, capacity, lanes,
-    )
-    (send_hid,) = hold([send_hid], mine)
-    hid = trade_rows(send_hid)
+        capacity, lanes,
+    )
+    combos = merge_experts(one(rep_i), merge_map, merge_coef, source_w, send_rows, reps)
+
+    rows = trade_rows(send_rows)
+    (combos,) = hold([combos], rows)
+    mine = trade(combos.reshape((lanes, 2) + combos.shape[1:]))
+    (rows,) = hold([rows], later(rows))
+
+    def summed(row):
+        first = lane_grads(one(2 * row + 1 - core_i), rows, None, blocks, reps)
+        return lane_grads(one(2 * row + core_i), rows, swap(first, "core"), blocks, reps)
+
+    distant, near = summed(1 - row_i), summed(row_i)
+    away = swap(distant, "row")
+    total = (near.astype(F32) + away.astype(F32)).astype(BF)
+    (mine,) = hold([mine], near)
+    (total,) = hold([total], mine)
+    arrived = trade(total).reshape(2 * lanes, row_share, width // reps)
+
     far = swap(mine, "row")
     pieces = [mine, swap(mine, "core"), far, swap(far, "core")]
-    (send_grd,) = hold([send_grd], hid)
-    grd = trade_rows(send_grd)
-    out_rows = run_lane(forward_kernel, one(rep_i), hid, hid, pieces, "lane_forward")
-    grd, out_rows = hold([grd, out_rows])
+    out_rows = run_lane(forward_kernel, one(rep_i), rows, 1, pieces, "lane_forward")
+    arrived, out_rows = hold([arrived, out_rows])
     home_out = trade_rows(out_rows)
-
-    def summed(row):
-        first = lane_grads(one(2 * row + 1 - core_i), grd, hid, None, blocks, reps)
-        return lane_grads(one(2 * row + core_i), grd, hid, swap(first, "core"), blocks, reps)
-
-    distant, near = summed(1 - row_i), summed(row_i)
-    away = swap(distant, "row")
-    (last_grd,) = hold([grd], distant, near)
-    back_rows = run_lane(backward_kernel, one(rep_i), last_grd, hid, pieces, "lane_backward")
-    total = (near.astype(F32) + away.astype(F32)).astype(BF)
-
+    (last_rows,) = hold([rows], later(arrived))
+    back_rows = run_lane(backward_kernel, one(rep_i), last_rows, 0, pieces, "lane_backward")
+    (arrived,) = hold([arrived], back_rows)
+    dots = coef_dots(one(rep_i), merge_map, source_w, arrived)
+    source_w_grad = finish(merge_map, merge_coef, arrived, dots, scale)
+    (home_out,) = hold([home_out], source_w_grad)
+    (back_rows,) = hold([back_rows], home_out)
+    home_back = trade_rows(back_rows)
+
+    (home_out,) = hold([home_out], later(back_rows))
     mixed, token_grad, part = combine(home_out, og, gates, pos, idx_t, rwt, xt)
-    home_back = trade_rows(back_rows)
-    hidden_grad = unplace(home_back, slot_pos)
-
-    (part,) = hold([part], back_rows)
+    part = part.reshape(blocks, 2, 2, part.shape[1]).transpose(2, 1, 0, 3).reshape(part.shape)
     part = add_up(
         part,
         [
+            ("core", 1, core_i),
+            ("row", 1, row_i),
             ("ctx", 4, ctx_i // 4),
             ("ctx", 2, ctx_i // 2 % 2),
             ("ctx", 1, ctx_i % 2),
-            ("row", 1, row_i),
-            ("core", 1, core_i),
         ],
     )
-    (total,) = hold([total], home_back)
-    arrived = trade(total).reshape(2 * lanes, row_share, width // reps)
-    (arrived,) = hold([arrived], hidden_grad, part)
-    dots = coef_dots(one(rep_i), merge_map, source_w, arrived)
     news = jnp.concatenate([part, dots[:1]], axis=1)
+    (news,) = hold([news], home_back)
     news = lax.all_to_all(
         jnp.broadcast_to(news[None], (devices,) + news.shape), ("ctx", "row", "core"),
         split_axis=0, concat_axis=0, tiled=True,
     )
-    source_w_grad = finish(merge_map, merge_coef, arrived, dots, scale)
+    hidden_grad = unplace(home_back, slot_pos)
     end = part.shape[1]
     return (
         mixed.reshape(1, tok, depth),

time: 391 us -> 411 us (1.051)
  waiting for transfers between devices: 246 us -> 258 us
  local copies, waits for them, and re-layouts: 10.4 us -> 21.3 us
    all_to_all x6 -> x5, waiting for transfers between devices: 123 us -> 139 us  [trade(): return lax.all_to_all(x, 'ctx', split_axis=0, concat_axis=0, tiled=True)]
    ppermute x5, waiting for transfers between devices: 64.5 us -> 52 us  [add_up(): lax.ppermute(give, axis, [(i, i ^ distance) for i in range(size)])]
    ppermute x6 -> x9, waiting for transfers between devices: 51.6 us -> 61.7 us  [swap(): return lax.ppermute(x, axis, [(0, 1), (1, 0)])]
    unnamed x17 -> x19, local copies, waits for them, and re-layouts: 4.85 us -> 9.43 us
    all_to_all x6 -> x5, starting transfers between devices: 29 us -> 26.6 us  [trade(): return lax.all_to_all(x, 'ctx', split_axis=0, concat_axis=0, tiled=True)]
  transfers between devices with their start and end apart: 18 -> 20, of which waited for: 10 -> 13; matrix products, arithmetic and copies ran while one was open for 2% -> 2% of each run, Pallas kernels for 17% -> 17%
where the time goes in v6:
time: 411 us; the launch traced here: 410 us
  waiting for transfers between devices  258 us (63%)
  Pallas kernels  83.2 us (20%)
  starting transfers between devices  39 us (9%)
  local copies, waits for them, and re-layouts  21.3 us (5%)
  other arithmetic  7.81 us (2%)
    all_to_all x5, waiting for transfers between devices, trade(): return lax.all_to_all(x, 'ctx', split_axis=0, concat_axis=0, tiled=True)  139 us
    ppermute x9, waiting for transfers between devices, swap(): return lax.ppermute(x, axis, [(0, 1), (1, 0)])  61.7 us
    ppermute x5, waiting for transfers between devices, add_up(): lax.ppermute(give, axis, [(i, i ^ distance) for i in range(size)])  52 us
    all_to_all x5, starting transfers between devices, trade(): return lax.all_to_all(x, 'ctx', split_axis=0, concat_axis=0, tiled=True)  26.6 us
    pallas_call x2, Pallas kernels, run_lane(): pl.pallas_call(kernel, grid=(1,), in_specs=[smem_spec(), pl.BlockSpec((co...  26.1 us
    pallas_call x4, Pallas kernels, lane_grads(): pl.pallas_call(functools.partial(lane_grad_kernel, other is not None), gr...  22.6 us
    unnamed x19, local copies, waits for them, and re-layouts  9.43 us
  transfers between devices with their start and end apart: 20, of which 13 were waited for; matrix products, arithmetic and copies ran while one was open for 2% of the time, Pallas kernels for 17%

profile of v6, /device:TPU:0, one launch (start us, length us, event | category | flops | bytes accessed | tf_op | source)
XLA Modules:
  0.0 410.0 jit_solution(3732346410178515072)
XLA Ops:
  4.3 7.6 %route.1 = (bf16[640,3200]{1,0:T(8,128)(2,1)}, f32[8,128]{1,0:T(8,128)}, s32[8,128]{1,0:T(8,128)}, s32[8,512]{1,0:T(8,128)}) custom-call(bf16[2880,128]{1,0:T(8,128)(2,1)} %bitcast.67, bf16[32,2880]{1,0:T(8,128)(2,1)} %bitcast.71, f32[1,32]{1,0:T(1,128)} %bitcast.75, s32[4,128]{1,0:T(4,128)} %bitcast.73, s32[1,32]{1,0:T(1,128)} %bitcast.66, ...), custom_call_target="tpu_custom_call" | custom-call | flops 5000000000 | bytes 5000000 | tf_op jit(solution)/shard_map/route/pallas_call | solution.py:409
  12.0 7.3 %all-to-all-start = ((bf16[8,80,3200]{2,1,0:T(8,128)(2,1)}), bf16[8,80,3200]{2,1,0:T(8,128)(2,1)}, u32[]{:S(2)}, u32[]{:S(2)}) async-start(bf16[8,80,3200]{2,1,0:T(8,128)(2,1)} %bitcast.59), calls=%async_computation | async-start | bytes 8192000 | tf_op jit(solution)/shard_map/all_to_all | solution.py:743
  19.2 91.2 %all-to-all-done = bf16[8,80,3200]{2,1,0:T(8,128)(2,1)} async-done(((bf16[8,80,3200]{2,1,0:T(8,128)(2,1)}), bf16[8,80,3200]{2,1,0:T(8,128)(2,1)}, u32[]{:S(2)}, u32[]{:S(2)}) %all-to-all-start) | async-done | bytes 4096032 | tf_op jit(solution)/shard_map/all_to_all | solution.py:743
  111.0 5.5 %merge_experts.1.refs_0_ = bf16[16,192,384]{2,1,0:T(8,128)(2,1)} custom-call(s32[1]{0:T(128)} %bitcast.8._.rep_ref, s32[32]{0:T(128)} %map_ref.5, f32[32]{0:T(128)} %coef_ref.3, bf16[32,192,1536]{2,1,0:T(8,128)(2,1)} %src_ref.3, bf16[640,3200]{1,0:T(8,128)(2,1)} %get-tuple-element.18._), custom_call_target="tpu_custom_call" | custom-call | flops 5000000000 | bytes 5000000 | tf_op jit(solution)/shard_map/merge_experts/pallas_call | solution.py:274
  120.8 5.4 %lane_grads_first.3 = bf16[8,2,192,384]{3,2,1,0:T(8,128)(2,1)} custom-call(s32[1]{0:T(128)} %bitcast.13._, bf16[640,3200]{1,0:T(8,128)(2,1)} %hold.15.grd_ref.hid_ref.flag_ref.rows_ref.refs_0_, bf16[640,3200]{1,0:T(8,128)(2,1)} %hold.15.grd_ref.hid_ref.flag_ref.rows_ref.refs_0_, bf16[640,3200]{1,0:T(8,128)(2,1)} %hold.15.grd_ref.hid_ref.flag_ref.rows_ref.refs_0_), custom_call_target="tpu_custom_call" | custom-call | flops 6000000000 | bytes 6000000 | tf_op jit(solution)/shard_map/lane_grads_first/pallas_call | solution.py:506
  126.7 5.5 %lane_grads_first.2 = bf16[8,2,192,384]{3,2,1,0:T(8,128)(2,1)} custom-call(s32[1]{0:T(128)} %bitcast.11._, bf16[640,3200]{1,0:T(8,128)(2,1)} %hold.15.grd_ref.hid_ref.flag_ref.rows_ref.refs_0_, bf16[640,3200]{1,0:T(8,128)(2,1)} %hold.15.grd_ref.hid_ref.flag_ref.rows_ref.refs_0_, bf16[640,3200]{1,0:T(8,128)(2,1)} %hold.15.grd_ref.hid_ref.flag_ref.rows_ref.refs_0_), custom_call_target="tpu_custom_call" | custom-call | flops 6000000000 | bytes 6000000 | tf_op jit(solution)/shard_map/lane_grads_first/pallas_call | solution.py:506
  132.2 5.8 %lane_grads_add.3 = bf16[8,2,192,384]{3,2,1,0:T(8,128)(2,1)} custom-call(s32[1]{0:T(128)} %bitcast.12._, bf16[640,3200]{1,0:T(8,128)(2,1)} %hold.15.grd_ref.hid_ref.flag_ref.rows_ref.refs_0_, bf16[640,3200]{1,0:T(8,128)(2,1)} %hold.15.grd_ref.hid_ref.flag_ref.rows_ref.refs_0_, bf16[640,3200]{1,0:T(8,128)(2,1)} %hold.15.grd_ref.hid_ref.flag_ref.rows_ref.refs_0_, ...), custom_call_target="tpu_custom_call" | custom-call | flops 6000000000 | bytes 6000000 | tf_op jit(solution)/shard_map/lane_grads_add/pallas_call | solution.py:506
  139.6 5.8 %lane_grads_add.2.refs_1_ = bf16[8,2,192,384]{3,2,1,0:T(8,128)(2,1)} custom-call(s32[1]{0:T(128)} %bitcast.8._.rep_ref, bf16[640,3200]{1,0:T(8,128)(2,1)} %hold.15.grd_ref.hid_ref.flag_ref.rows_ref.refs_0_, bf16[640,3200]{1,0:T(8,128)(2,1)} %hold.15.grd_ref.hid_ref.flag_ref.rows_ref.refs_0_, ...), custom_call_target="tpu_custom_call" | custom-call | flops 6000000000 | bytes 6000000 | tf_op jit(solution)/shard_map/lane_grads_add/pallas_call | solution.py:506
  145.4 29.5 %all-to-all-done.1.refs_0_ = bf16[8,2,192,384]{3,2,1,0:T(8,128)(2,1)S(1)} async-done(((bf16[8,2,192,384]{3,2,1,0:T(8,128)(2,1)}), bf16[8,2,192,384]{3,2,1,0:T(8,128)(2,1)S(1)}, u32[]{:S(2)}, u32[]{:S(2)}) %all-to-all-start.1) | async-done | bytes 2359328 | tf_op jit(solution)/shard_map/all_to_all | solution.py:743
  177.9 14.6 %collective-permute-done.3 = bf16[8,2,192,384]{3,2,1,0:T(8,128)(2,1)} collective-permute-done((bf16[8,2,192,384]{3,2,1,0:T(8,128)(2,1)}, bf16[8,2,192,384]{3,2,1,0:T(8,128)(2,1)}, u32[]{:S(2)}, u32[]{:S(2)}) %collective-permute-start.3) | collective-permute-done | bytes 2359328 | tf_op jit(solution)/shard_map/ppermute | solution.py:740
  192.4 4.5 %add_convert_fusion.refs_0_ = bf16[8,2,192,384]{3,2,1,0:T(8,128)(2,1)} fusion(bf16[8,2,192,384]{3,2,1,0:T(8,128)(2,1)} %collective-permute-done.3, bf16[8,2,192,384]{3,2,1,0:T(8,128)(2,1)} %lane_grads_add.2.refs_1_), kind=kLoop, calls=%fused_computation | loop fusion | flops 4718592 | bytes 7077888 | tf_op jit(solution)/shard_map/convert_element_type | solution.py:772
  196.9 6.0 %all-to-all-start.2 = ((bf16[8,2,192,384]{3,2,1,0:T(8,128)(2,1)}), bf16[8,2,192,384]{3,2,1,0:T(8,128)(2,1)S(1)}, u32[]{:S(2)}, u32[]{:S(2)}) async-start(bf16[8,2,192,384]{3,2,1,0:T(8,128)(2,1)} %hold.18), calls=%async_computation.2 | async-start | bytes 4718592 | tf_op jit(solution)/shard_map/all_to_all | solution.py:743
  202.9 39.6 %collective-permute-done.5.refs_2_ = bf16[8,2,192,384]{3,2,1,0:T(8,128)(2,1)} collective-permute-done((bf16[8,2,192,384]{3,2,1,0:T(8,128)(2,1)}, bf16[8,2,192,384]{3,2,1,0:T(8,128)(2,1)}, u32[]{:S(2)}, u32[]{:S(2)}) %collective-permute-start.5) | collective-permute-done | bytes 2359328 | tf_op jit(solution)/shard_map/ppermute | solution.py:740
  242.6 4.7 %collective-permute-done.6.refs_3_ = bf16[8,2,192,384]{3,2,1,0:T(8,128)(2,1)S(1)} collective-permute-done((bf16[8,2,192,384]{3,2,1,0:T(8,128)(2,1)}, bf16[8,2,192,384]{3,2,1,0:T(8,128)(2,1)S(1)}, u32[]{:S(2)}, u32[]{:S(2)}) %collective-permute-start.6) | collective-permute-done | bytes 2359328 | tf_op jit(solution)/shard_map/ppermute | solution.py:740
  248.7 13.0 %lane_forward.1.refs_1_ = bf16[640,1536]{1,0:T(8,128)(2,1)} custom-call(s32[1]{0:T(128)} %bitcast.8._.rep_ref, bf16[640,3200]{1,0:T(8,128)(2,1)} %hold.15.grd_ref.hid_ref.flag_ref.rows_ref.refs_0_, bf16[640,3200]{1,0:T(8,128)(2,1)} %hold.15.grd_ref.hid_ref.flag_ref.rows_ref.refs_0_, bf16[8,2,192,384]{3,2,1,0:T(8,128)(2,1)} %hold.17.refs_1_.refs_0_, ...), custom_call_target="tpu_custom_call" | custom-call | flops 12000000000 | bytes 12000000 | tf_op jit(solution)/shard_map/lane_forward/pallas_call | solution.py:464
  263.3 5.7 %all-to-all-start.3 = ((bf16[8,80,1536]{2,1,0:T(8,128)(2,1)}), bf16[8,80,1536]{2,1,0:T(8,128)(2,1)S(1)}, u32[]{:S(2)}, u32[]{:S(2)}) async-start(bf16[8,80,1536]{2,1,0:T(8,128)(2,1)} %bitcast.62), calls=%async_computation.3 | async-start | bytes 3932160 | tf_op jit(solution)/shard_map/all_to_all | solution.py:743
  271.5 13.0 %lane_backward.1.refs_1_.refs_0_ = bf16[640,1536]{1,0:T(8,128)(2,1)} custom-call(s32[1]{0:T(128)} %bitcast.8._.rep_ref, bf16[640,3200]{1,0:T(8,128)(2,1)} %hold.21.rows_ref.flag_ref, bf16[640,3200]{1,0:T(8,128)(2,1)} %hold.21.rows_ref.flag_ref, bf16[8,2,192,384]{3,2,1,0:T(8,128)(2,1)} %hold.17.refs_1_.refs_0_, bf16[8,2,192,384]{3,2,1,0:T(8,128)(2,1)} %copy-done.7, ...), custom_call_target="tpu_custom_call" | custom-call | flops 12000000000 | bytes 12000000 | tf_op jit(solution)/shard_map/lane_backward/pallas_call | solution.py:464
  284.6 6.6 %coef_dots.1._ = f32[8,128]{1,0:T(8,128)} custom-call(s32[1]{0:T(128)} %bitcast.8._.rep_ref, s32[32]{0:T(128)} %map_ref.5, bf16[32,192,1536]{2,1,0:T(8,128)(2,1)} %src_ref.3, bf16[16,192,384]{2,1,0:T(8,128)(2,1)} %hold.22.got_ref), custom_call_target="tpu_custom_call" | custom-call | flops 5000000000 | bytes 5000000 | tf_op jit(solution)/shard_map/coef_dots/pallas_call | solution.py:667
  291.2 5.6 %finish.1.refs_1_ = f32[32,192,384]{2,1,0:T(8,128)} custom-call(s32[32]{0:T(128)} %map_ref.5, f32[32]{0:T(128)} %coef_ref.3, f32[8,128]{1,0:T(8,128)} %coef_dots.1._, bf16[16,192,384]{2,1,0:T(8,128)(2,1)} %hold.22.got_ref), custom_call_target="tpu_custom_call" | custom-call | flops 5000000000 | bytes 5000000 | tf_op jit(solution)/shard_map/finish/pallas_call | solution.py:688
  296.8 17.9 %all-to-all-done.3 = bf16[8,80,1536]{2,1,0:T(8,128)(2,1)S(1)} async-done(((bf16[8,80,1536]{2,1,0:T(8,128)(2,1)}), bf16[8,80,1536]{2,1,0:T(8,128)(2,1)S(1)}, u32[]{:S(2)}, u32[]{:S(2)}) %all-to-all-start.3) | async-done | bytes 1966112 | tf_op jit(solution)/shard_map/all_to_all | solution.py:743
  318.5 5.1 %combine.1 = (bf16[128,1536]{1,0:T(8,128)(2,1)}, bf16[2880,128]{1,0:T(8,128)(2,1)}, f32[32,3072]{1,0:T(8,128)}) custom-call(bf16[128,1536]{1,0:T(8,128)(2,1)} %bitcast.70, f32[8,128]{1,0:T(8,128)} %get-tuple-element.16.gate_ref, s32[8,128]{1,0:T(8,128)} %get-tuple-element.17.pos_ref, s32[4,128]{1,0:T(4,128)} %bitcast.74, bf16[32,2880]{1,0:T(8,128)(2,1)} %bitcast.72, ...), custom_call_target="tpu_custom_call" | custom-call | flops 5000000000 | bytes 5000000 | tf_op jit(solution)/shard_map/combine/pallas_call | solution.py:568
  335.1 44.7 %collective-permute-done.11 = f32[4,3072]{1,0:T(4,128)S(1)} collective-permute-done((f32[4,3072]{1,0:T(4,128)S(1)}, f32[4,3072]{1,0:T(4,128)S(1)}, u32[]{:S(2)}, u32[]{:S(2)}) %collective-permute-start.11) | collective-permute-done | bytes 49184 | tf_op jit(solution)/shard_map/ppermute | solution.py:713
  393.9 4.1 %unplace.1 = bf16[512,1536]{1,0:T(8,128)(2,1)} custom-call(s32[8,512]{1,0:T(8,128)} %get-tuple-element.22.slot_ref, bf16[640,1536]{1,0:T(8,128)(2,1)} %bitcast.61), custom_call_target="tpu_custom_call" | custom-call | flops 5000000000 | bytes 5000000 | tf_op jit(solution)/shard_map/unplace/pallas_call | solution.py:592
  401.9 5.5 %all-to-all-done.5 = f32[32,1,3200]{2,1,0:T(1,128)S(1)} async-done(((f32[32,1,3200]{2,1,0:T(1,128)}), f32[32,1,3200]{2,1,0:T(1,128)S(1)}, u32[]{:S(2)}, u32[]{:S(2)}) %all-to-all-start.5) | async-done | bytes 409632 | tf_op jit(solution)/shard_map/all_to_all | solution.py:806
  (90 shorter events, 54.8 us)
Async XLA Ops:
  12.0 98.4 %all-to-all-start = ((bf16[8,80,3200]{2,1,0:T(8,128)(2,1)}), bf16[8,80,3200]{2,1,0:T(8,128)(2,1)}, u32[]{:S(2)}, u32[]{:S(2)}) async-start(bf16[8,80,3200]{2,1,0:T(8,128)(2,1)} %bitcast.59), calls=%async_computation | async-start | bytes 8192000 | tf_op jit(solution)/shard_map/all_to_all | solution.py:743
  111.0 9.2 %collective-permute-start = (f32[8,128]{1,0:T(8,128)}, f32[8,128]{1,0:T(8,128)S(1)}, u32[]{:S(2)}, u32[]{:S(2)}) collective-permute-start(f32[8,128]{1,0:T(8,128)} %hold.14), channel_id=1, source_target_pairs={{0,1},{1,0},{2,3},{3,2},{4,5},{5,4},{6,7},{7,6},{8,9},{9,8},{10,11... | collective-permute-start | bytes 12296 | tf_op jit(solution)/shard_map/ppermute | solution.py:740
  116.5 58.4 %all-to-all-start.1 = ((bf16[8,2,192,384]{3,2,1,0:T(8,128)(2,1)}), bf16[8,2,192,384]{3,2,1,0:T(8,128)(2,1)S(1)}, u32[]{:S(2)}, u32[]{:S(2)}) async-start(bf16[8,2,192,384]{3,2,1,0:T(8,128)(2,1)} %bitcast.58), calls=%async_computation.1 | async-start | bytes 4718592 | tf_op jit(solution)/shard_map/all_to_all | solution.py:743
  126.3 6.0 %collective-permute-start.2 = (bf16[8,2,192,384]{3,2,1,0:T(8,128)(2,1)}, bf16[8,2,192,384]{3,2,1,0:T(8,128)(2,1)}, u32[]{:S(2)}, u32[]{:S(2)}) collective-permute-start(bf16[8,2,192,384]{3,2,1,0:T(8,128)(2,1)} %lane_grads_first.3), channel_id=1, source_target_pairs={{0,1},{1,0},{2,3},{3,2},{4,5},{5,4},{6,7},{7,6},{8,9},{9,8},{10,11... | collective-permute-start | bytes 7077896 | tf_op jit(solution)/shard_map/ppermute | solution.py:740
  132.2 7.4 %collective-permute-start.1 = (bf16[8,2,192,384]{3,2,1,0:T(8,128)(2,1)}, bf16[8,2,192,384]{3,2,1,0:T(8,128)(2,1)}, u32[]{:S(2)}, u32[]{:S(2)}) collective-permute-start(bf16[8,2,192,384]{3,2,1,0:T(8,128)(2,1)} %lane_grads_first.2), channel_id=1, source_target_pairs={{0,1},{1,0},{2,3},{3,2},{4,5},{5,4},{6,7},{7,6},{8,9},{9,8},{10,11... | collective-permute-start | bytes 7077896 | tf_op jit(solution)/shard_map/ppermute | solution.py:740
  138.0 54.4 %collective-permute-start.3 = (bf16[8,2,192,384]{3,2,1,0:T(8,128)(2,1)}, bf16[8,2,192,384]{3,2,1,0:T(8,128)(2,1)}, u32[]{:S(2)}, u32[]{:S(2)}) collective-permute-start(bf16[8,2,192,384]{3,2,1,0:T(8,128)(2,1)} %lane_grads_add.3), channel_id=1, source_target_pairs={{0,2},{2,0},{1,3},{3,1},{4,6},{6,4},{5,7},{7,5},{8,10},{10,8},{9,1... | collective-permute-start | bytes 7077896 | tf_op jit(solution)/shard_map/ppermute | solution.py:740
  174.9 1.4 copy-start.2
  176.3 66.2 %collective-permute-start.5 = (bf16[8,2,192,384]{3,2,1,0:T(8,128)(2,1)}, bf16[8,2,192,384]{3,2,1,0:T(8,128)(2,1)}, u32[]{:S(2)}, u32[]{:S(2)}) collective-permute-start(bf16[8,2,192,384]{3,2,1,0:T(8,128)(2,1)} %hold.17.refs_1_.refs_0_), channel_id=1, source_target_pairs={{0,2},{2,0},{1,3},{3,1},{4,6},{6,4},{5,7},{7,5},{8,10},{10,8},{9,1... | collective-permute-start | bytes 7077896 | tf_op jit(solution)/shard_map/ppermute | solution.py:740
  196.9 64.9 %all-to-all-start.2 = ((bf16[8,2,192,384]{3,2,1,0:T(8,128)(2,1)}), bf16[8,2,192,384]{3,2,1,0:T(8,128)(2,1)S(1)}, u32[]{:S(2)}, u32[]{:S(2)}) async-start(bf16[8,2,192,384]{3,2,1,0:T(8,128)(2,1)} %hold.18), calls=%async_computation.2 | async-start | bytes 4718592 | tf_op jit(solution)/shard_map/all_to_all | solution.py:743
  202.9 39.6 %collective-permute-start.4 = (bf16[8,2,192,384]{3,2,1,0:T(8,128)(2,1)}, bf16[8,2,192,384]{3,2,1,0:T(8,128)(2,1)S(1)}, u32[]{:S(2)}, u32[]{:S(2)}) collective-permute-start(bf16[8,2,192,384]{3,2,1,0:T(8,128)(2,1)} %hold.17.refs_1_.refs_0_), channel_id=1, source_target_pairs={{0,1},{1,0},{2,3},{3,2},{4,5},{5,4},{6,7},{7,6},{8,9},{9,8},{10,11... | collective-permute-start | bytes 7077896 | tf_op jit(solution)/shard_map/ppermute | solution.py:740
  242.6 4.7 %collective-permute-start.6 = (bf16[8,2,192,384]{3,2,1,0:T(8,128)(2,1)}, bf16[8,2,192,384]{3,2,1,0:T(8,128)(2,1)S(1)}, u32[]{:S(2)}, u32[]{:S(2)}) collective-permute-start(bf16[8,2,192,384]{3,2,1,0:T(8,128)(2,1)} %collective-permute-done.5.refs_2_), channel_id=1, source_target_pairs={{0,1},{1,0},{2,3},{3,2},{4,5},{5,4},{6,7},{7,6},{8,9},{9,8},{10,11... | collective-permute-start | bytes 7077896 | tf_op jit(solution)/shard_map/ppermute | solution.py:740
  242.6 4.7 %copy-start.7 = (bf16[8,2,192,384]{3,2,1,0:T(8,128)(2,1)}, bf16[8,2,192,384]{3,2,1,0:T(8,128)(2,1)S(1)}, u32[]{:S(2)}) copy-start(bf16[8,2,192,384]{3,2,1,0:T(8,128)(2,1)S(1)} %collective-permute-done.4.refs_1_) | copy-start | bytes 7077892
  261.8 1.5 copy-start
  263.3 51.4 %all-to-all-start.3 = ((bf16[8,80,1536]{2,1,0:T(8,128)(2,1)}), bf16[8,80,1536]{2,1,0:T(8,128)(2,1)S(1)}, u32[]{:S(2)}, u32[]{:S(2)}) async-start(bf16[8,80,1536]{2,1,0:T(8,128)(2,1)} %bitcast.62), calls=%async_computation.3 | async-start | bytes 3932160 | tf_op jit(solution)/shard_map/all_to_all | solution.py:743
  269.6 1.4 collective-permute-start.7
  316.6 1.4 collective-permute-start.8
  325.1 1.5 collective-permute-start.9
  326.6 5.5 %collective-permute-start.10 = (f32[8,3072]{1,0:T(8,128)S(1)}, f32[8,3072]{1,0:T(8,128)S(1)}, u32[]{:S(2)}, u32[]{:S(2)}) collective-permute-start(f32[8,3072]{1,0:T(8,128)S(1)} %dynamic-slice_bitcast_fusion.1), channel_id=1, source_target_pairs={{0,2},{2,0},{1,3},{3,1},{4,6},{6,4},{5,7},{7,5},{8,10},{10,8},{9,1... | collective-permute-start | bytes 294920 | tf_op jit(solution)/shard_map/ppermute | solution.py:713
  328.2 59.3 %slice-start = ((f32[8,128]{1,0:T(8,128)}), f32[1,128]{1,0:T(1,128)S(1)}, s32[]{:S(2)}) async-start(f32[8,128]{1,0:T(8,128)} %coef_dots.1._), calls=%async_computation.6 | async-start | bytes 1024 | tf_op jit(solution)/shard_map/slice | solution.py:804
  328.2 60.0 %all-to-all-start.4 = ((bf16[8,80,1536]{2,1,0:T(8,128)(2,1)}), bf16[8,80,1536]{2,1,0:T(8,128)(2,1)S(1)}, u32[]{:S(2)}, u32[]{:S(2)}) async-start(bf16[8,80,1536]{2,1,0:T(8,128)(2,1)} %bitcast.19), calls=%async_computation.4 | async-start | bytes 3932160 | tf_op jit(solution)/shard_map/all_to_all | solution.py:743
  332.3 47.5 %collective-permute-start.11 = (f32[4,3072]{1,0:T(4,128)S(1)}, f32[4,3072]{1,0:T(4,128)S(1)}, u32[]{:S(2)}, u32[]{:S(2)}) collective-permute-start(f32[4,3072]{1,0:T(4,128)S(1)} %dynamic-slice_bitcast_fusion.2), channel_id=1, source_target_pairs={{0,16},{4,20},{8,24},{12,28},{16,0},{20,4},{24,8},{28,12},{1,17},{... | collective-permute-start | bytes 147464 | tf_op jit(solution)/shard_map/ppermute | solution.py:713
  379.8 3.9 collective-permute-start.12
  383.8 3.8 collective-permute-start.13
  391.2 16.2 %all-to-all-start.5 = ((f32[32,1,3200]{2,1,0:T(1,128)}), f32[32,1,3200]{2,1,0:T(1,128)S(1)}, u32[]{:S(2)}, u32[]{:S(2)}) async-start(f32[32,1,3200]{2,1,0:T(1,128)} %broadcast_in_dim.37), calls=%async_computation.5 | async-start | bytes 819200 | tf_op jit(solution)/shard_map/all_to_all | solution.py:806
  (6 other events, 5.7 us)

commit v7 on v4

--- a/solution.py
+++ b/solution.py
@@ -598,7 +598,9 @@
     )(slot_pos, home_back)
 
 
-def coef_kernel(rep_ref, map_ref, src_ref, got_ref, out_ref, order_ref, count_ref, held, weights, sems):
+def coef_kernel(
+    rep_ref, map_ref, row_ref, src_ref, got_ref, out_ref, order_ref, count_ref, held, weights, sems
+):
     count, rows, cols = weights.shape
     at = pl.ds(pl.multiple_of(rep_ref[0] * cols, cols), cols)
     copies = [
@@ -625,7 +627,11 @@
             total = total + jnp.where(lane == expert, small, 0.0)
         return total
 
-    out_ref[...] = lax.fori_loop(0, count // 2, one, jnp.zeros((8, 128), F32))
+    total = lax.fori_loop(0, count // 2, one, jnp.zeros((8, 128), F32))[:1]
+    end = row_ref.shape[1]
+    for n in range(out_ref.shape[0]):
+        out_ref[n, :, :end] = row_ref[...]
+        out_ref[n, :, end:] = total
 
 
 def finish_kernel(
@@ -659,14 +665,14 @@
         send(i).wait()
 
 
-def coef_dots(rep_index, merge_map, source_w, arrived):
+def coef_dots(rep_index, merge_map, row, source_w, arrived, devices):
     count = source_w.shape[0]
     _, rows, cols = arrived.shape
     return pl.pallas_call(
         coef_kernel,
-        in_specs=[smem_spec(), smem_spec(), hbm_spec(), any_spec()],
+        in_specs=[smem_spec(), smem_spec(), vmem_spec(), hbm_spec(), any_spec()],
         out_specs=vmem_spec(),
-        out_shape=jax.ShapeDtypeStruct((8, 128), F32),
+        out_shape=jax.ShapeDtypeStruct((devices, 1, row.shape[1] + 128), F32),
         scratch_shapes=[
             pltpu.SMEM((count,), I32),
             pltpu.SMEM((count // 2,), I32),
@@ -677,7 +683,7 @@
         compiler_params=params(56),
         cost_estimate=cost(5),
         name="coef_dots",
-    )(rep_index, merge_map, source_w, arrived)
+    )(rep_index, merge_map, row, source_w, arrived)
 
 
 def finish(merge_map, merge_coef, arrived, after, scale):
@@ -743,6 +749,9 @@
     def trade_rows(rows):
         return trade(rows.reshape(lanes, capacity, rows.shape[1])).reshape(rows.shape)
 
+    def later(*x):
+        return swap(hold([jnp.zeros((8, 128), F32)], *x)[0], "core")
+
     combos = merge_experts(one(rep_i), merge_map, merge_coef, source_w, reps)
     mine = trade(combos.reshape((lanes, 2) + combos.shape[1:]))
 
@@ -757,12 +766,14 @@
     (send_hid,) = hold([send_hid], mine)
     hid = trade_rows(send_hid)
     far = swap(mine, "row")
-    pieces = [mine, swap(mine, "core"), far, swap(far, "core")]
     (send_grd,) = hold([send_grd], hid)
     grd = trade_rows(send_grd)
+    (far,) = hold([far], later(hid))
+    pieces = [mine, swap(mine, "core"), far, swap(far, "core")]
     out_rows = run_lane(forward_kernel, one(rep_i), hid, hid, pieces, "lane_forward")
     grd, out_rows = hold([grd, out_rows])
     home_out = trade_rows(out_rows)
+    (grd,) = hold([grd], later(out_rows))
 
     def summed(row):
         first = lane_grads(one(2 * row + 1 - core_i), grd, hid, None, blocks, reps)
@@ -770,33 +781,32 @@
 
     distant, near = summed(1 - row_i), summed(row_i)
     away = swap(distant, "row")
-    (last_grd,) = hold([grd], distant, near)
+    (last_grd,) = hold([grd], later(distant, near))
     back_rows = run_lane(backward_kernel, one(rep_i), last_grd, hid, pieces, "lane_backward")
+    (away,) = hold([away], later(back_rows))
+    home_back = trade_rows(back_rows)
+
+    mixed, token_grad, part = combine(home_out, og, gates, pos, idx_t, rwt, xt)
     total = (near.astype(F32) + away.astype(F32)).astype(BF)
-
-    mixed, token_grad, part = combine(home_out, og, gates, pos, idx_t, rwt, xt)
-    home_back = trade_rows(back_rows)
-    hidden_grad = unplace(home_back, slot_pos)
-
-    (part,) = hold([part], back_rows)
+    (part,) = hold([part], total)
+    part = part.reshape(blocks, 2, 2, part.shape[1]).transpose(2, 1, 0, 3).reshape(part.shape)
     part = add_up(
         part,
         [
+            ("core", 1, core_i),
+            ("row", 1, row_i),
             ("ctx", 4, ctx_i // 4),
             ("ctx", 2, ctx_i // 2 % 2),
             ("ctx", 1, ctx_i % 2),
-            ("row", 1, row_i),
-            ("core", 1, core_i),
         ],
     )
     (total,) = hold([total], home_back)
     arrived = trade(total).reshape(2 * lanes, row_share, width // reps)
+    hidden_grad = unplace(home_back, slot_pos)
     (arrived,) = hold([arrived], hidden_grad, part)
-    dots = coef_dots(one(rep_i), merge_map, source_w, arrived)
-    news = jnp.concatenate([part, dots[:1]], axis=1)
+    dots = coef_dots(one(rep_i), merge_map, part, source_w, arrived, devices)
     news = lax.all_to_all(
-        jnp.broadcast_to(news[None], (devices,) + news.shape), ("ctx", "row", "core"),
-        split_axis=0, concat_axis=0, tiled=True,
+        dots, ("ctx", "row", "core"), split_axis=0, concat_axis=0, tiled=True
     )
     source_w_grad = finish(merge_map, merge_coef, arrived, dots, scale)
     end = part.shape[1]

time: 391 us -> 394 us (level)
  local copies, waits for them, and re-layouts: 10.4 us -> 16.4 us
    all_to_all x6, waiting for transfers between devices: 123 us -> 162 us  [trade(): return lax.all_to_all(x, 'ctx', split_axis=0, concat_axis=0, tiled=True)]
    ppermute x6 -> x10, waiting for transfers between devices: 51.6 us -> 14.2 us  [swap(): return lax.ppermute(x, axis, [(0, 1), (1, 0)])]
  transfers between devices with their start and end apart: 18 -> 22, of which waited for: 10 -> 13; matrix products, arithmetic and copies ran while one was open for 2% -> 3% of each run, Pallas kernels for 17% -> 17%
where the time goes in v7:
time: 394 us; the launch traced here: 393 us
  waiting for transfers between devices  244 us (62%)
  Pallas kernels  82.8 us (21%)
  starting transfers between devices  42.4 us (11%)
  local copies, waits for them, and re-layouts  16.4 us (4%)
  other arithmetic  6.34 us (2%)
    all_to_all x6, waiting for transfers between devices, trade(): return lax.all_to_all(x, 'ctx', split_axis=0, concat_axis=0, tiled=True)  162 us
    ppermute x5, waiting for transfers between devices, add_up(): lax.ppermute(give, axis, [(i, i ^ distance) for i in range(size)])  60.7 us
    all_to_all x6, starting transfers between devices, trade(): return lax.all_to_all(x, 'ctx', split_axis=0, concat_axis=0, tiled=True)  28.6 us
    pallas_call x2, Pallas kernels, run_lane(): pl.pallas_call(kernel, grid=(1,), in_specs=[smem_spec(), pl.BlockSpec((co...  26.1 us
    pallas_call x4, Pallas kernels, lane_grads(): pl.pallas_call(functools.partial(lane_grad_kernel, other is not None), gr...  22.6 us
    ppermute x10, waiting for transfers between devices, swap(): return lax.ppermute(x, axis, [(0, 1), (1, 0)])  14.2 us
  transfers between devices with their start and end apart: 22, of which 13 were waited for; matrix products, arithmetic and copies ran while one was open for 3% of the time, Pallas kernels for 17%

profile of v7, /device:TPU:0, one launch (start us, length us, event | category | flops | bytes accessed | tf_op | source)
XLA Modules:
  0.0 392.6 jit_solution(10027037603917410656)
XLA Ops:
  0.6 5.4 %merge_experts.1._ = bf16[16,192,384]{2,1,0:T(8,128)(2,1)} custom-call(s32[1]{0:T(128)} %bitcast.8.rep_ref._, s32[32]{0:T(128)} %map_ref.5, f32[32]{0:T(128)} %coef_ref.3, bf16[32,192,1536]{2,1,0:T(8,128)(2,1)} %src_ref.3), custom_call_target="tpu_custom_call" | custom-call | flops 5000000000 | bytes 5000000 | tf_op jit(solution)/shard_map/merge_experts/pallas_call | solution.py:272
  6.1 7.3 %all-to-all-start = ((bf16[8,2,192,384]{3,2,1,0:T(8,128)(2,1)}), bf16[8,2,192,384]{3,2,1,0:T(8,128)(2,1)S(1)}, u32[]{:S(2)}, u32[]{:S(2)}) async-start(bf16[8,2,192,384]{3,2,1,0:T(8,128)(2,1)} %bitcast.73), calls=%async_computation | async-start | bytes 4718592 | tf_op jit(solution)/shard_map/all_to_all | solution.py:747
  17.0 7.0 %route.1 = (bf16[640,1664]{1,0:T(8,128)(2,1)}, bf16[640,1536]{1,0:T(8,128)(2,1)}, f32[8,128]{1,0:T(8,128)}, s32[8,128]{1,0:T(8,128)}, s32[8,512]{1,0:T(8,128)}) custom-call(bf16[2880,128]{1,0:T(8,128)(2,1)} %bitcast.82, bf16[32,2880]{1,0:T(8,128)(2,1)} %bitcast.86, f32[1,32]{1,0:T(1,128)} %bitcast.90, s32[4,128]{1,0:T(4,128)} %bitcast.88, s32[1,32]{1,0:T(1,128)} %bitcast.81, ...), custom_call_target="tpu_custom_call" | custom-call | flops 5000000000 | bytes 5000000 | tf_op jit(solution)/shard_map/route/pallas_call | solution.py:406
  24.0 43.2 %all-to-all-done.refs_1_.refs_0_ = bf16[8,2,192,384]{3,2,1,0:T(8,128)(2,1)S(1)} async-done(((bf16[8,2,192,384]{3,2,1,0:T(8,128)(2,1)}), bf16[8,2,192,384]{3,2,1,0:T(8,128)(2,1)S(1)}, u32[]{:S(2)}, u32[]{:S(2)}) %all-to-all-start) | async-done | bytes 2359328 | tf_op jit(solution)/shard_map/all_to_all | solution.py:747
  73.8 47.6 %all-to-all-done.1 = bf16[8,80,1664]{2,1,0:T(8,128)(2,1)S(1)} async-done(((bf16[8,80,1664]{2,1,0:T(8,128)(2,1)}), bf16[8,80,1664]{2,1,0:T(8,128)(2,1)S(1)}, u32[]{:S(2)}, u32[]{:S(2)}) %all-to-all-start.1) | async-done | bytes 2129952 | tf_op jit(solution)/shard_map/all_to_all | solution.py:747
  126.0 5.7 %all-to-all-start.2 = ((bf16[8,80,1536]{2,1,0:T(8,128)(2,1)}), bf16[8,80,1536]{2,1,0:T(8,128)(2,1)S(1)}, u32[]{:S(2)}, u32[]{:S(2)}) async-start(bf16[8,80,1536]{2,1,0:T(8,128)(2,1)} %bitcast.76), calls=%async_computation.2 | async-start | bytes 3932160 | tf_op jit(solution)/shard_map/all_to_all | solution.py:747
  131.8 13.1 %lane_forward.1.refs_1_ = bf16[640,1536]{1,0:T(8,128)(2,1)} custom-call(s32[1]{0:T(128)} %bitcast.8.rep_ref._, bf16[640,1664]{1,0:T(8,128)(2,1)} %bitcast.62, bf16[640,1664]{1,0:T(8,128)(2,1)} %bitcast.63, bf16[8,2,192,384]{3,2,1,0:T(8,128)(2,1)} %copy-done.3, bf16[8,2,192,384]{3,2,1,0:T(8,128)(2,1)} %collective-permute-done.refs_1_, ...), custom_call_target="tpu_custom_call" | custom-call | flops 12000000000 | bytes 12000000 | tf_op jit(solution)/shard_map/lane_forward/pallas_call | solution.py:462
  144.8 33.0 %all-to-all-done.2 = bf16[8,80,1536]{2,1,0:T(8,128)(2,1)S(1)} async-done(((bf16[8,80,1536]{2,1,0:T(8,128)(2,1)}), bf16[8,80,1536]{2,1,0:T(8,128)(2,1)S(1)}, u32[]{:S(2)}, u32[]{:S(2)}) %all-to-all-start.2) | async-done | bytes 1966112 | tf_op jit(solution)/shard_map/all_to_all | solution.py:747
  181.7 5.5 %lane_grads_first.3 = bf16[8,2,192,384]{3,2,1,0:T(8,128)(2,1)} custom-call(s32[1]{0:T(128)} %bitcast.19._, bf16[640,1536]{1,0:T(8,128)(2,1)} %hold.20.grd_ref.refs_0_, bf16[640,1664]{1,0:T(8,128)(2,1)} %bitcast.64, bf16[640,1664]{1,0:T(8,128)(2,1)} %bitcast.65), custom_call_target="tpu_custom_call" | custom-call | flops 6000000000 | bytes 6000000 | tf_op jit(solution)/shard_map/lane_grads_first/pallas_call | solution.py:504
  187.3 5.5 %lane_grads_first.2 = bf16[8,2,192,384]{3,2,1,0:T(8,128)(2,1)} custom-call(s32[1]{0:T(128)} %bitcast.18._, bf16[640,1536]{1,0:T(8,128)(2,1)} %hold.20.grd_ref.refs_0_, bf16[640,1664]{1,0:T(8,128)(2,1)} %bitcast.66, bf16[640,1664]{1,0:T(8,128)(2,1)} %bitcast.67), custom_call_target="tpu_custom_call" | custom-call | flops 6000000000 | bytes 6000000 | tf_op jit(solution)/shard_map/lane_grads_first/pallas_call | solution.py:504
  197.0 5.9 %lane_grads_add.3.refs_2_ = bf16[8,2,192,384]{3,2,1,0:T(8,128)(2,1)} custom-call(s32[1]{0:T(128)} %bitcast.8.rep_ref._, bf16[640,1536]{1,0:T(8,128)(2,1)} %hold.20.grd_ref.refs_0_, bf16[640,1664]{1,0:T(8,128)(2,1)} %bitcast.68, bf16[640,1664]{1,0:T(8,128)(2,1)} %bitcast.69, bf16[8,2,192,384]{3,2,1,0:T(8,128)(2,1)} %collective-permute-done.6.refs_0_), custom_call_target="tpu_custom_call" | custom-call | flops 6000000000 | bytes 6000000 | tf_op jit(solution)/shard_map/lane_grads_add/pallas_call | solution.py:504
  202.8 5.8 %lane_grads_add.2.refs_1_ = bf16[8,2,192,384]{3,2,1,0:T(8,128)(2,1)} custom-call(s32[1]{0:T(128)} %bitcast.17._, bf16[640,1536]{1,0:T(8,128)(2,1)} %hold.20.grd_ref.refs_0_, bf16[640,1664]{1,0:T(8,128)(2,1)} %bitcast.70, bf16[640,1664]{1,0:T(8,128)(2,1)} %bitcast.71, bf16[8,2,192,384]{3,2,1,0:T(8,128)(2,1)} %collective-permute-done.5.refs_0_), custom_call_target="tpu_custom_call" | custom-call | flops 6000000000 | bytes 6000000 | tf_op jit(solution)/shard_map/lane_grads_add/pallas_call | solution.py:504
  211.6 13.0 %lane_backward.1.refs_1_ = bf16[640,1536]{1,0:T(8,128)(2,1)} custom-call(s32[1]{0:T(128)} %bitcast.8.rep_ref._, bf16[640,1536]{1,0:T(8,128)(2,1)} %hold.22.rows_ref, bf16[640,1664]{1,0:T(8,128)(2,1)} %bitcast.72, bf16[8,2,192,384]{3,2,1,0:T(8,128)(2,1)} %copy-done.3, bf16[8,2,192,384]{3,2,1,0:T(8,128)(2,1)} %collective-permute-done.refs_1_, ...), custom_call_target="tpu_custom_call" | custom-call | flops 12000000000 | bytes 12000000 | tf_op jit(solution)/shard_map/lane_backward/pallas_call | solution.py:462
  224.6 18.1 %all-to-all-done.3 = bf16[8,80,1536]{2,1,0:T(8,128)(2,1)S(1)} async-done(((bf16[8,80,1536]{2,1,0:T(8,128)(2,1)}), bf16[8,80,1536]{2,1,0:T(8,128)(2,1)S(1)}, u32[]{:S(2)}, u32[]{:S(2)}) %all-to-all-start.3) | async-done | bytes 1966112 | tf_op jit(solution)/shard_map/all_to_all | solution.py:747
  242.7 4.3 %all-to-all-start.4 = ((bf16[8,80,1536]{2,1,0:T(8,128)(2,1)}), bf16[8,80,1536]{2,1,0:T(8,128)(2,1)}, u32[]{:S(2)}, u32[]{:S(2)}) async-start(bf16[8,80,1536]{2,1,0:T(8,128)(2,1)} %bitcast.75), calls=%async_computation.4 | async-start | bytes 3932160 | tf_op jit(solution)/shard_map/all_to_all | solution.py:747
  247.6 5.0 %combine.1 = (bf16[128,1536]{1,0:T(8,128)(2,1)}, bf16[2880,128]{1,0:T(8,128)(2,1)}, f32[32,3072]{1,0:T(8,128)}) custom-call(bf16[128,1536]{1,0:T(8,128)(2,1)} %bitcast.85, f32[8,128]{1,0:T(8,128)} %get-tuple-element.17.gate_ref, s32[8,128]{1,0:T(8,128)} %get-tuple-element.18.pos_ref, s32[4,128]{1,0:T(4,128)} %bitcast.89, bf16[32,2880]{1,0:T(8,128)(2,1)} %bitcast.87, ...), custom_call_target="tpu_custom_call" | custom-call | flops 5000000000 | bytes 5000000 | tf_op jit(solution)/shard_map/combine/pallas_call | solution.py:566
  252.7 10.6 %collective-permute-done.8.refs_0_ = bf16[8,2,192,384]{3,2,1,0:T(8,128)(2,1)} collective-permute-done((bf16[8,2,192,384]{3,2,1,0:T(8,128)(2,1)}, bf16[8,2,192,384]{3,2,1,0:T(8,128)(2,1)}, u32[]{:S(2)}, u32[]{:S(2)}) %collective-permute-start.8) | collective-permute-done | bytes 2359328 | tf_op jit(solution)/shard_map/ppermute | solution.py:744
  271.7 20.4 %all-to-all-done.4 = bf16[8,80,1536]{2,1,0:T(8,128)(2,1)} async-done(((bf16[8,80,1536]{2,1,0:T(8,128)(2,1)}), bf16[8,80,1536]{2,1,0:T(8,128)(2,1)}, u32[]{:S(2)}, u32[]{:S(2)}) %all-to-all-start.4) | async-done | bytes 1966112 | tf_op jit(solution)/shard_map/all_to_all | solution.py:747
  292.1 3.9 all-to-all-start.5
  298.8 53.2 %collective-permute-done.12 = f32[4,3072]{1,0:T(4,128)S(1)} collective-permute-done((f32[4,3072]{1,0:T(4,128)S(1)}, f32[4,3072]{1,0:T(4,128)S(1)}, u32[]{:S(2)}, u32[]{:S(2)}) %collective-permute-start.12) | collective-permute-done | bytes 49184 | tf_op jit(solution)/shard_map/ppermute | solution.py:717
  360.4 4.1 %unplace.1.refs_1_ = bf16[512,1536]{1,0:T(8,128)(2,1)} custom-call(s32[8,512]{1,0:T(8,128)} %get-tuple-element.23.slot_ref, bf16[640,1536]{1,0:T(8,128)(2,1)} %bitcast.21.back_ref.refs_1_), custom_call_target="tpu_custom_call" | custom-call | flops 5000000000 | bytes 5000000 | tf_op jit(solution)/shard_map/unplace/pallas_call | solution.py:590
  365.9 7.0 %coef_dots.1._ = f32[32,1,3200]{2,1,0:T(1,128)} custom-call(s32[1]{0:T(128)} %bitcast.8.rep_ref._, s32[32]{0:T(128)} %map_ref.5, f32[1,3072]{1,0:T(1,128)} %dynamic-slice_add_fusion.refs_2_.row_ref, bf16[32,192,1536]{2,1,0:T(8,128)(2,1)} %src_ref.3, bf16[16,192,384]{2,1,0:T(8,128)(2,1)} %hold.27.got_ref), custom_call_target="tpu_custom_call" | custom-call | flops 5000000000 | bytes 5000000 | tf_op jit(solution)/shard_map/coef_dots/pallas_call | solution.py:671
  377.8 5.6 %finish.1 = f32[32,192,384]{2,1,0:T(8,128)} custom-call(s32[32]{0:T(128)} %map_ref.5, f32[32]{0:T(128)} %coef_ref.3, f32[32,1,3200]{2,1,0:T(1,128)} %coef_dots.1._, bf16[16,192,384]{2,1,0:T(8,128)(2,1)} %hold.27.got_ref), custom_call_target="tpu_custom_call" | custom-call | flops 5000000000 | bytes 5000000 | tf_op jit(solution)/shard_map/finish/pallas_call | solution.py:692
  383.4 6.5 %all-to-all-done.6 = f32[32,1,3200]{2,1,0:T(1,128)S(1)} async-done(((f32[32,1,3200]{2,1,0:T(1,128)}), f32[32,1,3200]{2,1,0:T(1,128)S(1)}, u32[]{:S(2)}, u32[]{:S(2)}) %all-to-all-start.6) | async-done | bytes 409632 | tf_op jit(solution)/shard_map/all_to_all | solution.py:808
  (94 shorter events, 55.1 us)
Async XLA Ops:
  6.1 61.1 %all-to-all-start = ((bf16[8,2,192,384]{3,2,1,0:T(8,128)(2,1)}), bf16[8,2,192,384]{3,2,1,0:T(8,128)(2,1)S(1)}, u32[]{:S(2)}, u32[]{:S(2)}) async-start(bf16[8,2,192,384]{3,2,1,0:T(8,128)(2,1)} %bitcast.73), calls=%async_computation | async-start | bytes 4718592 | tf_op jit(solution)/shard_map/all_to_all | solution.py:747
  68.6 52.8 %all-to-all-start.1 = ((bf16[8,80,1664]{2,1,0:T(8,128)(2,1)}), bf16[8,80,1664]{2,1,0:T(8,128)(2,1)S(1)}, u32[]{:S(2)}, u32[]{:S(2)}) async-start(bf16[8,80,1664]{2,1,0:T(8,128)(2,1)} %bitcast.74), calls=%async_computation.1 | async-start | bytes 4259840 | tf_op jit(solution)/shard_map/all_to_all | solution.py:747
  72.2 53.2 %collective-permute-start.1 = (bf16[8,2,192,384]{3,2,1,0:T(8,128)(2,1)}, bf16[8,2,192,384]{3,2,1,0:T(8,128)(2,1)}, u32[]{:S(2)}, u32[]{:S(2)}) collective-permute-start(bf16[8,2,192,384]{3,2,1,0:T(8,128)(2,1)} %copy-done.3), channel_id=1, source_target_pairs={{0,2},{2,0},{1,3},{3,1},{4,6},{6,4},{5,7},{7,5},{8,10},{10,8},{9,1... | collective-permute-start | bytes 7077896 | tf_op jit(solution)/shard_map/ppermute | solution.py:744
  122.7 2.7 collective-permute-start.2
  122.7 9.1 %collective-permute-start = (bf16[8,2,192,384]{3,2,1,0:T(8,128)(2,1)}, bf16[8,2,192,384]{3,2,1,0:T(8,128)(2,1)}, u32[]{:S(2)}, u32[]{:S(2)}) collective-permute-start(bf16[8,2,192,384]{3,2,1,0:T(8,128)(2,1)} %copy-done.3), channel_id=1, source_target_pairs={{0,1},{1,0},{2,3},{3,2},{4,5},{5,4},{6,7},{7,6},{8,9},{9,8},{10,11... | collective-permute-start | bytes 7077896 | tf_op jit(solution)/shard_map/ppermute | solution.py:744
  126.0 5.7 %collective-permute-start.3 = (bf16[8,2,192,384]{3,2,1,0:T(8,128)(2,1)}, bf16[8,2,192,384]{3,2,1,0:T(8,128)(2,1)}, u32[]{:S(2)}, u32[]{:S(2)}) collective-permute-start(bf16[8,2,192,384]{3,2,1,0:T(8,128)(2,1)} %hold.17.refs_2_), channel_id=1, source_target_pairs={{0,1},{1,0},{2,3},{3,2},{4,5},{5,4},{6,7},{7,6},{8,9},{9,8},{10,11... | collective-permute-start | bytes 7077896 | tf_op jit(solution)/shard_map/ppermute | solution.py:744
  126.0 51.8 %all-to-all-start.2 = ((bf16[8,80,1536]{2,1,0:T(8,128)(2,1)}), bf16[8,80,1536]{2,1,0:T(8,128)(2,1)S(1)}, u32[]{:S(2)}, u32[]{:S(2)}) async-start(bf16[8,80,1536]{2,1,0:T(8,128)(2,1)} %bitcast.76), calls=%async_computation.2 | async-start | bytes 3932160 | tf_op jit(solution)/shard_map/all_to_all | solution.py:747
  179.7 1.4 collective-permute-start.4
  187.2 9.8 %collective-permute-start.6 = (bf16[8,2,192,384]{3,2,1,0:T(8,128)(2,1)}, bf16[8,2,192,384]{3,2,1,0:T(8,128)(2,1)}, u32[]{:S(2)}, u32[]{:S(2)}) collective-permute-start(bf16[8,2,192,384]{3,2,1,0:T(8,128)(2,1)} %lane_grads_first.3), channel_id=1, source_target_pairs={{0,1},{1,0},{2,3},{3,2},{4,5},{5,4},{6,7},{7,6},{8,9},{9,8},{10,11... | collective-permute-start | bytes 7077896 | tf_op jit(solution)/shard_map/ppermute | solution.py:744
  192.8 10.1 %collective-permute-start.5 = (bf16[8,2,192,384]{3,2,1,0:T(8,128)(2,1)}, bf16[8,2,192,384]{3,2,1,0:T(8,128)(2,1)}, u32[]{:S(2)}, u32[]{:S(2)}) collective-permute-start(bf16[8,2,192,384]{3,2,1,0:T(8,128)(2,1)} %lane_grads_first.2), channel_id=1, source_target_pairs={{0,1},{1,0},{2,3},{3,2},{4,5},{5,4},{6,7},{7,6},{8,9},{9,8},{10,11... | collective-permute-start | bytes 7077896 | tf_op jit(solution)/shard_map/ppermute | solution.py:744
  193.1 49.6 %all-to-all-start.3 = ((bf16[8,80,1536]{2,1,0:T(8,128)(2,1)}), bf16[8,80,1536]{2,1,0:T(8,128)(2,1)S(1)}, u32[]{:S(2)}, u32[]{:S(2)}) async-start(bf16[8,80,1536]{2,1,0:T(8,128)(2,1)} %bitcast.14), calls=%async_computation.3 | async-start | bytes 3932160 | tf_op jit(solution)/shard_map/all_to_all | solution.py:747
  209.3 1.7 collective-permute-start.7
  209.4 53.8 %collective-permute-start.8 = (bf16[8,2,192,384]{3,2,1,0:T(8,128)(2,1)}, bf16[8,2,192,384]{3,2,1,0:T(8,128)(2,1)}, u32[]{:S(2)}, u32[]{:S(2)}) collective-permute-start(bf16[8,2,192,384]{3,2,1,0:T(8,128)(2,1)} %lane_grads_add.2.refs_1_), channel_id=1, source_target_pairs={{0,2},{2,0},{1,3},{3,1},{4,6},{6,4},{5,7},{7,5},{8,10},{10,8},{9,1... | collective-permute-start | bytes 7077896 | tf_op jit(solution)/shard_map/ppermute | solution.py:744
  242.7 49.4 %all-to-all-start.4 = ((bf16[8,80,1536]{2,1,0:T(8,128)(2,1)}), bf16[8,80,1536]{2,1,0:T(8,128)(2,1)}, u32[]{:S(2)}, u32[]{:S(2)}) async-start(bf16[8,80,1536]{2,1,0:T(8,128)(2,1)} %bitcast.75), calls=%async_computation.4 | async-start | bytes 3932160 | tf_op jit(solution)/shard_map/all_to_all | solution.py:747
  247.6 5.1 %collective-permute-start.9 = (f32[8,128]{1,0:T(8,128)}, f32[8,128]{1,0:T(8,128)S(1)}, u32[]{:S(2)}, u32[]{:S(2)}) collective-permute-start(f32[8,128]{1,0:T(8,128)} %hold.23), channel_id=1, source_target_pairs={{0,1},{1,0},{2,3},{3,2},{4,5},{5,4},{6,7},{7,6},{8,9},{9,8},{10,11... | collective-permute-start | bytes 12296 | tf_op jit(solution)/shard_map/ppermute | solution.py:744
  252.7 10.6 %copy-start.4 = (bf16[8,2,192,384]{3,2,1,0:T(8,128)(2,1)S(1)}, bf16[8,2,192,384]{3,2,1,0:T(8,128)(2,1)}, u32[]{:S(2)}) copy-start(bf16[8,2,192,384]{3,2,1,0:T(8,128)(2,1)} %lane_grads_add.3.refs_2_) | copy-start | bytes 7077892
  252.7 10.6 %copy-start.9 = (f32[8,128]{1,0:T(8,128)}, f32[8,128]{1,0:T(8,128)S(1)}, u32[]{:S(2)}) copy-start(f32[8,128]{1,0:T(8,128)S(1)} %collective-permute-done.9.refs_1_) | copy-start | bytes 12292
  268.5 1.5 collective-permute-start.10
  270.1 25.9 %collective-permute-start.11 = (f32[8,3072]{1,0:T(8,128)S(1)}, f32[8,3072]{1,0:T(8,128)S(1)}, u32[]{:S(2)}, u32[]{:S(2)}) collective-permute-start(f32[8,3072]{1,0:T(8,128)S(1)} %dynamic-slice_bitcast_fusion.1), channel_id=1, source_target_pairs={{0,2},{2,0},{1,3},{3,1},{4,6},{6,4},{5,7},{7,5},{8,10},{10,8},{9,1... | collective-permute-start | bytes 294920 | tf_op jit(solution)/shard_map/ppermute | solution.py:717
  292.1 72.4 %all-to-all-start.5 = ((bf16[8,2,192,384]{3,2,1,0:T(8,128)(2,1)}), bf16[8,2,192,384]{3,2,1,0:T(8,128)(2,1)S(1)}, u32[]{:S(2)}, u32[]{:S(2)}) async-start(bf16[8,2,192,384]{3,2,1,0:T(8,128)(2,1)} %hold.26), calls=%async_computation.5 | async-start | bytes 4718592 | tf_op jit(solution)/shard_map/all_to_all | solution.py:747
  296.1 55.9 %collective-permute-start.12 = (f32[4,3072]{1,0:T(4,128)S(1)}, f32[4,3072]{1,0:T(4,128)S(1)}, u32[]{:S(2)}, u32[]{:S(2)}) collective-permute-start(f32[4,3072]{1,0:T(4,128)S(1)} %dynamic-slice_bitcast_fusion.2), channel_id=1, source_target_pairs={{0,16},{4,20},{8,24},{12,28},{16,0},{20,4},{24,8},{28,12},{1,17},{... | collective-permute-start | bytes 147464 | tf_op jit(solution)/shard_map/ppermute | solution.py:717
  352.0 3.9 collective-permute-start.13
  356.0 3.8 collective-permute-start.14
  372.9 17.1 %all-to-all-start.6 = ((f32[32,1,3200]{2,1,0:T(1,128)}), f32[32,1,3200]{2,1,0:T(1,128)S(1)}, u32[]{:S(2)}, u32[]{:S(2)}) async-start(f32[32,1,3200]{2,1,0:T(1,128)} %coef_dots.1._), calls=%async_computation.6 | async-start | bytes 819200 | tf_op jit(solution)/shard_map/all_to_all | solution.py:808
  (9 other events, 22.7 us)

commit v8 on v2

--- a/solution.py
+++ b/solution.py
@@ -211,6 +211,10 @@
 TILE = 256
 
 
+def cost(us):
+    return pl.CostEstimate(flops=us * 10**9, bytes_accessed=us * 10**6, transcendentals=0)
+
+
 def any_spec():
     return pl.BlockSpec(memory_space=pl.ANY)
 
@@ -231,8 +235,7 @@
     return lax.dot_general(a, b, (dims, ((), ())), preferred_element_type=F32)
 
 
-def merge_kernel(map_ref, coef_ref, place_ref, src_ref, out_ref, order_ref, count_ref, held, sems):
-    halves, places = out_ref.shape[:2]
+def merge_start(map_ref, place_ref, src_ref, places, order_ref, count_ref, held, sems):
     half = held.shape[2]
     expert_order(map_ref, order_ref, count_ref)
     at = pl.ds(pl.multiple_of(place_ref[1] * half, half), half)
@@ -248,6 +251,11 @@
                     pltpu.make_async_copy(src_ref.at[expert, :, at], held.at[i], sems.at[i])
                 )
                 copies[-1].start()
+    return copies, experts
+
+
+def merge_finish(copies, experts, coef_ref, held, out_ref):
+    halves, places = out_ref.shape[:2]
     for j in range(places):
         for m in range(2):
             i = 4 * j + 2 * m
@@ -270,25 +278,6 @@
         n = count_ref[g]
         order_ref[2 * g + n] = e
         count_ref[g] = n + 1
-
-
-def merge_experts(where_am_i, merge_map, merge_coef, source_w, places):
-    count, rows, width = source_w.shape
-    half = width // 2
-    return pl.pallas_call(
-        merge_kernel,
-        in_specs=[smem_spec(), smem_spec(), smem_spec(), any_spec()],
-        out_specs=vmem_spec(),
-        out_shape=jax.ShapeDtypeStruct((2, places, 2, rows, half), BF),
-        scratch_shapes=[
-            pltpu.SMEM((count,), I32),
-            pltpu.SMEM((count // 2,), I32),
-            pltpu.VMEM((4 * places, rows, half), BF),
-            pltpu.SemaphoreType.DMA((4 * places,)),
-        ],
-        compiler_params=params(56),
-        name="merge_experts",
-    )(merge_map, merge_coef, where_am_i, source_w)
 
 
 def hbm_spec():
@@ -324,18 +313,16 @@
     return lax.broadcasted_iota(I32, (sources, tok), 0) == idx_ref[k : k + 1, :]
 
 
-def place_rows(refs, at, rows):
-    each = refs[0].shape[0]
-    rows = rows.astype(BF)
-    for d, ref in enumerate(refs):
-        ref[:, at : at + rows.shape[1]] = rows[d * each : (d + 1) * each]
-
-
-def route_kernel(
+def prepare_kernel(
     capacity, lanes,
-    me_ref, xt_ref, rwt_ref, rb_ref, idx_ref, map_ref, hid_ref, og_ref, _, *refs
+    combo_ref, coef_ref, place_ref, src_ref,
+    xt_ref, rwt_ref, rb_ref, idx_ref, map_ref, hid_ref, og_ref,
+    merged_ref, send_ref, gate_ref, pos_ref, slot_ref,
+    order_ref, count_ref, held, sems,
 ):
-    sends, (gate_ref, pos_ref, slot_ref) = refs[:-3], refs[-3:]
+    copies, experts = merge_start(
+        combo_ref, place_ref, src_ref, merged_ref.shape[1], order_ref, count_ref, held, sems
+    )
     top, tok = idx_ref.shape
     sources = rwt_ref.shape[0]
     slots, width = hid_ref.shape
@@ -354,7 +341,6 @@
     gates = [r / total for r in raised]
     lane = [jnp.right_shift(g, 1) for g in merged]
     member = [jnp.bitwise_and(g, 1) for g in merged]
-    partner = [jnp.bitwise_xor(l, me_ref[0]) for l in lane]
     onehot = [(lax.broadcasted_iota(I32, (lanes, tok), 0) == l).astype(F32) for l in lane]
     all_hot = onehot[0]
     for k in range(1, top):
@@ -367,7 +353,7 @@
     for k in range(top):
         rank = jnp.sum(before * onehot[k], axis=0, keepdims=True).astype(I32)
         before = before + onehot[k]
-        position.append(jnp.where(rank < capacity, partner[k] * capacity + rank, -1))
+        position.append(jnp.where(rank < capacity, lane[k] * capacity + rank, -1))
     gate_ref[...] = jnp.zeros_like(gate_ref)
     pos_ref[...] = jnp.full_like(pos_ref, -1)
     for k in range(top):
@@ -396,11 +382,11 @@
     take = lax.broadcasted_iota(I32, (places, slots), 0) == slot_pos
     placed = jnp.sum(jnp.where(take, spot[3:4].astype(F32), 0.0), axis=1, keepdims=True)
     depth = og_ref.shape[1]
-    place_rows(sends, depth + width, jnp.broadcast_to(placed, (places, 128)))
+    send_ref[:, depth + width :] = jnp.broadcast_to(placed, (places, 128)).astype(BF)
     take = take.astype(BF)
     for n in range(0, width, TILE):
         rows = jnp.dot(take, hid_ref[:, n : n + TILE], preferred_element_type=F32)
-        place_rows(sends, depth + n, rows)
+        send_ref[:, depth + n : depth + n + TILE] = rows.astype(BF)
     takes = [
         (lax.broadcasted_iota(I32, (places, tok), 0) == position[k]).astype(BF) for k in range(top)
     ]
@@ -410,25 +396,67 @@
         rows = jnp.zeros((places, TILE), F32)
         for k in range(top):
             rows = rows + jnp.dot(takes[k], (columns[k] * og).astype(BF), preferred_element_type=F32)
-        place_rows(sends, n, rows)
-
-
-def route(me, xt, rwt, router_b, idx_t, merge_map, hid, og, after, capacity, lanes):
+        send_ref[:, n : n + TILE] = rows.astype(BF)
+    merge_finish(copies, experts, coef_ref, held, merged_ref)
+
+
+def prepare(
+    place, merge_map, merge_coef, source_w, xt, rwt, router_b, idx_t, hid, og, capacity, lanes
+):
+    count, rows, whole = source_w.shape
     slots, width = hid.shape
     tok = idx_t.shape[1]
+    half, places = whole // 2, lanes // 2
     return pl.pallas_call(
-        functools.partial(route_kernel, capacity, lanes),
-        in_specs=[smem_spec()] + [vmem_spec()] * 7 + [any_spec()],
-        out_specs=[vmem_spec()] * (lanes + 3),
-        out_shape=[jax.ShapeDtypeStruct((capacity, og.shape[1] + width + 128), BF)] * lanes
-        + [
+        functools.partial(prepare_kernel, capacity, lanes),
+        in_specs=[smem_spec()] * 3 + [any_spec()] + [vmem_spec()] * 7,
+        out_specs=[vmem_spec()] * 5,
+        out_shape=[
+            jax.ShapeDtypeStruct((2, places, 2, rows, half), BF),
+            jax.ShapeDtypeStruct((lanes * capacity, og.shape[1] + width + 128), BF),
             jax.ShapeDtypeStruct((8, tok), F32),
             jax.ShapeDtypeStruct((8, tok), I32),
             jax.ShapeDtypeStruct((8, slots), I32),
         ],
+        scratch_shapes=[
+            pltpu.SMEM((count,), I32),
+            pltpu.SMEM((count // 2,), I32),
+            pltpu.VMEM((4 * places, rows, half), BF),
+            pltpu.SemaphoreType.DMA((4 * places,)),
+        ],
         compiler_params=params(56),
-        name="route",
-    )(me, xt, rwt, router_b[None, :], idx_t, merge_map[None, :], hid, og, after)
+        cost_estimate=cost(10),
+        name="prepare",
+    )(
+        merge_map, merge_coef, place, source_w,
+        xt, rwt, router_b[None, :], idx_t, merge_map[None, :], hid, og,
+    )
+
+
+def assemble_kernel(me_ref, *refs):
+    parts, (out_ref, sems) = refs[:-2], refs[-2:]
+    each = parts[0].shape[0]
+    copies = []
+    for d, part in enumerate(parts):
+        at = pl.ds(pl.multiple_of(jnp.bitwise_xor(me_ref[0], d) * each, each), each)
+        copies.append(pltpu.make_async_copy(part, out_ref.at[at, :], sems.at[d]))
+        copies[-1].start()
+    for copy in copies:
+        copy.wait()
+
+
+def assemble(me, parts):
+    each, width = parts[0].shape
+    return pl.pallas_call(
+        assemble_kernel,
+        in_specs=[smem_spec()] + [any_spec()] * len(parts),
+        out_specs=vmem_spec(),
+        out_shape=jax.ShapeDtypeStruct((each * len(parts), width), BF),
+        scratch_shapes=[pltpu.SemaphoreType.DMA((len(parts),))],
+        compiler_params=params(56),
+        cost_estimate=cost(2),
+        name="assemble",
+    )(me, *parts)
 
 
 def load_weights(core_ref, mine, other, w_ref, sems):
@@ -449,63 +477,62 @@
         copy.wait()
 
 
-def forward_kernel(core_ref, rows_ref, flag_ref, mine, other, *refs):
-    outs, (w_ref, sems) = refs[:-2], refs[-2:]
+def lane_kernel(
+    core_ref, me_ref, grd_ref, hid_ref, flag_ref, mine, other, *refs
+):
+    outs, (keep, w_ref, sems) = refs[:-3], refs[-3:]
     load_weights(core_ref, mine, other, w_ref, sems)
-    half = w_ref.shape[3]
-    member = flag_ref[:, :1].astype(F32)
-
-    for n in range(0, w_ref.shape[2], TILE):
+    half, depth = w_ref.shape[3], w_ref.shape[2]
+    first = flag_ref[:, :1].astype(F32) == 0.0
+    for n in range(0, depth, TILE):
         at = slice(n, n + TILE)
         both = [
-            dot(rows_ref[:, :half], w_ref[0, m, at, :], ((1,), (1,)))
-            + dot(rows_ref[:, half : 2 * half], w_ref[1, m, at, :], ((1,), (1,)))
+            dot(hid_ref[:, :half], w_ref[0, m, at, :], ((1,), (1,)))
+            + dot(hid_ref[:, half:], w_ref[1, m, at, :], ((1,), (1,)))
             for m in range(2)
         ]
-        place_rows(outs, n, jnp.where(member == 0.0, both[0], both[1]))
-
-
-def backward_kernel(core_ref, rows_ref, flag_ref, mine, other, *refs):
-    outs, (w_ref, sems) = refs[:-2], refs[-2:]
-    load_weights(core_ref, mine, other, w_ref, sems)
-    half = w_ref.shape[3]
-    member = flag_ref[:, :1].astype(F32)
+        keep[:, at] = jnp.where(first, both[0], both[1]).astype(BF)
     for h in range(2):
         for n in range(0, half, TILE):
             at = slice(n, n + TILE)
-            both = [dot(rows_ref[...], w_ref[h, m, :, at], ((1,), (0,))) for m in range(2)]
-            place_rows(outs, h * half + n, jnp.where(member == 0.0, both[0], both[1]))
-
-
-def run_lane(kernel, core, rows, which, mine, other, lanes, name):
+            both = [dot(grd_ref[...], w_ref[h, m, :, at], ((1,), (0,))) for m in range(2)]
+            to = depth + h * half + n
+            keep[:, to : to + TILE] = jnp.where(first, both[0], both[1]).astype(BF)
+    each = outs[0].shape[0]
+    for d, out_ref in enumerate(outs):
+        at = pl.ds(pl.multiple_of(jnp.bitwise_xor(me_ref[0], d) * each, each), each)
+        out_ref[...] = keep[at, :]
+
+
+def run_lane(core, me, rows, mine, other, lanes):
     blocks, members, share, half = mine.shape
     depth = share * blocks
     count = rows.shape[0]
     wide = (rows.shape[1] - 128) // 2
+    part = (count // lanes, 2 * wide)
     return pl.pallas_call(
-        kernel,
+        lane_kernel,
         grid=(1,),
         in_specs=[
             smem_spec(),
-            pl.BlockSpec((count, wide), lambda i: (0, which)),
+            smem_spec(),
+            pl.BlockSpec((count, wide), lambda i: (0, 0)),
+            pl.BlockSpec((count, wide), lambda i: (0, 1)),
             pl.BlockSpec((count, 128), lambda i: (0, 2 * wide // 128)),
-            hbm_spec(),
-            hbm_spec(),
+            any_spec(),
+            any_spec(),
         ],
-        out_specs=[pl.BlockSpec((count // lanes, wide), lambda i: (0, 0))] * lanes,
-        out_shape=[jax.ShapeDtypeStruct((count // lanes, wide), BF)] * lanes,
+        out_specs=[pl.BlockSpec(part, lambda i: (0, 0))] * lanes,
+        out_shape=[jax.ShapeDtypeStruct(part, BF)] * lanes,
         scratch_shapes=[
+            pltpu.VMEM((count, 2 * wide), BF),
             pltpu.VMEM((2, members, depth, half), BF),
             pltpu.SemaphoreType.DMA((2 * blocks,)),
         ],
-        compiler_params=params(56),
-        cost_estimate=pl.CostEstimate(
-            flops=4 * count * depth * 2 * half,
-            bytes_accessed=4 * members * depth * half + 8 * count * half,
-            transcendentals=0,
-        ),
-        name=name,
-    )(core, rows, rows, mine, other)
+        compiler_params=params(60),
+        cost_estimate=cost(20),
+        name="lane_products",
+    )(core, me, rows, rows, rows, mine, other)
 
 
 def lane_grad_kernel(has_other, _, grd_ref, hid_ref, flag_ref, *refs):
@@ -544,24 +571,14 @@
         ),
         out_shape=jax.ShapeDtypeStruct(shape, BF),
         compiler_params=params(56),
-        cost_estimate=pl.CostEstimate(
-            flops=8 * count * width * cols,
-            bytes_accessed=8 * width * cols + 4 * count * width,
-            transcendentals=0,
-        ),
+        cost_estimate=cost(8),
         name="lane_grads_add" if extra else "lane_grads_first",
     )(core, rows, rows, rows, *extra)
 
 
-def gather_rows(refs, keep):
-    each = refs[0].shape[0]
-    for d, ref in enumerate(refs):
-        keep[d * each : (d + 1) * each, :] = ref[...]
-
-
-def combine_kernel(og_ref, gate_ref, pos_ref, idx_ref, rwt_ref, xt_ref, *refs):
-    homes, (mixed_ref, tg_ref, part_ref, out_ref) = refs[:-4], refs[-4:]
-    gather_rows(homes, out_ref)
+def combine_kernel(
+    og_ref, gate_ref, pos_ref, idx_ref, rwt_ref, xt_ref, out_ref, mixed_ref, tg_ref, part_ref
+):
     places, width = out_ref.shape
     top, tok = idx_ref.shape
     sources, features = rwt_ref.shape
@@ -598,27 +615,29 @@
     part_ref[:, last:] = jnp.broadcast_to(bias, (sources, 128))
 
 
-def combine(homes, og, gates, pos, idx_t, rwt, xt):
+def combine(home, og, gates, pos, idx_t, rwt, xt):
     sources, features = rwt.shape
-    tok = idx_t.shape[1]
+    tok, width = og.shape
+    whole = lambda a: pl.BlockSpec(a.shape, lambda i: (0, 0))
+    outs = [
+        jax.ShapeDtypeStruct(og.shape, BF),
+        jax.ShapeDtypeStruct((features, tok), BF),
+        jax.ShapeDtypeStruct((sources, (features + 127) // 128 * 128 + 128), F32),
+    ]
     return pl.pallas_call(
         combine_kernel,
-        in_specs=[vmem_spec()] * (6 + len(homes)),
-        out_specs=[vmem_spec()] * 3,
-        out_shape=[
-            jax.ShapeDtypeStruct(og.shape, BF),
-            jax.ShapeDtypeStruct((features, tok), BF),
-            jax.ShapeDtypeStruct((sources, (features + 127) // 128 * 128 + 128), F32),
-        ],
-        scratch_shapes=[pltpu.VMEM((len(homes) * homes[0].shape[0], homes[0].shape[1]), BF)],
+        grid=(1,),
+        in_specs=[whole(a) for a in (og, gates, pos, idx_t, rwt, xt)]
+        + [pl.BlockSpec((home.shape[0], width), lambda i: (0, 0))],
+        out_specs=[whole(a) for a in outs],
+        out_shape=outs,
         compiler_params=params(56),
+        cost_estimate=cost(5),
         name="combine",
-    )(og, gates, pos, idx_t, rwt, xt, *homes)
-
-
-def unplace_kernel(slot_ref, *refs):
-    homes, (out_ref, back_ref) = refs[:-2], refs[-2:]
-    gather_rows(homes, back_ref)
+    )(og, gates, pos, idx_t, rwt, xt, home)
+
+
+def unplace_kernel(slot_ref, back_ref, out_ref):
     places, width = back_ref.shape
     slots = slot_ref.shape[1]
     take = (lax.broadcasted_iota(I32, (places, slots), 0) == slot_ref[0:1, :]).astype(BF)
@@ -626,17 +645,22 @@
         out_ref[:, n : n + TILE] = dot(take, back_ref[:, n : n + TILE], ((0,), (0,))).astype(BF)
 
 
-def unplace(homes, slot_pos):
-    rows, width = homes[0].shape
+def unplace(home, slot_pos):
+    places, width = home.shape[0], home.shape[1] // 2
+    slots = slot_pos.shape[1]
     return pl.pallas_call(
         unplace_kernel,
-        in_specs=[vmem_spec()] * (1 + len(homes)),
-        out_specs=vmem_spec(),
-        out_shape=jax.ShapeDtypeStruct((slot_pos.shape[1], width), BF),
-        scratch_shapes=[pltpu.VMEM((len(homes) * rows, width), BF)],
+        grid=(1,),
+        in_specs=[
+            pl.BlockSpec(slot_pos.shape, lambda i: (0, 0)),
+            pl.BlockSpec((places, width), lambda i: (0, 1)),
+        ],
+        out_specs=pl.BlockSpec((slots, width), lambda i: (0, 0)),
+        out_shape=jax.ShapeDtypeStruct((slots, width), BF),
         compiler_params=params(56),
+        cost_estimate=cost(4),
         name="unplace",
-    )(slot_pos, *homes)
+    )(slot_pos, home)
 
 
 def coef_kernel(rep_ref, map_ref, src_ref, got_ref, out_ref, order_ref, count_ref, held, weights, sems):
@@ -735,23 +759,9 @@
             pltpu.SemaphoreType.DMA((count,)),
         ],
         compiler_params=params(56),
-        cost_estimate=pl.CostEstimate(
-            flops=4 * count * rows * cols,
-            bytes_accessed=8 * count * rows * cols,
-            transcendentals=0,
-        ),
+        cost_estimate=cost(8),
         name="finish",
     )(merge_map, merge_coef, arrived, after)
-
-
-def add_up(x, bits):
-    for axis, distance, bit in bits:
-        x = x.reshape((2, x.shape[0] // 2) + x.shape[1:])
-        keep = lax.dynamic_index_in_dim(x, bit, 0, keepdims=False)
-        give = lax.dynamic_index_in_dim(x, 1 - bit, 0, keepdims=False)
-        size = lax.axis_size(axis)
-        x = keep + lax.ppermute(give, axis, [(i, i ^ distance) for i in range(size)])
-    return x
 
 
 def swap(x):
@@ -783,62 +793,54 @@
     def stack(numbers):
         return jnp.stack([jnp.asarray(n, I32) for n in numbers])
 
-    combos = merge_experts(stack([row_i, core_i]), merge_map, merge_coef, source_w, places)
-    mine = lax.all_to_all(
-        combos.reshape((blocks,) + combos.shape[2:]), ("half", "place"),
-        split_axis=0, concat_axis=0, tiled=True,
-    )
+    def later(*x):
+        return swap(hold([jnp.zeros((8, 128), F32)], *x)[0])
+
+    def trade(x, axes):
+        return lax.all_to_all(x, axes, split_axis=0, concat_axis=0, tiled=True)
 
     xt = tokens.reshape(tok, features).T
     rwt = router_w.T
     idx_t = teacher_idx.reshape(tok, top).T
     og = out_grad.reshape(tok, depth)
-    *parts, gates, pos, slot_pos = route(
-        stack([2 * place_i + row_i]), xt, rwt, router_b, idx_t, merge_map,
-        hidden.reshape(tok * top, width), og, combos, capacity, lanes,
-    )
-
-    def trade(parts):
-        return [parts[0]] + [
-            lax.ppermute(parts[d], ("place", "row"), [(i, i ^ d) for i in range(lanes)])
-            for d in range(1, lanes)
-        ]
-
-    rows = jnp.concatenate(trade(parts), axis=0)
+    combos, send_rows, gates, pos, slot_pos = prepare(
+        stack([row_i, core_i]), merge_map, merge_coef, source_w,
+        xt, rwt, router_b, idx_t, hidden.reshape(tok * top, width), og, capacity, lanes,
+    )
+    rows = trade(send_rows.reshape(lanes, capacity, send_rows.shape[1]), ("place", "row"))
+    rows = rows.reshape(send_rows.shape)
+    (combos,) = hold([combos.reshape((blocks,) + combos.shape[2:])], rows)
+    mine = trade(combos, ("half", "place"))
+    (rows,) = hold([rows], later(rows))
     here = stack([core_i])
     first = lane_grads(stack([1 - core_i]), rows, None, blocks, reps)
     summed = lane_grads(here, rows, swap(first), blocks, reps)
-    arrived = lax.all_to_all(
-        summed.reshape(2 * blocks, 2, row_share, width // reps),
-        ("half", "place", "row"), split_axis=0, concat_axis=0, tiled=True,
-    )
-
     (mine,) = hold([mine], summed)
+    (summed,) = hold([summed], mine)
+    arrived = trade(
+        summed.reshape(2 * blocks, 2, row_share, width // reps), ("half", "place", "row")
+    )
+
     other = swap(mine)
-    out_parts = run_lane(forward_kernel, here, rows, 1, mine, other, lanes, "lane_forward")
-    home_out = trade(out_parts)
-    back_parts = run_lane(backward_kernel, here, rows, 0, mine, other, lanes, "lane_backward")
-    mixed, token_grad, part = combine(home_out, og, gates, pos, idx_t, rwt, xt)
-    hidden_grad = unplace(trade(back_parts), slot_pos)
-
-    part = add_up(
-        part,
-        [
-            ("half", 1, half_i),
-            ("place", 2, place_i // 2),
-            ("place", 1, place_i % 2),
-            ("row", 1, row_i),
-            ("core", 1, core_i),
+    me = stack([2 * place_i + row_i])
+    (rows,) = hold([rows], later(summed))
+    parts = run_lane(here, me, rows, mine, other, lanes)
+    home = assemble(
+        me,
+        [parts[0]]
+        + [
+            lax.ppermute(parts[d], ("place", "row"), [(i, i ^ d) for i in range(lanes)])
+            for d in range(1, lanes)
         ],
     )
-    (arrived,) = hold([arrived], hidden_grad, part)
+    mixed, token_grad, part = combine(home, og, gates, pos, idx_t, rwt, xt)
+    part, arrived = hold([part, arrived])
+    part = jnp.sum(trade(part[:, None, :], everyone), axis=0)
+    hidden_grad = unplace(home, slot_pos)
     arrived = arrived.reshape(2, 2 * lanes, row_share, width // reps)
     dots = coef_dots(stack([2 * row_i + core_i]), merge_map, source_w, arrived)
     news = jnp.concatenate([part, dots[:1]], axis=1)
-    news = lax.all_to_all(
-        jnp.broadcast_to(news[None], (devices,) + news.shape), everyone,
-        split_axis=0, concat_axis=0, tiled=True,
-    )
+    news = trade(jnp.broadcast_to(news[None], (devices,) + news.shape), everyone)
     source_w_grad = finish(merge_map, merge_coef, arrived, dots, scale)
     end = part.shape[1]
     return (

time: 407 us -> 372 us (0.914)
  waiting for transfers between devices: 245 us -> 182 us
  blocking collectives: 0 us -> 54.7 us
  starting transfers between devices: 57.2 us -> 37.8 us
  Pallas kernels: 79.8 us -> 75.6 us
    ppermute x26 -> x7, waiting for transfers between devices: 229 us -> 89.3 us  [on_pairs(): lax.ppermute(parts[d], ('place', 'row'), [(i, i ^ d) for i in range(lanes)])]
    all_to_all x3 -> x4, waiting for transfers between devices: 6.44 us -> 76.8 us  [trade(): return lax.all_to_all(x, axes, split_axis=0, concat_axis=0, tiled=True)]
    all_to_all x0 -> x1, blocking collectives: none -> 54.7 us  [trade(): return lax.all_to_all(x, axes, split_axis=0, concat_axis=0, tiled=True)]
    ppermute x26 -> x7, starting transfers between devices: 41.5 us -> 8.04 us  [on_pairs(): lax.ppermute(parts[d], ('place', 'row'), [(i, i ^ d) for i in range(lanes)])]
    all_to_all x3 -> x4, starting transfers between devices: 15.4 us -> 29 us  [trade(): return lax.all_to_all(x, axes, split_axis=0, concat_axis=0, tiled=True)]
    ppermute x2 -> x4, waiting for transfers between devices: 9.32 us -> 16 us  [swap(): return lax.ppermute(x, 'core', [(0, 1), (1, 0)])]
    unnamed x44 -> x21, local copies, waits for them, and re-layouts: 10.2 us -> 4.85 us
    pallas_call x6 -> x5, Pallas kernels: 48.3 us -> 44.2 us  [the longest x1 20.3 us: run_lane(): pl.pallas_call(lane_kernel, grid=(1,), in_specs=[smem_spec(), smem_spec()...]
  transfers between devices with their start and end apart: 31 -> 15, of which waited for: 20 -> 10; matrix products, arithmetic and copies ran while one was open for 3% -> 2% of each run, Pallas kernels for 14% -> 18%
where the time goes in v8:
time: 372 us; the launch traced here: 371 us
  waiting for transfers between devices  182 us (49%)
  Pallas kernels  75.6 us (20%)
  blocking collectives  54.7 us (15%)
  starting transfers between devices  37.8 us (10%)
  local copies, waits for them, and re-layouts  17.4 us (5%)
    ppermute x7, waiting for transfers between devices, on_pairs(): lax.ppermute(parts[d], ('place', 'row'), [(i, i ^ d) for i in range(lanes)])  89.3 us
    all_to_all x4, waiting for transfers between devices, trade(): return lax.all_to_all(x, axes, split_axis=0, concat_axis=0, tiled=True)  76.8 us
    all_to_all x1, blocking collectives, trade(): return lax.all_to_all(x, axes, split_axis=0, concat_axis=0, tiled=True)  54.7 us
    all_to_all x4, starting transfers between devices, trade(): return lax.all_to_all(x, axes, split_axis=0, concat_axis=0, tiled=True)  29 us
    pallas_call x1, Pallas kernels, run_lane(): pl.pallas_call(lane_kernel, grid=(1,), in_specs=[smem_spec(), smem_spec()...  20.3 us
    pallas_call x2, Pallas kernels, lane_grads(): pl.pallas_call(functools.partial(lane_grad_kernel, other is not None), gr...  17.6 us
    ppermute x4, waiting for transfers between devices, swap(): return lax.ppermute(x, 'core', [(0, 1), (1, 0)])  16 us
    pallas_call x1, Pallas kernels, prepare(): pl.pallas_call(functools.partial(prepare_kernel, capacity, lanes), in_spe...  10.6 us
  transfers between devices with their start and end apart: 15, of which 10 were waited for; matrix products, arithmetic and copies ran while one was open for 2% of the time, Pallas kernels for 18%

profile of v8, /device:TPU:0, one launch (start us, length us, event | category | flops | bytes accessed | tf_op | source)
XLA Modules:
  0.0 371.2 jit_solution(8641373996942313591)
XLA Ops:
  0.6 3.7 reshape.61.hid_ref
  4.9 10.6 %prepare.1 = (bf16[2,4,2,192,768]{4,3,2,1,0:T(8,128)(2,1)}, bf16[640,3200]{1,0:T(8,128)(2,1)}, f32[8,128]{1,0:T(8,128)}, s32[8,128]{1,0:T(8,128)}, s32[8,512]{1,0:T(8,128)}) custom-call(s32[32]{0:T(128)} %a.1, f32[32]{0:T(128)} %b.1, s32[2]{0:T(128)} %pad_add_fusion.place_ref, bf16[32,192,1536]{2,1,0:T(8,128)(2,1)} %src_ref.3, bf16[2880,128]{1,0:T(8,128)(2,1)} %bitcast.41, ...), custom_call_target="tpu_custom_call" | custom-call | flops 10000000000 | bytes 10000000 | tf_op jit(solution)/shard_map/prepare/pallas_call | solution.py:410
  15.6 54.7 %all_to_all.25 = bf16[8,80,3200]{2,1,0:T(8,128)(2,1)} all-to-all(bf16[8,80,3200]{2,1,0:T(8,128)(2,1)} %bitcast.36), channel_id=1, replica_groups=mesh['half'=2,'place'=4,'row'=2,'core'=2] {'place','row'}, dimensions={0} | all-to-all | bytes 8192000 | tf_op jit(solution)/shard_map/all_to_all | solution.py:800
  70.3 4.6 %all-to-all-start.1 = ((bf16[8,2,192,768]{3,2,1,0:T(8,128)(2,1)}), bf16[8,2,192,768]{3,2,1,0:T(8,128)(2,1)}, u32[]{:S(2)}, u32[]{:S(2)}) async-start(bf16[8,2,192,768]{3,2,1,0:T(8,128)(2,1)} %hold.10), calls=%async_computation.1 | async-start | bytes 9437184 | tf_op jit(solution)/shard_map/all_to_all | solution.py:800
  77.5 8.4 %lane_grads_first.1 = bf16[8,2,2,192,384]{4,3,2,1,0:T(8,128)(2,1)} custom-call(s32[1]{0:T(128)} %bitcast.13._, bf16[640,3200]{1,0:T(8,128)(2,1)} %hold.9.grd_ref.hid_ref.flag_ref.refs_0_, bf16[640,3200]{1,0:T(8,128)(2,1)} %hold.9.grd_ref.hid_ref.flag_ref.refs_0_, bf16[640,3200]{1,0:T(8,128)(2,1)} %hold.9.grd_ref.hid_ref.flag_ref.refs_0_), custom_call_target="tpu_custom_call" | custom-call | flops 8000000000 | bytes 8000000 | tf_op jit(solution)/shard_map/lane_grads_first/pallas_call | solution.py:559
  86.0 8.0 %collective-permute-done.1.refs_0_ = bf16[8,2,2,192,384]{4,3,2,1,0:T(8,128)(2,1)S(1)} collective-permute-done((bf16[8,2,2,192,384]{4,3,2,1,0:T(8,128)(2,1)}, bf16[8,2,2,192,384]{4,3,2,1,0:T(8,128)(2,1)S(1)}, u32[]{:S(2)}, u32[]{:S(2)}) %collective-permute-start.1) | collective-permute-done | bytes 4718624 | tf_op jit(solution)/shard_map/ppermute | solution.py:768
  96.1 9.1 %lane_grads_add.1.refs_1_.refs_0_ = bf16[8,2,2,192,384]{4,3,2,1,0:T(8,128)(2,1)} custom-call(s32[1]{0:T(128)} %bitcast.2._.core_ref, bf16[640,3200]{1,0:T(8,128)(2,1)} %hold.9.grd_ref.hid_ref.flag_ref.refs_0_, bf16[640,3200]{1,0:T(8,128)(2,1)} %hold.9.grd_ref.hid_ref.flag_ref.refs_0_, bf16[640,3200]{1,0:T(8,128)(2,1)} %hold.9.grd_ref.hid_ref.flag_ref.refs_0_, ...), custom_call_target="tpu_custom_call" | custom-call | flops 8000000000 | bytes 8000000 | tf_op jit(solution)/shard_map/lane_grads_add/pallas_call | solution.py:559
  105.3 72.7 %all-to-all-done.1.refs_0_ = bf16[8,2,192,768]{3,2,1,0:T(8,128)(2,1)} async-done(((bf16[8,2,192,768]{3,2,1,0:T(8,128)(2,1)}), bf16[8,2,192,768]{3,2,1,0:T(8,128)(2,1)}, u32[]{:S(2)}, u32[]{:S(2)}) %all-to-all-start.1) | async-done | bytes 4718624 | tf_op jit(solution)/shard_map/all_to_all | solution.py:800
  178.0 4.7 %all-to-all-start.2 = ((bf16[16,2,192,384]{3,2,1,0:T(8,128)(2,1)}), bf16[16,2,192,384]{3,2,1,0:T(8,128)(2,1)}, u32[]{:S(2)}, u32[]{:S(2)}) async-start(bf16[16,2,192,384]{3,2,1,0:T(8,128)(2,1)} %bitcast.34), calls=%async_computation.2 | async-start | bytes 9437184 | tf_op jit(solution)/shard_map/all_to_all | solution.py:800
  183.9 6.7 %collective-permute-done.2.refs_1_ = f32[8,128]{1,0:T(8,128)S(1)} collective-permute-done((f32[8,128]{1,0:T(8,128)}, f32[8,128]{1,0:T(8,128)S(1)}, u32[]{:S(2)}, u32[]{:S(2)}) %collective-permute-start.2) | collective-permute-done | bytes 4128 | tf_op jit(solution)/shard_map/ppermute | solution.py:768
  191.2 20.3 %lane_products.1 = (bf16[80,3072]{1,0:T(8,128)(2,1)}, bf16[80,3072]{1,0:T(8,128)(2,1)}, bf16[80,3072]{1,0:T(8,128)(2,1)}, bf16[80,3072]{1,0:T(8,128)(2,1)}, bf16...) custom-call(s32[1]{0:T(128)} %bitcast.2._.core_ref, ...), custom_call_target="tpu_custom_call" | custom-call | flops 20000000000 | bytes 20000000 | tf_op jit(solution)/shard_map/lane_products/pallas_call | solution.py:513
  211.5 3.5 collective-permute-start.10
  219.0 57.8 %collective-permute-done.10.refs_7_ = bf16[80,3072]{1,0:T(8,128)(2,1)S(1)} collective-permute-done((bf16[80,3072]{1,0:T(8,128)(2,1)}, bf16[80,3072]{1,0:T(8,128)(2,1)S(1)}, u32[]{:S(2)}, u32[]{:S(2)}) %collective-permute-start.10) | collective-permute-done | bytes 491552 | tf_op jit(solution)/shard_map/ppermute | solution.py:832
  277.3 7.8 %collective-permute-done.4.refs_1_ = bf16[80,3072]{1,0:T(8,128)(2,1)S(1)} collective-permute-done((bf16[80,3072]{1,0:T(8,128)(2,1)}, bf16[80,3072]{1,0:T(8,128)(2,1)S(1)}, u32[]{:S(2)}, u32[]{:S(2)}) %collective-permute-start.4) | collective-permute-done | bytes 491552 | tf_op jit(solution)/shard_map/ppermute | solution.py:832
  286.9 12.6 %collective-permute-done.8.refs_5_ = bf16[80,3072]{1,0:T(8,128)(2,1)S(1)} collective-permute-done((bf16[80,3072]{1,0:T(8,128)(2,1)}, bf16[80,3072]{1,0:T(8,128)(2,1)S(1)}, u32[]{:S(2)}, u32[]{:S(2)}) %collective-permute-start.8) | collective-permute-done | bytes 491552 | tf_op jit(solution)/shard_map/ppermute | solution.py:832
  299.5 9.4 %collective-permute-done.9.refs_6_ = bf16[80,3072]{1,0:T(8,128)(2,1)S(1)} collective-permute-done((bf16[80,3072]{1,0:T(8,128)(2,1)}, bf16[80,3072]{1,0:T(8,128)(2,1)S(1)}, u32[]{:S(2)}, u32[]{:S(2)}) %collective-permute-start.9) | collective-permute-done | bytes 491552 | tf_op jit(solution)/shard_map/ppermute | solution.py:832
  309.7 4.1 %assemble.1.out_ref.back_ref = bf16[640,3072]{1,0:T(8,128)(2,1)} custom-call(s32[1]{0:T(128)} %bitcast.10.me_ref, bf16[80,3072]{1,0:T(8,128)(2,1)} %get-tuple-element.29.refs_0_, bf16[80,3072]{1,0:T(8,128)(2,1)} %copy-done.1, bf16[80,3072]{1,0:T(8,128)(2,1)} %copy-done.2, bf16[80,3072]{1,0:T(8,128)(2,1)} %copy-done.3, bf16[80,3072]{1,0:T(8,128)(2,1)} %copy-done.4, ...), custom_call_target="tpu_custom_call" | custom-call | flops 2000000000 | bytes 2000000 | tf_op jit(solution)/shard_map/assemble/pallas_call | solution.py:450
  313.7 5.1 %combine.1 = (bf16[128,1536]{1,0:T(8,128)(2,1)}, bf16[2880,128]{1,0:T(8,128)(2,1)}, f32[32,3072]{1,0:T(8,128)}) custom-call(bf16[128,1536]{1,0:T(8,128)(2,1)} %bitcast.44, f32[8,128]{1,0:T(8,128)} %get-tuple-element.25.gate_ref, s32[8,128]{1,0:T(8,128)} %get-tuple-element.26.pos_ref, s32[4,128]{1,0:T(4,128)} %bitcast.48, bf16[32,2880]{1,0:T(8,128)(2,1)} %bitcast.46, ...), custom_call_target="tpu_custom_call" | custom-call | flops 5000000000 | bytes 5000000 | tf_op jit(solution)/shard_map/combine/pallas_call | solution.py:627
  320.9 17.0 %all-to-all-start.3 = ((f32[32,1,3072]{2,1,0:T(1,128)}), f32[32,1,3072]{2,1,0:T(1,128)S(1)}, u32[]{:S(2)}, u32[]{:S(2)}) async-start(f32[32,1,3072]{2,1,0:T(1,128)} %copy.25), calls=%async_computation.3 | async-start | bytes 786432 | tf_op jit(solution)/shard_map/all_to_all | solution.py:800
  338.0 8.2 %coef_dots.1._ = f32[8,128]{1,0:T(8,128)} custom-call(s32[1]{0:T(128)} %bitcast.21.rep_ref, s32[32]{0:T(128)} %a.1, bf16[32,192,1536]{2,1,0:T(8,128)(2,1)} %src_ref.3, bf16[2,16,192,384]{3,2,1,0:T(8,128)(2,1)} %bitcast.22.got_ref.c), custom_call_target="tpu_custom_call" | custom-call | tf_op jit(solution)/shard_map/coef_dots/pallas_call | solution.py:728
  346.8 4.1 %all-to-all-done.3 = f32[32,1,3072]{2,1,0:T(1,128)S(1)} async-done(((f32[32,1,3072]{2,1,0:T(1,128)}), f32[32,1,3072]{2,1,0:T(1,128)S(1)}, u32[]{:S(2)}, u32[]{:S(2)}) %all-to-all-start.3) | async-done | bytes 393248 | tf_op jit(solution)/shard_map/all_to_all | solution.py:800
  354.8 4.2 %unplace.1 = bf16[512,1536]{1,0:T(8,128)(2,1)} custom-call(s32[8,512]{1,0:T(8,128)} %get-tuple-element.38.slot_ref, bf16[640,3072]{1,0:T(8,128)(2,1)} %assemble.1.out_ref.back_ref), custom_call_target="tpu_custom_call" | custom-call | flops 4000000000 | bytes 4000000 | tf_op jit(solution)/shard_map/unplace/pallas_call | solution.py:651
  359.0 3.8 %reshape.66 = bf16[1,128,4,1536]{3,2,1,0:T(4,128)(2,1)} reshape(bf16[512,1536]{1,0:T(8,128)(2,1)} %unplace.1) | data formatting | bytes 3145728 | tf_op jit(solution)/shard_map/reshape | solution.py:848
  362.8 5.7 %finish.1 = f32[32,192,384]{2,1,0:T(8,128)} custom-call(s32[32]{0:T(128)} %a.1, f32[32]{0:T(128)} %b.1, bf16[2,16,192,384]{3,2,1,0:T(8,128)(2,1)} %bitcast.22.got_ref.c, f32[8,128]{1,0:T(8,128)} %coef_dots.1._), custom_call_target="tpu_custom_call" | custom-call | flops 8000000000 | bytes 8000000 | tf_op jit(solution)/shard_map/finish/pallas_call | solution.py:748
  (59 shorter events, 23.7 us)
Async XLA Ops:
  70.3 107.7 %all-to-all-start.1 = ((bf16[8,2,192,768]{3,2,1,0:T(8,128)(2,1)}), bf16[8,2,192,768]{3,2,1,0:T(8,128)(2,1)}, u32[]{:S(2)}, u32[]{:S(2)}) async-start(bf16[8,2,192,768]{3,2,1,0:T(8,128)(2,1)} %hold.10), calls=%async_computation.1 | async-start | bytes 9437184 | tf_op jit(solution)/shard_map/all_to_all | solution.py:800
  75.5 1.4 collective-permute-start
  76.9 0.6 copy-start.8
  85.9 8.1 %collective-permute-start.1 = (bf16[8,2,2,192,384]{4,3,2,1,0:T(8,128)(2,1)}, bf16[8,2,2,192,384]{4,3,2,1,0:T(8,128)(2,1)S(1)}, u32[]{:S(2)}, u32[]{:S(2)}) collective-permute-start(bf16[8,2,2,192,384]{4,3,2,1,0:T(8,128)(2,1)} %lane_grads_first.1), channel_id=1, source_target_pairs={{0,1},{1,0},{2,3},{3,2},{4,5},{5,4},{6,7},{7,6},{8,9},{9,8},{10,11... | collective-permute-start | bytes 14155784 | tf_op jit(solution)/shard_map/ppermute | solution.py:768
  94.0 2.1 copy-start.9
  178.0 140.8 %all-to-all-start.2 = ((bf16[16,2,192,384]{3,2,1,0:T(8,128)(2,1)}), bf16[16,2,192,384]{3,2,1,0:T(8,128)(2,1)}, u32[]{:S(2)}, u32[]{:S(2)}) async-start(bf16[16,2,192,384]{3,2,1,0:T(8,128)(2,1)} %bitcast.34), calls=%async_computation.2 | async-start | bytes 9437184 | tf_op jit(solution)/shard_map/all_to_all | solution.py:800
  182.7 8.4 %collective-permute-start.3 = (bf16[8,2,192,768]{3,2,1,0:T(8,128)(2,1)}, bf16[8,2,192,768]{3,2,1,0:T(8,128)(2,1)}, u32[]{:S(2)}, u32[]{:S(2)}) collective-permute-start(bf16[8,2,192,768]{3,2,1,0:T(8,128)(2,1)} %hold.11.refs_1_.mine), channel_id=1, source_target_pairs={{0,1},{1,0},{2,3},{3,2},{4,5},{5,4},{6,7},{7,6},{8,9},{9,8},{10,11... | collective-permute-start | bytes 14155784 | tf_op jit(solution)/shard_map/ppermute | solution.py:768
  183.4 7.1 %collective-permute-start.2 = (f32[8,128]{1,0:T(8,128)}, f32[8,128]{1,0:T(8,128)S(1)}, u32[]{:S(2)}, u32[]{:S(2)}) collective-permute-start(f32[8,128]{1,0:T(8,128)} %hold.13), channel_id=1, source_target_pairs={{0,1},{1,0},{2,3},{3,2},{4,5},{5,4},{6,7},{7,6},{8,9},{9,8},{10,11... | collective-permute-start | bytes 12296 | tf_op jit(solution)/shard_map/ppermute | solution.py:768
  211.5 65.3 %collective-permute-start.10 = (bf16[80,3072]{1,0:T(8,128)(2,1)}, bf16[80,3072]{1,0:T(8,128)(2,1)S(1)}, u32[]{:S(2)}, u32[]{:S(2)}) collective-permute-start(bf16[80,3072]{1,0:T(8,128)(2,1)} %get-tuple-element.36), channel_id=1, source_target_pairs={{0,14},{2,12},{4,10},{6,8},{8,6},{10,4},{12,2},{14,0},{1,15},{3,13... | collective-permute-start | bytes 1474568 | tf_op jit(solution)/shard_map/ppermute | solution.py:832
  214.9 70.2 %collective-permute-start.4 = (bf16[80,3072]{1,0:T(8,128)(2,1)}, bf16[80,3072]{1,0:T(8,128)(2,1)S(1)}, u32[]{:S(2)}, u32[]{:S(2)}) collective-permute-start(bf16[80,3072]{1,0:T(8,128)(2,1)} %get-tuple-element.30), channel_id=1, source_target_pairs={{0,2},{2,0},{4,6},{6,4},{8,10},{10,8},{12,14},{14,12},{1,3},{3,1},... | collective-permute-start | bytes 1474568 | tf_op jit(solution)/shard_map/ppermute | solution.py:832
  215.5 69.6 %collective-permute-start.5 = (bf16[80,3072]{1,0:T(8,128)(2,1)}, bf16[80,3072]{1,0:T(8,128)(2,1)S(1)}, u32[]{:S(2)}, u32[]{:S(2)}) collective-permute-start(bf16[80,3072]{1,0:T(8,128)(2,1)} %get-tuple-element.31), channel_id=1, source_target_pairs={{0,4},{2,6},{4,0},{6,2},{8,12},{10,14},{12,8},{14,10},{1,5},{3,7},... | collective-permute-start | bytes 1474568 | tf_op jit(solution)/shard_map/ppermute | solution.py:832
  216.1 69.1 %collective-permute-start.6 = (bf16[80,3072]{1,0:T(8,128)(2,1)}, bf16[80,3072]{1,0:T(8,128)(2,1)S(1)}, u32[]{:S(2)}, u32[]{:S(2)}) collective-permute-start(bf16[80,3072]{1,0:T(8,128)(2,1)} %get-tuple-element.32), channel_id=1, source_target_pairs={{0,6},{2,4},{4,2},{6,0},{8,14},{10,12},{12,10},{14,8},{1,7},{3,5},... | collective-permute-start | bytes 1474568 | tf_op jit(solution)/shard_map/ppermute | solution.py:832
  218.4 68.5 %collective-permute-start.7 = (bf16[80,3072]{1,0:T(8,128)(2,1)}, bf16[80,3072]{1,0:T(8,128)(2,1)S(1)}, u32[]{:S(2)}, u32[]{:S(2)}) collective-permute-start(bf16[80,3072]{1,0:T(8,128)(2,1)} %get-tuple-element.33), channel_id=1, source_target_pairs={{0,8},{2,10},{4,12},{6,14},{8,0},{10,2},{12,4},{14,6},{1,9},{3,11}... | collective-permute-start | bytes 1474568 | tf_op jit(solution)/shard_map/ppermute | solution.py:832
  276.8 32.1 %copy-start = (bf16[80,3072]{1,0:T(8,128)(2,1)}, bf16[80,3072]{1,0:T(8,128)(2,1)S(1)}, u32[]{:S(2)}) copy-start(bf16[80,3072]{1,0:T(8,128)(2,1)S(1)} %collective-permute-done.10.refs_7_) | copy-start | bytes 1474564
  276.8 22.7 %collective-permute-start.8 = (bf16[80,3072]{1,0:T(8,128)(2,1)}, bf16[80,3072]{1,0:T(8,128)(2,1)S(1)}, u32[]{:S(2)}, u32[]{:S(2)}) collective-permute-start(bf16[80,3072]{1,0:T(8,128)(2,1)} %get-tuple-element.34), channel_id=1, source_target_pairs={{0,10},{2,8},{4,14},{6,12},{8,2},{10,0},{12,6},{14,4},{1,11},{3,9}... | collective-permute-start | bytes 1474568 | tf_op jit(solution)/shard_map/ppermute | solution.py:832
  285.1 23.8 %copy-start.1 = (bf16[80,3072]{1,0:T(8,128)(2,1)}, bf16[80,3072]{1,0:T(8,128)(2,1)S(1)}, u32[]{:S(2)}) copy-start(bf16[80,3072]{1,0:T(8,128)(2,1)S(1)} %collective-permute-done.4.refs_1_) | copy-start | bytes 1474564
  285.1 23.8 %collective-permute-start.9 = (bf16[80,3072]{1,0:T(8,128)(2,1)}, bf16[80,3072]{1,0:T(8,128)(2,1)S(1)}, u32[]{:S(2)}, u32[]{:S(2)}) collective-permute-start(bf16[80,3072]{1,0:T(8,128)(2,1)} %get-tuple-element.35), channel_id=1, source_target_pairs={{0,12},{2,14},{4,8},{6,10},{8,4},{10,6},{12,0},{14,2},{1,13},{3,15... | collective-permute-start | bytes 1474568 | tf_op jit(solution)/shard_map/ppermute | solution.py:832
  285.1 23.8 %copy-start.2 = (bf16[80,3072]{1,0:T(8,128)(2,1)}, bf16[80,3072]{1,0:T(8,128)(2,1)S(1)}, u32[]{:S(2)}) copy-start(bf16[80,3072]{1,0:T(8,128)(2,1)S(1)} %collective-permute-done.5.refs_2_) | copy-start | bytes 1474564
  285.1 23.8 %copy-start.3 = (bf16[80,3072]{1,0:T(8,128)(2,1)}, bf16[80,3072]{1,0:T(8,128)(2,1)S(1)}, u32[]{:S(2)}) copy-start(bf16[80,3072]{1,0:T(8,128)(2,1)S(1)} %collective-permute-done.6.refs_3_) | copy-start | bytes 1474564
  286.9 22.0 %copy-start.4 = (bf16[80,3072]{1,0:T(8,128)(2,1)}, bf16[80,3072]{1,0:T(8,128)(2,1)S(1)}, u32[]{:S(2)}) copy-start(bf16[80,3072]{1,0:T(8,128)(2,1)S(1)} %collective-permute-done.7.refs_4_) | copy-start | bytes 1474564
  299.5 9.4 %copy-start.5 = (bf16[80,3072]{1,0:T(8,128)(2,1)}, bf16[80,3072]{1,0:T(8,128)(2,1)S(1)}, u32[]{:S(2)}) copy-start(bf16[80,3072]{1,0:T(8,128)(2,1)S(1)} %collective-permute-done.8.refs_5_) | copy-start | bytes 1474564
  308.9 0.8 copy-start.6
  320.9 30.0 %all-to-all-start.3 = ((f32[32,1,3072]{2,1,0:T(1,128)}), f32[32,1,3072]{2,1,0:T(1,128)S(1)}, u32[]{:S(2)}, u32[]{:S(2)}) async-start(f32[32,1,3072]{2,1,0:T(1,128)} %copy.25), calls=%async_computation.3 | async-start | bytes 786432 | tf_op jit(solution)/shard_map/all_to_all | solution.py:800
  352.2 16.4 %all-to-all-start.4 = ((f32[32,1,3200]{2,1,0:T(1,128)}), f32[32,1,3200]{2,1,0:T(1,128)S(1)}, u32[]{:S(2)}, u32[]{:S(2)}) async-start(f32[32,1,3200]{2,1,0:T(1,128)} %broadcast_in_dim.21), calls=%async_computation.4 | async-start | bytes 819200 | tf_op jit(solution)/shard_map/all_to_all | solution.py:800
  (1 other events, 0.6 us)

commit v9 on v8

--- a/solution.py
+++ b/solution.py
@@ -349,16 +349,18 @@
         lax.broadcasted_iota(I32, (tok, tok), 0) < lax.broadcasted_iota(I32, (tok, tok), 1)
     ).astype(BF)
     before = jnp.dot(all_hot.astype(BF), earlier, preferred_element_type=F32)
-    position = []
+    position, back = [], []
     for k in range(top):
         rank = jnp.sum(before * onehot[k], axis=0, keepdims=True).astype(I32)
         before = before + onehot[k]
         position.append(jnp.where(rank < capacity, lane[k] * capacity + rank, -1))
+        partner = jnp.bitwise_xor(lane[k], place_ref[2])
+        back.append(jnp.where(rank < capacity, partner * capacity + rank, -1))
     gate_ref[...] = jnp.zeros_like(gate_ref)
     pos_ref[...] = jnp.full_like(pos_ref, -1)
     for k in range(top):
         gate_ref[k : k + 1, :] = gates[k]
-        pos_ref[k : k + 1, :] = position[k]
+        pos_ref[k : k + 1, :] = back[k]
     spot = jnp.zeros((8, slots), F32)
     for k in range(top):
         spread = (
@@ -367,8 +369,8 @@
         ).astype(BF)
         kept = position[k] >= 0
         parts = [
-            jnp.where(kept, jnp.right_shift(position[k], 5), 0),
-            jnp.where(kept, jnp.bitwise_and(position[k], 31), 0),
+            jnp.where(kept, lane[k], 0),
+            jnp.where(kept, position[k] - lane[k] * capacity, 0),
             jnp.where(kept, 1, 0),
             member[k],
         ]
@@ -377,8 +379,10 @@
         ).astype(BF)
         spot = spot + jnp.dot(stacked, spread, preferred_element_type=F32)
     spot = spot.astype(I32)
-    slot_pos = jnp.where(spot[2:3] > 0, spot[0:1] * 32 + spot[1:2], -1)
-    slot_ref[...] = jnp.broadcast_to(slot_pos, slot_ref.shape)
+    slot_pos = jnp.where(spot[2:3] > 0, spot[0:1] * capacity + spot[1:2], -1)
+    partner = jnp.bitwise_xor(spot[0:1], place_ref[2])
+    slot_back = jnp.where(spot[2:3] > 0, partner * capacity + spot[1:2], -1)
+    slot_ref[...] = jnp.broadcast_to(slot_back, slot_ref.shape)
     take = lax.broadcasted_iota(I32, (places, slots), 0) == slot_pos
     placed = jnp.sum(jnp.where(take, spot[3:4].astype(F32), 0.0), axis=1, keepdims=True)
     depth = og_ref.shape[1]
@@ -433,30 +437,10 @@
     )
 
 
-def assemble_kernel(me_ref, *refs):
-    parts, (out_ref, sems) = refs[:-2], refs[-2:]
-    each = parts[0].shape[0]
-    copies = []
-    for d, part in enumerate(parts):
-        at = pl.ds(pl.multiple_of(jnp.bitwise_xor(me_ref[0], d) * each, each), each)
-        copies.append(pltpu.make_async_copy(part, out_ref.at[at, :], sems.at[d]))
-        copies[-1].start()
-    for copy in copies:
-        copy.wait()
-
-
-def assemble(me, parts):
-    each, width = parts[0].shape
-    return pl.pallas_call(
-        assemble_kernel,
-        in_specs=[smem_spec()] + [any_spec()] * len(parts),
-        out_specs=vmem_spec(),
-        out_shape=jax.ShapeDtypeStruct((each * len(parts), width), BF),
-        scratch_shapes=[pltpu.SemaphoreType.DMA((len(parts),))],
-        compiler_params=params(56),
-        cost_estimate=cost(2),
-        name="assemble",
-    )(me, *parts)
+def gather_rows(refs, keep):
+    each = refs[0].shape[0]
+    for d, ref in enumerate(refs):
+        keep[d * each : (d + 1) * each, :] = ref[...]
 
 
 def load_weights(core_ref, mine, other, w_ref, sems):
@@ -576,9 +560,9 @@
     )(core, rows, rows, rows, *extra)
 
 
-def combine_kernel(
-    og_ref, gate_ref, pos_ref, idx_ref, rwt_ref, xt_ref, out_ref, mixed_ref, tg_ref, part_ref
-):
+def combine_kernel(og_ref, gate_ref, pos_ref, idx_ref, rwt_ref, xt_ref, *refs):
+    homes, (mixed_ref, tg_ref, part_ref, out_ref) = refs[:-4], refs[-4:]
+    gather_rows(homes, out_ref)
     places, width = out_ref.shape
     top, tok = idx_ref.shape
     sources, features = rwt_ref.shape
@@ -609,35 +593,39 @@
     logit_half = logit_grad.astype(BF)
     tg_ref[...] = dot(rwt_ref[...], logit_half, ((0,), (0,))).astype(BF)
     part_ref[...] = jnp.zeros_like(part_ref)
-    part_ref[:, :features] = dot(logit_half, xt_ref[...], ((1,), (1,)))
+    part_ref[:, 0, :features] = dot(logit_half, xt_ref[...], ((1,), (1,)))
     bias = jnp.sum(logit_grad, axis=1, keepdims=True)
-    last = part_ref.shape[1] - 128
-    part_ref[:, last:] = jnp.broadcast_to(bias, (sources, 128))
-
-
-def combine(home, og, gates, pos, idx_t, rwt, xt):
+    last = part_ref.shape[2] - 128
+    part_ref[:, 0, last:] = jnp.broadcast_to(bias, (sources, 128))
+
+
+def combine(homes, og, gates, pos, idx_t, rwt, xt):
     sources, features = rwt.shape
     tok, width = og.shape
-    whole = lambda a: pl.BlockSpec(a.shape, lambda i: (0, 0))
+    each = homes[0].shape[0]
+    whole = lambda a: pl.BlockSpec(a.shape, lambda i: (0,) * len(a.shape))
     outs = [
         jax.ShapeDtypeStruct(og.shape, BF),
         jax.ShapeDtypeStruct((features, tok), BF),
-        jax.ShapeDtypeStruct((sources, (features + 127) // 128 * 128 + 128), F32),
+        jax.ShapeDtypeStruct((sources, 1, (features + 127) // 128 * 128 + 128), F32),
     ]
     return pl.pallas_call(
         combine_kernel,
         grid=(1,),
         in_specs=[whole(a) for a in (og, gates, pos, idx_t, rwt, xt)]
-        + [pl.BlockSpec((home.shape[0], width), lambda i: (0, 0))],
+        + [pl.BlockSpec((each, width), lambda i: (0, 0))] * len(homes),
         out_specs=[whole(a) for a in outs],
         out_shape=outs,
+        scratch_shapes=[pltpu.VMEM((len(homes) * each, width), BF)],
         compiler_params=params(56),
         cost_estimate=cost(5),
         name="combine",
-    )(og, gates, pos, idx_t, rwt, xt, home)
-
-
-def unplace_kernel(slot_ref, back_ref, out_ref):
+    )(og, gates, pos, idx_t, rwt, xt, *homes)
+
+
+def unplace_kernel(slot_ref, *refs):
+    homes, (out_ref, back_ref) = refs[:-2], refs[-2:]
+    gather_rows(homes, back_ref)
     places, width = back_ref.shape
     slots = slot_ref.shape[1]
     take = (lax.broadcasted_iota(I32, (places, slots), 0) == slot_ref[0:1, :]).astype(BF)
@@ -645,22 +633,21 @@
         out_ref[:, n : n + TILE] = dot(take, back_ref[:, n : n + TILE], ((0,), (0,))).astype(BF)
 
 
-def unplace(home, slot_pos):
-    places, width = home.shape[0], home.shape[1] // 2
+def unplace(homes, slot_pos):
+    each, width = homes[0].shape[0], homes[0].shape[1] // 2
     slots = slot_pos.shape[1]
     return pl.pallas_call(
         unplace_kernel,
         grid=(1,),
-        in_specs=[
-            pl.BlockSpec(slot_pos.shape, lambda i: (0, 0)),
-            pl.BlockSpec((places, width), lambda i: (0, 1)),
-        ],
+        in_specs=[pl.BlockSpec(slot_pos.shape, lambda i: (0, 0))]
+        + [pl.BlockSpec((each, width), lambda i: (0, 1))] * len(homes),
         out_specs=pl.BlockSpec((slots, width), lambda i: (0, 0)),
         out_shape=jax.ShapeDtypeStruct((slots, width), BF),
+        scratch_shapes=[pltpu.VMEM((len(homes) * each, width), BF)],
         compiler_params=params(56),
         cost_estimate=cost(4),
         name="unplace",
-    )(slot_pos, home)
+    )(slot_pos, *homes)
 
 
 def coef_kernel(rep_ref, map_ref, src_ref, got_ref, out_ref, order_ref, count_ref, held, weights, sems):
@@ -804,7 +791,7 @@
     idx_t = teacher_idx.reshape(tok, top).T
     og = out_grad.reshape(tok, depth)
     combos, send_rows, gates, pos, slot_pos = prepare(
-        stack([row_i, core_i]), merge_map, merge_coef, source_w,
+        stack([row_i, core_i, 2 * place_i + row_i]), merge_map, merge_coef, source_w,
         xt, rwt, router_b, idx_t, hidden.reshape(tok * top, width), og, capacity, lanes,
     )
     rows = trade(send_rows.reshape(lanes, capacity, send_rows.shape[1]), ("place", "row"))
@@ -825,27 +812,24 @@
     me = stack([2 * place_i + row_i])
     (rows,) = hold([rows], later(summed))
     parts = run_lane(here, me, rows, mine, other, lanes)
-    home = assemble(
-        me,
-        [parts[0]]
-        + [
-            lax.ppermute(parts[d], ("place", "row"), [(i, i ^ d) for i in range(lanes)])
-            for d in range(1, lanes)
-        ],
-    )
+    home = [parts[0]] + [
+        lax.ppermute(parts[d], ("place", "row"), [(i, i ^ d) for i in range(lanes)])
+        for d in range(1, lanes)
+    ]
     mixed, token_grad, part = combine(home, og, gates, pos, idx_t, rwt, xt)
     part, arrived = hold([part, arrived])
-    part = jnp.sum(trade(part[:, None, :], everyone), axis=0)
-    hidden_grad = unplace(home, slot_pos)
+    part = jnp.sum(trade(part, everyone), axis=0)
+    hidden_grad = unplace(home, slot_pos).reshape(1, tok, top, width)
     arrived = arrived.reshape(2, 2 * lanes, row_share, width // reps)
     dots = coef_dots(stack([2 * row_i + core_i]), merge_map, source_w, arrived)
     news = jnp.concatenate([part, dots[:1]], axis=1)
+    (news,) = hold([news], hidden_grad)
     news = trade(jnp.broadcast_to(news[None], (devices,) + news.shape), everyone)
     source_w_grad = finish(merge_map, merge_coef, arrived, dots, scale)
     end = part.shape[1]
     return (
         mixed.reshape(1, tok, depth),
-        hidden_grad.reshape(1, tok, top, width),
+        hidden_grad,
         token_grad.T.reshape(1, tok, features),
         news[:, 0, :features].T * scale,
         news[:, 0, end - 1] * scale,

time: 372 us -> 374 us (level)
  Pallas kernels: 75.6 us -> 71.5 us
  waiting for transfers between devices: 182 us -> 186 us
    pallas_call x1 -> x0, Pallas kernels: 4.05 us -> none  [assemble(): pl.pallas_call(assemble_kernel, in_specs=[smem_spec()] + [any_spec()] * l...]
  transfers between devices with their start and end apart: 15 -> 15, of which waited for: 10 -> 10; matrix products, arithmetic and copies ran while one was open for 2% -> 2% of each run, Pallas kernels for 18% -> 16%
where the time goes in v9:
time: 374 us; the launch traced here: 373 us
  waiting for transfers between devices  186 us (50%)
  Pallas kernels  71.5 us (19%)
  blocking collectives  54.7 us (15%)
  starting transfers between devices  40.7 us (11%)
  local copies, waits for them, and re-layouts  15.3 us (4%)
  other arithmetic  4.07 us (1%)
    ppermute x7, waiting for transfers between devices, on_pairs(): lax.ppermute(parts[d], ('place', 'row'), [(i, i ^ d) for i in range(lanes)])  89.4 us
    all_to_all x4, waiting for transfers between devices, trade(): return lax.all_to_all(x, axes, split_axis=0, concat_axis=0, tiled=True)  80.4 us
    all_to_all x1, blocking collectives, trade(): return lax.all_to_all(x, axes, split_axis=0, concat_axis=0, tiled=True)  54.7 us
    all_to_all x4, starting transfers between devices, trade(): return lax.all_to_all(x, axes, split_axis=0, concat_axis=0, tiled=True)  32 us
    pallas_call x1, Pallas kernels, run_lane(): pl.pallas_call(lane_kernel, grid=(1,), in_specs=[smem_spec(), smem_spec()...  20.3 us
    pallas_call x2, Pallas kernels, lane_grads(): pl.pallas_call(functools.partial(lane_grad_kernel, other is not None), gr...  17.6 us
    ppermute x4, waiting for transfers between devices, swap(): return lax.ppermute(x, 'core', [(0, 1), (1, 0)])  16 us
    pallas_call x1, Pallas kernels, prepare(): pl.pallas_call(functools.partial(prepare_kernel, capacity, lanes), in_spe...  10.6 us
  transfers between devices with their start and end apart: 15, of which 10 were waited for; matrix products, arithmetic and copies ran while one was open for 2% of the time, Pallas kernels for 16%

profile of v9, /device:TPU:0, one launch (start us, length us, event | category | flops | bytes accessed | tf_op | source)
XLA Modules:
  0.0 372.9 jit_solution(5006235003734393158)
XLA Ops:
  0.6 3.7 reshape.61.hid_ref
  4.9 10.6 %prepare.1 = (bf16[2,4,2,192,768]{4,3,2,1,0:T(8,128)(2,1)}, bf16[640,3200]{1,0:T(8,128)(2,1)}, f32[8,128]{1,0:T(8,128)}, s32[8,128]{1,0:T(8,128)}, s32[8,512]{1,0:T(8,128)}) custom-call(s32[32]{0:T(128)} %a.1, f32[32]{0:T(128)} %b.1, s32[3]{0:T(128)} %pad_add_fusion.place_ref, bf16[32,192,1536]{2,1,0:T(8,128)(2,1)} %src_ref.3, bf16[2880,128]{1,0:T(8,128)(2,1)} %bitcast.39, ...), custom_call_target="tpu_custom_call" | custom-call | flops 10000000000 | bytes 10000000 | tf_op jit(solution)/shard_map/prepare/pallas_call | solution.py:414
  15.6 54.7 %all_to_all.25 = bf16[8,80,3200]{2,1,0:T(8,128)(2,1)} all-to-all(bf16[8,80,3200]{2,1,0:T(8,128)(2,1)} %bitcast.35), channel_id=1, replica_groups=mesh['half'=2,'place'=4,'row'=2,'core'=2] {'place','row'}, dimensions={0} | all-to-all | bytes 8192000 | tf_op jit(solution)/shard_map/all_to_all | solution.py:787
  70.3 4.6 %all-to-all-start.1 = ((bf16[8,2,192,768]{3,2,1,0:T(8,128)(2,1)}), bf16[8,2,192,768]{3,2,1,0:T(8,128)(2,1)}, u32[]{:S(2)}, u32[]{:S(2)}) async-start(bf16[8,2,192,768]{3,2,1,0:T(8,128)(2,1)} %hold.11), calls=%async_computation.1 | async-start | bytes 9437184 | tf_op jit(solution)/shard_map/all_to_all | solution.py:787
  77.5 8.4 %lane_grads_first.1 = bf16[8,2,2,192,384]{4,3,2,1,0:T(8,128)(2,1)} custom-call(s32[1]{0:T(128)} %bitcast.13._, bf16[640,3200]{1,0:T(8,128)(2,1)} %hold.10.grd_ref.hid_ref.flag_ref.refs_0_, bf16[640,3200]{1,0:T(8,128)(2,1)} %hold.10.grd_ref.hid_ref.flag_ref.refs_0_, bf16[640,3200]{1,0:T(8,128)(2,1)} %hold.10.grd_ref.hid_ref.flag_ref.refs_0_), custom_call_target="tpu_custom_call" | custom-call | flops 8000000000 | bytes 8000000 | tf_op jit(solution)/shard_map/lane_grads_first/pallas_call | solution.py:543
  86.1 8.0 %collective-permute-done.1.refs_0_ = bf16[8,2,2,192,384]{4,3,2,1,0:T(8,128)(2,1)S(1)} collective-permute-done((bf16[8,2,2,192,384]{4,3,2,1,0:T(8,128)(2,1)}, bf16[8,2,2,192,384]{4,3,2,1,0:T(8,128)(2,1)S(1)}, u32[]{:S(2)}, u32[]{:S(2)}) %collective-permute-start.1) | collective-permute-done | bytes 4718624 | tf_op jit(solution)/shard_map/ppermute | solution.py:755
  96.2 9.1 %lane_grads_add.1.refs_1_.refs_0_ = bf16[8,2,2,192,384]{4,3,2,1,0:T(8,128)(2,1)} custom-call(s32[1]{0:T(128)} %bitcast.2._.core_ref, bf16[640,3200]{1,0:T(8,128)(2,1)} %hold.10.grd_ref.hid_ref.flag_ref.refs_0_, bf16[640,3200]{1,0:T(8,128)(2,1)} %hold.10.grd_ref.hid_ref.flag_ref.refs_0_, bf16[640,3200]{1,0:T(8,128)(2,1)} %hold.10.grd_ref.hid_ref.flag_ref.refs_0_, ...), custom_call_target="tpu_custom_call" | custom-call | flops 8000000000 | bytes 8000000 | tf_op jit(solution)/shard_map/lane_grads_add/pallas_call | solution.py:543
  105.3 72.7 %all-to-all-done.1.refs_0_ = bf16[8,2,192,768]{3,2,1,0:T(8,128)(2,1)} async-done(((bf16[8,2,192,768]{3,2,1,0:T(8,128)(2,1)}), bf16[8,2,192,768]{3,2,1,0:T(8,128)(2,1)}, u32[]{:S(2)}, u32[]{:S(2)}) %all-to-all-start.1) | async-done | bytes 4718624 | tf_op jit(solution)/shard_map/all_to_all | solution.py:787
  178.0 4.7 %all-to-all-start.2 = ((bf16[16,2,192,384]{3,2,1,0:T(8,128)(2,1)}), bf16[16,2,192,384]{3,2,1,0:T(8,128)(2,1)}, u32[]{:S(2)}, u32[]{:S(2)}) async-start(bf16[16,2,192,384]{3,2,1,0:T(8,128)(2,1)} %bitcast.33), calls=%async_computation.2 | async-start | bytes 9437184 | tf_op jit(solution)/shard_map/all_to_all | solution.py:787
  183.9 6.7 %collective-permute-done.2.refs_1_ = f32[8,128]{1,0:T(8,128)S(1)} collective-permute-done((f32[8,128]{1,0:T(8,128)}, f32[8,128]{1,0:T(8,128)S(1)}, u32[]{:S(2)}, u32[]{:S(2)}) %collective-permute-start.2) | collective-permute-done | bytes 4128 | tf_op jit(solution)/shard_map/ppermute | solution.py:755
  191.1 20.3 %lane_products.1 = (bf16[80,3072]{1,0:T(8,128)(2,1)}, bf16[80,3072]{1,0:T(8,128)(2,1)}, bf16[80,3072]{1,0:T(8,128)(2,1)}, bf16[80,3072]{1,0:T(8,128)(2,1)}, bf16...) custom-call(s32[1]{0:T(128)} %bitcast.2._.core_ref, ...), custom_call_target="tpu_custom_call" | custom-call | flops 20000000000 | bytes 20000000 | tf_op jit(solution)/shard_map/lane_products/pallas_call | solution.py:497
  211.5 3.5 collective-permute-start.10
  219.0 57.8 %collective-permute-done.10.refs_7_ = bf16[80,3072]{1,0:T(8,128)(2,1)S(1)} collective-permute-done((bf16[80,3072]{1,0:T(8,128)(2,1)}, bf16[80,3072]{1,0:T(8,128)(2,1)S(1)}, u32[]{:S(2)}, u32[]{:S(2)}) %collective-permute-start.10) | collective-permute-done | bytes 491552 | tf_op jit(solution)/shard_map/ppermute | solution.py:816
  277.3 7.8 %collective-permute-done.4.refs_1_ = bf16[80,3072]{1,0:T(8,128)(2,1)S(1)} collective-permute-done((bf16[80,3072]{1,0:T(8,128)(2,1)}, bf16[80,3072]{1,0:T(8,128)(2,1)S(1)}, u32[]{:S(2)}, u32[]{:S(2)}) %collective-permute-start.4) | collective-permute-done | bytes 491552 | tf_op jit(solution)/shard_map/ppermute | solution.py:816
  286.9 12.6 %collective-permute-done.8.refs_5_ = bf16[80,3072]{1,0:T(8,128)(2,1)S(1)} collective-permute-done((bf16[80,3072]{1,0:T(8,128)(2,1)}, bf16[80,3072]{1,0:T(8,128)(2,1)S(1)}, u32[]{:S(2)}, u32[]{:S(2)}) %collective-permute-start.8) | collective-permute-done | bytes 491552 | tf_op jit(solution)/shard_map/ppermute | solution.py:816
  299.5 9.4 %collective-permute-done.9.refs_6_ = bf16[80,3072]{1,0:T(8,128)(2,1)S(1)} collective-permute-done((bf16[80,3072]{1,0:T(8,128)(2,1)}, bf16[80,3072]{1,0:T(8,128)(2,1)S(1)}, u32[]{:S(2)}, u32[]{:S(2)}) %collective-permute-start.9) | collective-permute-done | bytes 491552 | tf_op jit(solution)/shard_map/ppermute | solution.py:816
  309.7 5.0 %combine.1 = (bf16[128,1536]{1,0:T(8,128)(2,1)}, bf16[2880,128]{1,0:T(8,128)(2,1)}, f32[32,1,3072]{2,1,0:T(1,128)}) custom-call(bf16[128,1536]{1,0:T(8,128)(2,1)} %bitcast.42, f32[8,128]{1,0:T(8,128)} %get-tuple-element.25.gate_ref, s32[8,128]{1,0:T(8,128)} %get-tuple-element.26.pos_ref, s32[4,128]{1,0:T(4,128)} %bitcast.46, bf16[32,2880]{1,0:T(8,128)(2,1)} %bitcast.44, ...), custom_call_target="tpu_custom_call" | custom-call | flops 5000000000 | bytes 5000000 | tf_op jit(solution)/shard_map/combine/pallas_call | solution.py:612
  314.7 17.0 %all-to-all-start.3 = ((f32[32,1,3072]{2,1,0:T(1,128)}), f32[32,1,3072]{2,1,0:T(1,128)S(1)}, u32[]{:S(2)}, u32[]{:S(2)}) async-start(f32[32,1,3072]{2,1,0:T(1,128)} %get-tuple-element.41), calls=%async_computation.3 | async-start | bytes 786432 | tf_op jit(solution)/shard_map/all_to_all | solution.py:787
  331.7 4.2 %unplace.1 = bf16[512,1536]{1,0:T(8,128)(2,1)} custom-call(s32[8,512]{1,0:T(8,128)} %get-tuple-element.38.slot_ref, bf16[80,3072]{1,0:T(8,128)(2,1)} %get-tuple-element.29.refs_0_, bf16[80,3072]{1,0:T(8,128)(2,1)} %copy-done.4, bf16[80,3072]{1,0:T(8,128)(2,1)} %copy-done.5, bf16[80,3072]{1,0:T(8,128)(2,1)} %copy-done.6, bf16[80,3072]{1,0:T(8,128)(2,1)} %copy-done.7, ...), custom_call_target="tpu_custom_call" | custom-call | flops 4000000000 | bytes 4000000 | tf_op jit(solution)/shard_map/unplace/pallas_call | solution.py:639
  335.9 3.8 %reshape.66.refs_1_ = bf16[1,128,4,1536]{3,2,1,0:T(4,128)(2,1)} reshape(bf16[512,1536]{1,0:T(8,128)(2,1)} %unplace.1) | data formatting | bytes 3145728 | tf_op jit(solution)/shard_map/reshape | solution.py:822
  339.8 8.1 %coef_dots.1._ = f32[8,128]{1,0:T(8,128)} custom-call(s32[1]{0:T(128)} %bitcast.20.rep_ref, s32[32]{0:T(128)} %a.1, bf16[32,192,1536]{2,1,0:T(8,128)(2,1)} %src_ref.3, bf16[2,16,192,384]{3,2,1,0:T(8,128)(2,1)} %bitcast.21.got_ref.c), custom_call_target="tpu_custom_call" | custom-call | tf_op jit(solution)/shard_map/coef_dots/pallas_call | solution.py:715
  351.2 5.6 %all-to-all-start.4 = ((f32[32,1,3200]{2,1,0:T(1,128)}), f32[32,1,3200]{2,1,0:T(1,128)S(1)}, u32[]{:S(2)}, u32[]{:S(2)}) async-start(f32[32,1,3200]{2,1,0:T(1,128)} %broadcast_in_dim.17), calls=%async_computation.4 | async-start | bytes 819200 | tf_op jit(solution)/shard_map/all_to_all | solution.py:787
  356.8 5.7 %finish.1 = f32[32,192,384]{2,1,0:T(8,128)} custom-call(s32[32]{0:T(128)} %a.1, f32[32]{0:T(128)} %b.1, bf16[2,16,192,384]{3,2,1,0:T(8,128)(2,1)} %bitcast.21.got_ref.c, f32[8,128]{1,0:T(8,128)} %coef_dots.1._), custom_call_target="tpu_custom_call" | custom-call | flops 8000000000 | bytes 8000000 | tf_op jit(solution)/shard_map/finish/pallas_call | solution.py:735
  362.5 7.8 %all-to-all-done.4 = f32[32,1,3200]{2,1,0:T(1,128)S(1)} async-done(((f32[32,1,3200]{2,1,0:T(1,128)}), f32[32,1,3200]{2,1,0:T(1,128)S(1)}, u32[]{:S(2)}, u32[]{:S(2)}) %all-to-all-start.4) | async-done | bytes 409632 | tf_op jit(solution)/shard_map/all_to_all | solution.py:787
  (59 shorter events, 20.2 us)
Async XLA Ops:
  70.3 107.7 %all-to-all-start.1 = ((bf16[8,2,192,768]{3,2,1,0:T(8,128)(2,1)}), bf16[8,2,192,768]{3,2,1,0:T(8,128)(2,1)}, u32[]{:S(2)}, u32[]{:S(2)}) async-start(bf16[8,2,192,768]{3,2,1,0:T(8,128)(2,1)} %hold.11), calls=%async_computation.1 | async-start | bytes 9437184 | tf_op jit(solution)/shard_map/all_to_all | solution.py:787
  75.5 1.4 collective-permute-start
  76.9 0.6 copy-start
  85.9 8.1 %collective-permute-start.1 = (bf16[8,2,2,192,384]{4,3,2,1,0:T(8,128)(2,1)}, bf16[8,2,2,192,384]{4,3,2,1,0:T(8,128)(2,1)S(1)}, u32[]{:S(2)}, u32[]{:S(2)}) collective-permute-start(bf16[8,2,2,192,384]{4,3,2,1,0:T(8,128)(2,1)} %lane_grads_first.1), channel_id=1, source_target_pairs={{0,1},{1,0},{2,3},{3,2},{4,5},{5,4},{6,7},{7,6},{8,9},{9,8},{10,11... | collective-permute-start | bytes 14155784 | tf_op jit(solution)/shard_map/ppermute | solution.py:755
  94.0 2.1 copy-start.2
  178.0 136.7 %all-to-all-start.2 = ((bf16[16,2,192,384]{3,2,1,0:T(8,128)(2,1)}), bf16[16,2,192,384]{3,2,1,0:T(8,128)(2,1)}, u32[]{:S(2)}, u32[]{:S(2)}) async-start(bf16[16,2,192,384]{3,2,1,0:T(8,128)(2,1)} %bitcast.33), calls=%async_computation.2 | async-start | bytes 9437184 | tf_op jit(solution)/shard_map/all_to_all | solution.py:787
  182.7 8.4 %collective-permute-start.3 = (bf16[8,2,192,768]{3,2,1,0:T(8,128)(2,1)}, bf16[8,2,192,768]{3,2,1,0:T(8,128)(2,1)}, u32[]{:S(2)}, u32[]{:S(2)}) collective-permute-start(bf16[8,2,192,768]{3,2,1,0:T(8,128)(2,1)} %hold.12.refs_1_.mine), channel_id=1, source_target_pairs={{0,1},{1,0},{2,3},{3,2},{4,5},{5,4},{6,7},{7,6},{8,9},{9,8},{10,11... | collective-permute-start | bytes 14155784 | tf_op jit(solution)/shard_map/ppermute | solution.py:755
  183.4 7.1 %collective-permute-start.2 = (f32[8,128]{1,0:T(8,128)}, f32[8,128]{1,0:T(8,128)S(1)}, u32[]{:S(2)}, u32[]{:S(2)}) collective-permute-start(f32[8,128]{1,0:T(8,128)} %hold.14), channel_id=1, source_target_pairs={{0,1},{1,0},{2,3},{3,2},{4,5},{5,4},{6,7},{7,6},{8,9},{9,8},{10,11... | collective-permute-start | bytes 12296 | tf_op jit(solution)/shard_map/ppermute | solution.py:755
  211.5 65.3 %collective-permute-start.10 = (bf16[80,3072]{1,0:T(8,128)(2,1)}, bf16[80,3072]{1,0:T(8,128)(2,1)S(1)}, u32[]{:S(2)}, u32[]{:S(2)}) collective-permute-start(bf16[80,3072]{1,0:T(8,128)(2,1)} %get-tuple-element.36), channel_id=1, source_target_pairs={{0,14},{2,12},{4,10},{6,8},{8,6},{10,4},{12,2},{14,0},{1,15},{3,13... | collective-permute-start | bytes 1474568 | tf_op jit(solution)/shard_map/ppermute | solution.py:816
  214.9 70.2 %collective-permute-start.4 = (bf16[80,3072]{1,0:T(8,128)(2,1)}, bf16[80,3072]{1,0:T(8,128)(2,1)S(1)}, u32[]{:S(2)}, u32[]{:S(2)}) collective-permute-start(bf16[80,3072]{1,0:T(8,128)(2,1)} %get-tuple-element.30), channel_id=1, source_target_pairs={{0,2},{2,0},{4,6},{6,4},{8,10},{10,8},{12,14},{14,12},{1,3},{3,1},... | collective-permute-start | bytes 1474568 | tf_op jit(solution)/shard_map/ppermute | solution.py:816
  215.5 69.6 %collective-permute-start.5 = (bf16[80,3072]{1,0:T(8,128)(2,1)}, bf16[80,3072]{1,0:T(8,128)(2,1)S(1)}, u32[]{:S(2)}, u32[]{:S(2)}) collective-permute-start(bf16[80,3072]{1,0:T(8,128)(2,1)} %get-tuple-element.31), channel_id=1, source_target_pairs={{0,4},{2,6},{4,0},{6,2},{8,12},{10,14},{12,8},{14,10},{1,5},{3,7},... | collective-permute-start | bytes 1474568 | tf_op jit(solution)/shard_map/ppermute | solution.py:816
  216.1 69.1 %collective-permute-start.6 = (bf16[80,3072]{1,0:T(8,128)(2,1)}, bf16[80,3072]{1,0:T(8,128)(2,1)S(1)}, u32[]{:S(2)}, u32[]{:S(2)}) collective-permute-start(bf16[80,3072]{1,0:T(8,128)(2,1)} %get-tuple-element.32), channel_id=1, source_target_pairs={{0,6},{2,4},{4,2},{6,0},{8,14},{10,12},{12,10},{14,8},{1,7},{3,5},... | collective-permute-start | bytes 1474568 | tf_op jit(solution)/shard_map/ppermute | solution.py:816
  218.4 68.5 %collective-permute-start.7 = (bf16[80,3072]{1,0:T(8,128)(2,1)}, bf16[80,3072]{1,0:T(8,128)(2,1)S(1)}, u32[]{:S(2)}, u32[]{:S(2)}) collective-permute-start(bf16[80,3072]{1,0:T(8,128)(2,1)} %get-tuple-element.33), channel_id=1, source_target_pairs={{0,8},{2,10},{4,12},{6,14},{8,0},{10,2},{12,4},{14,6},{1,9},{3,11}... | collective-permute-start | bytes 1474568 | tf_op jit(solution)/shard_map/ppermute | solution.py:816
  276.8 32.1 %copy-start.3 = (bf16[80,3072]{1,0:T(8,128)(2,1)}, bf16[80,3072]{1,0:T(8,128)(2,1)S(1)}, u32[]{:S(2)}) copy-start(bf16[80,3072]{1,0:T(8,128)(2,1)S(1)} %collective-permute-done.10.refs_7_) | copy-start | bytes 1474564
  276.8 22.7 %collective-permute-start.8 = (bf16[80,3072]{1,0:T(8,128)(2,1)}, bf16[80,3072]{1,0:T(8,128)(2,1)S(1)}, u32[]{:S(2)}, u32[]{:S(2)}) collective-permute-start(bf16[80,3072]{1,0:T(8,128)(2,1)} %get-tuple-element.34), channel_id=1, source_target_pairs={{0,10},{2,8},{4,14},{6,12},{8,2},{10,0},{12,6},{14,4},{1,11},{3,9}... | collective-permute-start | bytes 1474568 | tf_op jit(solution)/shard_map/ppermute | solution.py:816
  285.1 23.8 %copy-start.4 = (bf16[80,3072]{1,0:T(8,128)(2,1)}, bf16[80,3072]{1,0:T(8,128)(2,1)S(1)}, u32[]{:S(2)}) copy-start(bf16[80,3072]{1,0:T(8,128)(2,1)S(1)} %collective-permute-done.4.refs_1_) | copy-start | bytes 1474564
  285.1 23.8 %collective-permute-start.9 = (bf16[80,3072]{1,0:T(8,128)(2,1)}, bf16[80,3072]{1,0:T(8,128)(2,1)S(1)}, u32[]{:S(2)}, u32[]{:S(2)}) collective-permute-start(bf16[80,3072]{1,0:T(8,128)(2,1)} %get-tuple-element.35), channel_id=1, source_target_pairs={{0,12},{2,14},{4,8},{6,10},{8,4},{10,6},{12,0},{14,2},{1,13},{3,15... | collective-permute-start | bytes 1474568 | tf_op jit(solution)/shard_map/ppermute | solution.py:816
  285.1 23.8 %copy-start.5 = (bf16[80,3072]{1,0:T(8,128)(2,1)}, bf16[80,3072]{1,0:T(8,128)(2,1)S(1)}, u32[]{:S(2)}) copy-start(bf16[80,3072]{1,0:T(8,128)(2,1)S(1)} %collective-permute-done.5.refs_2_) | copy-start | bytes 1474564
  285.1 23.7 %copy-start.6 = (bf16[80,3072]{1,0:T(8,128)(2,1)}, bf16[80,3072]{1,0:T(8,128)(2,1)S(1)}, u32[]{:S(2)}) copy-start(bf16[80,3072]{1,0:T(8,128)(2,1)S(1)} %collective-permute-done.6.refs_3_) | copy-start | bytes 1474564
  286.9 22.0 %copy-start.7 = (bf16[80,3072]{1,0:T(8,128)(2,1)}, bf16[80,3072]{1,0:T(8,128)(2,1)S(1)}, u32[]{:S(2)}) copy-start(bf16[80,3072]{1,0:T(8,128)(2,1)S(1)} %collective-permute-done.7.refs_4_) | copy-start | bytes 1474564
  299.5 9.4 %copy-start.8 = (bf16[80,3072]{1,0:T(8,128)(2,1)}, bf16[80,3072]{1,0:T(8,128)(2,1)S(1)}, u32[]{:S(2)}) copy-start(bf16[80,3072]{1,0:T(8,128)(2,1)S(1)} %collective-permute-done.8.refs_5_) | copy-start | bytes 1474564
  308.9 0.8 copy-start.9
  314.7 33.9 %all-to-all-start.3 = ((f32[32,1,3072]{2,1,0:T(1,128)}), f32[32,1,3072]{2,1,0:T(1,128)S(1)}, u32[]{:S(2)}, u32[]{:S(2)}) async-start(f32[32,1,3072]{2,1,0:T(1,128)} %get-tuple-element.41), calls=%async_computation.3 | async-start | bytes 786432 | tf_op jit(solution)/shard_map/all_to_all | solution.py:787
  351.2 19.1 %all-to-all-start.4 = ((f32[32,1,3200]{2,1,0:T(1,128)}), f32[32,1,3200]{2,1,0:T(1,128)S(1)}, u32[]{:S(2)}, u32[]{:S(2)}) async-start(f32[32,1,3200]{2,1,0:T(1,128)} %broadcast_in_dim.17), calls=%async_computation.4 | async-start | bytes 819200 | tf_op jit(solution)/shard_map/all_to_all | solution.py:787
  (1 other events, 0.6 us)

commit v10 on v9

--- a/solution.py
+++ b/solution.py
@@ -816,16 +816,16 @@
         lax.ppermute(parts[d], ("place", "row"), [(i, i ^ d) for i in range(lanes)])
         for d in range(1, lanes)
     ]
+    arrived = arrived.reshape(2, 2 * lanes, row_share, width // reps)
+    dots = coef_dots(stack([2 * row_i + core_i]), merge_map, source_w, arrived)
+    source_w_grad = finish(merge_map, merge_coef, arrived, dots, scale)
+    home = hold(home, source_w_grad)
     mixed, token_grad, part = combine(home, og, gates, pos, idx_t, rwt, xt)
-    part, arrived = hold([part, arrived])
     part = jnp.sum(trade(part, everyone), axis=0)
     hidden_grad = unplace(home, slot_pos).reshape(1, tok, top, width)
-    arrived = arrived.reshape(2, 2 * lanes, row_share, width // reps)
-    dots = coef_dots(stack([2 * row_i + core_i]), merge_map, source_w, arrived)
     news = jnp.concatenate([part, dots[:1]], axis=1)
     (news,) = hold([news], hidden_grad)
     news = trade(jnp.broadcast_to(news[None], (devices,) + news.shape), everyone)
-    source_w_grad = finish(merge_map, merge_coef, arrived, dots, scale)
     end = part.shape[1]
     return (
         mixed.reshape(1, tok, depth),

time: 374 us -> 373 us (level)
  waiting for transfers between devices: 186 us -> 162 us
  blocking collectives: 54.7 us -> 70.7 us
  starting transfers between devices: 40.7 us -> 50 us
    ppermute x7, waiting for transfers between devices: 89.4 us -> 15.2 us  [on_pairs(): lax.ppermute(parts[d], ('place', 'row'), [(i, i ^ d) for i in range(lanes)])]
    all_to_all x4 -> x3, waiting for transfers between devices: 80.4 us -> 131 us  [trade(): return lax.all_to_all(x, axes, split_axis=0, concat_axis=0, tiled=True)]
    ppermute x7, starting transfers between devices: 8.01 us -> 35.8 us  [on_pairs(): lax.ppermute(parts[d], ('place', 'row'), [(i, i ^ d) for i in range(lanes)])]
    all_to_all x4 -> x3, starting transfers between devices: 32 us -> 13.4 us  [trade(): return lax.all_to_all(x, axes, split_axis=0, concat_axis=0, tiled=True)]
    all_to_all x1 -> x2, blocking collectives: 54.7 us -> 70.7 us  [trade(): return lax.all_to_all(x, axes, split_axis=0, concat_axis=0, tiled=True)]
  transfers between devices with their start and end apart: 15 -> 14, of which waited for: 10 -> 8; matrix products, arithmetic and copies ran while one was open for 2% -> 1% of each run, Pallas kernels for 16% -> 15%
where the time goes in v10:
time: 373 us
  waiting for transfers between devices  162 us (43%)
  Pallas kernels  71.6 us (19%)
  blocking collectives  70.7 us (19%)
  starting transfers between devices  50 us (13%)
  local copies, waits for them, and re-layouts  13.1 us (4%)
  other arithmetic  4.07 us (1%)
    all_to_all x3, waiting for transfers between devices, trade(): return lax.all_to_all(x, axes, split_axis=0, concat_axis=0, tiled=True)  131 us
    all_to_all x2, blocking collectives, trade(): return lax.all_to_all(x, axes, split_axis=0, concat_axis=0, tiled=True)  70.7 us
    ppermute x7, starting transfers between devices, on_pairs(): lax.ppermute(parts[d], ('place', 'row'), [(i, i ^ d) for i in range(lanes)])  35.8 us
    pallas_call x1, Pallas kernels, run_lane(): pl.pallas_call(lane_kernel, grid=(1,), in_specs=[smem_spec(), smem_spec()...  20.3 us
    pallas_call x2, Pallas kernels, lane_grads(): pl.pallas_call(functools.partial(lane_grad_kernel, other is not None), gr...  17.5 us
    ppermute x4, waiting for transfers between devices, swap(): return lax.ppermute(x, 'core', [(0, 1), (1, 0)])  16 us
    ppermute x7, waiting for transfers between devices, on_pairs(): lax.ppermute(parts[d], ('place', 'row'), [(i, i ^ d) for i in range(lanes)])  15.2 us
    all_to_all x3, starting transfers between devices, trade(): return lax.all_to_all(x, axes, split_axis=0, concat_axis=0, tiled=True)  13.4 us
  transfers between devices with their start and end apart: 14, of which 8 were waited for; matrix products, arithmetic and copies ran while one was open for 1% of the time, Pallas kernels for 15%

profile of v10, /device:TPU:0, one launch (start us, length us, event | category | flops | bytes accessed | tf_op | source)
XLA Modules:
  0.0 372.6 jit_solution(3740949292614017567)
XLA Ops:
  0.6 3.7 reshape.61.hid_ref
  4.9 10.6 %prepare.1 = (bf16[2,4,2,192,768]{4,3,2,1,0:T(8,128)(2,1)}, bf16[640,3200]{1,0:T(8,128)(2,1)}, f32[8,128]{1,0:T(8,128)}, s32[8,128]{1,0:T(8,128)}, s32[8,512]{1,0:T(8,128)}) custom-call(s32[32]{0:T(128)} %a.1, f32[32]{0:T(128)} %b.1, s32[3]{0:T(128)} %pad_add_fusion.place_ref, bf16[32,192,1536]{2,1,0:T(8,128)(2,1)} %src_ref.3, bf16[2880,128]{1,0:T(8,128)(2,1)} %bitcast.39, ...), custom_call_target="tpu_custom_call" | custom-call | flops 10000000000 | bytes 10000000 | tf_op jit(solution)/shard_map/prepare/pallas_call | solution.py:414
  15.6 54.7 %all_to_all.25 = bf16[8,80,3200]{2,1,0:T(8,128)(2,1)} all-to-all(bf16[8,80,3200]{2,1,0:T(8,128)(2,1)} %bitcast.35), channel_id=1, replica_groups=mesh['half'=2,'place'=4,'row'=2,'core'=2] {'place','row'}, dimensions={0} | all-to-all | bytes 8192000 | tf_op jit(solution)/shard_map/all_to_all | solution.py:787
  70.3 4.6 %all-to-all-start.1 = ((bf16[8,2,192,768]{3,2,1,0:T(8,128)(2,1)}), bf16[8,2,192,768]{3,2,1,0:T(8,128)(2,1)}, u32[]{:S(2)}, u32[]{:S(2)}) async-start(bf16[8,2,192,768]{3,2,1,0:T(8,128)(2,1)} %hold.11), calls=%async_computation.1 | async-start | bytes 9437184 | tf_op jit(solution)/shard_map/all_to_all | solution.py:787
  77.5 8.4 %lane_grads_first.1 = bf16[8,2,2,192,384]{4,3,2,1,0:T(8,128)(2,1)} custom-call(s32[1]{0:T(128)} %bitcast.13._, bf16[640,3200]{1,0:T(8,128)(2,1)} %hold.10.grd_ref.hid_ref.flag_ref.refs_0_, bf16[640,3200]{1,0:T(8,128)(2,1)} %hold.10.grd_ref.hid_ref.flag_ref.refs_0_, bf16[640,3200]{1,0:T(8,128)(2,1)} %hold.10.grd_ref.hid_ref.flag_ref.refs_0_), custom_call_target="tpu_custom_call" | custom-call | flops 8000000000 | bytes 8000000 | tf_op jit(solution)/shard_map/lane_grads_first/pallas_call | solution.py:543
  86.0 8.0 %collective-permute-done.1.refs_0_ = bf16[8,2,2,192,384]{4,3,2,1,0:T(8,128)(2,1)S(1)} collective-permute-done((bf16[8,2,2,192,384]{4,3,2,1,0:T(8,128)(2,1)}, bf16[8,2,2,192,384]{4,3,2,1,0:T(8,128)(2,1)S(1)}, u32[]{:S(2)}, u32[]{:S(2)}) %collective-permute-start.1) | collective-permute-done | bytes 4718624 | tf_op jit(solution)/shard_map/ppermute | solution.py:755
  94.0 2.1 copy-done.8
  96.1 9.2 %lane_grads_add.1.refs_1_.refs_0_ = bf16[8,2,2,192,384]{4,3,2,1,0:T(8,128)(2,1)} custom-call(s32[1]{0:T(128)} %bitcast.2._.core_ref, bf16[640,3200]{1,0:T(8,128)(2,1)} %hold.10.grd_ref.hid_ref.flag_ref.refs_0_, bf16[640,3200]{1,0:T(8,128)(2,1)} %hold.10.grd_ref.hid_ref.flag_ref.refs_0_, bf16[640,3200]{1,0:T(8,128)(2,1)} %hold.10.grd_ref.hid_ref.flag_ref.refs_0_, ...), custom_call_target="tpu_custom_call" | custom-call | flops 8000000000 | bytes 8000000 | tf_op jit(solution)/shard_map/lane_grads_add/pallas_call | solution.py:543
  105.3 72.7 %all-to-all-done.1.refs_0_ = bf16[8,2,192,768]{3,2,1,0:T(8,128)(2,1)} async-done(((bf16[8,2,192,768]{3,2,1,0:T(8,128)(2,1)}), bf16[8,2,192,768]{3,2,1,0:T(8,128)(2,1)}, u32[]{:S(2)}, u32[]{:S(2)}) %all-to-all-start.1) | async-done | bytes 4718624 | tf_op jit(solution)/shard_map/all_to_all | solution.py:787
  178.0 4.8 %all-to-all-start.2 = ((bf16[16,2,192,384]{3,2,1,0:T(8,128)(2,1)}), bf16[16,2,192,384]{3,2,1,0:T(8,128)(2,1)}, u32[]{:S(2)}, u32[]{:S(2)}) async-start(bf16[16,2,192,384]{3,2,1,0:T(8,128)(2,1)} %bitcast.33), calls=%async_computation.2 | async-start | bytes 9437184 | tf_op jit(solution)/shard_map/all_to_all | solution.py:787
  183.9 6.7 %collective-permute-done.2.refs_1_ = f32[8,128]{1,0:T(8,128)S(1)} collective-permute-done((f32[8,128]{1,0:T(8,128)}, f32[8,128]{1,0:T(8,128)S(1)}, u32[]{:S(2)}, u32[]{:S(2)}) %collective-permute-start.2) | collective-permute-done | bytes 4128 | tf_op jit(solution)/shard_map/ppermute | solution.py:755
  191.2 20.3 %lane_products.1 = (bf16[80,3072]{1,0:T(8,128)(2,1)}, bf16[80,3072]{1,0:T(8,128)(2,1)}, bf16[80,3072]{1,0:T(8,128)(2,1)}, bf16[80,3072]{1,0:T(8,128)(2,1)}, bf16...) custom-call(s32[1]{0:T(128)} %bitcast.2._.core_ref, ...), custom_call_target="tpu_custom_call" | custom-call | flops 20000000000 | bytes 20000000 | tf_op jit(solution)/shard_map/lane_products/pallas_call | solution.py:497
  218.1 53.5 %all-to-all-done.2 = bf16[16,2,192,384]{3,2,1,0:T(8,128)(2,1)} async-done(((bf16[16,2,192,384]{3,2,1,0:T(8,128)(2,1)}), bf16[16,2,192,384]{3,2,1,0:T(8,128)(2,1)}, u32[]{:S(2)}, u32[]{:S(2)}) %all-to-all-start.2) | async-done | bytes 4718624 | tf_op jit(solution)/shard_map/all_to_all | solution.py:787
  271.6 8.3 %coef_dots.1._ = f32[8,128]{1,0:T(8,128)} custom-call(s32[1]{0:T(128)} %bitcast.17.rep_ref, s32[32]{0:T(128)} %a.1, bf16[32,192,1536]{2,1,0:T(8,128)(2,1)} %src_ref.3, bf16[2,16,192,384]{3,2,1,0:T(8,128)(2,1)} %bitcast.16.got_ref.c), custom_call_target="tpu_custom_call" | custom-call | tf_op jit(solution)/shard_map/coef_dots/pallas_call | solution.py:715
  279.9 29.1 %collective-permute-start.9 = (bf16[80,3072]{1,0:T(8,128)(2,1)S(1)}, bf16[80,3072]{1,0:T(8,128)(2,1)S(1)}, u32[]{:S(2)}, u32[]{:S(2)}) collective-permute-start(bf16[80,3072]{1,0:T(8,128)(2,1)S(1)} %copy-done.10), channel_id=1, source_target_pairs={{0,12},{2,14},{4,8},{6,10},{8,4},{10,6},{12,0},{14,2},{1,13},{3,15... | collective-permute-start | bytes 1474568 | tf_op jit(solution)/shard_map/ppermute | solution.py:816
  309.1 5.7 %finish.1.refs_8_ = f32[32,192,384]{2,1,0:T(8,128)} custom-call(s32[32]{0:T(128)} %a.1, f32[32]{0:T(128)} %b.1, bf16[2,16,192,384]{3,2,1,0:T(8,128)(2,1)} %bitcast.16.got_ref.c, f32[8,128]{1,0:T(8,128)} %coef_dots.1._), custom_call_target="tpu_custom_call" | custom-call | flops 8000000000 | bytes 8000000 | tf_op jit(solution)/shard_map/finish/pallas_call | solution.py:735
  314.9 6.2 %collective-permute-done.9.refs_6_ = bf16[80,3072]{1,0:T(8,128)(2,1)S(1)} collective-permute-done((bf16[80,3072]{1,0:T(8,128)(2,1)S(1)}, bf16[80,3072]{1,0:T(8,128)(2,1)S(1)}, u32[]{:S(2)}, u32[]{:S(2)}) %collective-permute-start.9) | collective-permute-done | bytes 491552 | tf_op jit(solution)/shard_map/ppermute | solution.py:816
  321.1 9.0 %collective-permute-done.10.refs_7_ = bf16[80,3072]{1,0:T(8,128)(2,1)} collective-permute-done((bf16[80,3072]{1,0:T(8,128)(2,1)S(1)}, bf16[80,3072]{1,0:T(8,128)(2,1)}, u32[]{:S(2)}, u32[]{:S(2)}) %collective-permute-start.10) | collective-permute-done | bytes 491552 | tf_op jit(solution)/shard_map/ppermute | solution.py:816
  330.1 5.0 %combine.1 = (bf16[128,1536]{1,0:T(8,128)(2,1)}, bf16[2880,128]{1,0:T(8,128)(2,1)}, f32[32,1,3072]{2,1,0:T(1,128)}) custom-call(bf16[128,1536]{1,0:T(8,128)(2,1)} %bitcast.42, f32[8,128]{1,0:T(8,128)} %get-tuple-element.31.gate_ref, s32[8,128]{1,0:T(8,128)} %get-tuple-element.32.pos_ref, s32[4,128]{1,0:T(4,128)} %bitcast.46, bf16[32,2880]{1,0:T(8,128)(2,1)} %bitcast.44, ...), custom_call_target="tpu_custom_call" | custom-call | flops 5000000000 | bytes 5000000 | tf_op jit(solution)/shard_map/combine/pallas_call | solution.py:612
  335.1 4.1 %all-to-all-start.3 = ((f32[32,1,3072]{2,1,0:T(1,128)}), f32[32,1,3072]{2,1,0:T(1,128)S(1)}, u32[]{:S(2)}, u32[]{:S(2)}) async-start(f32[32,1,3072]{2,1,0:T(1,128)} %get-tuple-element.54), calls=%async_computation.3 | async-start | bytes 786432 | tf_op jit(solution)/shard_map/all_to_all | solution.py:787
  339.2 4.2 %unplace.1 = bf16[512,1536]{1,0:T(8,128)(2,1)} custom-call(s32[8,512]{1,0:T(8,128)} %get-tuple-element.52.slot_ref, bf16[80,3072]{1,0:T(8,128)(2,1)} %get-tuple-element.43.refs_0_, bf16[80,3072]{1,0:T(8,128)(2,1)} %get-tuple-element.44.refs_1_, bf16[80,3072]{1,0:T(8,128)(2,1)} %get-tuple-element.45.refs_2_, bf16[80,3072]{1,0:T(8,128)(2,1)} %get-tuple-element.46.refs_3_, ...), custom_call_target="tpu_custom_call" | custom-call | flops 4000000000 | bytes 4000000 | tf_op jit(solution)/shard_map/unplace/pallas_call | solution.py:639
  343.4 3.8 %reshape.68.refs_1_ = bf16[1,128,4,1536]{3,2,1,0:T(4,128)(2,1)} reshape(bf16[512,1536]{1,0:T(8,128)(2,1)} %unplace.1) | data formatting | bytes 3145728 | tf_op jit(solution)/shard_map/reshape | solution.py:825
  347.3 4.9 %all-to-all-done.3 = f32[32,1,3072]{2,1,0:T(1,128)S(1)} async-done(((f32[32,1,3072]{2,1,0:T(1,128)}), f32[32,1,3072]{2,1,0:T(1,128)S(1)}, u32[]{:S(2)}, u32[]{:S(2)}) %all-to-all-start.3) | async-done | bytes 393248 | tf_op jit(solution)/shard_map/all_to_all | solution.py:787
  354.0 15.9 %all_to_all.26 = f32[32,1,3200]{2,1,0:T(1,128)S(1)} all-to-all(f32[32,1,3200]{2,1,0:T(1,128)S(1)} %broadcast_in_dim.17), channel_id=1, replica_groups=mesh['half'=2,'place'=4,'row'=2,'core'=2] {'half','place','row','core'}, dimensions={0} | all-to-all | bytes 819200 | tf_op jit(solution)/shard_map/all_to_all | solution.py:787
  (61 shorter events, 16.3 us)
Async XLA Ops:
  70.3 107.7 %all-to-all-start.1 = ((bf16[8,2,192,768]{3,2,1,0:T(8,128)(2,1)}), bf16[8,2,192,768]{3,2,1,0:T(8,128)(2,1)}, u32[]{:S(2)}, u32[]{:S(2)}) async-start(bf16[8,2,192,768]{3,2,1,0:T(8,128)(2,1)} %hold.11), calls=%async_computation.1 | async-start | bytes 9437184 | tf_op jit(solution)/shard_map/all_to_all | solution.py:787
  75.5 1.4 collective-permute-start
  85.9 8.1 %collective-permute-start.1 = (bf16[8,2,2,192,384]{4,3,2,1,0:T(8,128)(2,1)}, bf16[8,2,2,192,384]{4,3,2,1,0:T(8,128)(2,1)S(1)}, u32[]{:S(2)}, u32[]{:S(2)}) collective-permute-start(bf16[8,2,2,192,384]{4,3,2,1,0:T(8,128)(2,1)} %lane_grads_first.1), channel_id=1, source_target_pairs={{0,1},{1,0},{2,3},{3,2},{4,5},{5,4},{6,7},{7,6},{8,9},{9,8},{10,11... | collective-permute-start | bytes 14155784 | tf_op jit(solution)/shard_map/ppermute | solution.py:755
  94.0 2.1 copy-start.8
  178.0 93.6 %all-to-all-start.2 = ((bf16[16,2,192,384]{3,2,1,0:T(8,128)(2,1)}), bf16[16,2,192,384]{3,2,1,0:T(8,128)(2,1)}, u32[]{:S(2)}, u32[]{:S(2)}) async-start(bf16[16,2,192,384]{3,2,1,0:T(8,128)(2,1)} %bitcast.33), calls=%async_computation.2 | async-start | bytes 9437184 | tf_op jit(solution)/shard_map/all_to_all | solution.py:787
  182.7 8.4 %collective-permute-start.3 = (bf16[8,2,192,768]{3,2,1,0:T(8,128)(2,1)}, bf16[8,2,192,768]{3,2,1,0:T(8,128)(2,1)}, u32[]{:S(2)}, u32[]{:S(2)}) collective-permute-start(bf16[8,2,192,768]{3,2,1,0:T(8,128)(2,1)} %hold.12.refs_1_.mine), channel_id=1, source_target_pairs={{0,1},{1,0},{2,3},{3,2},{4,5},{5,4},{6,7},{7,6},{8,9},{9,8},{10,11... | collective-permute-start | bytes 14155784 | tf_op jit(solution)/shard_map/ppermute | solution.py:755
  183.4 7.1 %collective-permute-start.2 = (f32[8,128]{1,0:T(8,128)}, f32[8,128]{1,0:T(8,128)S(1)}, u32[]{:S(2)}, u32[]{:S(2)}) collective-permute-start(f32[8,128]{1,0:T(8,128)} %hold.14), channel_id=1, source_target_pairs={{0,1},{1,0},{2,3},{3,2},{4,5},{5,4},{6,7},{7,6},{8,9},{9,8},{10,11... | collective-permute-start | bytes 12296 | tf_op jit(solution)/shard_map/ppermute | solution.py:755
  211.5 68.4 %collective-permute-start.4 = (bf16[80,3072]{1,0:T(8,128)(2,1)}, bf16[80,3072]{1,0:T(8,128)(2,1)S(1)}, u32[]{:S(2)}, u32[]{:S(2)}) collective-permute-start(bf16[80,3072]{1,0:T(8,128)(2,1)} %get-tuple-element.36), channel_id=1, source_target_pairs={{0,2},{2,0},{4,6},{6,4},{8,10},{10,8},{12,14},{14,12},{1,3},{3,1},... | collective-permute-start | bytes 1474568 | tf_op jit(solution)/shard_map/ppermute | solution.py:816
  213.1 95.8 %collective-permute-start.5 = (bf16[80,3072]{1,0:T(8,128)(2,1)}, bf16[80,3072]{1,0:T(8,128)(2,1)S(1)}, u32[]{:S(2)}, u32[]{:S(2)}) collective-permute-start(bf16[80,3072]{1,0:T(8,128)(2,1)} %get-tuple-element.37), channel_id=1, source_target_pairs={{0,4},{2,6},{4,0},{6,2},{8,12},{10,14},{12,8},{14,10},{1,5},{3,7},... | collective-permute-start | bytes 1474568 | tf_op jit(solution)/shard_map/ppermute | solution.py:816
  214.6 100.2 %collective-permute-start.6 = (bf16[80,3072]{1,0:T(8,128)(2,1)}, bf16[80,3072]{1,0:T(8,128)(2,1)S(1)}, u32[]{:S(2)}, u32[]{:S(2)}) collective-permute-start(bf16[80,3072]{1,0:T(8,128)(2,1)} %get-tuple-element.38), channel_id=1, source_target_pairs={{0,6},{2,4},{4,2},{6,0},{8,14},{10,12},{12,10},{14,8},{1,7},{3,5},... | collective-permute-start | bytes 1474568 | tf_op jit(solution)/shard_map/ppermute | solution.py:816
  215.1 99.8 %collective-permute-start.7 = (bf16[80,3072]{1,0:T(8,128)(2,1)}, bf16[80,3072]{1,0:T(8,128)(2,1)S(1)}, u32[]{:S(2)}, u32[]{:S(2)}) collective-permute-start(bf16[80,3072]{1,0:T(8,128)(2,1)} %get-tuple-element.39), channel_id=1, source_target_pairs={{0,8},{2,10},{4,12},{6,14},{8,0},{10,2},{12,4},{14,6},{1,9},{3,11}... | collective-permute-start | bytes 1474568 | tf_op jit(solution)/shard_map/ppermute | solution.py:816
  216.6 98.2 %collective-permute-start.8 = (bf16[80,3072]{1,0:T(8,128)(2,1)}, bf16[80,3072]{1,0:T(8,128)(2,1)S(1)}, u32[]{:S(2)}, u32[]{:S(2)}) collective-permute-start(bf16[80,3072]{1,0:T(8,128)(2,1)} %get-tuple-element.40), channel_id=1, source_target_pairs={{0,10},{2,8},{4,14},{6,12},{8,2},{10,0},{12,6},{14,4},{1,11},{3,9}... | collective-permute-start | bytes 1474568 | tf_op jit(solution)/shard_map/ppermute | solution.py:816
  271.6 8.3 %copy-start.10 = (bf16[80,3072]{1,0:T(8,128)(2,1)S(1)}, bf16[80,3072]{1,0:T(8,128)(2,1)}, u32[]{:S(2)}) copy-start(bf16[80,3072]{1,0:T(8,128)(2,1)} %get-tuple-element.41) | copy-start | bytes 1474564
  271.6 37.4 %copy-start.9 = (bf16[80,3072]{1,0:T(8,128)(2,1)S(1)}, bf16[80,3072]{1,0:T(8,128)(2,1)}, u32[]{:S(2)}) copy-start(bf16[80,3072]{1,0:T(8,128)(2,1)} %get-tuple-element.42) | copy-start | bytes 1474564
  279.9 35.0 %copy-start = (bf16[80,3072]{1,0:T(8,128)(2,1)}, bf16[80,3072]{1,0:T(8,128)(2,1)S(1)}, u32[]{:S(2)}) copy-start(bf16[80,3072]{1,0:T(8,128)(2,1)S(1)} %collective-permute-done.4.refs_1_) | copy-start | bytes 1474564
  279.9 41.2 %collective-permute-start.9 = (bf16[80,3072]{1,0:T(8,128)(2,1)S(1)}, bf16[80,3072]{1,0:T(8,128)(2,1)S(1)}, u32[]{:S(2)}, u32[]{:S(2)}) collective-permute-start(bf16[80,3072]{1,0:T(8,128)(2,1)S(1)} %copy-done.10), channel_id=1, source_target_pairs={{0,12},{2,14},{4,8},{6,10},{8,4},{10,6},{12,0},{14,2},{1,13},{3,15... | collective-permute-start | bytes 1474568 | tf_op jit(solution)/shard_map/ppermute | solution.py:816
  309.0 5.9 %copy-start.1 = (bf16[80,3072]{1,0:T(8,128)(2,1)}, bf16[80,3072]{1,0:T(8,128)(2,1)S(1)}, u32[]{:S(2)}) copy-start(bf16[80,3072]{1,0:T(8,128)(2,1)S(1)} %collective-permute-done.5.refs_2_) | copy-start | bytes 1474564
  309.0 21.1 %collective-permute-start.10 = (bf16[80,3072]{1,0:T(8,128)(2,1)S(1)}, bf16[80,3072]{1,0:T(8,128)(2,1)}, u32[]{:S(2)}, u32[]{:S(2)}) collective-permute-start(bf16[80,3072]{1,0:T(8,128)(2,1)S(1)} %copy-done.9), channel_id=1, source_target_pairs={{0,14},{2,12},{4,10},{6,8},{8,6},{10,4},{12,2},{14,0},{1,15},{3,13... | collective-permute-start | bytes 1474568 | tf_op jit(solution)/shard_map/ppermute | solution.py:816
  314.9 15.2 %copy-start.2 = (bf16[80,3072]{1,0:T(8,128)(2,1)}, bf16[80,3072]{1,0:T(8,128)(2,1)S(1)}, u32[]{:S(2)}) copy-start(bf16[80,3072]{1,0:T(8,128)(2,1)S(1)} %collective-permute-done.6.refs_3_) | copy-start | bytes 1474564
  314.9 15.2 %copy-start.3 = (bf16[80,3072]{1,0:T(8,128)(2,1)}, bf16[80,3072]{1,0:T(8,128)(2,1)S(1)}, u32[]{:S(2)}) copy-start(bf16[80,3072]{1,0:T(8,128)(2,1)S(1)} %collective-permute-done.7.refs_4_) | copy-start | bytes 1474564
  314.9 15.2 %copy-start.4 = (bf16[80,3072]{1,0:T(8,128)(2,1)}, bf16[80,3072]{1,0:T(8,128)(2,1)S(1)}, u32[]{:S(2)}) copy-start(bf16[80,3072]{1,0:T(8,128)(2,1)S(1)} %collective-permute-done.8.refs_5_) | copy-start | bytes 1474564
  321.1 9.0 %copy-start.5 = (bf16[80,3072]{1,0:T(8,128)(2,1)}, bf16[80,3072]{1,0:T(8,128)(2,1)S(1)}, u32[]{:S(2)}) copy-start(bf16[80,3072]{1,0:T(8,128)(2,1)S(1)} %collective-permute-done.9.refs_6_) | copy-start | bytes 1474564
  335.1 17.0 %all-to-all-start.3 = ((f32[32,1,3072]{2,1,0:T(1,128)}), f32[32,1,3072]{2,1,0:T(1,128)S(1)}, u32[]{:S(2)}, u32[]{:S(2)}) async-start(f32[32,1,3072]{2,1,0:T(1,128)} %get-tuple-element.54), calls=%async_computation.3 | async-start | bytes 786432 | tf_op jit(solution)/shard_map/all_to_all | solution.py:787
  339.2 13.2 %slice-start = ((f32[8,128]{1,0:T(8,128)}), f32[1,128]{1,0:T(1,128)S(1)}, s32[]{:S(2)}) async-start(f32[8,128]{1,0:T(8,128)} %coef_dots.1._), calls=%async_computation.5 | async-start | bytes 1024 | tf_op jit(solution)/shard_map/slice | solution.py:826
  (2 other events, 1.2 us)

commit v11 on v10

--- a/solution.py
+++ b/solution.py
@@ -812,10 +812,16 @@
     me = stack([2 * place_i + row_i])
     (rows,) = hold([rows], later(summed))
     parts = run_lane(here, me, rows, mine, other, lanes)
-    home = [parts[0]] + [
-        lax.ppermute(parts[d], ("place", "row"), [(i, i ^ d) for i in range(lanes)])
-        for d in range(1, lanes)
-    ]
+
+    def give(part, d):
+        return lax.ppermute(part, ("place", "row"), [(i, i ^ d) for i in range(lanes)])
+
+    home = {d: give(parts[d], d) for d in range(4, lanes)}
+    home[0], home[1] = parts[0], give(parts[1], 1)
+    for d in (2, 3):
+        home[d] = give(hold([parts[d]], home[d - 1])[0], d)
+    home = [home[d] for d in range(lanes)]
+    (arrived,) = hold([arrived], home[3])
     arrived = arrived.reshape(2, 2 * lanes, row_share, width // reps)
     dots = coef_dots(stack([2 * row_i + core_i]), merge_map, source_w, arrived)
     source_w_grad = finish(merge_map, merge_coef, arrived, dots, scale)

time: 373 us -> 375 us (level)
  starting transfers between devices: 50 us -> 28.7 us
  waiting for transfers between devices: 162 us -> 182 us
    ppermute x7, waiting for transfers between devices: 15.2 us -> 88.8 us  [give(): lax.ppermute(part, ('place', 'row'), [(i, i ^ d) for i in range(lanes)])]
    all_to_all x3, waiting for transfers between devices: 131 us -> 77.5 us  [trade(): return lax.all_to_all(x, axes, split_axis=0, concat_axis=0, tiled=True)]
    ppermute x7, starting transfers between devices: 35.8 us -> 8.14 us  [give(): lax.ppermute(part, ('place', 'row'), [(i, i ^ d) for i in range(lanes)])]
    all_to_all x3, starting transfers between devices: 13.4 us -> 19.9 us  [trade(): return lax.all_to_all(x, axes, split_axis=0, concat_axis=0, tiled=True)]
  transfers between devices with their start and end apart: 14 -> 14, of which waited for: 8 -> 9; matrix products, arithmetic and copies ran while one was open for 1% -> 1% of each run, Pallas kernels for 15% -> 15%
where the time goes in v11:
time: 375 us
  waiting for transfers between devices  182 us (49%)
  Pallas kernels  71.6 us (19%)
  blocking collectives  70.7 us (19%)
  starting transfers between devices  28.7 us (8%)
  local copies, waits for them, and re-layouts  16.2 us (4%)
  other arithmetic  4.07 us (1%)
    ppermute x7, waiting for transfers between devices, give(): lax.ppermute(part, ('place', 'row'), [(i, i ^ d) for i in range(lanes)])  88.8 us
    all_to_all x3, waiting for transfers between devices, trade(): return lax.all_to_all(x, axes, split_axis=0, concat_axis=0, tiled=True)  77.5 us
    all_to_all x2, blocking collectives, trade(): return lax.all_to_all(x, axes, split_axis=0, concat_axis=0, tiled=True)  70.7 us
    pallas_call x1, Pallas kernels, run_lane(): pl.pallas_call(lane_kernel, grid=(1,), in_specs=[smem_spec(), smem_spec()...  20.3 us
    all_to_all x3, starting transfers between devices, trade(): return lax.all_to_all(x, axes, split_axis=0, concat_axis=0, tiled=True)  19.9 us
    pallas_call x2, Pallas kernels, lane_grads(): pl.pallas_call(functools.partial(lane_grad_kernel, other is not None), gr...  17.6 us
    ppermute x4, waiting for transfers between devices, swap(): return lax.ppermute(x, 'core', [(0, 1), (1, 0)])  16 us
    pallas_call x1, Pallas kernels, prepare(): pl.pallas_call(functools.partial(prepare_kernel, capacity, lanes), in_spe...  10.6 us
  transfers between devices with their start and end apart: 14, of which 9 were waited for; matrix products, arithmetic and copies ran while one was open for 1% of the time, Pallas kernels for 15%

profile of v11, /device:TPU:0, one launch (start us, length us, event | category | flops | bytes accessed | tf_op | source)
XLA Modules:
  0.0 374.5 jit_solution(3908699385273304557)
XLA Ops:
  0.6 3.7 reshape.61.hid_ref
  4.9 10.6 %prepare.1 = (bf16[2,4,2,192,768]{4,3,2,1,0:T(8,128)(2,1)}, bf16[640,3200]{1,0:T(8,128)(2,1)}, f32[8,128]{1,0:T(8,128)}, s32[8,128]{1,0:T(8,128)}, s32[8,512]{1,0:T(8,128)}) custom-call(s32[32]{0:T(128)} %a.1, f32[32]{0:T(128)} %b.1, s32[3]{0:T(128)} %pad_add_fusion.place_ref, bf16[32,192,1536]{2,1,0:T(8,128)(2,1)} %src_ref.3, bf16[2880,128]{1,0:T(8,128)(2,1)} %bitcast.39, ...), custom_call_target="tpu_custom_call" | custom-call | flops 10000000000 | bytes 10000000 | tf_op jit(solution)/shard_map/prepare/pallas_call | solution.py:414
  15.6 54.7 %all_to_all.25 = bf16[8,80,3200]{2,1,0:T(8,128)(2,1)} all-to-all(bf16[8,80,3200]{2,1,0:T(8,128)(2,1)} %bitcast.35), channel_id=1, replica_groups=mesh['half'=2,'place'=4,'row'=2,'core'=2] {'place','row'}, dimensions={0} | all-to-all | bytes 8192000 | tf_op jit(solution)/shard_map/all_to_all | solution.py:787
  70.3 4.6 %all-to-all-start.1 = ((bf16[8,2,192,768]{3,2,1,0:T(8,128)(2,1)}), bf16[8,2,192,768]{3,2,1,0:T(8,128)(2,1)}, u32[]{:S(2)}, u32[]{:S(2)}) async-start(bf16[8,2,192,768]{3,2,1,0:T(8,128)(2,1)} %hold.14), calls=%async_computation.1 | async-start | bytes 9437184 | tf_op jit(solution)/shard_map/all_to_all | solution.py:787
  77.5 8.4 %lane_grads_first.1 = bf16[8,2,2,192,384]{4,3,2,1,0:T(8,128)(2,1)} custom-call(s32[1]{0:T(128)} %bitcast.13._, bf16[640,3200]{1,0:T(8,128)(2,1)} %hold.13.grd_ref.hid_ref.flag_ref.refs_0_, bf16[640,3200]{1,0:T(8,128)(2,1)} %hold.13.grd_ref.hid_ref.flag_ref.refs_0_, bf16[640,3200]{1,0:T(8,128)(2,1)} %hold.13.grd_ref.hid_ref.flag_ref.refs_0_), custom_call_target="tpu_custom_call" | custom-call | flops 8000000000 | bytes 8000000 | tf_op jit(solution)/shard_map/lane_grads_first/pallas_call | solution.py:543
  86.1 8.0 %collective-permute-done.1.refs_0_ = bf16[8,2,2,192,384]{4,3,2,1,0:T(8,128)(2,1)S(1)} collective-permute-done((bf16[8,2,2,192,384]{4,3,2,1,0:T(8,128)(2,1)}, bf16[8,2,2,192,384]{4,3,2,1,0:T(8,128)(2,1)S(1)}, u32[]{:S(2)}, u32[]{:S(2)}) %collective-permute-start.1) | collective-permute-done | bytes 4718624 | tf_op jit(solution)/shard_map/ppermute | solution.py:755
  96.2 9.1 %lane_grads_add.1.refs_1_.refs_0_ = bf16[8,2,2,192,384]{4,3,2,1,0:T(8,128)(2,1)} custom-call(s32[1]{0:T(128)} %bitcast.2._.core_ref, bf16[640,3200]{1,0:T(8,128)(2,1)} %hold.13.grd_ref.hid_ref.flag_ref.refs_0_, bf16[640,3200]{1,0:T(8,128)(2,1)} %hold.13.grd_ref.hid_ref.flag_ref.refs_0_, bf16[640,3200]{1,0:T(8,128)(2,1)} %hold.13.grd_ref.hid_ref.flag_ref.refs_0_, ...), custom_call_target="tpu_custom_call" | custom-call | flops 8000000000 | bytes 8000000 | tf_op jit(solution)/shard_map/lane_grads_add/pallas_call | solution.py:543
  105.3 72.7 %all-to-all-done.1.refs_0_ = bf16[8,2,192,768]{3,2,1,0:T(8,128)(2,1)} async-done(((bf16[8,2,192,768]{3,2,1,0:T(8,128)(2,1)}), bf16[8,2,192,768]{3,2,1,0:T(8,128)(2,1)}, u32[]{:S(2)}, u32[]{:S(2)}) %all-to-all-start.1) | async-done | bytes 4718624 | tf_op jit(solution)/shard_map/all_to_all | solution.py:787
  178.0 4.7 %all-to-all-start.2 = ((bf16[16,2,192,384]{3,2,1,0:T(8,128)(2,1)}), bf16[16,2,192,384]{3,2,1,0:T(8,128)(2,1)}, u32[]{:S(2)}, u32[]{:S(2)}) async-start(bf16[16,2,192,384]{3,2,1,0:T(8,128)(2,1)} %bitcast.33), calls=%async_computation.2 | async-start | bytes 9437184 | tf_op jit(solution)/shard_map/all_to_all | solution.py:787
  183.9 6.7 %collective-permute-done.2.refs_1_ = f32[8,128]{1,0:T(8,128)S(1)} collective-permute-done((f32[8,128]{1,0:T(8,128)}, f32[8,128]{1,0:T(8,128)S(1)}, u32[]{:S(2)}, u32[]{:S(2)}) %collective-permute-start.2) | collective-permute-done | bytes 4128 | tf_op jit(solution)/shard_map/ppermute | solution.py:755
  191.1 20.3 %lane_products.1 = (bf16[80,3072]{1,0:T(8,128)(2,1)}, bf16[80,3072]{1,0:T(8,128)(2,1)}, bf16[80,3072]{1,0:T(8,128)(2,1)}, bf16[80,3072]{1,0:T(8,128)(2,1)}, bf16...) custom-call(s32[1]{0:T(128)} %bitcast.2._.core_ref, ...), custom_call_target="tpu_custom_call" | custom-call | flops 20000000000 | bytes 20000000 | tf_op jit(solution)/shard_map/lane_products/pallas_call | solution.py:497
  213.1 35.3 %collective-permute-done.4.refs_1_ = bf16[80,3072]{1,0:T(8,128)(2,1)S(1)} collective-permute-done((bf16[80,3072]{1,0:T(8,128)(2,1)}, bf16[80,3072]{1,0:T(8,128)(2,1)S(1)}, u32[]{:S(2)}, u32[]{:S(2)}) %collective-permute-start.4) | collective-permute-done | bytes 491552 | tf_op jit(solution)/shard_map/ppermute | solution.py:817
  249.2 25.5 %collective-permute-done.5.refs_1_.refs_2_ = bf16[80,3072]{1,0:T(8,128)(2,1)S(1)} collective-permute-done((bf16[80,3072]{1,0:T(8,128)(2,1)}, bf16[80,3072]{1,0:T(8,128)(2,1)S(1)}, u32[]{:S(2)}, u32[]{:S(2)}) %collective-permute-start.5) | collective-permute-done | bytes 491552 | tf_op jit(solution)/shard_map/ppermute | solution.py:817
  276.2 3.7 collective-permute-start.7
  282.0 20.9 %collective-permute-done.6.refs_1_.refs_3_ = bf16[80,3072]{1,0:T(8,128)(2,1)S(1)} collective-permute-done((bf16[80,3072]{1,0:T(8,128)(2,1)}, bf16[80,3072]{1,0:T(8,128)(2,1)S(1)}, u32[]{:S(2)}, u32[]{:S(2)}) %collective-permute-start.6) | collective-permute-done | bytes 491552 | tf_op jit(solution)/shard_map/ppermute | solution.py:817
  303.7 8.1 %coef_dots.1._ = f32[8,128]{1,0:T(8,128)} custom-call(s32[1]{0:T(128)} %bitcast.17.rep_ref, s32[32]{0:T(128)} %a.1, bf16[32,192,1536]{2,1,0:T(8,128)(2,1)} %src_ref.3, bf16[2,16,192,384]{3,2,1,0:T(8,128)(2,1)} %bitcast.16.got_ref.c), custom_call_target="tpu_custom_call" | custom-call | tf_op jit(solution)/shard_map/coef_dots/pallas_call | solution.py:715
  311.8 5.7 %finish.1.refs_8_ = f32[32,192,384]{2,1,0:T(8,128)} custom-call(s32[32]{0:T(128)} %a.1, f32[32]{0:T(128)} %b.1, bf16[2,16,192,384]{3,2,1,0:T(8,128)(2,1)} %bitcast.16.got_ref.c, f32[8,128]{1,0:T(8,128)} %coef_dots.1._), custom_call_target="tpu_custom_call" | custom-call | flops 8000000000 | bytes 8000000 | tf_op jit(solution)/shard_map/finish/pallas_call | solution.py:735
  317.6 7.2 %collective-permute-done.9.refs_6_ = bf16[80,3072]{1,0:T(8,128)(2,1)S(1)} collective-permute-done((bf16[80,3072]{1,0:T(8,128)(2,1)}, bf16[80,3072]{1,0:T(8,128)(2,1)S(1)}, u32[]{:S(2)}, u32[]{:S(2)}) %collective-permute-start.9) | collective-permute-done | bytes 491552 | tf_op jit(solution)/shard_map/ppermute | solution.py:817
  325.6 5.0 %combine.1 = (bf16[128,1536]{1,0:T(8,128)(2,1)}, bf16[2880,128]{1,0:T(8,128)(2,1)}, f32[32,1,3072]{2,1,0:T(1,128)}) custom-call(bf16[128,1536]{1,0:T(8,128)(2,1)} %bitcast.42, f32[8,128]{1,0:T(8,128)} %get-tuple-element.31.gate_ref, s32[8,128]{1,0:T(8,128)} %get-tuple-element.32.pos_ref, s32[4,128]{1,0:T(4,128)} %bitcast.46, bf16[32,2880]{1,0:T(8,128)(2,1)} %bitcast.44, ...), custom_call_target="tpu_custom_call" | custom-call | flops 5000000000 | bytes 5000000 | tf_op jit(solution)/shard_map/combine/pallas_call | solution.py:612
  330.6 10.5 %all-to-all-start.3 = ((f32[32,1,3072]{2,1,0:T(1,128)}), f32[32,1,3072]{2,1,0:T(1,128)S(1)}, u32[]{:S(2)}, u32[]{:S(2)}) async-start(f32[32,1,3072]{2,1,0:T(1,128)} %get-tuple-element.54), calls=%async_computation.3 | async-start | bytes 786432 | tf_op jit(solution)/shard_map/all_to_all | solution.py:787
  341.2 4.2 %unplace.1 = bf16[512,1536]{1,0:T(8,128)(2,1)} custom-call(s32[8,512]{1,0:T(8,128)} %get-tuple-element.52.slot_ref, bf16[80,3072]{1,0:T(8,128)(2,1)} %get-tuple-element.43.refs_0_, bf16[80,3072]{1,0:T(8,128)(2,1)} %get-tuple-element.44.refs_1_, bf16[80,3072]{1,0:T(8,128)(2,1)} %get-tuple-element.45.refs_2_, bf16[80,3072]{1,0:T(8,128)(2,1)} %get-tuple-element.46.refs_3_, ...), custom_call_target="tpu_custom_call" | custom-call | flops 4000000000 | bytes 4000000 | tf_op jit(solution)/shard_map/unplace/pallas_call | solution.py:639
  345.4 3.8 %reshape.68.refs_1_ = bf16[1,128,4,1536]{3,2,1,0:T(4,128)(2,1)} reshape(bf16[512,1536]{1,0:T(8,128)(2,1)} %unplace.1) | data formatting | bytes 3145728 | tf_op jit(solution)/shard_map/reshape | solution.py:831
  349.2 4.9 %all-to-all-done.3 = f32[32,1,3072]{2,1,0:T(1,128)S(1)} async-done(((f32[32,1,3072]{2,1,0:T(1,128)}), f32[32,1,3072]{2,1,0:T(1,128)S(1)}, u32[]{:S(2)}, u32[]{:S(2)}) %all-to-all-start.3) | async-done | bytes 393248 | tf_op jit(solution)/shard_map/all_to_all | solution.py:787
  355.9 15.9 %all_to_all.26 = f32[32,1,3200]{2,1,0:T(1,128)S(1)} all-to-all(f32[32,1,3200]{2,1,0:T(1,128)S(1)} %broadcast_in_dim.17), channel_id=1, replica_groups=mesh['half'=2,'place'=4,'row'=2,'core'=2] {'half','place','row','core'}, dimensions={0} | all-to-all | bytes 819200 | tf_op jit(solution)/shard_map/all_to_all | solution.py:787
  (62 shorter events, 19.3 us)
Async XLA Ops:
  70.3 107.7 %all-to-all-start.1 = ((bf16[8,2,192,768]{3,2,1,0:T(8,128)(2,1)}), bf16[8,2,192,768]{3,2,1,0:T(8,128)(2,1)}, u32[]{:S(2)}, u32[]{:S(2)}) async-start(bf16[8,2,192,768]{3,2,1,0:T(8,128)(2,1)} %hold.14), calls=%async_computation.1 | async-start | bytes 9437184 | tf_op jit(solution)/shard_map/all_to_all | solution.py:787
  75.5 1.4 collective-permute-start
  76.9 0.6 copy-start.7
  85.9 8.1 %collective-permute-start.1 = (bf16[8,2,2,192,384]{4,3,2,1,0:T(8,128)(2,1)}, bf16[8,2,2,192,384]{4,3,2,1,0:T(8,128)(2,1)S(1)}, u32[]{:S(2)}, u32[]{:S(2)}) collective-permute-start(bf16[8,2,2,192,384]{4,3,2,1,0:T(8,128)(2,1)} %lane_grads_first.1), channel_id=1, source_target_pairs={{0,1},{1,0},{2,3},{3,2},{4,5},{5,4},{6,7},{7,6},{8,9},{9,8},{10,11... | collective-permute-start | bytes 14155784 | tf_op jit(solution)/shard_map/ppermute | solution.py:755
  94.0 2.1 copy-start.9
  178.0 124.9 %all-to-all-start.2 = ((bf16[16,2,192,384]{3,2,1,0:T(8,128)(2,1)}), bf16[16,2,192,384]{3,2,1,0:T(8,128)(2,1)}, u32[]{:S(2)}, u32[]{:S(2)}) async-start(bf16[16,2,192,384]{3,2,1,0:T(8,128)(2,1)} %bitcast.33), calls=%async_computation.2 | async-start | bytes 9437184 | tf_op jit(solution)/shard_map/all_to_all | solution.py:787
  182.7 8.4 %collective-permute-start.3 = (bf16[8,2,192,768]{3,2,1,0:T(8,128)(2,1)}, bf16[8,2,192,768]{3,2,1,0:T(8,128)(2,1)}, u32[]{:S(2)}, u32[]{:S(2)}) collective-permute-start(bf16[8,2,192,768]{3,2,1,0:T(8,128)(2,1)} %hold.15.refs_1_.mine), channel_id=1, source_target_pairs={{0,1},{1,0},{2,3},{3,2},{4,5},{5,4},{6,7},{7,6},{8,9},{9,8},{10,11... | collective-permute-start | bytes 14155784 | tf_op jit(solution)/shard_map/ppermute | solution.py:755
  183.4 7.1 %collective-permute-start.2 = (f32[8,128]{1,0:T(8,128)}, f32[8,128]{1,0:T(8,128)S(1)}, u32[]{:S(2)}, u32[]{:S(2)}) collective-permute-start(f32[8,128]{1,0:T(8,128)} %hold.17), channel_id=1, source_target_pairs={{0,1},{1,0},{2,3},{3,2},{4,5},{5,4},{6,7},{7,6},{8,9},{9,8},{10,11... | collective-permute-start | bytes 12296 | tf_op jit(solution)/shard_map/ppermute | solution.py:755
  211.5 36.9 %collective-permute-start.4 = (bf16[80,3072]{1,0:T(8,128)(2,1)}, bf16[80,3072]{1,0:T(8,128)(2,1)S(1)}, u32[]{:S(2)}, u32[]{:S(2)}) collective-permute-start(bf16[80,3072]{1,0:T(8,128)(2,1)} %get-tuple-element.36), channel_id=1, source_target_pairs={{0,2},{2,0},{4,6},{6,4},{8,10},{10,8},{12,14},{14,12},{1,3},{3,1},... | collective-permute-start | bytes 1474568 | tf_op jit(solution)/shard_map/ppermute | solution.py:817
  248.4 0.8 copy-start
  249.2 25.5 %collective-permute-start.5 = (bf16[80,3072]{1,0:T(8,128)(2,1)}, bf16[80,3072]{1,0:T(8,128)(2,1)S(1)}, u32[]{:S(2)}, u32[]{:S(2)}) collective-permute-start(bf16[80,3072]{1,0:T(8,128)(2,1)} %hold.19), channel_id=1, source_target_pairs={{0,4},{2,6},{4,0},{6,2},{8,12},{10,14},{12,8},{14,10},{1,5},{3,7},... | collective-permute-start | bytes 1474568 | tf_op jit(solution)/shard_map/ppermute | solution.py:817
  274.7 0.8 copy-start.1
  275.5 27.4 %collective-permute-start.6 = (bf16[80,3072]{1,0:T(8,128)(2,1)}, bf16[80,3072]{1,0:T(8,128)(2,1)S(1)}, u32[]{:S(2)}, u32[]{:S(2)}) collective-permute-start(bf16[80,3072]{1,0:T(8,128)(2,1)} %hold.20), channel_id=1, source_target_pairs={{0,6},{2,4},{4,2},{6,0},{8,14},{10,12},{12,10},{14,8},{1,7},{3,5},... | collective-permute-start | bytes 1474568 | tf_op jit(solution)/shard_map/ppermute | solution.py:817
  276.2 41.4 %collective-permute-start.10 = (bf16[80,3072]{1,0:T(8,128)(2,1)}, bf16[80,3072]{1,0:T(8,128)(2,1)S(1)}, u32[]{:S(2)}, u32[]{:S(2)}) collective-permute-start(bf16[80,3072]{1,0:T(8,128)(2,1)} %get-tuple-element.42), channel_id=1, source_target_pairs={{0,14},{2,12},{4,10},{6,8},{8,6},{10,4},{12,2},{14,0},{1,15},{3,13... | collective-permute-start | bytes 1474568 | tf_op jit(solution)/shard_map/ppermute | solution.py:817
  276.2 41.4 %collective-permute-start.7 = (bf16[80,3072]{1,0:T(8,128)(2,1)}, bf16[80,3072]{1,0:T(8,128)(2,1)S(1)}, u32[]{:S(2)}, u32[]{:S(2)}) collective-permute-start(bf16[80,3072]{1,0:T(8,128)(2,1)} %get-tuple-element.39), channel_id=1, source_target_pairs={{0,8},{2,10},{4,12},{6,14},{8,0},{10,2},{12,4},{14,6},{1,9},{3,11}... | collective-permute-start | bytes 1474568 | tf_op jit(solution)/shard_map/ppermute | solution.py:817
  279.9 37.7 %collective-permute-start.8 = (bf16[80,3072]{1,0:T(8,128)(2,1)}, bf16[80,3072]{1,0:T(8,128)(2,1)S(1)}, u32[]{:S(2)}, u32[]{:S(2)}) collective-permute-start(bf16[80,3072]{1,0:T(8,128)(2,1)} %get-tuple-element.40), channel_id=1, source_target_pairs={{0,10},{2,8},{4,14},{6,12},{8,2},{10,0},{12,6},{14,4},{1,11},{3,9}... | collective-permute-start | bytes 1474568 | tf_op jit(solution)/shard_map/ppermute | solution.py:817
  280.9 43.9 %collective-permute-start.9 = (bf16[80,3072]{1,0:T(8,128)(2,1)}, bf16[80,3072]{1,0:T(8,128)(2,1)S(1)}, u32[]{:S(2)}, u32[]{:S(2)}) collective-permute-start(bf16[80,3072]{1,0:T(8,128)(2,1)} %get-tuple-element.41), channel_id=1, source_target_pairs={{0,12},{2,14},{4,8},{6,10},{8,4},{10,6},{12,0},{14,2},{1,13},{3,15... | collective-permute-start | bytes 1474568 | tf_op jit(solution)/shard_map/ppermute | solution.py:817
  302.9 0.8 copy-start.2
  317.5 7.2 %copy-start.3 = (bf16[80,3072]{1,0:T(8,128)(2,1)}, bf16[80,3072]{1,0:T(8,128)(2,1)S(1)}, u32[]{:S(2)}) copy-start(bf16[80,3072]{1,0:T(8,128)(2,1)S(1)} %collective-permute-done.10.refs_7_) | copy-start | bytes 1474564
  317.6 7.2 %copy-start.4 = (bf16[80,3072]{1,0:T(8,128)(2,1)}, bf16[80,3072]{1,0:T(8,128)(2,1)S(1)}, u32[]{:S(2)}) copy-start(bf16[80,3072]{1,0:T(8,128)(2,1)S(1)} %collective-permute-done.7.refs_4_) | copy-start | bytes 1474564
  317.6 7.2 %copy-start.5 = (bf16[80,3072]{1,0:T(8,128)(2,1)}, bf16[80,3072]{1,0:T(8,128)(2,1)S(1)}, u32[]{:S(2)}) copy-start(bf16[80,3072]{1,0:T(8,128)(2,1)S(1)} %collective-permute-done.8.refs_5_) | copy-start | bytes 1474564
  324.8 0.8 copy-start.6
  330.6 23.5 %all-to-all-start.3 = ((f32[32,1,3072]{2,1,0:T(1,128)}), f32[32,1,3072]{2,1,0:T(1,128)S(1)}, u32[]{:S(2)}, u32[]{:S(2)}) async-start(f32[32,1,3072]{2,1,0:T(1,128)} %get-tuple-element.54), calls=%async_computation.3 | async-start | bytes 786432 | tf_op jit(solution)/shard_map/all_to_all | solution.py:787
  341.1 13.2 %slice-start = ((f32[8,128]{1,0:T(8,128)}), f32[1,128]{1,0:T(1,128)S(1)}, s32[]{:S(2)}) async-start(f32[8,128]{1,0:T(8,128)} %coef_dots.1._), calls=%async_computation.5 | async-start | bytes 1024 | tf_op jit(solution)/shard_map/slice | solution.py:832
  (1 other events, 0.6 us)

commit v12 on v10

--- a/solution.py
+++ b/solution.py
@@ -380,9 +380,7 @@
         spot = spot + jnp.dot(stacked, spread, preferred_element_type=F32)
     spot = spot.astype(I32)
     slot_pos = jnp.where(spot[2:3] > 0, spot[0:1] * capacity + spot[1:2], -1)
-    partner = jnp.bitwise_xor(spot[0:1], place_ref[2])
-    slot_back = jnp.where(spot[2:3] > 0, partner * capacity + spot[1:2], -1)
-    slot_ref[...] = jnp.broadcast_to(slot_back, slot_ref.shape)
+    slot_ref[...] = jnp.broadcast_to(slot_pos, slot_ref.shape)
     take = lax.broadcasted_iota(I32, (places, slots), 0) == slot_pos
     placed = jnp.sum(jnp.where(take, spot[3:4].astype(F32), 0.0), axis=1, keepdims=True)
     depth = og_ref.shape[1]
@@ -464,7 +462,7 @@
 def lane_kernel(
     core_ref, me_ref, grd_ref, hid_ref, flag_ref, mine, other, *refs
 ):
-    outs, (keep, w_ref, sems) = refs[:-3], refs[-3:]
+    outs, (back_ref, keep, w_ref, sems) = refs[:-4], refs[-4:]
     load_weights(core_ref, mine, other, w_ref, sems)
     half, depth = w_ref.shape[3], w_ref.shape[2]
     first = flag_ref[:, :1].astype(F32) == 0.0
@@ -480,8 +478,8 @@
         for n in range(0, half, TILE):
             at = slice(n, n + TILE)
             both = [dot(grd_ref[...], w_ref[h, m, :, at], ((1,), (0,))) for m in range(2)]
-            to = depth + h * half + n
-            keep[:, to : to + TILE] = jnp.where(first, both[0], both[1]).astype(BF)
+            to = h * half + n
+            back_ref[:, to : to + TILE] = jnp.where(first, both[0], both[1]).astype(BF)
     each = outs[0].shape[0]
     for d, out_ref in enumerate(outs):
         at = pl.ds(pl.multiple_of(jnp.bitwise_xor(me_ref[0], d) * each, each), each)
@@ -493,7 +491,7 @@
     depth = share * blocks
     count = rows.shape[0]
     wide = (rows.shape[1] - 128) // 2
-    part = (count // lanes, 2 * wide)
+    part = (count // lanes, wide)
     return pl.pallas_call(
         lane_kernel,
         grid=(1,),
@@ -506,10 +504,12 @@
             any_spec(),
             any_spec(),
         ],
-        out_specs=[pl.BlockSpec(part, lambda i: (0, 0))] * lanes,
-        out_shape=[jax.ShapeDtypeStruct(part, BF)] * lanes,
+        out_specs=[pl.BlockSpec(part, lambda i: (0, 0))] * lanes
+        + [pl.BlockSpec((count, wide), lambda i: (0, 0))],
+        out_shape=[jax.ShapeDtypeStruct(part, BF)] * lanes
+        + [jax.ShapeDtypeStruct((count, wide), BF)],
         scratch_shapes=[
-            pltpu.VMEM((count, 2 * wide), BF),
+            pltpu.VMEM((count, wide), BF),
             pltpu.VMEM((2, members, depth, half), BF),
             pltpu.SemaphoreType.DMA((2 * blocks,)),
         ],
@@ -623,9 +623,7 @@
     )(og, gates, pos, idx_t, rwt, xt, *homes)
 
 
-def unplace_kernel(slot_ref, *refs):
-    homes, (out_ref, back_ref) = refs[:-2], refs[-2:]
-    gather_rows(homes, back_ref)
+def unplace_kernel(slot_ref, back_ref, out_ref):
     places, width = back_ref.shape
     slots = slot_ref.shape[1]
     take = (lax.broadcasted_iota(I32, (places, slots), 0) == slot_ref[0:1, :]).astype(BF)
@@ -633,21 +631,16 @@
         out_ref[:, n : n + TILE] = dot(take, back_ref[:, n : n + TILE], ((0,), (0,))).astype(BF)
 
 
-def unplace(homes, slot_pos):
-    each, width = homes[0].shape[0], homes[0].shape[1] // 2
-    slots = slot_pos.shape[1]
+def unplace(home, slot_pos):
     return pl.pallas_call(
         unplace_kernel,
-        grid=(1,),
-        in_specs=[pl.BlockSpec(slot_pos.shape, lambda i: (0, 0))]
-        + [pl.BlockSpec((each, width), lambda i: (0, 1))] * len(homes),
-        out_specs=pl.BlockSpec((slots, width), lambda i: (0, 0)),
-        out_shape=jax.ShapeDtypeStruct((slots, width), BF),
-        scratch_shapes=[pltpu.VMEM((len(homes) * each, width), BF)],
+        in_specs=[vmem_spec()] * 2,
+        out_specs=vmem_spec(),
+        out_shape=jax.ShapeDtypeStruct((slot_pos.shape[1], home.shape[1]), BF),
         compiler_params=params(56),
         cost_estimate=cost(4),
         name="unplace",
-    )(slot_pos, *homes)
+    )(slot_pos, home)
 
 
 def coef_kernel(rep_ref, map_ref, src_ref, got_ref, out_ref, order_ref, count_ref, held, weights, sems):
@@ -794,8 +787,11 @@
         stack([row_i, core_i, 2 * place_i + row_i]), merge_map, merge_coef, source_w,
         xt, rwt, router_b, idx_t, hidden.reshape(tok * top, width), og, capacity, lanes,
     )
-    rows = trade(send_rows.reshape(lanes, capacity, send_rows.shape[1]), ("place", "row"))
-    rows = rows.reshape(send_rows.shape)
+    def trade_rows(rows):
+        cut = rows.reshape(lanes, capacity, rows.shape[1])
+        return trade(cut, ("place", "row")).reshape(rows.shape)
+
+    rows = trade_rows(send_rows)
     (combos,) = hold([combos.reshape((blocks,) + combos.shape[2:])], rows)
     mine = trade(combos, ("half", "place"))
     (rows,) = hold([rows], later(rows))
@@ -811,18 +807,21 @@
     other = swap(mine)
     me = stack([2 * place_i + row_i])
     (rows,) = hold([rows], later(summed))
-    parts = run_lane(here, me, rows, mine, other, lanes)
+    *parts, back_rows = run_lane(here, me, rows, mine, other, lanes)
     home = [parts[0]] + [
         lax.ppermute(parts[d], ("place", "row"), [(i, i ^ d) for i in range(lanes)])
         for d in range(1, lanes)
     ]
+    (back_rows,) = hold([back_rows], arrived)
+    home_back = trade_rows(back_rows)
+    (arrived,) = hold([arrived], later(arrived))
     arrived = arrived.reshape(2, 2 * lanes, row_share, width // reps)
     dots = coef_dots(stack([2 * row_i + core_i]), merge_map, source_w, arrived)
     source_w_grad = finish(merge_map, merge_coef, arrived, dots, scale)
     home = hold(home, source_w_grad)
     mixed, token_grad, part = combine(home, og, gates, pos, idx_t, rwt, xt)
     part = jnp.sum(trade(part, everyone), axis=0)
-    hidden_grad = unplace(home, slot_pos).reshape(1, tok, top, width)
+    hidden_grad = unplace(home_back, slot_pos).reshape(1, tok, top, width)
     news = jnp.concatenate([part, dots[:1]], axis=1)
     (news,) = hold([news], hidden_grad)
     news = trade(jnp.broadcast_to(news[None], (devices,) + news.shape), everyone)

time: 373 us -> 404 us (1.083)
  blocking collectives: 70.7 us -> 89.7 us
  waiting for transfers between devices: 162 us -> 175 us
    all_to_all x3, waiting for transfers between devices: 131 us -> 154 us  [trade(): return lax.all_to_all(x, axes, split_axis=0, concat_axis=0, tiled=True)]
    all_to_all x2 -> x3, blocking collectives: 70.7 us -> 89.7 us  [trade(): return lax.all_to_all(x, axes, split_axis=0, concat_axis=0, tiled=True)]
    ppermute x7, waiting for transfers between devices: 15.2 us -> 4.85 us  [on_pairs(): lax.ppermute(parts[d], ('place', 'row'), [(i, i ^ d) for i in range(lanes)])]
    ppermute x4 -> x5, waiting for transfers between devices: 16 us -> 16 us  [swap(): return lax.ppermute(x, 'core', [(0, 1), (1, 0)])]
  transfers between devices with their start and end apart: 14 -> 15, of which waited for: 8 -> 7; matrix products, arithmetic and copies ran while one was open for 1% -> 1% of each run, Pallas kernels for 15% -> 13%
where the time goes in v12:
time: 404 us; the launch traced here: 403 us
  waiting for transfers between devices  175 us (43%)
  blocking collectives  89.7 us (22%)
  Pallas kernels  70.8 us (18%)
  starting transfers between devices  46.4 us (11%)
  local copies, waits for them, and re-layouts  15.7 us (4%)
  other arithmetic  4.07 us (1%)
    all_to_all x3, waiting for transfers between devices, trade(): return lax.all_to_all(x, axes, split_axis=0, concat_axis=0, tiled=True)  154 us
    all_to_all x3, blocking collectives, trade(): return lax.all_to_all(x, axes, split_axis=0, concat_axis=0, tiled=True)  89.7 us
    ppermute x7, starting transfers between devices, on_pairs(): lax.ppermute(parts[d], ('place', 'row'), [(i, i ^ d) for i in range(lanes)])  32.5 us
    pallas_call x1, Pallas kernels, run_lane(): pl.pallas_call(lane_kernel, grid=(1,), in_specs=[smem_spec(), smem_spec()...  19.7 us
    pallas_call x2, Pallas kernels, lane_grads(): pl.pallas_call(functools.partial(lane_grad_kernel, other is not None), gr...  17.5 us
    ppermute x5, waiting for transfers between devices, swap(): return lax.ppermute(x, 'core', [(0, 1), (1, 0)])  16 us
    all_to_all x3, starting transfers between devices, trade(): return lax.all_to_all(x, axes, split_axis=0, concat_axis=0, tiled=True)  13.2 us
    pallas_call x1, Pallas kernels, prepare(): pl.pallas_call(functools.partial(prepare_kernel, capacity, lanes), in_spe...  10.6 us
  transfers between devices with their start and end apart: 15, of which 7 were waited for; matrix products, arithmetic and copies ran while one was open for 1% of the time, Pallas kernels for 13%

profile of v12, /device:TPU:0, one launch (start us, length us, event | category | flops | bytes accessed | tf_op | source)
XLA Modules:
  0.0 402.8 jit_solution(11953891811677486818)
XLA Ops:
  0.6 3.7 reshape.67.hid_ref
  4.9 10.6 %prepare.1 = (bf16[2,4,2,192,768]{4,3,2,1,0:T(8,128)(2,1)}, bf16[640,3200]{1,0:T(8,128)(2,1)}, f32[8,128]{1,0:T(8,128)}, s32[8,128]{1,0:T(8,128)}, s32[8,512]{1,0:T(8,128)}) custom-call(s32[32]{0:T(128)} %a.1, f32[32]{0:T(128)} %b.1, s32[3]{0:T(128)} %pad_add_fusion.place_ref, bf16[32,192,1536]{2,1,0:T(8,128)(2,1)} %src_ref.3, bf16[2880,128]{1,0:T(8,128)(2,1)} %bitcast.42, ...), custom_call_target="tpu_custom_call" | custom-call | flops 10000000000 | bytes 10000000 | tf_op jit(solution)/shard_map/prepare/pallas_call | solution.py:412
  15.6 54.7 %all_to_all.30 = bf16[8,80,3200]{2,1,0:T(8,128)(2,1)} all-to-all(bf16[8,80,3200]{2,1,0:T(8,128)(2,1)} %bitcast.37), channel_id=1, replica_groups=mesh['half'=2,'place'=4,'row'=2,'core'=2] {'place','row'}, dimensions={0} | all-to-all | bytes 8192000 | tf_op jit(solution)/shard_map/all_to_all | solution.py:780
  70.3 4.6 %all-to-all-start.1 = ((bf16[8,2,192,768]{3,2,1,0:T(8,128)(2,1)}), bf16[8,2,192,768]{3,2,1,0:T(8,128)(2,1)}, u32[]{:S(2)}, u32[]{:S(2)}) async-start(bf16[8,2,192,768]{3,2,1,0:T(8,128)(2,1)} %hold.14), calls=%async_computation.1 | async-start | bytes 9437184 | tf_op jit(solution)/shard_map/all_to_all | solution.py:780
  77.5 8.4 %lane_grads_first.1 = bf16[8,2,2,192,384]{4,3,2,1,0:T(8,128)(2,1)} custom-call(s32[1]{0:T(128)} %bitcast.13._, bf16[640,3200]{1,0:T(8,128)(2,1)} %hold.13.grd_ref.hid_ref.flag_ref.refs_0_, bf16[640,3200]{1,0:T(8,128)(2,1)} %hold.13.grd_ref.hid_ref.flag_ref.refs_0_, bf16[640,3200]{1,0:T(8,128)(2,1)} %hold.13.grd_ref.hid_ref.flag_ref.refs_0_), custom_call_target="tpu_custom_call" | custom-call | flops 8000000000 | bytes 8000000 | tf_op jit(solution)/shard_map/lane_grads_first/pallas_call | solution.py:543
  86.0 8.0 %collective-permute-done.1.refs_0_ = bf16[8,2,2,192,384]{4,3,2,1,0:T(8,128)(2,1)S(1)} collective-permute-done((bf16[8,2,2,192,384]{4,3,2,1,0:T(8,128)(2,1)}, bf16[8,2,2,192,384]{4,3,2,1,0:T(8,128)(2,1)S(1)}, u32[]{:S(2)}, u32[]{:S(2)}) %collective-permute-start.1) | collective-permute-done | bytes 4718624 | tf_op jit(solution)/shard_map/ppermute | solution.py:748
  96.1 9.1 %lane_grads_add.1.refs_1_.refs_0_ = bf16[8,2,2,192,384]{4,3,2,1,0:T(8,128)(2,1)} custom-call(s32[1]{0:T(128)} %bitcast.2._.core_ref, bf16[640,3200]{1,0:T(8,128)(2,1)} %hold.13.grd_ref.hid_ref.flag_ref.refs_0_, bf16[640,3200]{1,0:T(8,128)(2,1)} %hold.13.grd_ref.hid_ref.flag_ref.refs_0_, bf16[640,3200]{1,0:T(8,128)(2,1)} %hold.13.grd_ref.hid_ref.flag_ref.refs_0_, ...), custom_call_target="tpu_custom_call" | custom-call | flops 8000000000 | bytes 8000000 | tf_op jit(solution)/shard_map/lane_grads_add/pallas_call | solution.py:543
  105.2 72.7 %all-to-all-done.1.refs_0_ = bf16[8,2,192,768]{3,2,1,0:T(8,128)(2,1)} async-done(((bf16[8,2,192,768]{3,2,1,0:T(8,128)(2,1)}), bf16[8,2,192,768]{3,2,1,0:T(8,128)(2,1)}, u32[]{:S(2)}, u32[]{:S(2)}) %all-to-all-start.1) | async-done | bytes 4718624 | tf_op jit(solution)/shard_map/all_to_all | solution.py:780
  178.0 4.7 %all-to-all-start.2 = ((bf16[16,2,192,384]{3,2,1,0:T(8,128)(2,1)}), bf16[16,2,192,384]{3,2,1,0:T(8,128)(2,1)}, u32[]{:S(2)}, u32[]{:S(2)}) async-start(bf16[16,2,192,384]{3,2,1,0:T(8,128)(2,1)} %bitcast.35), calls=%async_computation.2 | async-start | bytes 9437184 | tf_op jit(solution)/shard_map/all_to_all | solution.py:780
  183.9 6.7 %collective-permute-done.2.refs_1_ = f32[8,128]{1,0:T(8,128)S(1)} collective-permute-done((f32[8,128]{1,0:T(8,128)}, f32[8,128]{1,0:T(8,128)S(1)}, u32[]{:S(2)}, u32[]{:S(2)}) %collective-permute-start.2) | collective-permute-done | bytes 4128 | tf_op jit(solution)/shard_map/ppermute | solution.py:748
  191.1 19.7 %lane_products.1 = (bf16[80,1536]{1,0:T(8,128)(2,1)}, bf16[80,1536]{1,0:T(8,128)(2,1)}, bf16[80,1536]{1,0:T(8,128)(2,1)}, bf16[80,1536]{1,0:T(8,128)(2,1)}, bf16...) custom-call(s32[1]{0:T(128)} %bitcast.2._.core_ref, ...), custom_call_target="tpu_custom_call" | custom-call | flops 20000000000 | bytes 20000000 | tf_op jit(solution)/shard_map/lane_products/pallas_call | solution.py:495
  214.9 58.4 %all-to-all-done.2.refs_1_.refs_0_ = bf16[16,2,192,384]{3,2,1,0:T(8,128)(2,1)} async-done(((bf16[16,2,192,384]{3,2,1,0:T(8,128)(2,1)}), bf16[16,2,192,384]{3,2,1,0:T(8,128)(2,1)}, u32[]{:S(2)}, u32[]{:S(2)}) %all-to-all-start.2) | async-done | bytes 4718624 | tf_op jit(solution)/shard_map/all_to_all | solution.py:780
  273.8 9.5 %collective-permute-start.5 = (bf16[80,1536]{1,0:T(8,128)(2,1)S(1)}, bf16[80,1536]{1,0:T(8,128)(2,1)S(1)}, u32[]{:S(2)}, u32[]{:S(2)}) collective-permute-start(bf16[80,1536]{1,0:T(8,128)(2,1)S(1)} %copy-done.16), channel_id=1, source_target_pairs={{0,4},{2,6},{4,0},{6,2},{8,12},{10,14},{12,8},{14,10},{1,5},{3,7},... | collective-permute-start | bytes 737288 | tf_op jit(solution)/shard_map/ppermute | solution.py:812
  283.5 14.4 %collective-permute-start.7 = (bf16[80,1536]{1,0:T(8,128)(2,1)S(1)}, bf16[80,1536]{1,0:T(8,128)(2,1)S(1)}, u32[]{:S(2)}, u32[]{:S(2)}) collective-permute-start(bf16[80,1536]{1,0:T(8,128)(2,1)S(1)} %copy-done.14), channel_id=1, source_target_pairs={{0,8},{2,10},{4,12},{6,14},{8,0},{10,2},{12,4},{14,6},{1,9},{3,11}... | collective-permute-start | bytes 737288 | tf_op jit(solution)/shard_map/ppermute | solution.py:812
  297.9 8.3 %coef_dots.1._ = f32[8,128]{1,0:T(8,128)} custom-call(s32[1]{0:T(128)} %bitcast.17.rep_ref, s32[32]{0:T(128)} %a.1, bf16[32,192,1536]{2,1,0:T(8,128)(2,1)} %src_ref.3, bf16[2,16,192,384]{3,2,1,0:T(8,128)(2,1)} %bitcast.16.got_ref.c), custom_call_target="tpu_custom_call" | custom-call | tf_op jit(solution)/shard_map/coef_dots/pallas_call | solution.py:708
  310.6 5.7 %finish.1.refs_8_ = f32[32,192,384]{2,1,0:T(8,128)} custom-call(s32[32]{0:T(128)} %a.1, f32[32]{0:T(128)} %b.1, bf16[2,16,192,384]{3,2,1,0:T(8,128)(2,1)} %bitcast.16.got_ref.c, f32[8,128]{1,0:T(8,128)} %coef_dots.1._), custom_call_target="tpu_custom_call" | custom-call | flops 8000000000 | bytes 8000000 | tf_op jit(solution)/shard_map/finish/pallas_call | solution.py:728
  316.4 4.8 %collective-permute-done.9.refs_6_ = bf16[80,1536]{1,0:T(8,128)(2,1)S(1)} collective-permute-done((bf16[80,1536]{1,0:T(8,128)(2,1)S(1)}, bf16[80,1536]{1,0:T(8,128)(2,1)S(1)}, u32[]{:S(2)}, u32[]{:S(2)}) %collective-permute-start.9) | collective-permute-done | bytes 245792 | tf_op jit(solution)/shard_map/ppermute | solution.py:812
  321.9 5.0 %combine.1 = (bf16[128,1536]{1,0:T(8,128)(2,1)}, bf16[2880,128]{1,0:T(8,128)(2,1)}, f32[32,1,3072]{2,1,0:T(1,128)}) custom-call(bf16[128,1536]{1,0:T(8,128)(2,1)} %bitcast.45, f32[8,128]{1,0:T(8,128)} %get-tuple-element.32.gate_ref, s32[8,128]{1,0:T(8,128)} %get-tuple-element.33.pos_ref, s32[4,128]{1,0:T(4,128)} %bitcast.49, bf16[32,2880]{1,0:T(8,128)(2,1)} %bitcast.47, ...), custom_call_target="tpu_custom_call" | custom-call | flops 5000000000 | bytes 5000000 | tf_op jit(solution)/shard_map/combine/pallas_call | solution.py:612
  326.9 15.9 %all_to_all.31 = f32[32,1,3072]{2,1,0:T(1,128)S(1)} all-to-all(f32[32,1,3072]{2,1,0:T(1,128)} %get-tuple-element.56), channel_id=1, replica_groups=mesh['half'=2,'place'=4,'row'=2,'core'=2] {'half','place','row','core'}, dimensions={0} | all-to-all | bytes 786432 | tf_op jit(solution)/shard_map/all_to_all | solution.py:780
  342.8 3.8 all-to-all-start.3
  347.5 23.3 %all-to-all-done.3 = bf16[8,80,1536]{2,1,0:T(8,128)(2,1)S(1)} async-done(((bf16[8,80,1536]{2,1,0:T(8,128)(2,1)}), bf16[8,80,1536]{2,1,0:T(8,128)(2,1)S(1)}, u32[]{:S(2)}, u32[]{:S(2)}) %all-to-all-start.3) | async-done | bytes 1966112 | tf_op jit(solution)/shard_map/all_to_all | solution.py:780
  372.1 4.1 %unplace.1 = bf16[512,1536]{1,0:T(8,128)(2,1)} custom-call(s32[8,512]{1,0:T(8,128)} %get-tuple-element.53.slot_ref, bf16[640,1536]{1,0:T(8,128)(2,1)} %bitcast.38), custom_call_target="tpu_custom_call" | custom-call | flops 4000000000 | bytes 4000000 | tf_op jit(solution)/shard_map/unplace/pallas_call | solution.py:635
  376.2 3.8 reshape.76.refs_1_
  381.0 19.1 %all_to_all.32 = f32[32,1,3200]{2,1,0:T(1,128)S(1)} all-to-all(f32[32,1,3200]{2,1,0:T(1,128)S(1)} %broadcast_in_dim.17), channel_id=1, replica_groups=mesh['half'=2,'place'=4,'row'=2,'core'=2] {'half','place','row','core'}, dimensions={0} | all-to-all | bytes 819200 | tf_op jit(solution)/shard_map/all_to_all | solution.py:780
  (80 shorter events, 22.9 us)
Async XLA Ops:
  70.3 107.7 %all-to-all-start.1 = ((bf16[8,2,192,768]{3,2,1,0:T(8,128)(2,1)}), bf16[8,2,192,768]{3,2,1,0:T(8,128)(2,1)}, u32[]{:S(2)}, u32[]{:S(2)}) async-start(bf16[8,2,192,768]{3,2,1,0:T(8,128)(2,1)} %hold.14), calls=%async_computation.1 | async-start | bytes 9437184 | tf_op jit(solution)/shard_map/all_to_all | solution.py:780
  75.5 1.4 collective-permute-start
  85.8 8.1 %collective-permute-start.1 = (bf16[8,2,2,192,384]{4,3,2,1,0:T(8,128)(2,1)}, bf16[8,2,2,192,384]{4,3,2,1,0:T(8,128)(2,1)S(1)}, u32[]{:S(2)}, u32[]{:S(2)}) collective-permute-start(bf16[8,2,2,192,384]{4,3,2,1,0:T(8,128)(2,1)} %lane_grads_first.1), channel_id=1, source_target_pairs={{0,1},{1,0},{2,3},{3,2},{4,5},{5,4},{6,7},{7,6},{8,9},{9,8},{10,11... | collective-permute-start | bytes 14155784 | tf_op jit(solution)/shard_map/ppermute | solution.py:748
  178.0 95.3 %all-to-all-start.2 = ((bf16[16,2,192,384]{3,2,1,0:T(8,128)(2,1)}), bf16[16,2,192,384]{3,2,1,0:T(8,128)(2,1)}, u32[]{:S(2)}, u32[]{:S(2)}) async-start(bf16[16,2,192,384]{3,2,1,0:T(8,128)(2,1)} %bitcast.35), calls=%async_computation.2 | async-start | bytes 9437184 | tf_op jit(solution)/shard_map/all_to_all | solution.py:780
  182.7 8.4 %collective-permute-start.3 = (bf16[8,2,192,768]{3,2,1,0:T(8,128)(2,1)}, bf16[8,2,192,768]{3,2,1,0:T(8,128)(2,1)}, u32[]{:S(2)}, u32[]{:S(2)}) collective-permute-start(bf16[8,2,192,768]{3,2,1,0:T(8,128)(2,1)} %hold.15.refs_1_.mine), channel_id=1, source_target_pairs={{0,1},{1,0},{2,3},{3,2},{4,5},{5,4},{6,7},{7,6},{8,9},{9,8},{10,11... | collective-permute-start | bytes 14155784 | tf_op jit(solution)/shard_map/ppermute | solution.py:748
  183.4 7.1 %collective-permute-start.2 = (f32[8,128]{1,0:T(8,128)}, f32[8,128]{1,0:T(8,128)S(1)}, u32[]{:S(2)}, u32[]{:S(2)}) collective-permute-start(f32[8,128]{1,0:T(8,128)} %hold.17), channel_id=1, source_target_pairs={{0,1},{1,0},{2,3},{3,2},{4,5},{5,4},{6,7},{7,6},{8,9},{9,8},{10,11... | collective-permute-start | bytes 12296 | tf_op jit(solution)/shard_map/ppermute | solution.py:748
  210.8 63.0 %copy-start.16 = (bf16[80,1536]{1,0:T(8,128)(2,1)S(1)}, bf16[80,1536]{1,0:T(8,128)(2,1)}, u32[]{:S(2)}) copy-start(bf16[80,1536]{1,0:T(8,128)(2,1)} %get-tuple-element.38) | copy-start | bytes 737284
  210.8 72.6 %copy-start.15 = (bf16[80,1536]{1,0:T(8,128)(2,1)S(1)}, bf16[80,1536]{1,0:T(8,128)(2,1)}, u32[]{:S(2)}) copy-start(bf16[80,1536]{1,0:T(8,128)(2,1)} %get-tuple-element.39) | copy-start | bytes 737284
  210.8 95.3 %collective-permute-start.10 = (bf16[80,1536]{1,0:T(8,128)(2,1)}, bf16[80,1536]{1,0:T(8,128)(2,1)S(1)}, u32[]{:S(2)}, u32[]{:S(2)}) collective-permute-start(bf16[80,1536]{1,0:T(8,128)(2,1)} %get-tuple-element.43), channel_id=1, source_target_pairs={{0,14},{2,12},{4,10},{6,8},{8,6},{10,4},{12,2},{14,0},{1,15},{3,13... | collective-permute-start | bytes 737288 | tf_op jit(solution)/shard_map/ppermute | solution.py:812
  214.3 93.3 %collective-permute-start.4 = (bf16[80,1536]{1,0:T(8,128)(2,1)}, bf16[80,1536]{1,0:T(8,128)(2,1)S(1)}, u32[]{:S(2)}, u32[]{:S(2)}) collective-permute-start(bf16[80,1536]{1,0:T(8,128)(2,1)} %get-tuple-element.37), channel_id=1, source_target_pairs={{0,2},{2,0},{4,6},{6,4},{8,10},{10,8},{12,14},{14,12},{1,3},{3,1},... | collective-permute-start | bytes 737288 | tf_op jit(solution)/shard_map/ppermute | solution.py:812
  273.8 9.7 %copy-start.14 = (bf16[80,1536]{1,0:T(8,128)(2,1)S(1)}, bf16[80,1536]{1,0:T(8,128)(2,1)}, u32[]{:S(2)}) copy-start(bf16[80,1536]{1,0:T(8,128)(2,1)} %get-tuple-element.40) | copy-start | bytes 737284
  273.8 9.6 %collective-permute-start.11 = (f32[8,128]{1,0:T(8,128)}, f32[8,128]{1,0:T(8,128)S(1)}, u32[]{:S(2)}, u32[]{:S(2)}) collective-permute-start(f32[8,128]{1,0:T(8,128)} %hold.19), channel_id=1, source_target_pairs={{0,1},{1,0},{2,3},{3,2},{4,5},{5,4},{6,7},{7,6},{8,9},{9,8},{10,11... | collective-permute-start | bytes 12296 | tf_op jit(solution)/shard_map/ppermute | solution.py:748
  273.8 42.5 %collective-permute-start.5 = (bf16[80,1536]{1,0:T(8,128)(2,1)S(1)}, bf16[80,1536]{1,0:T(8,128)(2,1)S(1)}, u32[]{:S(2)}, u32[]{:S(2)}) collective-permute-start(bf16[80,1536]{1,0:T(8,128)(2,1)S(1)} %copy-done.16), channel_id=1, source_target_pairs={{0,4},{2,6},{4,0},{6,2},{8,12},{10,14},{12,8},{14,10},{1,5},{3,7},... | collective-permute-start | bytes 737288 | tf_op jit(solution)/shard_map/ppermute | solution.py:812
  283.4 33.0 %collective-permute-start.6 = (bf16[80,1536]{1,0:T(8,128)(2,1)S(1)}, bf16[80,1536]{1,0:T(8,128)(2,1)S(1)}, u32[]{:S(2)}, u32[]{:S(2)}) collective-permute-start(bf16[80,1536]{1,0:T(8,128)(2,1)S(1)} %copy-done.15), channel_id=1, source_target_pairs={{0,6},{2,4},{4,2},{6,0},{8,14},{10,12},{12,10},{14,8},{1,7},{3,5},... | collective-permute-start | bytes 737288 | tf_op jit(solution)/shard_map/ppermute | solution.py:812
  283.5 14.4 %copy-start.10 = (f32[8,128]{1,0:T(8,128)}, f32[8,128]{1,0:T(8,128)S(1)}, u32[]{:S(2)}) copy-start(f32[8,128]{1,0:T(8,128)S(1)} %collective-permute-done.11.refs_1_) | copy-start | bytes 12292
  283.5 32.9 %collective-permute-start.7 = (bf16[80,1536]{1,0:T(8,128)(2,1)S(1)}, bf16[80,1536]{1,0:T(8,128)(2,1)S(1)}, u32[]{:S(2)}, u32[]{:S(2)}) collective-permute-start(bf16[80,1536]{1,0:T(8,128)(2,1)S(1)} %copy-done.14), channel_id=1, source_target_pairs={{0,8},{2,10},{4,12},{6,14},{8,0},{10,2},{12,4},{14,6},{1,9},{3,11}... | collective-permute-start | bytes 737288 | tf_op jit(solution)/shard_map/ppermute | solution.py:812
  297.9 8.3 %copy-start.13 = (bf16[80,1536]{1,0:T(8,128)(2,1)S(1)}, bf16[80,1536]{1,0:T(8,128)(2,1)}, u32[]{:S(2)}) copy-start(bf16[80,1536]{1,0:T(8,128)(2,1)} %get-tuple-element.41) | copy-start | bytes 737284
  297.9 9.8 %copy-start.12 = (bf16[80,1536]{1,0:T(8,128)(2,1)S(1)}, bf16[80,1536]{1,0:T(8,128)(2,1)}, u32[]{:S(2)}) copy-start(bf16[80,1536]{1,0:T(8,128)(2,1)} %get-tuple-element.42) | copy-start | bytes 737284
  306.2 10.1 %copy-start.1 = (bf16[80,1536]{1,0:T(8,128)(2,1)}, bf16[80,1536]{1,0:T(8,128)(2,1)S(1)}, u32[]{:S(2)}) copy-start(bf16[80,1536]{1,0:T(8,128)(2,1)S(1)} %collective-permute-done.10.refs_7_) | copy-start | bytes 737284
  306.2 10.2 %collective-permute-start.8 = (bf16[80,1536]{1,0:T(8,128)(2,1)S(1)}, bf16[80,1536]{1,0:T(8,128)(2,1)S(1)}, u32[]{:S(2)}, u32[]{:S(2)}) collective-permute-start(bf16[80,1536]{1,0:T(8,128)(2,1)S(1)} %copy-done.13), channel_id=1, source_target_pairs={{0,10},{2,8},{4,14},{6,12},{8,2},{10,0},{12,6},{14,4},{1,11},{3,9}... | collective-permute-start | bytes 737288 | tf_op jit(solution)/shard_map/ppermute | solution.py:812
  307.7 8.7 %copy-start.2 = (bf16[80,1536]{1,0:T(8,128)(2,1)}, bf16[80,1536]{1,0:T(8,128)(2,1)S(1)}, u32[]{:S(2)}) copy-start(bf16[80,1536]{1,0:T(8,128)(2,1)S(1)} %collective-permute-done.4.refs_1_) | copy-start | bytes 737284
  307.7 13.6 %collective-permute-start.9 = (bf16[80,1536]{1,0:T(8,128)(2,1)S(1)}, bf16[80,1536]{1,0:T(8,128)(2,1)S(1)}, u32[]{:S(2)}, u32[]{:S(2)}) collective-permute-start(bf16[80,1536]{1,0:T(8,128)(2,1)S(1)} %copy-done.12), channel_id=1, source_target_pairs={{0,12},{2,14},{4,8},{6,10},{8,4},{10,6},{12,0},{14,2},{1,13},{3,15... | collective-permute-start | bytes 737288 | tf_op jit(solution)/shard_map/ppermute | solution.py:812
  326.9 20.0 %slice-start = ((f32[8,128]{1,0:T(8,128)}), f32[1,128]{1,0:T(1,128)S(1)}, s32[]{:S(2)}) async-start(f32[8,128]{1,0:T(8,128)} %coef_dots.1._), calls=%async_computation.6 | async-start | bytes 1024 | tf_op jit(solution)/shard_map/slice | solution.py:825
  342.8 28.0 %all-to-all-start.3 = ((bf16[8,80,1536]{2,1,0:T(8,128)(2,1)}), bf16[8,80,1536]{2,1,0:T(8,128)(2,1)S(1)}, u32[]{:S(2)}, u32[]{:S(2)}) async-start(bf16[8,80,1536]{2,1,0:T(8,128)(2,1)} %bitcast.19), calls=%async_computation.3 | async-start | bytes 3932160 | tf_op jit(solution)/shard_map/all_to_all | solution.py:780
  (9 other events, 24.9 us)

commit v13 on v10

--- a/solution.py
+++ b/solution.py
@@ -725,6 +725,7 @@
             pltpu.SemaphoreType.DMA((2,)),
         ],
         compiler_params=params(56),
+        cost_estimate=cost(0),
         name="coef_dots",
     )(rep_index, merge_map, source_w, arrived)
 
@@ -746,7 +747,7 @@
             pltpu.SemaphoreType.DMA((count,)),
         ],
         compiler_params=params(56),
-        cost_estimate=cost(8),
+        cost_estimate=cost(0),
         name="finish",
     )(merge_map, merge_coef, arrived, after)
 

time: 373 us -> 361 us (0.968)
  starting transfers between devices: 50 us -> 25.6 us
  waiting for transfers between devices: 162 us -> 175 us
    ppermute x7, waiting for transfers between devices: 15.2 us -> 81.4 us  [on_pairs(): lax.ppermute(parts[d], ('place', 'row'), [(i, i ^ d) for i in range(lanes)])]
    all_to_all x3, waiting for transfers between devices: 131 us -> 77.5 us  [trade(): return lax.all_to_all(x, axes, split_axis=0, concat_axis=0, tiled=True)]
    ppermute x7, starting transfers between devices: 35.8 us -> 10.6 us  [on_pairs(): lax.ppermute(parts[d], ('place', 'row'), [(i, i ^ d) for i in range(lanes)])]
  transfers between devices with their start and end apart: 14 -> 14, of which waited for: 8 -> 9; matrix products, arithmetic and copies ran while one was open for 1% -> 1% of each run, Pallas kernels for 15% -> 16%
where the time goes in v13:
time: 361 us
  waiting for transfers between devices  175 us (48%)
  Pallas kernels  71.5 us (20%)
  blocking collectives  70.7 us (20%)
  starting transfers between devices  25.6 us (7%)
  local copies, waits for them, and re-layouts  13.1 us (4%)
  other arithmetic  4.07 us (1%)
    ppermute x7, waiting for transfers between devices, on_pairs(): lax.ppermute(parts[d], ('place', 'row'), [(i, i ^ d) for i in range(lanes)])  81.4 us
    all_to_all x3, waiting for transfers between devices, trade(): return lax.all_to_all(x, axes, split_axis=0, concat_axis=0, tiled=True)  77.5 us
    all_to_all x2, blocking collectives, trade(): return lax.all_to_all(x, axes, split_axis=0, concat_axis=0, tiled=True)  70.7 us
    pallas_call x1, Pallas kernels, run_lane(): pl.pallas_call(lane_kernel, grid=(1,), in_specs=[smem_spec(), smem_spec()...  20.3 us
    pallas_call x2, Pallas kernels, lane_grads(): pl.pallas_call(functools.partial(lane_grad_kernel, other is not None), gr...  17.6 us
    ppermute x4, waiting for transfers between devices, swap(): return lax.ppermute(x, 'core', [(0, 1), (1, 0)])  16 us
    all_to_all x3, starting transfers between devices, trade(): return lax.all_to_all(x, axes, split_axis=0, concat_axis=0, tiled=True)  14.3 us
    pallas_call x1, Pallas kernels, prepare(): pl.pallas_call(functools.partial(prepare_kernel, capacity, lanes), in_spe...  10.6 us
  transfers between devices with their start and end apart: 14, of which 9 were waited for; matrix products, arithmetic and copies ran while one was open for 1% of the time, Pallas kernels for 16%

profile of v13, /device:TPU:0, one launch (start us, length us, event | category | flops | bytes accessed | tf_op | source)
XLA Modules:
  0.0 360.6 jit_solution(9665642447869442653)
XLA Ops:
  0.6 3.7 %reshape.61.hid_ref = bf16[512,1536]{1,0:T(8,128)(2,1)} reshape(bf16[1,128,4,1536]{3,2,1,0:T(4,128)(2,1)} %param.12) | data formatting | bytes 3145728 | tf_op jit(solution)/shard_map/reshape | solution.py:796
  4.9 10.6 %prepare.1 = (bf16[2,4,2,192,768]{4,3,2,1,0:T(8,128)(2,1)}, bf16[640,3200]{1,0:T(8,128)(2,1)}, f32[8,128]{1,0:T(8,128)}, s32[8,128]{1,0:T(8,128)}, s32[8,512]{1,0:T(8,128)}) custom-call(s32[32]{0:T(128)} %a.1, f32[32]{0:T(128)} %b.1, s32[3]{0:T(128)} %pad_add_fusion.place_ref, bf16[32,192,1536]{2,1,0:T(8,128)(2,1)} %src_ref.3, bf16[2880,128]{1,0:T(8,128)(2,1)} %bitcast.39, ...), custom_call_target="tpu_custom_call" | custom-call | flops 10000000000 | bytes 10000000 | tf_op jit(solution)/shard_map/prepare/pallas_call | solution.py:414
  15.6 54.7 %all_to_all.25 = bf16[8,80,3200]{2,1,0:T(8,128)(2,1)} all-to-all(bf16[8,80,3200]{2,1,0:T(8,128)(2,1)} %bitcast.35), channel_id=1, replica_groups=mesh['half'=2,'place'=4,'row'=2,'core'=2] {'place','row'}, dimensions={0} | all-to-all | bytes 8192000 | tf_op jit(solution)/shard_map/all_to_all | solution.py:788
  70.3 4.6 %all-to-all-start.1 = ((bf16[8,2,192,768]{3,2,1,0:T(8,128)(2,1)}), bf16[8,2,192,768]{3,2,1,0:T(8,128)(2,1)}, u32[]{:S(2)}, u32[]{:S(2)}) async-start(bf16[8,2,192,768]{3,2,1,0:T(8,128)(2,1)} %hold.11), calls=%async_computation.1 | async-start | bytes 9437184 | tf_op jit(solution)/shard_map/all_to_all | solution.py:788
  77.5 8.4 %lane_grads_first.1 = bf16[8,2,2,192,384]{4,3,2,1,0:T(8,128)(2,1)} custom-call(s32[1]{0:T(128)} %bitcast.13._, bf16[640,3200]{1,0:T(8,128)(2,1)} %hold.10.grd_ref.hid_ref.flag_ref.refs_0_, bf16[640,3200]{1,0:T(8,128)(2,1)} %hold.10.grd_ref.hid_ref.flag_ref.refs_0_, bf16[640,3200]{1,0:T(8,128)(2,1)} %hold.10.grd_ref.hid_ref.flag_ref.refs_0_), custom_call_target="tpu_custom_call" | custom-call | flops 8000000000 | bytes 8000000 | tf_op jit(solution)/shard_map/lane_grads_first/pallas_call | solution.py:543
  86.1 8.0 %collective-permute-done.1.refs_0_ = bf16[8,2,2,192,384]{4,3,2,1,0:T(8,128)(2,1)S(1)} collective-permute-done((bf16[8,2,2,192,384]{4,3,2,1,0:T(8,128)(2,1)}, bf16[8,2,2,192,384]{4,3,2,1,0:T(8,128)(2,1)S(1)}, u32[]{:S(2)}, u32[]{:S(2)}) %collective-permute-start.1) | collective-permute-done | bytes 4718624 | tf_op jit(solution)/shard_map/ppermute | solution.py:756
  96.1 9.2 %lane_grads_add.1.refs_1_.refs_0_ = bf16[8,2,2,192,384]{4,3,2,1,0:T(8,128)(2,1)} custom-call(s32[1]{0:T(128)} %bitcast.2._.core_ref, bf16[640,3200]{1,0:T(8,128)(2,1)} %hold.10.grd_ref.hid_ref.flag_ref.refs_0_, bf16[640,3200]{1,0:T(8,128)(2,1)} %hold.10.grd_ref.hid_ref.flag_ref.refs_0_, bf16[640,3200]{1,0:T(8,128)(2,1)} %hold.10.grd_ref.hid_ref.flag_ref.refs_0_, ...), custom_call_target="tpu_custom_call" | custom-call | flops 8000000000 | bytes 8000000 | tf_op jit(solution)/shard_map/lane_grads_add/pallas_call | solution.py:543
  105.3 72.7 %all-to-all-done.1.refs_0_ = bf16[8,2,192,768]{3,2,1,0:T(8,128)(2,1)} async-done(((bf16[8,2,192,768]{3,2,1,0:T(8,128)(2,1)}), bf16[8,2,192,768]{3,2,1,0:T(8,128)(2,1)}, u32[]{:S(2)}, u32[]{:S(2)}) %all-to-all-start.1) | async-done | bytes 4718624 | tf_op jit(solution)/shard_map/all_to_all | solution.py:788
  178.0 4.7 %all-to-all-start.2 = ((bf16[16,2,192,384]{3,2,1,0:T(8,128)(2,1)}), bf16[16,2,192,384]{3,2,1,0:T(8,128)(2,1)}, u32[]{:S(2)}, u32[]{:S(2)}) async-start(bf16[16,2,192,384]{3,2,1,0:T(8,128)(2,1)} %bitcast.33), calls=%async_computation.2 | async-start | bytes 9437184 | tf_op jit(solution)/shard_map/all_to_all | solution.py:788
  183.9 6.7 %collective-permute-done.2.refs_1_ = f32[8,128]{1,0:T(8,128)S(1)} collective-permute-done((f32[8,128]{1,0:T(8,128)}, f32[8,128]{1,0:T(8,128)S(1)}, u32[]{:S(2)}, u32[]{:S(2)}) %collective-permute-start.2) | collective-permute-done | bytes 4128 | tf_op jit(solution)/shard_map/ppermute | solution.py:756
  191.1 20.3 %lane_products.1 = (bf16[80,3072]{1,0:T(8,128)(2,1)}, bf16[80,3072]{1,0:T(8,128)(2,1)}, bf16[80,3072]{1,0:T(8,128)(2,1)}, bf16[80,3072]{1,0:T(8,128)(2,1)}, bf16...) custom-call(s32[1]{0:T(128)} %bitcast.2._.core_ref, ...), custom_call_target="tpu_custom_call" | custom-call | flops 20000000000 | bytes 20000000 | tf_op jit(solution)/shard_map/lane_products/pallas_call | solution.py:497
  218.0 53.9 %collective-permute-done.4.refs_1_ = bf16[80,3072]{1,0:T(8,128)(2,1)S(1)} collective-permute-done((bf16[80,3072]{1,0:T(8,128)(2,1)}, bf16[80,3072]{1,0:T(8,128)(2,1)S(1)}, u32[]{:S(2)}, u32[]{:S(2)}) %collective-permute-start.4) | collective-permute-done | bytes 491552 | tf_op jit(solution)/shard_map/ppermute | solution.py:817
  272.0 4.0 %collective-permute-start.10 = (bf16[80,3072]{1,0:T(8,128)(2,1)}, bf16[80,3072]{1,0:T(8,128)(2,1)}, u32[]{:S(2)}, u32[]{:S(2)}) collective-permute-start(bf16[80,3072]{1,0:T(8,128)(2,1)} %get-tuple-element.42), channel_id=1, source_target_pairs={{0,14},{2,12},{4,10},{6,8},{8,6},{10,4},{12,2},{14,0},{1,15},{3,13... | collective-permute-start | bytes 1474568 | tf_op jit(solution)/shard_map/ppermute | solution.py:817
  275.9 8.2 %coef_dots.1._ = f32[8,128]{1,0:T(8,128)} custom-call(s32[1]{0:T(128)} %bitcast.17.rep_ref, s32[32]{0:T(128)} %a.1, bf16[32,192,1536]{2,1,0:T(8,128)(2,1)} %src_ref.3, bf16[2,16,192,384]{3,2,1,0:T(8,128)(2,1)} %bitcast.16.got_ref.c), custom_call_target="tpu_custom_call" | custom-call | tf_op jit(solution)/shard_map/coef_dots/pallas_call | solution.py:715
  284.1 5.7 %finish.1.refs_8_ = f32[32,192,384]{2,1,0:T(8,128)} custom-call(s32[32]{0:T(128)} %a.1, f32[32]{0:T(128)} %b.1, bf16[2,16,192,384]{3,2,1,0:T(8,128)(2,1)} %bitcast.16.got_ref.c, f32[8,128]{1,0:T(8,128)} %coef_dots.1._), custom_call_target="tpu_custom_call" | custom-call | tf_op jit(solution)/shard_map/finish/pallas_call | solution.py:736
  289.9 8.1 %collective-permute-done.8.refs_5_ = bf16[80,3072]{1,0:T(8,128)(2,1)S(1)} collective-permute-done((bf16[80,3072]{1,0:T(8,128)(2,1)}, bf16[80,3072]{1,0:T(8,128)(2,1)S(1)}, u32[]{:S(2)}, u32[]{:S(2)}) %collective-permute-start.8) | collective-permute-done | bytes 491552 | tf_op jit(solution)/shard_map/ppermute | solution.py:817
  297.9 10.8 %collective-permute-done.9.refs_6_ = bf16[80,3072]{1,0:T(8,128)(2,1)S(1)} collective-permute-done((bf16[80,3072]{1,0:T(8,128)(2,1)}, bf16[80,3072]{1,0:T(8,128)(2,1)S(1)}, u32[]{:S(2)}, u32[]{:S(2)}) %collective-permute-start.9) | collective-permute-done | bytes 491552 | tf_op jit(solution)/shard_map/ppermute | solution.py:817
  308.7 8.6 %collective-permute-done.10.refs_7_ = bf16[80,3072]{1,0:T(8,128)(2,1)} collective-permute-done((bf16[80,3072]{1,0:T(8,128)(2,1)}, bf16[80,3072]{1,0:T(8,128)(2,1)}, u32[]{:S(2)}, u32[]{:S(2)}) %collective-permute-start.10) | collective-permute-done | bytes 491552 | tf_op jit(solution)/shard_map/ppermute | solution.py:817
  317.3 5.0 %combine.1 = (bf16[128,1536]{1,0:T(8,128)(2,1)}, bf16[2880,128]{1,0:T(8,128)(2,1)}, f32[32,1,3072]{2,1,0:T(1,128)}) custom-call(bf16[128,1536]{1,0:T(8,128)(2,1)} %bitcast.42, f32[8,128]{1,0:T(8,128)} %get-tuple-element.31.gate_ref, s32[8,128]{1,0:T(8,128)} %get-tuple-element.32.pos_ref, s32[4,128]{1,0:T(4,128)} %bitcast.46, bf16[32,2880]{1,0:T(8,128)(2,1)} %bitcast.44, ...), custom_call_target="tpu_custom_call" | custom-call | flops 5000000000 | bytes 5000000 | tf_op jit(solution)/shard_map/combine/pallas_call | solution.py:612
  322.3 4.9 %all-to-all-start.3 = ((f32[32,1,3072]{2,1,0:T(1,128)}), f32[32,1,3072]{2,1,0:T(1,128)S(1)}, u32[]{:S(2)}, u32[]{:S(2)}) async-start(f32[32,1,3072]{2,1,0:T(1,128)} %get-tuple-element.54), calls=%async_computation.3 | async-start | bytes 786432 | tf_op jit(solution)/shard_map/all_to_all | solution.py:788
  327.3 4.2 %unplace.1 = bf16[512,1536]{1,0:T(8,128)(2,1)} custom-call(s32[8,512]{1,0:T(8,128)} %get-tuple-element.52.slot_ref, bf16[80,3072]{1,0:T(8,128)(2,1)} %get-tuple-element.43.refs_0_, bf16[80,3072]{1,0:T(8,128)(2,1)} %get-tuple-element.44.refs_1_, bf16[80,3072]{1,0:T(8,128)(2,1)} %get-tuple-element.45.refs_2_, bf16[80,3072]{1,0:T(8,128)(2,1)} %get-tuple-element.46.refs_3_, ...), custom_call_target="tpu_custom_call" | custom-call | flops 4000000000 | bytes 4000000 | tf_op jit(solution)/shard_map/unplace/pallas_call | solution.py:639
  331.5 3.8 %reshape.68.refs_1_ = bf16[1,128,4,1536]{3,2,1,0:T(4,128)(2,1)} reshape(bf16[512,1536]{1,0:T(8,128)(2,1)} %unplace.1) | data formatting | bytes 3145728 | tf_op jit(solution)/shard_map/reshape | solution.py:826
  335.3 4.9 %all-to-all-done.3 = f32[32,1,3072]{2,1,0:T(1,128)S(1)} async-done(((f32[32,1,3072]{2,1,0:T(1,128)}), f32[32,1,3072]{2,1,0:T(1,128)S(1)}, u32[]{:S(2)}, u32[]{:S(2)}) %all-to-all-start.3) | async-done | bytes 393248 | tf_op jit(solution)/shard_map/all_to_all | solution.py:788
  342.0 15.9 %all_to_all.26 = f32[32,1,3200]{2,1,0:T(1,128)S(1)} all-to-all(f32[32,1,3200]{2,1,0:T(1,128)S(1)} %broadcast_in_dim.17), channel_id=1, replica_groups=mesh['half'=2,'place'=4,'row'=2,'core'=2] {'half','place','row','core'}, dimensions={0} | all-to-all | bytes 819200 | tf_op jit(solution)/shard_map/all_to_all | solution.py:788
  (57 shorter events, 18.3 us)
Async XLA Ops:
  70.3 107.7 %all-to-all-start.1 = ((bf16[8,2,192,768]{3,2,1,0:T(8,128)(2,1)}), bf16[8,2,192,768]{3,2,1,0:T(8,128)(2,1)}, u32[]{:S(2)}, u32[]{:S(2)}) async-start(bf16[8,2,192,768]{3,2,1,0:T(8,128)(2,1)} %hold.11), calls=%async_computation.1 | async-start | bytes 9437184 | tf_op jit(solution)/shard_map/all_to_all | solution.py:788
  75.5 1.4 collective-permute-start
  76.9 0.6 copy-start.6
  85.9 8.1 %collective-permute-start.1 = (bf16[8,2,2,192,384]{4,3,2,1,0:T(8,128)(2,1)}, bf16[8,2,2,192,384]{4,3,2,1,0:T(8,128)(2,1)S(1)}, u32[]{:S(2)}, u32[]{:S(2)}) collective-permute-start(bf16[8,2,2,192,384]{4,3,2,1,0:T(8,128)(2,1)} %lane_grads_first.1), channel_id=1, source_target_pairs={{0,1},{1,0},{2,3},{3,2},{4,5},{5,4},{6,7},{7,6},{8,9},{9,8},{10,11... | collective-permute-start | bytes 14155784 | tf_op jit(solution)/shard_map/ppermute | solution.py:756
  94.0 2.1 copy-start.8
  178.0 98.0 %all-to-all-start.2 = ((bf16[16,2,192,384]{3,2,1,0:T(8,128)(2,1)}), bf16[16,2,192,384]{3,2,1,0:T(8,128)(2,1)}, u32[]{:S(2)}, u32[]{:S(2)}) async-start(bf16[16,2,192,384]{3,2,1,0:T(8,128)(2,1)} %bitcast.33), calls=%async_computation.2 | async-start | bytes 9437184 | tf_op jit(solution)/shard_map/all_to_all | solution.py:788
  182.7 8.4 %collective-permute-start.3 = (bf16[8,2,192,768]{3,2,1,0:T(8,128)(2,1)}, bf16[8,2,192,768]{3,2,1,0:T(8,128)(2,1)}, u32[]{:S(2)}, u32[]{:S(2)}) collective-permute-start(bf16[8,2,192,768]{3,2,1,0:T(8,128)(2,1)} %hold.12.refs_1_.mine), channel_id=1, source_target_pairs={{0,1},{1,0},{2,3},{3,2},{4,5},{5,4},{6,7},{7,6},{8,9},{9,8},{10,11... | collective-permute-start | bytes 14155784 | tf_op jit(solution)/shard_map/ppermute | solution.py:756
  183.4 7.1 %collective-permute-start.2 = (f32[8,128]{1,0:T(8,128)}, f32[8,128]{1,0:T(8,128)S(1)}, u32[]{:S(2)}, u32[]{:S(2)}) collective-permute-start(f32[8,128]{1,0:T(8,128)} %hold.14), channel_id=1, source_target_pairs={{0,1},{1,0},{2,3},{3,2},{4,5},{5,4},{6,7},{7,6},{8,9},{9,8},{10,11... | collective-permute-start | bytes 12296 | tf_op jit(solution)/shard_map/ppermute | solution.py:756
  190.5 0.6 copy-start.7
  211.4 60.5 %collective-permute-start.4 = (bf16[80,3072]{1,0:T(8,128)(2,1)}, bf16[80,3072]{1,0:T(8,128)(2,1)S(1)}, u32[]{:S(2)}, u32[]{:S(2)}) collective-permute-start(bf16[80,3072]{1,0:T(8,128)(2,1)} %get-tuple-element.36), channel_id=1, source_target_pairs={{0,2},{2,0},{4,6},{6,4},{8,10},{10,8},{12,14},{14,12},{1,3},{3,1},... | collective-permute-start | bytes 1474568 | tf_op jit(solution)/shard_map/ppermute | solution.py:817
  213.1 58.9 %collective-permute-start.5 = (bf16[80,3072]{1,0:T(8,128)(2,1)}, bf16[80,3072]{1,0:T(8,128)(2,1)S(1)}, u32[]{:S(2)}, u32[]{:S(2)}) collective-permute-start(bf16[80,3072]{1,0:T(8,128)(2,1)} %get-tuple-element.37), channel_id=1, source_target_pairs={{0,4},{2,6},{4,0},{6,2},{8,12},{10,14},{12,8},{14,10},{1,5},{3,7},... | collective-permute-start | bytes 1474568 | tf_op jit(solution)/shard_map/ppermute | solution.py:817
  214.5 75.3 %collective-permute-start.6 = (bf16[80,3072]{1,0:T(8,128)(2,1)}, bf16[80,3072]{1,0:T(8,128)(2,1)S(1)}, u32[]{:S(2)}, u32[]{:S(2)}) collective-permute-start(bf16[80,3072]{1,0:T(8,128)(2,1)} %get-tuple-element.38), channel_id=1, source_target_pairs={{0,6},{2,4},{4,2},{6,0},{8,14},{10,12},{12,10},{14,8},{1,7},{3,5},... | collective-permute-start | bytes 1474568 | tf_op jit(solution)/shard_map/ppermute | solution.py:817
  215.0 74.8 %collective-permute-start.7 = (bf16[80,3072]{1,0:T(8,128)(2,1)}, bf16[80,3072]{1,0:T(8,128)(2,1)S(1)}, u32[]{:S(2)}, u32[]{:S(2)}) collective-permute-start(bf16[80,3072]{1,0:T(8,128)(2,1)} %get-tuple-element.39), channel_id=1, source_target_pairs={{0,8},{2,10},{4,12},{6,14},{8,0},{10,2},{12,4},{14,6},{1,9},{3,11}... | collective-permute-start | bytes 1474568 | tf_op jit(solution)/shard_map/ppermute | solution.py:817
  216.6 81.3 %collective-permute-start.8 = (bf16[80,3072]{1,0:T(8,128)(2,1)}, bf16[80,3072]{1,0:T(8,128)(2,1)S(1)}, u32[]{:S(2)}, u32[]{:S(2)}) collective-permute-start(bf16[80,3072]{1,0:T(8,128)(2,1)} %get-tuple-element.40), channel_id=1, source_target_pairs={{0,10},{2,8},{4,14},{6,12},{8,2},{10,0},{12,6},{14,4},{1,11},{3,9}... | collective-permute-start | bytes 1474568 | tf_op jit(solution)/shard_map/ppermute | solution.py:817
  271.9 12.2 %copy-start = (bf16[80,3072]{1,0:T(8,128)(2,1)}, bf16[80,3072]{1,0:T(8,128)(2,1)S(1)}, u32[]{:S(2)}) copy-start(bf16[80,3072]{1,0:T(8,128)(2,1)S(1)} %collective-permute-done.4.refs_1_) | copy-start | bytes 1474564
  272.0 36.8 %collective-permute-start.9 = (bf16[80,3072]{1,0:T(8,128)(2,1)}, bf16[80,3072]{1,0:T(8,128)(2,1)S(1)}, u32[]{:S(2)}, u32[]{:S(2)}) collective-permute-start(bf16[80,3072]{1,0:T(8,128)(2,1)} %get-tuple-element.41), channel_id=1, source_target_pairs={{0,12},{2,14},{4,8},{6,10},{8,4},{10,6},{12,0},{14,2},{1,13},{3,15... | collective-permute-start | bytes 1474568 | tf_op jit(solution)/shard_map/ppermute | solution.py:817
  272.0 12.2 %copy-start.1 = (bf16[80,3072]{1,0:T(8,128)(2,1)}, bf16[80,3072]{1,0:T(8,128)(2,1)S(1)}, u32[]{:S(2)}) copy-start(bf16[80,3072]{1,0:T(8,128)(2,1)S(1)} %collective-permute-done.5.refs_2_) | copy-start | bytes 1474564
  272.0 45.3 %collective-permute-start.10 = (bf16[80,3072]{1,0:T(8,128)(2,1)}, bf16[80,3072]{1,0:T(8,128)(2,1)}, u32[]{:S(2)}, u32[]{:S(2)}) collective-permute-start(bf16[80,3072]{1,0:T(8,128)(2,1)} %get-tuple-element.42), channel_id=1, source_target_pairs={{0,14},{2,12},{4,10},{6,8},{8,6},{10,4},{12,2},{14,0},{1,15},{3,13... | collective-permute-start | bytes 1474568 | tf_op jit(solution)/shard_map/ppermute | solution.py:817
  289.8 27.5 %copy-start.2 = (bf16[80,3072]{1,0:T(8,128)(2,1)}, bf16[80,3072]{1,0:T(8,128)(2,1)S(1)}, u32[]{:S(2)}) copy-start(bf16[80,3072]{1,0:T(8,128)(2,1)S(1)} %collective-permute-done.6.refs_3_) | copy-start | bytes 1474564
  289.9 27.5 %copy-start.3 = (bf16[80,3072]{1,0:T(8,128)(2,1)}, bf16[80,3072]{1,0:T(8,128)(2,1)S(1)}, u32[]{:S(2)}) copy-start(bf16[80,3072]{1,0:T(8,128)(2,1)S(1)} %collective-permute-done.7.refs_4_) | copy-start | bytes 1474564
  297.9 19.4 %copy-start.4 = (bf16[80,3072]{1,0:T(8,128)(2,1)}, bf16[80,3072]{1,0:T(8,128)(2,1)S(1)}, u32[]{:S(2)}) copy-start(bf16[80,3072]{1,0:T(8,128)(2,1)S(1)} %collective-permute-done.8.refs_5_) | copy-start | bytes 1474564
  308.7 8.6 %copy-start.5 = (bf16[80,3072]{1,0:T(8,128)(2,1)}, bf16[80,3072]{1,0:T(8,128)(2,1)S(1)}, u32[]{:S(2)}) copy-start(bf16[80,3072]{1,0:T(8,128)(2,1)S(1)} %collective-permute-done.9.refs_6_) | copy-start | bytes 1474564
  322.3 17.9 %all-to-all-start.3 = ((f32[32,1,3072]{2,1,0:T(1,128)}), f32[32,1,3072]{2,1,0:T(1,128)S(1)}, u32[]{:S(2)}, u32[]{:S(2)}) async-start(f32[32,1,3072]{2,1,0:T(1,128)} %get-tuple-element.54), calls=%async_computation.3 | async-start | bytes 786432 | tf_op jit(solution)/shard_map/all_to_all | solution.py:788
  327.2 13.2 %slice-start = ((f32[8,128]{1,0:T(8,128)}), f32[1,128]{1,0:T(1,128)S(1)}, s32[]{:S(2)}) async-start(f32[8,128]{1,0:T(8,128)} %coef_dots.1._), calls=%async_computation.5 | async-start | bytes 1024 | tf_op jit(solution)/shard_map/slice | solution.py:827

commit v14 on v13

--- a/solution.py
+++ b/solution.py
@@ -813,14 +813,17 @@
     me = stack([2 * place_i + row_i])
     (rows,) = hold([rows], later(summed))
     parts = run_lane(here, me, rows, mine, other, lanes)
-    home = [parts[0]] + [
-        lax.ppermute(parts[d], ("place", "row"), [(i, i ^ d) for i in range(lanes)])
-        for d in range(1, lanes)
-    ]
+
+    def give(d):
+        return lax.ppermute(parts[d], ("place", "row"), [(i, i ^ d) for i in range(lanes)])
+
+    order = [3] + list(range(4, lanes)) + [2, 1]
+    home = [give(d) for d in order]
     arrived = arrived.reshape(2, 2 * lanes, row_share, width // reps)
     dots = coef_dots(stack([2 * row_i + core_i]), merge_map, source_w, arrived)
     source_w_grad = finish(merge_map, merge_coef, arrived, dots, scale)
-    home = hold(home, source_w_grad)
+    home = dict(zip(order, hold(home, source_w_grad)))
+    home = [parts[0]] + [home[d] for d in range(1, lanes)]
     mixed, token_grad, part = combine(home, og, gates, pos, idx_t, rwt, xt)
     part = jnp.sum(trade(part, everyone), axis=0)
     hidden_grad = unplace(home, slot_pos).reshape(1, tok, top, width)

time: 361 us -> 365 us (1.011)
  transfers between devices with their start and end apart: 14 -> 14, of which waited for: 9 -> 10; matrix products, arithmetic and copies ran while one was open for 1% -> 1% of each run, Pallas kernels for 16% -> 15%
where the time goes in v14:
time: 365 us; the launch traced here: 364 us
  waiting for transfers between devices  176 us (48%)
  Pallas kernels  71.5 us (20%)
  blocking collectives  70.7 us (19%)
  starting transfers between devices  27.3 us (7%)
  local copies, waits for them, and re-layouts  14 us (4%)
  other arithmetic  4.07 us (1%)
    ppermute x7, waiting for transfers between devices, give(): lax.ppermute(parts[d], ('place', 'row'), [(i, i ^ d) for i in range(lanes)])  82.4 us
    all_to_all x3, waiting for transfers between devices, trade(): return lax.all_to_all(x, axes, split_axis=0, concat_axis=0, tiled=True)  77.5 us
    all_to_all x2, blocking collectives, trade(): return lax.all_to_all(x, axes, split_axis=0, concat_axis=0, tiled=True)  70.7 us
    pallas_call x1, Pallas kernels, run_lane(): pl.pallas_call(lane_kernel, grid=(1,), in_specs=[smem_spec(), smem_spec()...  20.3 us
    pallas_call x2, Pallas kernels, lane_grads(): pl.pallas_call(functools.partial(lane_grad_kernel, other is not None), gr...  17.6 us
    ppermute x4, waiting for transfers between devices, swap(): return lax.ppermute(x, 'core', [(0, 1), (1, 0)])  16 us
    all_to_all x3, starting transfers between devices, trade(): return lax.all_to_all(x, axes, split_axis=0, concat_axis=0, tiled=True)  14.3 us
    ppermute x7, starting transfers between devices, give(): lax.ppermute(parts[d], ('place', 'row'), [(i, i ^ d) for i in range(lanes)])  12.2 us
  transfers between devices with their start and end apart: 14, of which 10 were waited for; matrix products, arithmetic and copies ran while one was open for 1% of the time, Pallas kernels for 15%

profile of v14, /device:TPU:0, one launch (start us, length us, event | category | flops | bytes accessed | tf_op | source)
XLA Modules:
  0.0 364.2 jit_solution(6750414142813387191)
XLA Ops:
  0.6 3.7 %reshape.61.hid_ref = bf16[512,1536]{1,0:T(8,128)(2,1)} reshape(bf16[1,128,4,1536]{3,2,1,0:T(4,128)(2,1)} %param.12) | data formatting | bytes 3145728 | tf_op jit(solution)/shard_map/reshape | solution.py:796
  4.9 10.6 %prepare.1 = (bf16[2,4,2,192,768]{4,3,2,1,0:T(8,128)(2,1)}, bf16[640,3200]{1,0:T(8,128)(2,1)}, f32[8,128]{1,0:T(8,128)}, s32[8,128]{1,0:T(8,128)}, s32[8,512]{1,0:T(8,128)}) custom-call(s32[32]{0:T(128)} %a.1, f32[32]{0:T(128)} %b.1, s32[3]{0:T(128)} %pad_add_fusion.place_ref, bf16[32,192,1536]{2,1,0:T(8,128)(2,1)} %src_ref.3, bf16[2880,128]{1,0:T(8,128)(2,1)} %bitcast.39, ...), custom_call_target="tpu_custom_call" | custom-call | flops 10000000000 | bytes 10000000 | tf_op jit(solution)/shard_map/prepare/pallas_call | solution.py:414
  15.6 54.7 %all_to_all.25 = bf16[8,80,3200]{2,1,0:T(8,128)(2,1)} all-to-all(bf16[8,80,3200]{2,1,0:T(8,128)(2,1)} %bitcast.35), channel_id=1, replica_groups=mesh['half'=2,'place'=4,'row'=2,'core'=2] {'place','row'}, dimensions={0} | all-to-all | bytes 8192000 | tf_op jit(solution)/shard_map/all_to_all | solution.py:788
  70.3 4.6 %all-to-all-start.1 = ((bf16[8,2,192,768]{3,2,1,0:T(8,128)(2,1)}), bf16[8,2,192,768]{3,2,1,0:T(8,128)(2,1)}, u32[]{:S(2)}, u32[]{:S(2)}) async-start(bf16[8,2,192,768]{3,2,1,0:T(8,128)(2,1)} %hold.11), calls=%async_computation.1 | async-start | bytes 9437184 | tf_op jit(solution)/shard_map/all_to_all | solution.py:788
  77.5 8.4 %lane_grads_first.1 = bf16[8,2,2,192,384]{4,3,2,1,0:T(8,128)(2,1)} custom-call(s32[1]{0:T(128)} %bitcast.13._, bf16[640,3200]{1,0:T(8,128)(2,1)} %hold.10.grd_ref.hid_ref.flag_ref.refs_0_, bf16[640,3200]{1,0:T(8,128)(2,1)} %hold.10.grd_ref.hid_ref.flag_ref.refs_0_, bf16[640,3200]{1,0:T(8,128)(2,1)} %hold.10.grd_ref.hid_ref.flag_ref.refs_0_), custom_call_target="tpu_custom_call" | custom-call | flops 8000000000 | bytes 8000000 | tf_op jit(solution)/shard_map/lane_grads_first/pallas_call | solution.py:543
  86.1 8.0 %collective-permute-done.1.refs_0_ = bf16[8,2,2,192,384]{4,3,2,1,0:T(8,128)(2,1)S(1)} collective-permute-done((bf16[8,2,2,192,384]{4,3,2,1,0:T(8,128)(2,1)}, bf16[8,2,2,192,384]{4,3,2,1,0:T(8,128)(2,1)S(1)}, u32[]{:S(2)}, u32[]{:S(2)}) %collective-permute-start.1) | collective-permute-done | bytes 4718624 | tf_op jit(solution)/shard_map/ppermute | solution.py:756
  96.1 9.2 %lane_grads_add.1.refs_1_.refs_0_ = bf16[8,2,2,192,384]{4,3,2,1,0:T(8,128)(2,1)} custom-call(s32[1]{0:T(128)} %bitcast.2._.core_ref, bf16[640,3200]{1,0:T(8,128)(2,1)} %hold.10.grd_ref.hid_ref.flag_ref.refs_0_, bf16[640,3200]{1,0:T(8,128)(2,1)} %hold.10.grd_ref.hid_ref.flag_ref.refs_0_, bf16[640,3200]{1,0:T(8,128)(2,1)} %hold.10.grd_ref.hid_ref.flag_ref.refs_0_, ...), custom_call_target="tpu_custom_call" | custom-call | flops 8000000000 | bytes 8000000 | tf_op jit(solution)/shard_map/lane_grads_add/pallas_call | solution.py:543
  105.3 72.7 %all-to-all-done.1.refs_0_ = bf16[8,2,192,768]{3,2,1,0:T(8,128)(2,1)} async-done(((bf16[8,2,192,768]{3,2,1,0:T(8,128)(2,1)}), bf16[8,2,192,768]{3,2,1,0:T(8,128)(2,1)}, u32[]{:S(2)}, u32[]{:S(2)}) %all-to-all-start.1) | async-done | bytes 4718624 | tf_op jit(solution)/shard_map/all_to_all | solution.py:788
  178.0 4.7 %all-to-all-start.2 = ((bf16[16,2,192,384]{3,2,1,0:T(8,128)(2,1)}), bf16[16,2,192,384]{3,2,1,0:T(8,128)(2,1)}, u32[]{:S(2)}, u32[]{:S(2)}) async-start(bf16[16,2,192,384]{3,2,1,0:T(8,128)(2,1)} %bitcast.33), calls=%async_computation.2 | async-start | bytes 9437184 | tf_op jit(solution)/shard_map/all_to_all | solution.py:788
  183.9 6.7 %collective-permute-done.2.refs_1_ = f32[8,128]{1,0:T(8,128)S(1)} collective-permute-done((f32[8,128]{1,0:T(8,128)}, f32[8,128]{1,0:T(8,128)S(1)}, u32[]{:S(2)}, u32[]{:S(2)}) %collective-permute-start.2) | collective-permute-done | bytes 4128 | tf_op jit(solution)/shard_map/ppermute | solution.py:756
  191.1 20.3 %lane_products.1 = (bf16[80,3072]{1,0:T(8,128)(2,1)}, bf16[80,3072]{1,0:T(8,128)(2,1)}, bf16[80,3072]{1,0:T(8,128)(2,1)}, bf16[80,3072]{1,0:T(8,128)(2,1)}, bf16...) custom-call(s32[1]{0:T(128)} %bitcast.2._.core_ref, ...), custom_call_target="tpu_custom_call" | custom-call | flops 20000000000 | bytes 20000000 | tf_op jit(solution)/shard_map/lane_products/pallas_call | solution.py:497
  219.8 36.0 %collective-permute-done.4.refs_0_ = bf16[80,3072]{1,0:T(8,128)(2,1)S(1)} collective-permute-done((bf16[80,3072]{1,0:T(8,128)(2,1)}, bf16[80,3072]{1,0:T(8,128)(2,1)S(1)}, u32[]{:S(2)}, u32[]{:S(2)}) %collective-permute-start.4) | collective-permute-done | bytes 491552 | tf_op jit(solution)/shard_map/ppermute | solution.py:818
  258.3 18.8 %collective-permute-done.5.refs_1_ = bf16[80,3072]{1,0:T(8,128)(2,1)S(1)} collective-permute-done((bf16[80,3072]{1,0:T(8,128)(2,1)}, bf16[80,3072]{1,0:T(8,128)(2,1)S(1)}, u32[]{:S(2)}, u32[]{:S(2)}) %collective-permute-start.5) | collective-permute-done | bytes 491552 | tf_op jit(solution)/shard_map/ppermute | solution.py:818
  278.5 8.1 %coef_dots.1._ = f32[8,128]{1,0:T(8,128)} custom-call(s32[1]{0:T(128)} %bitcast.17.rep_ref, s32[32]{0:T(128)} %a.1, bf16[32,192,1536]{2,1,0:T(8,128)(2,1)} %src_ref.3, bf16[2,16,192,384]{3,2,1,0:T(8,128)(2,1)} %bitcast.16.got_ref.c), custom_call_target="tpu_custom_call" | custom-call | tf_op jit(solution)/shard_map/coef_dots/pallas_call | solution.py:715
  286.7 5.7 %finish.1.refs_7_ = f32[32,192,384]{2,1,0:T(8,128)} custom-call(s32[32]{0:T(128)} %a.1, f32[32]{0:T(128)} %b.1, bf16[2,16,192,384]{3,2,1,0:T(8,128)(2,1)} %bitcast.16.got_ref.c, f32[8,128]{1,0:T(8,128)} %coef_dots.1._), custom_call_target="tpu_custom_call" | custom-call | tf_op jit(solution)/shard_map/finish/pallas_call | solution.py:736
  292.4 5.8 %collective-permute-done.6.refs_2_ = bf16[80,3072]{1,0:T(8,128)(2,1)S(1)} collective-permute-done((bf16[80,3072]{1,0:T(8,128)(2,1)}, bf16[80,3072]{1,0:T(8,128)(2,1)S(1)}, u32[]{:S(2)}, u32[]{:S(2)}) %collective-permute-start.6) | collective-permute-done | bytes 491552 | tf_op jit(solution)/shard_map/ppermute | solution.py:818
  298.2 13.2 %collective-permute-done.7.refs_3_ = bf16[80,3072]{1,0:T(8,128)(2,1)S(1)} collective-permute-done((bf16[80,3072]{1,0:T(8,128)(2,1)}, bf16[80,3072]{1,0:T(8,128)(2,1)S(1)}, u32[]{:S(2)}, u32[]{:S(2)}) %collective-permute-start.7) | collective-permute-done | bytes 491552 | tf_op jit(solution)/shard_map/ppermute | solution.py:818
  311.3 8.6 %collective-permute-done.8.refs_4_ = bf16[80,3072]{1,0:T(8,128)(2,1)S(1)} collective-permute-done((bf16[80,3072]{1,0:T(8,128)(2,1)}, bf16[80,3072]{1,0:T(8,128)(2,1)S(1)}, u32[]{:S(2)}, u32[]{:S(2)}) %collective-permute-start.8) | collective-permute-done | bytes 491552 | tf_op jit(solution)/shard_map/ppermute | solution.py:818
  320.9 5.0 %combine.1 = (bf16[128,1536]{1,0:T(8,128)(2,1)}, bf16[2880,128]{1,0:T(8,128)(2,1)}, f32[32,1,3072]{2,1,0:T(1,128)}) custom-call(bf16[128,1536]{1,0:T(8,128)(2,1)} %bitcast.42, f32[8,128]{1,0:T(8,128)} %get-tuple-element.30.gate_ref, s32[8,128]{1,0:T(8,128)} %get-tuple-element.31.pos_ref, s32[4,128]{1,0:T(4,128)} %bitcast.46, bf16[32,2880]{1,0:T(8,128)(2,1)} %bitcast.44, ...), custom_call_target="tpu_custom_call" | custom-call | flops 5000000000 | bytes 5000000 | tf_op jit(solution)/shard_map/combine/pallas_call | solution.py:612
  325.8 5.0 %all-to-all-start.3 = ((f32[32,1,3072]{2,1,0:T(1,128)}), f32[32,1,3072]{2,1,0:T(1,128)S(1)}, u32[]{:S(2)}, u32[]{:S(2)}) async-start(f32[32,1,3072]{2,1,0:T(1,128)} %get-tuple-element.52), calls=%async_computation.3 | async-start | bytes 786432 | tf_op jit(solution)/shard_map/all_to_all | solution.py:788
  330.8 4.2 %unplace.1 = bf16[512,1536]{1,0:T(8,128)(2,1)} custom-call(s32[8,512]{1,0:T(8,128)} %get-tuple-element.50.slot_ref, bf16[80,3072]{1,0:T(8,128)(2,1)} %get-tuple-element.34.refs_0_, bf16[80,3072]{1,0:T(8,128)(2,1)} %get-tuple-element.42.refs_1_, bf16[80,3072]{1,0:T(8,128)(2,1)} %get-tuple-element.43.refs_2_, bf16[80,3072]{1,0:T(8,128)(2,1)} %get-tuple-element.44.refs_3_, ...), custom_call_target="tpu_custom_call" | custom-call | flops 4000000000 | bytes 4000000 | tf_op jit(solution)/shard_map/unplace/pallas_call | solution.py:639
  335.0 3.8 %reshape.68.refs_1_ = bf16[1,128,4,1536]{3,2,1,0:T(4,128)(2,1)} reshape(bf16[512,1536]{1,0:T(8,128)(2,1)} %unplace.1) | data formatting | bytes 3145728 | tf_op jit(solution)/shard_map/reshape | solution.py:829
  338.9 4.9 %all-to-all-done.3 = f32[32,1,3072]{2,1,0:T(1,128)S(1)} async-done(((f32[32,1,3072]{2,1,0:T(1,128)}), f32[32,1,3072]{2,1,0:T(1,128)S(1)}, u32[]{:S(2)}, u32[]{:S(2)}) %all-to-all-start.3) | async-done | bytes 393248 | tf_op jit(solution)/shard_map/all_to_all | solution.py:788
  345.6 15.9 %all_to_all.26 = f32[32,1,3200]{2,1,0:T(1,128)S(1)} all-to-all(f32[32,1,3200]{2,1,0:T(1,128)S(1)} %broadcast_in_dim.17), channel_id=1, replica_groups=mesh['half'=2,'place'=4,'row'=2,'core'=2] {'half','place','row','core'}, dimensions={0} | all-to-all | bytes 819200 | tf_op jit(solution)/shard_map/all_to_all | solution.py:788
  (57 shorter events, 24.9 us)
Async XLA Ops:
  70.3 107.7 %all-to-all-start.1 = ((bf16[8,2,192,768]{3,2,1,0:T(8,128)(2,1)}), bf16[8,2,192,768]{3,2,1,0:T(8,128)(2,1)}, u32[]{:S(2)}, u32[]{:S(2)}) async-start(bf16[8,2,192,768]{3,2,1,0:T(8,128)(2,1)} %hold.11), calls=%async_computation.1 | async-start | bytes 9437184 | tf_op jit(solution)/shard_map/all_to_all | solution.py:788
  75.5 1.4 collective-permute-start
  76.9 0.6 copy-start.6
  85.9 8.1 %collective-permute-start.1 = (bf16[8,2,2,192,384]{4,3,2,1,0:T(8,128)(2,1)}, bf16[8,2,2,192,384]{4,3,2,1,0:T(8,128)(2,1)S(1)}, u32[]{:S(2)}, u32[]{:S(2)}) collective-permute-start(bf16[8,2,2,192,384]{4,3,2,1,0:T(8,128)(2,1)} %lane_grads_first.1), channel_id=1, source_target_pairs={{0,1},{1,0},{2,3},{3,2},{4,5},{5,4},{6,7},{7,6},{8,9},{9,8},{10,11... | collective-permute-start | bytes 14155784 | tf_op jit(solution)/shard_map/ppermute | solution.py:756
  94.0 2.1 copy-start.8
  178.0 100.5 %all-to-all-start.2 = ((bf16[16,2,192,384]{3,2,1,0:T(8,128)(2,1)}), bf16[16,2,192,384]{3,2,1,0:T(8,128)(2,1)}, u32[]{:S(2)}, u32[]{:S(2)}) async-start(bf16[16,2,192,384]{3,2,1,0:T(8,128)(2,1)} %bitcast.33), calls=%async_computation.2 | async-start | bytes 9437184 | tf_op jit(solution)/shard_map/all_to_all | solution.py:788
  182.7 8.4 %collective-permute-start.3 = (bf16[8,2,192,768]{3,2,1,0:T(8,128)(2,1)}, bf16[8,2,192,768]{3,2,1,0:T(8,128)(2,1)}, u32[]{:S(2)}, u32[]{:S(2)}) collective-permute-start(bf16[8,2,192,768]{3,2,1,0:T(8,128)(2,1)} %hold.12.refs_1_.mine), channel_id=1, source_target_pairs={{0,1},{1,0},{2,3},{3,2},{4,5},{5,4},{6,7},{7,6},{8,9},{9,8},{10,11... | collective-permute-start | bytes 14155784 | tf_op jit(solution)/shard_map/ppermute | solution.py:756
  183.4 7.1 %collective-permute-start.2 = (f32[8,128]{1,0:T(8,128)}, f32[8,128]{1,0:T(8,128)S(1)}, u32[]{:S(2)}, u32[]{:S(2)}) collective-permute-start(f32[8,128]{1,0:T(8,128)} %hold.14), channel_id=1, source_target_pairs={{0,1},{1,0},{2,3},{3,2},{4,5},{5,4},{6,7},{7,6},{8,9},{9,8},{10,11... | collective-permute-start | bytes 12296 | tf_op jit(solution)/shard_map/ppermute | solution.py:756
  190.5 0.6 copy-start.7
  211.4 44.4 %collective-permute-start.4 = (bf16[80,3072]{1,0:T(8,128)(2,1)}, bf16[80,3072]{1,0:T(8,128)(2,1)S(1)}, u32[]{:S(2)}, u32[]{:S(2)}) collective-permute-start(bf16[80,3072]{1,0:T(8,128)(2,1)} %get-tuple-element.35), channel_id=1, source_target_pairs={{0,6},{2,4},{4,2},{6,0},{8,14},{10,12},{12,10},{14,8},{1,7},{3,5},... | collective-permute-start | bytes 1474568 | tf_op jit(solution)/shard_map/ppermute | solution.py:818
  214.0 63.1 %collective-permute-start.5 = (bf16[80,3072]{1,0:T(8,128)(2,1)}, bf16[80,3072]{1,0:T(8,128)(2,1)S(1)}, u32[]{:S(2)}, u32[]{:S(2)}) collective-permute-start(bf16[80,3072]{1,0:T(8,128)(2,1)} %get-tuple-element.36), channel_id=1, source_target_pairs={{0,8},{2,10},{4,12},{6,14},{8,0},{10,2},{12,4},{14,6},{1,9},{3,11}... | collective-permute-start | bytes 1474568 | tf_op jit(solution)/shard_map/ppermute | solution.py:818
  215.5 82.7 %collective-permute-start.6 = (bf16[80,3072]{1,0:T(8,128)(2,1)}, bf16[80,3072]{1,0:T(8,128)(2,1)S(1)}, u32[]{:S(2)}, u32[]{:S(2)}) collective-permute-start(bf16[80,3072]{1,0:T(8,128)(2,1)} %get-tuple-element.37), channel_id=1, source_target_pairs={{0,10},{2,8},{4,14},{6,12},{8,2},{10,0},{12,6},{14,4},{1,11},{3,9}... | collective-permute-start | bytes 1474568 | tf_op jit(solution)/shard_map/ppermute | solution.py:818
  216.0 95.3 %collective-permute-start.7 = (bf16[80,3072]{1,0:T(8,128)(2,1)}, bf16[80,3072]{1,0:T(8,128)(2,1)S(1)}, u32[]{:S(2)}, u32[]{:S(2)}) collective-permute-start(bf16[80,3072]{1,0:T(8,128)(2,1)} %get-tuple-element.38), channel_id=1, source_target_pairs={{0,12},{2,14},{4,8},{6,10},{8,4},{10,6},{12,0},{14,2},{1,13},{3,15... | collective-permute-start | bytes 1474568 | tf_op jit(solution)/shard_map/ppermute | solution.py:818
  217.5 102.4 %collective-permute-start.8 = (bf16[80,3072]{1,0:T(8,128)(2,1)}, bf16[80,3072]{1,0:T(8,128)(2,1)S(1)}, u32[]{:S(2)}, u32[]{:S(2)}) collective-permute-start(bf16[80,3072]{1,0:T(8,128)(2,1)} %get-tuple-element.39), channel_id=1, source_target_pairs={{0,14},{2,12},{4,10},{6,8},{8,6},{10,4},{12,2},{14,0},{1,15},{3,13... | collective-permute-start | bytes 1474568 | tf_op jit(solution)/shard_map/ppermute | solution.py:818
  255.9 30.8 %copy-start = (bf16[80,3072]{1,0:T(8,128)(2,1)}, bf16[80,3072]{1,0:T(8,128)(2,1)S(1)}, u32[]{:S(2)}) copy-start(bf16[80,3072]{1,0:T(8,128)(2,1)S(1)} %collective-permute-done.4.refs_0_) | copy-start | bytes 1474564
  255.9 64.1 %collective-permute-start.9 = (bf16[80,3072]{1,0:T(8,128)(2,1)}, bf16[80,3072]{1,0:T(8,128)(2,1)S(1)}, u32[]{:S(2)}, u32[]{:S(2)}) collective-permute-start(bf16[80,3072]{1,0:T(8,128)(2,1)} %get-tuple-element.40), channel_id=1, source_target_pairs={{0,4},{2,6},{4,0},{6,2},{8,12},{10,14},{12,8},{14,10},{1,5},{3,7},... | collective-permute-start | bytes 1474568 | tf_op jit(solution)/shard_map/ppermute | solution.py:818
  277.0 9.6 %copy-start.1 = (bf16[80,3072]{1,0:T(8,128)(2,1)}, bf16[80,3072]{1,0:T(8,128)(2,1)S(1)}, u32[]{:S(2)}) copy-start(bf16[80,3072]{1,0:T(8,128)(2,1)S(1)} %collective-permute-done.5.refs_1_) | copy-start | bytes 1474564
  277.1 42.9 %collective-permute-start.10 = (bf16[80,3072]{1,0:T(8,128)(2,1)}, bf16[80,3072]{1,0:T(8,128)(2,1)}, u32[]{:S(2)}, u32[]{:S(2)}) collective-permute-start(bf16[80,3072]{1,0:T(8,128)(2,1)} %get-tuple-element.41), channel_id=1, source_target_pairs={{0,2},{2,0},{4,6},{6,4},{8,10},{10,8},{12,14},{14,12},{1,3},{3,1},... | collective-permute-start | bytes 1474568 | tf_op jit(solution)/shard_map/ppermute | solution.py:818
  298.2 21.8 %copy-start.2 = (bf16[80,3072]{1,0:T(8,128)(2,1)}, bf16[80,3072]{1,0:T(8,128)(2,1)S(1)}, u32[]{:S(2)}) copy-start(bf16[80,3072]{1,0:T(8,128)(2,1)S(1)} %collective-permute-done.6.refs_2_) | copy-start | bytes 1474564
  311.3 8.6 %copy-start.3 = (bf16[80,3072]{1,0:T(8,128)(2,1)}, bf16[80,3072]{1,0:T(8,128)(2,1)S(1)}, u32[]{:S(2)}) copy-start(bf16[80,3072]{1,0:T(8,128)(2,1)S(1)} %collective-permute-done.7.refs_3_) | copy-start | bytes 1474564
  319.9 0.8 copy-start.4
  319.9 0.9 copy-start.5
  325.8 17.9 %all-to-all-start.3 = ((f32[32,1,3072]{2,1,0:T(1,128)}), f32[32,1,3072]{2,1,0:T(1,128)S(1)}, u32[]{:S(2)}, u32[]{:S(2)}) async-start(f32[32,1,3072]{2,1,0:T(1,128)} %get-tuple-element.52), calls=%async_computation.3 | async-start | bytes 786432 | tf_op jit(solution)/shard_map/all_to_all | solution.py:788
  330.8 13.2 %slice-start = ((f32[8,128]{1,0:T(8,128)}), f32[1,128]{1,0:T(1,128)S(1)}, s32[]{:S(2)}) async-start(f32[8,128]{1,0:T(8,128)} %coef_dots.1._), calls=%async_computation.5 | async-start | bytes 1024 | tf_op jit(solution)/shard_map/slice | solution.py:830
